TPU v7x, 128 devices: a whole 4x4x4 slice. The times are simulated.
128 devices in a mesh: gx: 8 (over x_lo, z), gy: 4 (over x_hi, core), gz: 4 (over y).
Axes of the slice: x: 4 (x_hi: 2, x_lo: 2; x = x_hi * 2 + x_lo), y: 4, z: 4, core: 2. Of those that a mesh axis runs over, the one named last changes fastest.
Arguments:
- implicit_source: float32 [2, 64, 128, 512], P(None, 'gz', 'gx', 'gy'), may hold values from -6 to 6
- capacity: float32 [2, 64, 128, 512], P(None, 'gz', 'gx', 'gy'), may hold values from 0.02 to 0.5
- transfer_coefficient: float32 [64, 128, 512], P('gz', 'gx', 'gy'), may hold values from 0.05 to 2
- observed_state_vector: float32 [2, 64, 128, 512], P(None, 'gz', 'gx', 'gy'), may hold values from -6 to 6
- soil_class: int32 [64, 128, 512], P('gz', 'gx', 'gy'), may hold values from 0 to 11
- conductivity: float32 [2, 12], replicated, may hold values from 0.2 to 4
- filter_rates: float32 [3, 2, 12], replicated, may hold values from 0.004 to 0.5
Outputs:
- predicted_state: float32 [2, 64, 128, 512], P(None, 'gz', 'gx', 'gy')
- analysis: float32 [2, 64, 128, 512], P(None, 'gz', 'gx', 'gy')
All inputs are finite; a program needn't handle non-finite values.
Results may differ from a plain program's by a relative error of at most 0.00002.
Values sent between devices are 32-bit elements; how exact they have to be, the bound alone decides.
No kernel may reach another device: no remote copies, remote signals or barrier semaphores. Data moves between devices by JAX's collectives and lax.ppermute only.
A program may use at most 64 MiB of HBM per device.

v0:
```python
import jax
import jax.numpy as jnp
from jax import lax
from jax.sharding import PartitionSpec as P

JACOBI_PASSES = 8


def shifted(value, axis, steps):
    count = lax.axis_size(axis)
    first, last = (max(0, -steps), min(count, count - steps))
    return lax.ppermute(value, axis, [(source, source + steps) for source in range(first, last)])


def lookup(table, classes):
    picked = jnp.zeros((table.shape[0],) + classes.shape, jnp.float32)
    for entry in range(table.shape[1]):
        picked = jnp.where((classes == entry)[None], table[:, entry][:, None, None, None], picked)
    return picked


def position_along(shape, axis_dim):
    return lax.broadcasted_iota(jnp.int32, shape, axis_dim)


def scan_local(retain, inflow, axis_dim, backward):
    length = retain.shape[axis_dim]
    position = position_along(retain.shape, axis_dim)
    factor, offset = (retain, inflow)
    stride = 1
    while stride < length:
        if backward:
            valid = position < length - stride
            moved_factor = jnp.roll(factor, -stride, axis_dim)
            moved_offset = jnp.roll(offset, -stride, axis_dim)
        else:
            valid = position >= stride
            moved_factor = jnp.roll(factor, stride, axis_dim)
            moved_offset = jnp.roll(offset, stride, axis_dim)
        new_factor = jnp.where(valid, moved_factor * factor, factor)
        new_offset = jnp.where(valid, factor * moved_offset + offset, offset)
        factor, offset = (new_factor, new_offset)
        stride = stride * 2
    return (factor, offset)


def edge_planes(values, axis_dim, axis_name):
    length = values.shape[axis_dim]
    last_plane = lax.slice_in_dim(values, length - 1, length, axis=axis_dim)
    first_plane = lax.slice_in_dim(values, 0, 1, axis=axis_dim)
    if axis_name == "gz":
        from_below = shifted(last_plane, "gz", 1)
        from_above = shifted(first_plane, "gz", -1)
    elif axis_name == "gx":
        from_below = shifted(last_plane, "gx", 1)
        from_above = shifted(first_plane, "gx", -1)
    else:
        from_below = shifted(last_plane, "gy", 1)
        from_above = shifted(first_plane, "gy", -1)
    return (from_below, from_above)


def neighbours_along(values, axis_dim, axis_name):
    length = values.shape[axis_dim]
    position = position_along(values.shape, axis_dim)
    from_below, from_above = edge_planes(values, axis_dim, axis_name)
    lower = jnp.where(position == 0, from_below, jnp.roll(values, 1, axis_dim))
    upper = jnp.where(position == length - 1, from_above, jnp.roll(values, -1, axis_dim))
    return lower + upper


def neighbour_total(values):
    summed = neighbours_along(values, 1, "gz")
    summed = summed + neighbours_along(values, 2, "gx")
    return summed + neighbours_along(values, 3, "gy")


def axis_length(axis_name):
    if axis_name == "gx":
        return lax.axis_size("gx")
    elif axis_name == "gy":
        return lax.axis_size("gy")
    return lax.axis_size("gz")


def carry_in(ends, axis_name, backward):
    step_by = -1 if backward else 1

    def advance(position, incoming):
        leaving = ends[0] * incoming + ends[1]
        if axis_name == "gx":
            return shifted(leaving, "gx", step_by)
        elif axis_name == "gy":
            return shifted(leaving, "gy", step_by)
        return shifted(leaving, "gz", step_by)

    return lax.fori_loop(0, axis_length(axis_name) - 1, advance, jnp.zeros_like(ends[1]))


def smooth_carried(values, weight_table, axis_dim, axis_name):
    retain = 1.0 - weight_table
    for backward in (False, True):
        edge = 0 if backward else values.shape[axis_dim] - 1
        for order_step in range(4):
            running, partial_value = scan_local(retain, weight_table * values, axis_dim, backward)
            ends = (
                jnp.take(running, edge, axis=axis_dim),
                jnp.take(partial_value, edge, axis=axis_dim),
            )
            incoming = carry_in(ends, axis_name, backward)
            values = partial_value + running * jnp.expand_dims(incoming, axis_dim)
    return values


def local(
    implicit_source,
    capacity,
    transfer_coefficient,
    observed_state_vector,
    soil_class,
    conductivity,
    filter_rates,
):
    hydraulic_transmissivity = lookup(conductivity, soil_class)
    principal_coefficients = capacity + 6.0 * hydraulic_transmissivity + transfer_coefficient[None]
    predicted_state = jnp.zeros_like(implicit_source)
    for repeat in range(JACOBI_PASSES):
        predicted_state = (
            implicit_source
            + hydraulic_transmissivity * neighbour_total(predicted_state)
            + transfer_coefficient[None] * predicted_state[::-1]
        ) / principal_coefficients
    wetness_correction = observed_state_vector - predicted_state
    rate_x = lookup(filter_rates[0], soil_class)
    wetness_correction = smooth_carried(wetness_correction, rate_x, 2, "gx")
    wetness_correction = smooth_carried(
        wetness_correction, lookup(filter_rates[1], soil_class), 3, "gy"
    )
    wetness_correction = smooth_carried(
        wetness_correction, lookup(filter_rates[2], soil_class), 1, "gz"
    )
    return (predicted_state, wetness_correction)


def solution(mesh):
    return jax.shard_map(
        local,
        mesh=mesh,
        in_specs=(
            P(None, "gz", "gx", "gy"),
            P(None, "gz", "gx", "gy"),
            P("gz", "gx", "gy"),
            P(None, "gz", "gx", "gy"),
            P("gz", "gx", "gy"),
            P(),
            P(),
        ),
        out_specs=(P(None, "gz", "gx", "gy"), P(None, "gz", "gx", "gy")),
        check_vma=False,
    )
```

profile of v0, /device:TPU:108, one launch (start us, length us, event | category | flops | bytes accessed | tf_op | source)
XLA Modules:
  0.0 1036.0 jit_solution(16668415004352309000)
XLA Ops:
  261.3 53.1 %while.246 = (s32[]{:T(128)}, f32[2,16,128]{2,1,0:T(8,128)S(1)}, f32[2,16,128]{2,1,0:T(8,128)S(1)}, f32[2,16,128]{2,1,0:T(8,128)S(1)}, s32[]{:T(128)}) while((s32[]{:T(128)}, f32[2,16,128]{2,1,0:T(8,128)S(1)}, f32[2,16,128]{2,1,0:T(8,128)S(1)}, f32[2,16,128]{2,1,0:T(8,128)S(1)}, s32[]{:T(128)}) %tuple.559), condition=%wide.region_1.3_spmd, body=%wide.region_0.2_spmd.sunk | while | flops 8194 | bytes 131173 | solution.py:97
  267.9 6.3 collective-permute-start
  275.7 6.3 collective-permute-start
  283.4 6.3 collective-permute-start
  291.2 6.3 collective-permute-start
  298.9 6.3 collective-permute-start
  306.7 6.3 collective-permute-start
  315.0 54.4 %while.247 = (s32[]{:T(128)}, f32[2,16,128]{2,1,0:T(8,128)S(1)}, f32[2,16,128]{2,1,0:T(8,128)S(1)}, f32[2,16,128]{2,1,0:T(8,128)S(1)}, s32[]{:T(128)}) while((s32[]{:T(128)}, f32[2,16,128]{2,1,0:T(8,128)S(1)}, f32[2,16,128]{2,1,0:T(8,128)S(1)}, f32[2,16,128]{2,1,0:T(8,128)S(1)}, s32[]{:T(128)}) %tuple.648), condition=%wide.region_3.5_spmd, body=%wide.region_2.4_spmd.sunk | while | flops 8194 | bytes 131173 | solution.py:97
  315.0 6.3 collective-permute-start.1
  322.8 6.3 collective-permute-start.1
  330.5 6.5 collective-permute-start.1
  338.4 6.3 collective-permute-start.1
  346.2 6.3 collective-permute-start.1
  353.9 6.3 collective-permute-start.1
  361.6 6.3 collective-permute-start.1
  370.0 54.3 %while.248 = (s32[]{:T(128)}, f32[2,16,128]{2,1,0:T(8,128)S(1)}, f32[2,16,128]{2,1,0:T(8,128)S(1)}, f32[2,16,128]{2,1,0:T(8,128)S(1)}, s32[]{:T(128)}) while((s32[]{:T(128)}, f32[2,16,128]{2,1,0:T(8,128)S(1)}, f32[2,16,128]{2,1,0:T(8,128)S(1)}, f32[2,16,128]{2,1,0:T(8,128)S(1)}, s32[]{:T(128)}) %tuple.649), condition=%wide.region_5.7_spmd, body=%wide.region_4.6_spmd.sunk | while | flops 8194 | bytes 131173 | solution.py:97
  370.0 6.3 collective-permute-start.2
  377.8 6.4 collective-permute-start.2
  385.6 6.3 collective-permute-start.2
  393.4 6.3 collective-permute-start.2
  401.1 6.3 collective-permute-start.2
  408.9 6.3 collective-permute-start.2
  416.6 6.3 collective-permute-start.2
  424.9 54.2 %while.249 = (s32[]{:T(128)}, f32[2,16,128]{2,1,0:T(8,128)S(1)}, f32[2,16,128]{2,1,0:T(8,128)S(1)}, f32[2,16,128]{2,1,0:T(8,128)S(1)}, s32[]{:T(128)}) while((s32[]{:T(128)}, f32[2,16,128]{2,1,0:T(8,128)S(1)}, f32[2,16,128]{2,1,0:T(8,128)S(1)}, f32[2,16,128]{2,1,0:T(8,128)S(1)}, s32[]{:T(128)}) %tuple.650), condition=%wide.region_7.9_spmd, body=%wide.region_6.8_spmd.sunk | while | flops 8194 | bytes 131173 | solution.py:97
  425.0 6.3 collective-permute-start.3
  432.7 6.3 collective-permute-start.3
  440.5 6.3 collective-permute-start.3
  448.2 6.3 collective-permute-start.3
  455.9 6.3 collective-permute-start.3
  463.7 6.3 collective-permute-start.3
  471.4 6.3 collective-permute-start.3
  482.3 54.5 %while.250 = (s32[]{:T(128)}, f32[2,16,128]{2,1,0:T(8,128)S(1)}, f32[2,16,128]{2,1,0:T(8,128)S(1)}, f32[2,16,128]{2,1,0:T(8,128)S(1)}, s32[]{:T(128)}) while((s32[]{:T(128)}, f32[2,16,128]{2,1,0:T(8,128)S(1)}, f32[2,16,128]{2,1,0:T(8,128)S(1)}, f32[2,16,128]{2,1,0:T(8,128)S(1)}, s32[]{:T(128)}) %tuple.571), condition=%wide.region_9.12_spmd, body=%wide.region_8.11_spmd.sunk | while | flops 8194 | bytes 131173 | solution.py:97
  484.2 6.1 collective-permute-done.4
  492.3 5.8 collective-permute-done.4
  500.0 5.8 collective-permute-done.4
  507.7 5.8 collective-permute-done.4
  515.5 5.8 collective-permute-done.4
  523.2 5.8 collective-permute-done.4
  530.9 5.8 collective-permute-done.4
  537.4 54.4 %while.251 = (s32[]{:T(128)}, f32[2,16,128]{2,1,0:T(8,128)S(1)}, f32[2,16,128]{2,1,0:T(8,128)S(1)}, f32[2,16,128]{2,1,0:T(8,128)S(1)}, s32[]{:T(128)}) while((s32[]{:T(128)}, f32[2,16,128]{2,1,0:T(8,128)S(1)}, f32[2,16,128]{2,1,0:T(8,128)S(1)}, f32[2,16,128]{2,1,0:T(8,128)S(1)}, s32[]{:T(128)}) %tuple.642), condition=%wide.region_11.14_spmd, body=%wide.region_10.13_spmd.sunk | while | flops 8194 | bytes 131173 | solution.py:97
  539.3 5.8 collective-permute-done.5
  547.1 5.8 collective-permute-done.5
  554.8 5.8 collective-permute-done.5
  562.5 6.0 collective-permute-done.5
  570.4 5.8 collective-permute-done.5
  592.3 54.3 %while.252 = (s32[]{:T(128)}, f32[2,16,128]{2,1,0:T(8,128)S(1)}, f32[2,16,128]{2,1,0:T(8,128)S(1)}, f32[2,16,128]{2,1,0:T(8,128)S(1)}, s32[]{:T(128)}) while((s32[]{:T(128)}, f32[2,16,128]{2,1,0:T(8,128)S(1)}, f32[2,16,128]{2,1,0:T(8,128)S(1)}, f32[2,16,128]{2,1,0:T(8,128)S(1)}, s32[]{:T(128)}) %tuple.643), condition=%wide.region_13.16_spmd, body=%wide.region_12.15_spmd.sunk | while | flops 8194 | bytes 131173 | solution.py:97
  609.8 6.0 collective-permute-done.6
  647.3 54.2 %while.253 = (s32[]{:T(128)}, f32[2,16,128]{2,1,0:T(8,128)S(1)}, f32[2,16,128]{2,1,0:T(8,128)S(1)}, f32[2,16,128]{2,1,0:T(8,128)S(1)}, s32[]{:T(128)}) while((s32[]{:T(128)}, f32[2,16,128]{2,1,0:T(8,128)S(1)}, f32[2,16,128]{2,1,0:T(8,128)S(1)}, f32[2,16,128]{2,1,0:T(8,128)S(1)}, s32[]{:T(128)}) %tuple.644), condition=%wide.region_15.18_spmd, body=%wide.region_14.17_spmd.sunk | while | flops 8194 | bytes 131173 | solution.py:97
  710.5 19.7 %while.254 = (s32[]{:T(128)}, f32[2,16,16]{2,1,0:T(8,128)S(1)}, f32[2,16,16]{2,1,0:T(8,128)S(1)}, f32[2,16,16]{2,1,0:T(8,128)S(1)}, s32[]{:T(128)}) while((s32[]{:T(128)}, f32[2,16,16]{2,1,0:T(8,128)S(1)}, f32[2,16,16]{2,1,0:T(8,128)S(1)}, f32[2,16,16]{2,1,0:T(8,128)S(1)}, s32[]{:T(128)}) %tuple.652), condition=%wide.region_17.21_spmd, body=%wide.region_16.20_spmd.sunk | while | flops 1026 | bytes 16485 | solution.py:97
  732.9 19.7 %while.255 = (s32[]{:T(128)}, f32[2,16,16]{2,1,0:T(8,128)S(1)}, f32[2,16,16]{2,1,0:T(8,128)S(1)}, f32[2,16,16]{2,1,0:T(8,128)S(1)}, s32[]{:T(128)}) while((s32[]{:T(128)}, f32[2,16,16]{2,1,0:T(8,128)S(1)}, f32[2,16,16]{2,1,0:T(8,128)S(1)}, f32[2,16,16]{2,1,0:T(8,128)S(1)}, s32[]{:T(128)}) %tuple.653), condition=%wide.region_19.23_spmd, body=%wide.region_18.22_spmd.sunk | while | flops 1026 | bytes 16485 | solution.py:97
  755.2 20.1 %while.256 = (s32[]{:T(128)}, f32[2,16,16]{2,1,0:T(8,128)S(1)}, f32[2,16,16]{2,1,0:T(8,128)S(1)}, f32[2,16,16]{2,1,0:T(8,128)S(1)}, s32[]{:T(128)}) while((s32[]{:T(128)}, f32[2,16,16]{2,1,0:T(8,128)S(1)}, f32[2,16,16]{2,1,0:T(8,128)S(1)}, f32[2,16,16]{2,1,0:T(8,128)S(1)}, s32[]{:T(128)}) %tuple.654), condition=%wide.region_21.25_spmd, body=%wide.region_20.24_spmd.sunk | while | flops 1026 | bytes 16485 | solution.py:97
  777.9 19.7 %while.257 = (s32[]{:T(128)}, f32[2,16,16]{2,1,0:T(8,128)S(1)}, f32[2,16,16]{2,1,0:T(8,128)S(1)}, f32[2,16,16]{2,1,0:T(8,128)S(1)}, s32[]{:T(128)}) while((s32[]{:T(128)}, f32[2,16,16]{2,1,0:T(8,128)S(1)}, f32[2,16,16]{2,1,0:T(8,128)S(1)}, f32[2,16,16]{2,1,0:T(8,128)S(1)}, s32[]{:T(128)}) %tuple.651), condition=%wide.region_23.27_spmd, body=%wide.region_22.26_spmd.sunk | while | flops 1026 | bytes 16485 | solution.py:97
  806.6 16.5 %while.258 = (s32[]{:T(128)}, f32[2,16,16]{2,1,0:T(8,128)S(1)}, f32[2,16,16]{2,1,0:T(8,128)S(1)}, f32[2,16,16]{2,1,0:T(8,128)S(1)}, s32[]{:T(128)}) while((s32[]{:T(128)}, f32[2,16,16]{2,1,0:T(8,128)S(1)}, f32[2,16,16]{2,1,0:T(8,128)S(1)}, f32[2,16,16]{2,1,0:T(8,128)S(1)}, s32[]{:T(128)}) %tuple.656), condition=%wide.region_25.30_spmd, body=%wide.region_24.29_spmd.sunk | while | flops 1026 | bytes 16485 | solution.py:97
  825.6 19.7 %while.259 = (s32[]{:T(128)}, f32[2,16,16]{2,1,0:T(8,128)S(1)}, f32[2,16,16]{2,1,0:T(8,128)S(1)}, f32[2,16,16]{2,1,0:T(8,128)S(1)}, s32[]{:T(128)}) while((s32[]{:T(128)}, f32[2,16,16]{2,1,0:T(8,128)S(1)}, f32[2,16,16]{2,1,0:T(8,128)S(1)}, f32[2,16,16]{2,1,0:T(8,128)S(1)}, s32[]{:T(128)}) %tuple.657), condition=%wide.region_27.32_spmd, body=%wide.region_26.31_spmd.sunk | while | flops 1026 | bytes 16485 | solution.py:97
  847.8 19.7 %while.260 = (s32[]{:T(128)}, f32[2,16,16]{2,1,0:T(8,128)S(1)}, f32[2,16,16]{2,1,0:T(8,128)S(1)}, f32[2,16,16]{2,1,0:T(8,128)S(1)}, s32[]{:T(128)}) while((s32[]{:T(128)}, f32[2,16,16]{2,1,0:T(8,128)S(1)}, f32[2,16,16]{2,1,0:T(8,128)S(1)}, f32[2,16,16]{2,1,0:T(8,128)S(1)}, s32[]{:T(128)}) %tuple.658), condition=%wide.region_29.34_spmd, body=%wide.region_28.33_spmd.sunk | while | flops 1026 | bytes 16485 | solution.py:97
  870.0 19.7 %while.261 = (s32[]{:T(128)}, f32[2,16,16]{2,1,0:T(8,128)S(1)}, f32[2,16,16]{2,1,0:T(8,128)S(1)}, f32[2,16,16]{2,1,0:T(8,128)S(1)}, s32[]{:T(128)}) while((s32[]{:T(128)}, f32[2,16,16]{2,1,0:T(8,128)S(1)}, f32[2,16,16]{2,1,0:T(8,128)S(1)}, f32[2,16,16]{2,1,0:T(8,128)S(1)}, s32[]{:T(128)}) %tuple.655), condition=%wide.region_31.36_spmd, body=%wide.region_30.35_spmd.sunk | while | flops 1026 | bytes 16485 | solution.py:97
  891.7 16.9 %while.262 = (s32[]{:T(128)}, f32[2,16,128]{2,1,0:T(8,128)S(1)}, f32[2,16,128]{2,1,0:T(8,128)S(1)}, f32[2,16,128]{2,1,0:T(8,128)S(1)}, s32[]{:T(128)}) while((s32[]{:T(128)}, f32[2,16,128]{2,1,0:T(8,128)S(1)}, f32[2,16,128]{2,1,0:T(8,128)S(1)}, f32[2,16,128]{2,1,0:T(8,128)S(1)}, s32[]{:T(128)}) %tuple.607), condition=%wide.region_33.39_spmd, body=%wide.region_32.38_spmd.sunk | while | flops 8194 | bytes 131173 | solution.py:97
  909.3 17.2 %while.263 = (s32[]{:T(128)}, f32[2,16,128]{2,1,0:T(8,128)S(1)}, f32[2,16,128]{2,1,0:T(8,128)S(1)}, f32[2,16,128]{2,1,0:T(8,128)S(1)}, s32[]{:T(128)}) while((s32[]{:T(128)}, f32[2,16,128]{2,1,0:T(8,128)S(1)}, f32[2,16,128]{2,1,0:T(8,128)S(1)}, f32[2,16,128]{2,1,0:T(8,128)S(1)}, s32[]{:T(128)}) %tuple.645), condition=%wide.region_35.41_spmd, body=%wide.region_34.40_spmd.sunk | while | flops 8194 | bytes 131173 | solution.py:97
  927.2 16.9 %while.264 = (s32[]{:T(128)}, f32[2,16,128]{2,1,0:T(8,128)S(1)}, f32[2,16,128]{2,1,0:T(8,128)S(1)}, f32[2,16,128]{2,1,0:T(8,128)S(1)}, s32[]{:T(128)}) while((s32[]{:T(128)}, f32[2,16,128]{2,1,0:T(8,128)S(1)}, f32[2,16,128]{2,1,0:T(8,128)S(1)}, f32[2,16,128]{2,1,0:T(8,128)S(1)}, s32[]{:T(128)}) %tuple.646), condition=%wide.region_37.43_spmd, body=%wide.region_36.42_spmd.sunk | while | flops 8194 | bytes 131173 | solution.py:97
  944.8 16.9 %while.265 = (s32[]{:T(128)}, f32[2,16,128]{2,1,0:T(8,128)S(1)}, f32[2,16,128]{2,1,0:T(8,128)S(1)}, f32[2,16,128]{2,1,0:T(8,128)S(1)}, s32[]{:T(128)}) while((s32[]{:T(128)}, f32[2,16,128]{2,1,0:T(8,128)S(1)}, f32[2,16,128]{2,1,0:T(8,128)S(1)}, f32[2,16,128]{2,1,0:T(8,128)S(1)}, s32[]{:T(128)}) %tuple.647), condition=%wide.region_39.45_spmd, body=%wide.region_38.44_spmd.sunk | while | flops 8194 | bytes 131173 | solution.py:97
  963.8 17.2 %while.266 = (s32[]{:T(128)}, f32[2,16,128]{2,1,0:T(8,128)S(1)}, f32[2,16,128]{2,1,0:T(8,128)S(1)}, f32[2,16,128]{2,1,0:T(8,128)S(1)}, s32[]{:T(128)}) while((s32[]{:T(128)}, f32[2,16,128]{2,1,0:T(8,128)S(1)}, f32[2,16,128]{2,1,0:T(8,128)S(1)}, f32[2,16,128]{2,1,0:T(8,128)S(1)}, s32[]{:T(128)}) %tuple.619), condition=%wide.region_41.48_spmd, body=%wide.region_40.47_spmd.sunk | while | flops 8194 | bytes 131173 | solution.py:97
  981.7 16.9 %while.267 = (s32[]{:T(128)}, f32[2,16,128]{2,1,0:T(8,128)S(1)}, f32[2,16,128]{2,1,0:T(8,128)S(1)}, f32[2,16,128]{2,1,0:T(8,128)S(1)}, s32[]{:T(128)}) while((s32[]{:T(128)}, f32[2,16,128]{2,1,0:T(8,128)S(1)}, f32[2,16,128]{2,1,0:T(8,128)S(1)}, f32[2,16,128]{2,1,0:T(8,128)S(1)}, s32[]{:T(128)}) %tuple.639), condition=%wide.region_43.50_spmd, body=%wide.region_42.49_spmd.sunk | while | flops 8194 | bytes 131173 | solution.py:97
  999.4 16.9 %while.268 = (s32[]{:T(128)}, f32[2,16,128]{2,1,0:T(8,128)S(1)}, f32[2,16,128]{2,1,0:T(8,128)S(1)}, f32[2,16,128]{2,1,0:T(8,128)S(1)}, s32[]{:T(128)}) while((s32[]{:T(128)}, f32[2,16,128]{2,1,0:T(8,128)S(1)}, f32[2,16,128]{2,1,0:T(8,128)S(1)}, f32[2,16,128]{2,1,0:T(8,128)S(1)}, s32[]{:T(128)}) %tuple.640), condition=%wide.region_45.52_spmd, body=%wide.region_44.51_spmd.sunk | while | flops 8194 | bytes 131173 | solution.py:97
  1017.1 16.9 %while.269 = (s32[]{:T(128)}, f32[2,16,128]{2,1,0:T(8,128)S(1)}, f32[2,16,128]{2,1,0:T(8,128)S(1)}, f32[2,16,128]{2,1,0:T(8,128)S(1)}, s32[]{:T(128)}) while((s32[]{:T(128)}, f32[2,16,128]{2,1,0:T(8,128)S(1)}, f32[2,16,128]{2,1,0:T(8,128)S(1)}, f32[2,16,128]{2,1,0:T(8,128)S(1)}, s32[]{:T(128)}) %tuple.641), condition=%wide.region_47.54_spmd, body=%wide.region_46.53_spmd.sunk | while | flops 8194 | bytes 131173 | solution.py:97
  (1040 shorter events, 782.1 us)
Async XLA Ops:
  0.6 36.1 %collective-permute-start.24 = (f32[2,1,16,128]{3,0,2,1:T(2,128)S(1)}, f32[2,1,16,128]{3,0,2,1:T(2,128)S(1)}, u32[]{:S(2)}, u32[]{:S(2)}) collective-permute-start(f32[2,1,16,128]{3,0,2,1:T(2,128)S(1)} %broadcast.271), channel_id=1, source_target_pairs={{0,1},{1,2},{2,3},{4,5},{5,6},{6,7},{8,9},{9,10},{10,11},{12,13},{... | collective-permute-start | bytes 49160 | tf_op jit(solution)/shard_map/ppermute | solution.py:12
  4.1 32.6 %collective-permute-start.25 = (f32[2,1,16,128]{3,0,2,1:T(2,128)S(1)}, f32[2,1,16,128]{3,0,2,1:T(2,128)S(1)}, u32[]{:S(2)}, u32[]{:S(2)}) collective-permute-start(f32[2,1,16,128]{3,0,2,1:T(2,128)S(1)} %broadcast.271), channel_id=1, source_target_pairs={{1,0},{2,1},{3,2},{5,4},{6,5},{7,6},{9,8},{10,9},{11,10},{13,12},{... | collective-permute-start | bytes 49160 | tf_op jit(solution)/shard_map/ppermute | solution.py:12
  6.5 30.2 %collective-permute-start.26 = (f32[2,16,1,128]{3,1,0,2:T(8,128)S(1)}, f32[2,16,1,128]{3,1,0,2:T(8,128)S(1)}, u32[]{:S(2)}, u32[]{:S(2)}) collective-permute-start(f32[2,16,1,128]{3,1,0,2:T(8,128)S(1)} %broadcast.273), channel_id=1, source_target_pairs={{0,16},{16,32},{32,48},{48,64},{64,80},{80,96},{96,112},{1,17},{17... | collective-permute-start | bytes 49160 | tf_op jit(solution)/shard_map/ppermute | solution.py:12
  8.5 21.9 %collective-permute-start.28 = (f32[2,16,16,1]{1,0,2,3:T(2,128)S(1)}, f32[2,16,16,1]{1,0,2,3:T(2,128)S(1)}, u32[]{:S(2)}, u32[]{:S(2)}) collective-permute-start(f32[2,16,16,1]{1,0,2,3:T(2,128)S(1)} %broadcast.275), channel_id=1, source_target_pairs={{0,4},{4,8},{8,12},{1,5},{5,9},{9,13},{2,6},{6,10},{10,14},{3,7},{... | collective-permute-start | bytes 6152 | tf_op jit(solution)/shard_map/ppermute | solution.py:12
  26.5 10.2 collective-permute-start.27
  39.2 18.7 %collective-permute-start.34 = (f32[2,16,16,1]{3,1,0,2:T(8,128)S(1)}, f32[2,16,16,1]{3,1,0,2:T(8,128)S(1)}, u32[]{:S(2)}, u32[]{:S(2)}) collective-permute-start(f32[2,16,16,1]{3,1,0,2:T(8,128)S(1)} %get-tuple-element.1171), channel_id=1, source_target_pairs={{0,4},{4,8},{8,12},{1,5},{5,9},{9,13},{2,6},{6,10},{10,14},{3,7},{... | collective-permute-start | bytes 6152 | tf_op jit(solution)/shard_map/ppermute | solution.py:12
  41.7 21.3 %collective-permute-start.35 = (f32[2,16,16,1]{3,1,0,2:T(8,128)S(1)}, f32[2,16,16,1]{3,1,0,2:T(8,128)}, u32[]{:S(2)}, u32[]{:S(2)}) collective-permute-start(f32[2,16,16,1]{3,1,0,2:T(8,128)S(1)} %get-tuple-element.1170), channel_id=1, source_target_pairs={{4,0},{8,4},{12,8},{5,1},{9,5},{13,9},{6,2},{10,6},{14,10},{7,3},{... | collective-permute-start | bytes 6152 | tf_op jit(solution)/shard_map/ppermute | solution.py:12
  46.9 18.0 %collective-permute-start.30 = (f32[2,1,16,128]{3,1,0,2:T(1,128)}, f32[2,1,16,128]{3,1,0,2:T(1,128)}, u32[]{:S(2)}, u32[]{:S(2)}) collective-permute-start(f32[2,1,16,128]{3,1,0,2:T(1,128)} %get-tuple-element.1179), channel_id=1, source_target_pairs={{0,1},{1,2},{2,3},{4,5},{5,6},{6,7},{8,9},{9,10},{10,11},{12,13},{... | collective-permute-start | bytes 49160 | tf_op jit(solution)/shard_map/ppermute | solution.py:12
  50.4 14.5 %collective-permute-start.31 = (f32[2,1,16,128]{3,1,0,2:T(1,128)}, f32[2,1,16,128]{3,1,0,2:T(1,128)}, u32[]{:S(2)}, u32[]{:S(2)}) collective-permute-start(f32[2,1,16,128]{3,1,0,2:T(1,128)} %get-tuple-element.1178), channel_id=1, source_target_pairs={{1,0},{2,1},{3,2},{5,4},{6,5},{7,6},{9,8},{10,9},{11,10},{13,12},{... | collective-permute-start | bytes 49160 | tf_op jit(solution)/shard_map/ppermute | solution.py:12
  53.3 11.6 %collective-permute-start.32 = (f32[2,16,1,128]{3,1,0,2:T(8,128)}, f32[2,16,1,128]{3,1,0,2:T(8,128)}, u32[]{:S(2)}, u32[]{:S(2)}) collective-permute-start(f32[2,16,1,128]{3,1,0,2:T(8,128)} %get-tuple-element.1175), channel_id=1, source_target_pairs={{0,16},{16,32},{32,48},{48,64},{64,80},{80,96},{96,112},{1,17},{17... | collective-permute-start | bytes 49160 | tf_op jit(solution)/shard_map/ppermute | solution.py:12
  58.0 8.1 collective-permute-start.33
  70.3 19.1 %collective-permute-start.40 = (f32[2,16,16,1]{3,1,0,2:T(8,128)S(1)}, f32[2,16,16,1]{3,1,0,2:T(8,128)S(1)}, u32[]{:S(2)}, u32[]{:S(2)}) collective-permute-start(f32[2,16,16,1]{3,1,0,2:T(8,128)S(1)} %get-tuple-element.1159), channel_id=1, source_target_pairs={{0,4},{4,8},{8,12},{1,5},{5,9},{9,13},{2,6},{6,10},{10,14},{3,7},{... | collective-permute-start | bytes 6152 | tf_op jit(solution)/shard_map/ppermute | solution.py:12
  72.8 21.6 %collective-permute-start.41 = (f32[2,16,16,1]{3,1,0,2:T(8,128)S(1)}, f32[2,16,16,1]{3,1,0,2:T(8,128)}, u32[]{:S(2)}, u32[]{:S(2)}) collective-permute-start(f32[2,16,16,1]{3,1,0,2:T(8,128)S(1)} %get-tuple-element.1158), channel_id=1, source_target_pairs={{4,0},{8,4},{12,8},{5,1},{9,5},{13,9},{6,2},{10,6},{14,10},{7,3},{... | collective-permute-start | bytes 6152 | tf_op jit(solution)/shard_map/ppermute | solution.py:12
  77.9 18.4 %collective-permute-start.36 = (f32[2,1,16,128]{3,1,0,2:T(1,128)}, f32[2,1,16,128]{3,1,0,2:T(1,128)}, u32[]{:S(2)}, u32[]{:S(2)}) collective-permute-start(f32[2,1,16,128]{3,1,0,2:T(1,128)} %get-tuple-element.1167), channel_id=1, source_target_pairs={{0,1},{1,2},{2,3},{4,5},{5,6},{6,7},{8,9},{9,10},{10,11},{12,13},{... | collective-permute-start | bytes 49160 | tf_op jit(solution)/shard_map/ppermute | solution.py:12
  80.9 15.5 %collective-permute-start.37 = (f32[2,1,16,128]{3,1,0,2:T(1,128)}, f32[2,1,16,128]{3,1,0,2:T(1,128)}, u32[]{:S(2)}, u32[]{:S(2)}) collective-permute-start(f32[2,1,16,128]{3,1,0,2:T(1,128)} %get-tuple-element.1166), channel_id=1, source_target_pairs={{1,0},{2,1},{3,2},{5,4},{6,5},{7,6},{9,8},{10,9},{11,10},{13,12},{... | collective-permute-start | bytes 49160 | tf_op jit(solution)/shard_map/ppermute | solution.py:12
  84.4 12.0 %collective-permute-start.38 = (f32[2,16,1,128]{3,1,0,2:T(8,128)}, f32[2,16,1,128]{3,1,0,2:T(8,128)}, u32[]{:S(2)}, u32[]{:S(2)}) collective-permute-start(f32[2,16,1,128]{3,1,0,2:T(8,128)} %get-tuple-element.1163), channel_id=1, source_target_pairs={{0,16},{16,32},{32,48},{48,64},{64,80},{80,96},{96,112},{1,17},{17... | collective-permute-start | bytes 49160 | tf_op jit(solution)/shard_map/ppermute | solution.py:12
  89.4 8.1 collective-permute-start.39
  101.7 19.1 %collective-permute-start.46 = (f32[2,16,16,1]{3,1,0,2:T(8,128)S(1)}, f32[2,16,16,1]{3,1,0,2:T(8,128)S(1)}, u32[]{:S(2)}, u32[]{:S(2)}) collective-permute-start(f32[2,16,16,1]{3,1,0,2:T(8,128)S(1)} %get-tuple-element.1147), channel_id=1, source_target_pairs={{0,4},{4,8},{8,12},{1,5},{5,9},{9,13},{2,6},{6,10},{10,14},{3,7},{... | collective-permute-start | bytes 6152 | tf_op jit(solution)/shard_map/ppermute | solution.py:12
  104.2 21.6 %collective-permute-start.47 = (f32[2,16,16,1]{3,1,0,2:T(8,128)S(1)}, f32[2,16,16,1]{3,1,0,2:T(8,128)}, u32[]{:S(2)}, u32[]{:S(2)}) collective-permute-start(f32[2,16,16,1]{3,1,0,2:T(8,128)S(1)} %get-tuple-element.1146), channel_id=1, source_target_pairs={{4,0},{8,4},{12,8},{5,1},{9,5},{13,9},{6,2},{10,6},{14,10},{7,3},{... | collective-permute-start | bytes 6152 | tf_op jit(solution)/shard_map/ppermute | solution.py:12
  109.4 18.4 %collective-permute-start.42 = (f32[2,1,16,128]{3,1,0,2:T(1,128)}, f32[2,1,16,128]{3,1,0,2:T(1,128)}, u32[]{:S(2)}, u32[]{:S(2)}) collective-permute-start(f32[2,1,16,128]{3,1,0,2:T(1,128)} %get-tuple-element.1155), channel_id=1, source_target_pairs={{0,1},{1,2},{2,3},{4,5},{5,6},{6,7},{8,9},{9,10},{10,11},{12,13},{... | collective-permute-start | bytes 49160 | tf_op jit(solution)/shard_map/ppermute | solution.py:12
  111.7 16.0 %collective-permute-start.43 = (f32[2,1,16,128]{3,1,0,2:T(1,128)}, f32[2,1,16,128]{3,1,0,2:T(1,128)}, u32[]{:S(2)}, u32[]{:S(2)}) collective-permute-start(f32[2,1,16,128]{3,1,0,2:T(1,128)} %get-tuple-element.1154), channel_id=1, source_target_pairs={{1,0},{2,1},{3,2},{5,4},{6,5},{7,6},{9,8},{10,9},{11,10},{13,12},{... | collective-permute-start | bytes 49160 | tf_op jit(solution)/shard_map/ppermute | solution.py:12
  115.8 12.0 %collective-permute-start.44 = (f32[2,16,1,128]{3,1,0,2:T(8,128)}, f32[2,16,1,128]{3,1,0,2:T(8,128)}, u32[]{:S(2)}, u32[]{:S(2)}) collective-permute-start(f32[2,16,1,128]{3,1,0,2:T(8,128)} %get-tuple-element.1151), channel_id=1, source_target_pairs={{0,16},{16,32},{32,48},{48,64},{64,80},{80,96},{96,112},{1,17},{17... | collective-permute-start | bytes 49160 | tf_op jit(solution)/shard_map/ppermute | solution.py:12
  120.8 8.1 collective-permute-start.45
  133.2 19.1 %collective-permute-start.52 = (f32[2,16,16,1]{3,1,0,2:T(8,128)S(1)}, f32[2,16,16,1]{3,1,0,2:T(8,128)S(1)}, u32[]{:S(2)}, u32[]{:S(2)}) collective-permute-start(f32[2,16,16,1]{3,1,0,2:T(8,128)S(1)} %get-tuple-element.1135), channel_id=1, source_target_pairs={{0,4},{4,8},{8,12},{1,5},{5,9},{9,13},{2,6},{6,10},{10,14},{3,7},{... | collective-permute-start | bytes 6152 | tf_op jit(solution)/shard_map/ppermute | solution.py:12
  135.7 21.8 %collective-permute-start.53 = (f32[2,16,16,1]{3,1,0,2:T(8,128)S(1)}, f32[2,16,16,1]{3,1,0,2:T(8,128)}, u32[]{:S(2)}, u32[]{:S(2)}) collective-permute-start(f32[2,16,16,1]{3,1,0,2:T(8,128)S(1)} %get-tuple-element.1134), channel_id=1, source_target_pairs={{4,0},{8,4},{12,8},{5,1},{9,5},{13,9},{6,2},{10,6},{14,10},{7,3},{... | collective-permute-start | bytes 6152 | tf_op jit(solution)/shard_map/ppermute | solution.py:12
  140.8 18.6 %collective-permute-start.48 = (f32[2,1,16,128]{3,1,0,2:T(1,128)}, f32[2,1,16,128]{3,1,0,2:T(1,128)}, u32[]{:S(2)}, u32[]{:S(2)}) collective-permute-start(f32[2,1,16,128]{3,1,0,2:T(1,128)} %get-tuple-element.1143), channel_id=1, source_target_pairs={{0,1},{1,2},{2,3},{4,5},{5,6},{6,7},{8,9},{9,10},{10,11},{12,13},{... | collective-permute-start | bytes 49160 | tf_op jit(solution)/shard_map/ppermute | solution.py:12
  143.0 16.4 %collective-permute-start.49 = (f32[2,1,16,128]{3,1,0,2:T(1,128)}, f32[2,1,16,128]{3,1,0,2:T(1,128)}, u32[]{:S(2)}, u32[]{:S(2)}) collective-permute-start(f32[2,1,16,128]{3,1,0,2:T(1,128)} %get-tuple-element.1142), channel_id=1, source_target_pairs={{1,0},{2,1},{3,2},{5,4},{6,5},{7,6},{9,8},{10,9},{11,10},{13,12},{... | collective-permute-start | bytes 49160 | tf_op jit(solution)/shard_map/ppermute | solution.py:12
  147.2 12.1 %collective-permute-start.50 = (f32[2,16,1,128]{3,1,0,2:T(8,128)}, f32[2,16,1,128]{3,1,0,2:T(8,128)}, u32[]{:S(2)}, u32[]{:S(2)}) collective-permute-start(f32[2,16,1,128]{3,1,0,2:T(8,128)} %get-tuple-element.1139), channel_id=1, source_target_pairs={{0,16},{16,32},{32,48},{48,64},{64,80},{80,96},{96,112},{1,17},{17... | collective-permute-start | bytes 49160 | tf_op jit(solution)/shard_map/ppermute | solution.py:12
  152.3 8.1 collective-permute-start.51
  164.6 19.3 %collective-permute-start.58 = (f32[2,16,16,1]{3,1,0,2:T(8,128)S(1)}, f32[2,16,16,1]{3,1,0,2:T(8,128)S(1)}, u32[]{:S(2)}, u32[]{:S(2)}) collective-permute-start(f32[2,16,16,1]{3,1,0,2:T(8,128)S(1)} %get-tuple-element.1123), channel_id=1, source_target_pairs={{0,4},{4,8},{8,12},{1,5},{5,9},{9,13},{2,6},{6,10},{10,14},{3,7},{... | collective-permute-start | bytes 6152 | tf_op jit(solution)/shard_map/ppermute | solution.py:12
  167.1 21.8 %collective-permute-start.59 = (f32[2,16,16,1]{3,1,0,2:T(8,128)S(1)}, f32[2,16,16,1]{3,1,0,2:T(8,128)}, u32[]{:S(2)}, u32[]{:S(2)}) collective-permute-start(f32[2,16,16,1]{3,1,0,2:T(8,128)S(1)} %get-tuple-element.1122), channel_id=1, source_target_pairs={{4,0},{8,4},{12,8},{5,1},{9,5},{13,9},{6,2},{10,6},{14,10},{7,3},{... | collective-permute-start | bytes 6152 | tf_op jit(solution)/shard_map/ppermute | solution.py:12
  172.2 18.6 %collective-permute-start.54 = (f32[2,1,16,128]{3,1,0,2:T(1,128)}, f32[2,1,16,128]{3,1,0,2:T(1,128)}, u32[]{:S(2)}, u32[]{:S(2)}) collective-permute-start(f32[2,1,16,128]{3,1,0,2:T(1,128)} %get-tuple-element.1131), channel_id=1, source_target_pairs={{0,1},{1,2},{2,3},{4,5},{5,6},{6,7},{8,9},{9,10},{10,11},{12,13},{... | collective-permute-start | bytes 49160 | tf_op jit(solution)/shard_map/ppermute | solution.py:12
  174.4 16.4 %collective-permute-start.55 = (f32[2,1,16,128]{3,1,0,2:T(1,128)}, f32[2,1,16,128]{3,1,0,2:T(1,128)}, u32[]{:S(2)}, u32[]{:S(2)}) collective-permute-start(f32[2,1,16,128]{3,1,0,2:T(1,128)} %get-tuple-element.1130), channel_id=1, source_target_pairs={{1,0},{2,1},{3,2},{5,4},{6,5},{7,6},{9,8},{10,9},{11,10},{13,12},{... | collective-permute-start | bytes 49160 | tf_op jit(solution)/shard_map/ppermute | solution.py:12
  178.7 12.1 %collective-permute-start.56 = (f32[2,16,1,128]{3,1,0,2:T(8,128)}, f32[2,16,1,128]{3,1,0,2:T(8,128)}, u32[]{:S(2)}, u32[]{:S(2)}) collective-permute-start(f32[2,16,1,128]{3,1,0,2:T(8,128)} %get-tuple-element.1127), channel_id=1, source_target_pairs={{0,16},{16,32},{32,48},{48,64},{64,80},{80,96},{96,112},{1,17},{17... | collective-permute-start | bytes 49160 | tf_op jit(solution)/shard_map/ppermute | solution.py:12
  183.9 8.1 collective-permute-start.57
  196.2 19.1 %collective-permute-start.64 = (f32[2,16,16,1]{3,1,0,2:T(8,128)S(1)}, f32[2,16,16,1]{3,1,0,2:T(8,128)S(1)}, u32[]{:S(2)}, u32[]{:S(2)}) collective-permute-start(f32[2,16,16,1]{3,1,0,2:T(8,128)S(1)} %get-tuple-element.1111), channel_id=1, source_target_pairs={{0,4},{4,8},{8,12},{1,5},{5,9},{9,13},{2,6},{6,10},{10,14},{3,7},{... | collective-permute-start | bytes 6152 | tf_op jit(solution)/shard_map/ppermute | solution.py:12
  198.7 21.6 %collective-permute-start.65 = (f32[2,16,16,1]{3,1,0,2:T(8,128)S(1)}, f32[2,16,16,1]{3,1,0,2:T(8,128)}, u32[]{:S(2)}, u32[]{:S(2)}) collective-permute-start(f32[2,16,16,1]{3,1,0,2:T(8,128)S(1)} %get-tuple-element.1110), channel_id=1, source_target_pairs={{4,0},{8,4},{12,8},{5,1},{9,5},{13,9},{6,2},{10,6},{14,10},{7,3},{... | collective-permute-start | bytes 6152 | tf_op jit(solution)/shard_map/ppermute | solution.py:12
  203.9 18.4 %collective-permute-start.60 = (f32[2,1,16,128]{3,1,0,2:T(1,128)}, f32[2,1,16,128]{3,1,0,2:T(1,128)}, u32[]{:S(2)}, u32[]{:S(2)}) collective-permute-start(f32[2,1,16,128]{3,1,0,2:T(1,128)} %get-tuple-element.1119), channel_id=1, source_target_pairs={{0,1},{1,2},{2,3},{4,5},{5,6},{6,7},{8,9},{9,10},{10,11},{12,13},{... | collective-permute-start | bytes 49160 | tf_op jit(solution)/shard_map/ppermute | solution.py:12
  206.1 16.2 %collective-permute-start.61 = (f32[2,1,16,128]{3,1,0,2:T(1,128)}, f32[2,1,16,128]{3,1,0,2:T(1,128)}, u32[]{:S(2)}, u32[]{:S(2)}) collective-permute-start(f32[2,1,16,128]{3,1,0,2:T(1,128)} %get-tuple-element.1118), channel_id=1, source_target_pairs={{1,0},{2,1},{3,2},{5,4},{6,5},{7,6},{9,8},{10,9},{11,10},{13,12},{... | collective-permute-start | bytes 49160 | tf_op jit(solution)/shard_map/ppermute | solution.py:12
  210.3 12.0 %collective-permute-start.62 = (f32[2,16,1,128]{3,1,0,2:T(8,128)}, f32[2,16,1,128]{3,1,0,2:T(8,128)}, u32[]{:S(2)}, u32[]{:S(2)}) collective-permute-start(f32[2,16,1,128]{3,1,0,2:T(8,128)} %get-tuple-element.1115), channel_id=1, source_target_pairs={{0,16},{16,32},{32,48},{48,64},{64,80},{80,96},{96,112},{1,17},{17... | collective-permute-start | bytes 49160 | tf_op jit(solution)/shard_map/ppermute | solution.py:12
  215.3 8.1 collective-permute-start.63
  227.6 19.1 %collective-permute-start.70 = (f32[2,16,16,1]{3,1,0,2:T(8,128)S(1)}, f32[2,16,16,1]{3,1,0,2:T(8,128)S(1)}, u32[]{:S(2)}, u32[]{:S(2)}) collective-permute-start(f32[2,16,16,1]{3,1,0,2:T(8,128)S(1)} %get-tuple-element.1104), channel_id=1, source_target_pairs={{0,4},{4,8},{8,12},{1,5},{5,9},{9,13},{2,6},{6,10},{10,14},{3,7},{... | collective-permute-start | bytes 6152 | tf_op jit(solution)/shard_map/ppermute | solution.py:12
  230.2 21.6 %collective-permute-start.71 = (f32[2,16,16,1]{3,1,0,2:T(8,128)S(1)}, f32[2,16,16,1]{3,1,0,2:T(8,128)}, u32[]{:S(2)}, u32[]{:S(2)}) collective-permute-start(f32[2,16,16,1]{3,1,0,2:T(8,128)S(1)} %get-tuple-element.1105), channel_id=1, source_target_pairs={{4,0},{8,4},{12,8},{5,1},{9,5},{13,9},{6,2},{10,6},{14,10},{7,3},{... | collective-permute-start | bytes 6152 | tf_op jit(solution)/shard_map/ppermute | solution.py:12
  235.3 18.4 %collective-permute-start.66 = (f32[2,1,16,128]{3,1,0,2:T(1,128)}, f32[2,1,16,128]{3,1,0,2:T(1,128)}, u32[]{:S(2)}, u32[]{:S(2)}) collective-permute-start(f32[2,1,16,128]{3,1,0,2:T(1,128)} %get-tuple-element.1096), channel_id=1, source_target_pairs={{0,1},{1,2},{2,3},{4,5},{5,6},{6,7},{8,9},{9,10},{10,11},{12,13},{... | collective-permute-start | bytes 49160 | tf_op jit(solution)/shard_map/ppermute | solution.py:12
  237.5 16.2 %collective-permute-start.67 = (f32[2,1,16,128]{3,1,0,2:T(1,128)}, f32[2,1,16,128]{3,1,0,2:T(1,128)}, u32[]{:S(2)}, u32[]{:S(2)}) collective-permute-start(f32[2,1,16,128]{3,1,0,2:T(1,128)} %get-tuple-element.1097), channel_id=1, source_target_pairs={{1,0},{2,1},{3,2},{5,4},{6,5},{7,6},{9,8},{10,9},{11,10},{13,12},{... | collective-permute-start | bytes 49160 | tf_op jit(solution)/shard_map/ppermute | solution.py:12
  241.7 12.0 %collective-permute-start.68 = (f32[2,16,1,128]{3,1,0,2:T(8,128)}, f32[2,16,1,128]{3,1,0,2:T(8,128)}, u32[]{:S(2)}, u32[]{:S(2)}) collective-permute-start(f32[2,16,1,128]{3,1,0,2:T(8,128)} %get-tuple-element.1100), channel_id=1, source_target_pairs={{0,16},{16,32},{32,48},{48,64},{64,80},{80,96},{96,112},{1,17},{17... | collective-permute-start | bytes 49160 | tf_op jit(solution)/shard_map/ppermute | solution.py:12
  246.8 8.1 collective-permute-start.69
  283.4 7.8 collective-permute-start
  291.2 7.7 collective-permute-start
  315.0 7.7 collective-permute-start.1
  330.5 7.9 collective-permute-start.1
  338.4 7.7 collective-permute-start.1
  353.9 7.7 collective-permute-start.1
  370.0 7.7 collective-permute-start.2
  377.8 7.9 collective-permute-start.2
  385.6 7.7 collective-permute-start.2
  401.1 7.7 collective-permute-start.2
  425.0 7.7 collective-permute-start.3
  482.3 8.0 collective-permute-start.4
  537.4 7.7 collective-permute-start.5
  560.6 7.9 collective-permute-start.5
  592.4 7.7 collective-permute-start.6
  607.9 7.9 collective-permute-start.6
  647.3 7.7 collective-permute-start.7
  (148 other events, 695.8 us)
where the time goes:
time: 1050 us; the launch traced here: 1040 us
  starting transfers between devices  524 us (50%)
  waiting for transfers between devices  367 us (35%)
  local copies, waits for them, and re-layouts  94.8 us (9%)
  other arithmetic  43.6 us (4%)
    ppermute x152, starting transfers between devices, shifted(): lax.ppermute(value, axis, [(source, source + steps) for source in range(f...  524 us
    ppermute x152, waiting for transfers between devices, shifted(): lax.ppermute(value, axis, [(source, source + steps) for source in range(f...  367 us
    unnamed x123, local copies, waits for them, and re-layouts  23 us
  transfers between devices with their start and end apart: 152, of which 112 were waited for; matrix products, arithmetic and copies ran while one was open for 5% of the time, Pallas kernels for 0%

commit v1 on v0

v1 whole, which is shorter than its diff:
```python
import jax
import jax.numpy as jnp
from jax import lax
from jax.experimental import pallas as pl
from jax.experimental.pallas import tpu as pltpu
from jax.sharding import PartitionSpec as P

SWEEPS = 8
DEEP = SWEEPS - 1
NEAR = DEEP - 1
CLASSES = 12
STEPS = 16
PLANES = STEPS + 2 * DEEP
F32 = jnp.float32
VMEM = pl.BlockSpec(memory_space=pltpu.VMEM)
SMEM = pl.BlockSpec(memory_space=pltpu.SMEM)


def call(body, outs, specs, scratch=(), flops=1000000):
    return pl.pallas_call(
        body,
        out_shape=[jax.ShapeDtypeStruct(shape, F32) for shape in outs],
        in_specs=specs,
        out_specs=[VMEM] * len(outs),
        scratch_shapes=[pltpu.VMEM(shape, F32) for shape in scratch],
        compiler_params=pltpu.CompilerParams(vmem_limit_bytes=40 * 1024 * 1024),
        cost_estimate=pl.CostEstimate(flops=flops, bytes_accessed=1000000, transcendentals=0),
    )


def picked(table, row, classes):
    value = jnp.full(classes.shape, table[row, 0], F32)
    for entry in range(1, CLASSES):
        value = jnp.where(classes == entry, table[row, entry], value)
    return value


def lanes(shape):
    return lax.broadcasted_iota(jnp.int32, shape, len(shape) - 1)


def first_mask(lane):
    return (lane % 14 < 7) & (lane < 84)


def last_mask(lane):
    return ((lane % 14 >= 7) & (lane < 70)) | (lane >= 121)


def coefficients_kernel(source, capacity, transfer, classes, conductivity, units, to_low, to_high, edges):
    def layer(z, _):
        transfer_z = transfer[z]
        classes_z = classes[z]
        lane = lanes(classes_z.shape)
        packed = jnp.zeros(classes_z.shape, F32)
        for f in range(2):
            conduct = picked(conductivity, f, classes_z)
            inverse = 1.0 / (capacity[f, z] + 6.0 * conduct + transfer_z)
            for unit, value in (
                (f, source[f, z] * inverse),
                (2 + f, conduct * inverse),
                (4 + f, transfer_z * inverse),
            ):
                units[unit, z] = value
                turned = pltpu.roll(value, 14 * unit, 1) if unit else value
                packed = jnp.where((lane - 14 * unit + 7 + 128) % 128 < 14, turned, packed)
        edges[z] = packed
        return 0

    lax.fori_loop(0, STEPS, layer, 0)

    def pair(z, _):
        upper, lower = (edges[z], edges[z + 8])
        lane = lanes(upper.shape)
        to_low[z] = jnp.where(first_mask(lane), upper, pltpu.roll(lower, 121, 1))
        to_high[z] = jnp.where(last_mask(lane), upper, pltpu.roll(lower, 7, 1))
        return 0

    lax.fori_loop(0, 8, pair, 0)


def face_rows():
    offset, rows = (0, [])
    for unit in range(7):
        count = DEEP if unit < 2 else NEAR
        rows.append((unit, offset, count))
        offset += count
    return rows, offset


def corner_rows():
    offset, rows = (0, [])
    for unit in range(7):
        for d in range(NEAR):
            count = NEAR - d if unit < 2 else NEAR - d - 1
            if count > 0:
                rows.append((unit, d, offset, count))
                offset += count
    return rows, -(-offset // 8) * 8


def halo_kernel(place, units, from_high, from_low, strips, z_low, z_high, x_low, x_high, ll, lh, hl, hh):
    has_low = place[1] > 0
    has_high = place[1] < place[4] - 1

    def pair(z, _):
        high = jnp.where(has_high, from_high[z], 0.0)
        low = jnp.where(has_low, from_low[z], 0.0)
        first = first_mask(lanes(high.shape))
        strips[z] = jnp.where(first, high, low)
        strips[z + 8] = jnp.where(first, pltpu.roll(high, 7, 1), pltpu.roll(low, 121, 1))
        return 0

    lax.fori_loop(0, 8, pair, 0)

    def read(unit, z, start, count):
        return strips[z, pl.ds(start, count)] if unit == 6 else units[unit, z, pl.ds(start, count)]

    for out, side in ((z_low, 0), (z_high, 1)):
        for d in range(DEEP):
            z = STEPS - 1 - d if side else d
            for unit in range(7):
                if d < NEAR:
                    out[unit * NEAR + d] = read(unit, z, 0, STEPS)
                elif unit < 2:
                    out[7 * NEAR + unit] = read(unit, z, 0, STEPS)

    def layer(z, _):
        for out, side in ((x_low, 0), (x_high, 1)):
            for unit, offset, count in face_rows()[0]:
                out[z, pl.ds(offset, count)] = read(unit, z, STEPS - count if side else 0, count)
        return 0

    lax.fori_loop(0, STEPS, layer, 0)
    for out, z_side, x_side in ((ll, 0, 0), (lh, 0, 1), (hl, 1, 0), (hh, 1, 1)):
        for unit, d, offset, count in corner_rows()[0]:
            z = STEPS - 1 - d if z_side else d
            out[pl.ds(offset, count)] = read(unit, z, STEPS - count if x_side else 0, count)


def forward(read_value, read_weight, state, write, count=4):
    for i in range(STEPS):
        for g in range(count):
            weight = read_weight(i, g)
            value = read_value(i, g)
            keep = 1.0 - weight
            for k in range(4):
                value = keep * state[g][k] + weight * value
                state[g][k] = value
            write(i, g, value)
    return state


def backward(read_value, read_weight, state, write, count=4):
    return forward(
        lambda i, g: read_value(STEPS - 1 - i, g),
        lambda i, g: read_weight(STEPS - 1 - i, g),
        state,
        lambda i, g, value: write(STEPS - 1 - i, g, value),
        count,
    )


def zeros(count=4):
    return [[jnp.zeros((8, 128), F32) for _ in range(4)] for _ in range(count)]


PAIRS = [(a, b) for a in range(4) for b in range(a, 4)]


def block_maps(read_weight, g):
    def step(i, carry):
        chain, sums = (list(carry[:4]), list(carry[4:]))
        weight = read_weight(i, g)
        keep = 1.0 - weight
        for k in range(1, 4):
            chain[k] = chain[k] + weight * chain[k - 1]
        scaled = [weight * value for value in chain]
        chain = [keep * value for value in chain]
        sums = [total + scaled[a] * chain[b] for total, (a, b) in zip(sums, PAIRS)]
        return tuple(chain + sums)

    zero = jnp.zeros((8, 128), F32)
    return lax.fori_loop(0, STEPS, step, (zero + 1.0,) + (zero,) * 13, unroll=4)


def pass_map(maps, state):
    return [sum(maps[k - m] * state[m] for m in range(k + 1)) for k in range(4)]


def coupling(maps, a, b):
    return maps[4 + PAIRS.index((min(a, b), max(a, b)))]


def couple(maps, state):
    return [sum(coupling(maps, k, 3 - m) * state[m] for m in range(4)) for k in range(4)]


def plus(left, right):
    return [a + b for a, b in zip(left, right)]


def chained(maps, ends, low, high):
    count = len(maps)
    lows = [low]
    for s in range(count):
        lows.append(plus(pass_map(maps[s], lows[s]), ends[s][:4]))
    highs = [high]
    for s in reversed(range(count)):
        highs.insert(0, plus(plus(pass_map(maps[s], highs[0]), couple(maps[s], lows[s])), ends[s][4:]))
    return lows, highs


def merged_maps(maps):
    chain, total = (list(maps[0][:4]), list(maps[0][4:]))
    for s in range(1, len(maps)):
        part = maps[s]
        half = [
            [sum(chain[i] * coupling(part, a - i, b) for i in range(a + 1)) for b in range(4)]
            for a in range(4)
        ]
        total = [
            value + sum(chain[j] * half[a][b - j] for j in range(b + 1))
            for value, (a, b) in zip(total, PAIRS)
        ]
        chain = [sum(part[k - m] * chain[m] for m in range(k + 1)) for k in range(4)]
    return chain + total


def maps_kernel(classes, rates, _, wx, wy, wz, mx, my, my_all, mz, by_x, turned):
    def by_layer(z, _):
        here = classes[z]
        for f in range(2):
            wz[f, z] = picked(rates, 4 + f, here)
        return 0

    lax.fori_loop(0, STEPS, by_layer, 0)

    def by_row(z, _):
        by_x[pl.ds(z, STEPS, stride=STEPS), :] = classes[z].astype(F32)
        return 0

    lax.fori_loop(0, STEPS, by_row, 0)

    def x_weights(i, _):
        here = by_x[pl.ds(pl.multiple_of(i * STEPS, 8), STEPS)]
        for f in range(2):
            wx[f, i] = picked(rates, f, here)
        return 0

    lax.fori_loop(0, STEPS, x_weights, 0)
    for h in range(2):
        turned[h] = by_x[128 * h : 128 * h + 128].T

    def y_weights(i, _):
        rows = pl.ds(pl.multiple_of(i * 8, 8), 8)
        for h in range(2):
            here = turned[h, rows]
            for f in range(2):
                wy[2 * f + h, rows] = picked(rates, 2 + f, here)
        return 0

    lax.fori_loop(0, STEPS, y_weights, 0)
    for g in range(4):
        part = pl.ds(8 * (g % 2), 8)
        for v, value in enumerate(block_maps(lambda i, g: wx[g // 2, i, part], g)):
            mx[v, pl.ds(8 * g, 8)] = value
        for v, value in enumerate(block_maps(lambda i, g: wz[g // 2, i, part], g)):
            mz[v, pl.ds(8 * g, 8)] = value
        for v, value in enumerate(block_maps(lambda i, g: wy[g, pl.ds(i, 8, stride=STEPS)], g)):
            my[v, pl.ds(8 * g, 8)] = value
    blocks = [[my[v, pl.ds(s, 4, stride=8)] for v in range(14)] for s in range(8)]
    for v, value in enumerate(merged_maps(blocks)):
        my_all[pl.ds(4 * v, 4)] = value


def sweep_kernel(
    place, units, strips, z_from_high, z_from_low, x_from_high, x_from_low, hh, hl, lh, ll, observed, wx, mx,
    predicted, increment, message,
    grid, side, even, odd, passed, ends,
):
    inside = slice(8, 8 + STEPS)
    has = {
        "x_low": place[0] > 0,
        "x_high": place[0] < place[3] - 1,
        "z_low": place[2] > 0,
        "z_high": place[2] < place[5] - 1,
    }

    def own(z, _):
        for unit in range(6):
            grid[unit, z + DEEP, inside] = units[unit, z]
        grid[6, z + DEEP, inside] = strips[z]
        for ref, name in ((x_from_high, "x_high"), (x_from_low, "x_low")):
            for unit, offset, count in face_rows()[0]:
                start = 8 + STEPS if name == "x_high" else 8 - count
                value = jnp.where(has[name], ref[z, pl.ds(offset, count)], 0.0)
                grid[unit, z + DEEP, pl.ds(start, count)] = value
        return 0

    lax.fori_loop(0, STEPS, own, 0)
    for ref, name in ((z_from_high, "z_high"), (z_from_low, "z_low")):
        for d in range(DEEP):
            z = DEEP + STEPS + d if name == "z_high" else DEEP - 1 - d
            for unit in range(7):
                if d < NEAR:
                    grid[unit, z, inside] = jnp.where(has[name], ref[unit * NEAR + d], 0.0)
                elif unit < 2:
                    grid[unit, z, inside] = jnp.where(has[name], ref[7 * NEAR + unit], 0.0)
    for ref, z_name, x_name in ((hh, "z_high", "x_high"), (hl, "z_high", "x_low"), (lh, "z_low", "x_high"), (ll, "z_low", "x_low")):
        valid = has[z_name] & has[x_name]
        for unit, d, offset, count in corner_rows()[0]:
            z = DEEP + STEPS + d if z_name == "z_high" else DEEP - 1 - d
            start = 8 + STEPS if x_name == "x_high" else 8 - count
            grid[unit, z, pl.ds(start, count)] = jnp.where(valid, ref[pl.ds(offset, count)], 0.0)

    def unpack(z, _):
        packed = grid[6, z]
        for unit in range(6):
            side[unit, z] = pltpu.roll(packed, 128 - 14 * unit, 1) if unit else packed
        return 0

    lax.fori_loop(0, PLANES, unpack, 0)

    def sweep(main_from, side_from, write):
        def layer(z, _):
            main = [main_from(f, z) for f in range(2)]
            edge = [side_from(f, z) for f in range(2)]
            lane = lanes(main[0].shape)
            new_main, new_edge = ([], [])
            for f in range(2):
                below = (pltpu.roll(main[f], 1, 1), pltpu.roll(edge[f], 1, 1))
                above = (pltpu.roll(main[f], 127, 1), pltpu.roll(edge[f], 127, 1))
                for i, (here, source) in enumerate(((main[f], main_from), (edge[f], side_from))):
                    total = source(f, z - 1) + source(f, z + 1)
                    total = total + (pltpu.roll(here, 1, 0) + pltpu.roll(here, 31, 0))
                    total = total + jnp.where(lane == 0, below[1 - i], below[i])
                    total = total + jnp.where(lane == 127, above[1 - i], above[i])
                    ref = side if i else grid
                    other = edge[1 - f] if i else main[1 - f]
                    new = ref[f, z] + ref[2 + f, z] * total + ref[4 + f, z] * other
                    (new_edge if i else new_main).append(new)
            write(z, new_main, new_edge)
            return 0

        return layer

    buffers = (even, odd)
    for s in range(2, SWEEPS + 1):
        reach = SWEEPS - s
        if s == 2:
            main_from, side_from = (lambda f, z: grid[f, z], lambda f, z: side[f, z])
        else:
            old = buffers[s % 2]
            main_from = lambda f, z, old=old: old[f, z]
            side_from = lambda f, z, old=old: old[2 + f, z]
        if s < SWEEPS:
            new = buffers[(s + 1) % 2]

            def write(z, new_main, new_edge, new=new):
                for f in range(2):
                    new[f, z] = new_main[f]
                    new[2 + f, z] = new_edge[f]
        else:

            def write(z, new_main, new_edge):
                for f in range(2):
                    value = new_main[f][inside]
                    predicted[f, z - DEEP] = value
                    change = observed[f, z - DEEP] - value
                    increment[f, pl.ds(z - DEEP, STEPS, stride=STEPS), :] = change

        lax.fori_loop(DEEP - reach, DEEP + STEPS + reach, sweep(main_from, side_from, write), 0)

    def weight(i, g):
        return wx[g // 2, i, pl.ds(8 * (g % 2), 8)]

    def put(i, g, value):
        passed[i, pl.ds(8 * g, 8)] = value

    def value(i, g):
        return increment[g // 2, pl.ds(STEPS * i + 8 * (g % 2), 8)]

    low = forward(value, weight, zeros(), put)
    high = backward(lambda i, g: passed[i, pl.ds(8 * g, 8)], weight, zeros(), lambda i, g, value: None)
    for g in range(4):
        for k in range(4):
            ends[k, pl.ds(8 * g, 8)] = low[g][k]
            ends[4 + k, pl.ds(8 * g, 8)] = high[g][k]
    for j in range(8):
        for v in range(22):
            rows = pl.ds(4 * j, 4)
            message[j, pl.ds(4 * v, 4)] = ends[v, rows] if v < 8 else mx[v - 8, rows]


def solve_kernel(gathered, inflow):
    parts = [[gathered[s, pl.ds(4 * v, 4)] for v in range(22)] for s in range(8)]
    zero = [jnp.zeros((4, 128), F32)] * 4
    lows, highs = chained([p[8:] for p in parts], [p[:8] for p in parts], zero, zero)
    for s in range(8):
        for k in range(4):
            inflow[s, pl.ds(4 * k, 4)] = lows[s][k]
            inflow[s, pl.ds(16 + 4 * k, 4)] = highs[s + 1][k]


def y_value(ref):
    return lambda i, g: ref[g, pl.ds(i, 8, stride=STEPS)]


def x_finish_kernel(increment, wx, inflow, wy, my, my_all, lines, ends, message, passed, start):
    for k in range(8):
        for j in range(8):
            start[k, pl.ds(4 * j, 4)] = inflow[j, pl.ds(4 * k, 4)]

    def weight(i, g):
        return wx[g // 2, i, pl.ds(8 * (g % 2), 8)]

    def value(i, g):
        return increment[g // 2, pl.ds(STEPS * i + 8 * (g % 2), 8)]

    def put(i, g, value):
        passed[g // 2, pl.ds(STEPS * i + 8 * (g % 2), 8)] = value

    def passed_value(i, g):
        return passed[g // 2, pl.ds(STEPS * i + 8 * (g % 2), 8)]

    low = [[start[k, pl.ds(8 * g, 8)] for k in range(4)] for g in range(4)]
    high = [[start[4 + k, pl.ds(8 * g, 8)] for k in range(4)] for g in range(4)]
    forward(value, weight, low, put)
    backward(passed_value, weight, high, put)
    for f in range(2):
        for h in range(2):
            lines[2 * f + h] = passed[f, pl.ds(128 * h, 128)].T

    def y_put(i, g, value):
        passed[g // 2, pl.ds(128 * (g % 2) + 8 * i, 8)] = value

    def y_passed(i, g):
        return passed[g // 2, pl.ds(128 * (g % 2) + 8 * i, 8)]

    low = forward(y_value(lines), y_value(wy), zeros(), y_put)
    high = backward(y_passed, y_value(wy), zeros(), lambda i, g, value: None)
    for g in range(4):
        for k in range(4):
            ends[k, pl.ds(8 * g, 8)] = low[g][k]
            ends[4 + k, pl.ds(8 * g, 8)] = high[g][k]
    maps = [[my[v, pl.ds(s, 4, stride=8)] for v in range(14)] for s in range(8)]
    block_ends = [[ends[v, pl.ds(s, 4, stride=8)] for v in range(8)] for s in range(8)]
    zero = [jnp.zeros((4, 128), F32)] * 4
    lows, highs = chained(maps, block_ends, zero, zero)
    for k in range(4):
        message[pl.ds(4 * k, 4)] = lows[8][k]
        message[pl.ds(16 + 4 * k, 4)] = highs[0][k]
    message[pl.ds(32, 56)] = my_all[...]


def own_inflow(position, count, maps, ends, zero):
    def keep(valid, state):
        return [jnp.where(valid, value, 0.0) for value in state]

    low = zero
    for s in range(count - 1, 0, -1):
        low = keep(position >= s, plus(pass_map(maps(s), low), ends(s)[:4]))
    right = [plus(pass_map(maps(0), low), ends(0)[:4])]
    for d in range(1, count - 1):
        right.append(plus(pass_map(maps(count - d), right[-1]), ends(count - d)[:4]))
    high = zero
    for d in range(count - 1, 0, -1):
        s = count - d
        state = plus(plus(pass_map(maps(s), high), couple(maps(s), right[d - 1])), ends(s)[4:])
        high = keep(position + d < count, state)
    return low, high


def y_finish_kernel(
    place, lines, wy, my, block_ends, own, back_1, back_2, back_3, wz, unsmoothed, message, passed, start, done, by_row
):
    refs = (own, back_1, back_2, back_3)
    low, high = own_inflow(
        place[1],
        4,
        lambda s: [refs[s][pl.ds(32 + 4 * v, 4)] for v in range(14)],
        lambda s: [refs[s][pl.ds(4 * v, 4)] for v in range(8)],
        [jnp.zeros((4, 128), F32)] * 4,
    )
    maps = [[my[v, pl.ds(s, 4, stride=8)] for v in range(14)] for s in range(8)]
    blocks = [[block_ends[v, pl.ds(s, 4, stride=8)] for v in range(8)] for s in range(8)]
    lows, highs = chained(maps, blocks, low, high)
    for s in range(8):
        for k in range(4):
            start[k, pl.ds(s, 4, stride=8), :] = lows[s][k]
            start[4 + k, pl.ds(s, 4, stride=8), :] = highs[s + 1][k]

    def put(i, g, value):
        passed[g // 2, pl.ds(128 * (g % 2) + 8 * i, 8)] = value

    def passed_value(i, g):
        return passed[g // 2, pl.ds(128 * (g % 2) + 8 * i, 8)]

    def put_line(i, g, value):
        done[g, pl.ds(i, 8, stride=STEPS), :] = value

    low = [[start[k, pl.ds(8 * g, 8)] for k in range(4)] for g in range(4)]
    high = [[start[4 + k, pl.ds(8 * g, 8)] for k in range(4)] for g in range(4)]
    forward(y_value(lines), y_value(wy), low, put)
    backward(passed_value, y_value(wy), high, put_line)
    for g in range(4):
        by_row[g // 2, pl.ds(128 * (g % 2), 128)] = done[g].T

    def value(i, g):
        return by_row[g // 2, pl.ds(i + 128 * (g % 2), 8, stride=STEPS)]

    def weight(i, g):
        return wz[g // 2, i, pl.ds(8 * (g % 2), 8)]

    for i in range(STEPS):
        for g in range(4):
            unsmoothed[g // 2, i, pl.ds(8 * (g % 2), 8)] = value(i, g)

    low = forward(value, weight, zeros(), put)
    high = backward(passed_value, weight, zeros(), lambda i, g, value: None)
    for g in range(4):
        for k in range(4):
            message[k, pl.ds(8 * g, 8)] = low[g][k]
            message[4 + k, pl.ds(8 * g, 8)] = high[g][k]


def z_finish_kernel(
    place, unsmoothed, wz, maps_0, maps_1, maps_2, maps_3, ends_0, ends_1, ends_2, ends_3, smoothed, passed
):
    maps = (maps_0, maps_1, maps_2, maps_3)
    ends = (ends_0, ends_1, ends_2, ends_3)
    lows, highs = ([], [])
    for g in range(4):
        rows = pl.ds(8 * g, 8)
        low, high = own_inflow(
            place[2],
            4,
            lambda s: [maps[s][v, rows] for v in range(14)],
            lambda s: [ends[s][v, rows] for v in range(8)],
            [jnp.zeros((8, 128), F32)] * 4,
        )
        lows.append(low)
        highs.append(high)

    def value(i, g):
        return unsmoothed[g // 2, i, pl.ds(8 * (g % 2), 8)]

    def weight(i, g):
        return wz[g // 2, i, pl.ds(8 * (g % 2), 8)]

    def put(i, g, value):
        passed[g // 2, i, pl.ds(8 * (g % 2), 8)] = value

    def put_last(i, g, value):
        smoothed[g // 2, i, pl.ds(8 * (g % 2), 8)] = value

    forward(value, weight, lows, put)
    backward(lambda i, g: passed[g // 2, i, pl.ds(8 * (g % 2), 8)], weight, highs, put_last)


def turned_by(value, axis, step):
    count = lax.axis_size(axis)
    return lax.ppermute(value, axis, [(i, (i + step) % count) for i in range(count)])


def turned_both(value, x_step, z_step):
    nx, nz = (lax.axis_size("gx"), lax.axis_size("gz"))
    moves = [
        (x * nz + z, (x + x_step) % nx * nz + (z + z_step) % nz) for x in range(nx) for z in range(nz)
    ]
    return lax.ppermute(value, ("gx", "gz"), moves)


def local(source, capacity, transfer, observed, classes, conductivity, filter_rates):
    axes = ("gx", "gy", "gz")
    place = jnp.stack([lax.axis_index(a) for a in axes] + [jnp.int32(lax.axis_size(a)) for a in axes])
    rates = filter_rates.reshape(6, CLASSES)
    plane = (STEPS, STEPS, 128)
    units, to_low, to_high, _ = call(
        coefficients_kernel, [(6,) + plane, (8, STEPS, 128), (8, STEPS, 128), plane], [VMEM] * 4 + [SMEM]
    )(source, capacity, transfer, classes, conductivity)
    from_high = turned_by(to_low, "gy", -1)
    from_low = turned_by(to_high, "gy", 1)

    z_face = (7 * NEAR + 2, STEPS, 128)
    x_face = (STEPS, face_rows()[1], 128)
    corner = (corner_rows()[1], 128)
    strips, z_low, z_high, x_low, x_high, ll, lh, hl, hh = call(
        halo_kernel, [plane, z_face, z_face, x_face, x_face] + [corner] * 4, [SMEM] + [VMEM] * 3
    )(place, units, from_high, from_low)
    z_from_high = turned_by(z_low, "gz", -1)
    z_from_low = turned_by(z_high, "gz", 1)
    x_from_high = turned_by(x_low, "gx", -1)
    x_from_low = turned_by(x_high, "gx", 1)
    from_hh = turned_both(ll, -1, -1)
    from_hl = turned_both(lh, 1, -1)
    from_lh = turned_both(hl, -1, 1)
    from_ll = turned_both(hh, 1, 1)

    rows = (32, 128)
    wx, wy, wz, mx, my, my_all, mz, _, _ = call(
        maps_kernel,
        [(2,) + plane, (4, 128, 128), (2,) + plane, (14,) + rows, (14,) + rows, (56, 128), (14,) + rows,
         (256, 128), (2, 128, 128)],
        [VMEM, SMEM, VMEM],
    )(classes, rates, ll)
    z_maps = [mz] + [turned_by(mz, "gz", s) for s in (1, 2, 3)]

    padded = (PLANES, 32, 128)
    predicted, increment, message = call(
        sweep_kernel,
        [(2,) + plane, (2, 256, 128), (8, 88, 128)],
        [SMEM] + [VMEM] * 13,
        [(7,) + padded, (6,) + padded, (4,) + padded, (4,) + padded, (STEPS,) + rows, (8,) + rows],
        flops=100000000,
    )(place, units, strips, z_from_high, z_from_low, x_from_high, x_from_low, from_hh, from_hl, from_lh, from_ll,
      observed, wx, mx)
    gathered = lax.all_to_all(message, "gx", 0, 0, tiled=True)
    inflow, = call(solve_kernel, [(8, 32, 128)], [VMEM])(gathered)
    inflow = lax.all_to_all(inflow, "gx", 0, 0, tiled=True)
    lines, block_ends, y_ends = call(
        x_finish_kernel,
        [(4, 128, 128), (8,) + rows, (88, 128)],
        [VMEM] * 6,
        [(2, 256, 128), (8,) + rows],
    )(increment, wx, inflow, wy, my, my_all)
    y_all = [y_ends] + [turned_by(y_ends, "gy", s) for s in (1, 2, 3)]
    unsmoothed, z_ends = call(
        y_finish_kernel,
        [(2,) + plane, (8,) + rows],
        [SMEM] + [VMEM] * 9,
        [(2, 256, 128), (8,) + rows, (4, 128, 128), (2, 256, 128)],
    )(place, lines, wy, my, block_ends, *y_all, wz)
    z_all = [z_ends] + [turned_by(z_ends, "gz", s) for s in (1, 2, 3)]
    smoothed, = call(z_finish_kernel, [(2,) + plane], [SMEM] + [VMEM] * 10, [(2,) + plane])(
        place, unsmoothed, wz, *z_maps, *z_all
    )
    return (predicted, smoothed)


def solution(mesh):
    cells = P(None, "gz", "gx", "gy")
    return jax.shard_map(
        local,
        mesh=mesh,
        in_specs=(cells, cells, P("gz", "gx", "gy"), cells, P("gz", "gx", "gy"), P(), P()),
        out_specs=(cells, cells),
        check_vma=False,
    )
```

time: 1050 us -> 127 us (0.12)
  the two profiles are of different devices: /device:TPU:108 before, /device:TPU:0 now
where the time goes in v1:
time: 127 us
  waiting for transfers between devices  49.5 us (39%)
  Pallas kernels  34.8 us (27%)
  starting transfers between devices  32.2 us (25%)
  local copies, waits for them, and re-layouts  9.57 us (8%)
    ppermute x4, waiting for transfers between devices, turned_both(): return lax.ppermute(value, ('gx', 'gz'), moves)  25.6 us
    ppermute x15, starting transfers between devices, turned_by(): lax.ppermute(value, axis, [(i, (i + step) % count) for i in range(count)])  22.6 us
    pallas_call x1, Pallas kernels, local(): call(sweep_kernel, [(2,) + plane, (2, 256, 128), (8, 88, 128)], [SMEM] +...  21 us
    ppermute x15, waiting for transfers between devices, turned_by(): lax.ppermute(value, axis, [(i, (i + step) % count) for i in range(count)])  14.2 us
    unnamed x36, local copies, waits for them, and re-layouts  9.48 us
    all_to_all x1, waiting for transfers between devices, local(): gathered = lax.all_to_all(message, 'gx', 0, 0, tiled=True)  5.85 us
    all_to_all x1, waiting for transfers between devices, local(): inflow = lax.all_to_all(inflow, 'gx', 0, 0, tiled=True)  3.89 us
    pallas_call x1, Pallas kernels, local(): call(maps_kernel, [(2,) + plane, (4, 128, 128), (2,) + plane, (14,) + row...  3.8 us
  transfers between devices with their start and end apart: 21, of which 13 were waited for; matrix products, arithmetic and copies ran while one was open for 0% of the time, Pallas kernels for 5%

profile of v1, /device:TPU:0, one launch (start us, length us, event | category | flops | bytes accessed | tf_op | source)
XLA Modules:
  0.0 126.9 jit_solution(8250525780012556418)
XLA Ops:
  0.6 0.0 copy-start
  0.6 0.9 copy-done
  1.5 0.9 copy-done.3
  2.5 0.9 copy-done.4
  3.4 0.9 copy-done.11
  4.3 0.7 copy-done.16
  5.0 3.3 %shard_map.86 = (f32[6,16,16,128]{3,2,1,0:T(8,128)S(1)}, f32[8,16,128]{2,1,0:T(8,128)S(1)}, f32[8,16,128]{2,1,0:T(8,128)S(1)}, f32[16,16,128]{2,1,0:T(8,128)}) custom-call(f32[2,16,16,128]{3,2,1,0:T(8,128)S(1)} %copy-done.3, f32[2,16,16,128]{3,2,1,0:T(8,128)S(1)} %copy-done.4, f32[16,16,128]{2,1,0:T(8,128)S(1)} %copy-done.11, s32[16,16,128]{2,1,0:T(8,128)S(1)} %copy-done, ...), custom_call_target="tpu_custom_call" | custom-call | flops 1000000 | bytes 1000000 | tf_op jit(solution)/shard_map/pallas_call | solution.py:580
  8.3 2.5 %collective-permute-start = (f32[8,16,128]{2,1,0:T(8,128)S(1)}, f32[8,16,128]{2,1,0:T(8,128)S(1)}, u32[]{:S(2)}, u32[]{:S(2)}) collective-permute-start(f32[8,16,128]{2,1,0:T(8,128)S(1)} %get-tuple-element.30), channel_id=1, source_target_pairs={{0,12},{4,0},{8,4},{12,8},{1,13},{5,1},{9,5},{13,9},{2,14},{6,2},{... | collective-permute-start | bytes 196616 | tf_op jit(solution)/shard_map/ppermute | solution.py:564
  10.9 0.0 collective-permute-start.1
  10.9 0.1 stack.15.place
  11.0 2.4 %collective-permute-done.from_high = f32[8,16,128]{2,1,0:T(8,128)S(1)} collective-permute-done((f32[8,16,128]{2,1,0:T(8,128)S(1)}, f32[8,16,128]{2,1,0:T(8,128)S(1)}, u32[]{:S(2)}, u32[]{:S(2)}) %collective-permute-start) | collective-permute-done | bytes 65568 | tf_op jit(solution)/shard_map/ppermute | solution.py:564
  13.4 2.7 %collective-permute-done.1.from_low = f32[8,16,128]{2,1,0:T(8,128)S(1)} collective-permute-done((f32[8,16,128]{2,1,0:T(8,128)S(1)}, f32[8,16,128]{2,1,0:T(8,128)S(1)}, u32[]{:S(2)}, u32[]{:S(2)}) %collective-permute-start.1) | collective-permute-done | bytes 65568 | tf_op jit(solution)/shard_map/ppermute | solution.py:564
  16.1 2.5 %shard_map.87 = (f32[16,16,128]{2,1,0:T(8,128)S(1)}, f32[44,16,128]{2,1,0:T(8,128)}, f32[44,16,128]{2,1,0:T(8,128)}, f32[16,44,128]{2,1,0:T(8,128)}, f32[16,44,1...) custom-call(s32[6]{0:T(128)S(1)} %stack.15.place, ...), custom_call_target="tpu_custom_call" | custom-call | flops 1000000 | bytes 1000000 | tf_op jit(solution)/shard_map/pallas_call | solution.py:589
  18.5 0.7 copy-done.9
  19.2 3.0 %collective-permute-start.2 = (f32[44,16,128]{2,1,0:T(8,128)}, f32[44,16,128]{2,1,0:T(8,128)S(1)}, u32[]{:S(2)}, u32[]{:S(2)}) collective-permute-start(f32[44,16,128]{2,1,0:T(8,128)} %get-tuple-element.33), channel_id=1, source_target_pairs={{0,3},{1,0},{2,1},{3,2},{4,7},{5,4},{6,5},{7,6},{8,11},{9,8},{10,9... | collective-permute-start | bytes 1081352 | tf_op jit(solution)/shard_map/ppermute | solution.py:564
  22.2 0.0 collective-permute-start.3
  22.2 4.1 %collective-permute-start.4 = (f32[16,44,128]{2,1,0:T(8,128)}, f32[16,44,128]{2,1,0:T(8,128)S(1)}, u32[]{:S(2)}, u32[]{:S(2)}) collective-permute-start(f32[16,44,128]{2,1,0:T(8,128)} %get-tuple-element.35), channel_id=1, source_target_pairs={{0,112},{16,0},{32,16},{48,32},{64,48},{80,64},{96,80},{112,96},{1... | collective-permute-start | bytes 1081352 | tf_op jit(solution)/shard_map/ppermute | solution.py:564
  26.3 0.0 collective-permute-start.5
  26.3 2.5 %collective-permute-start.7 = (f32[120,128]{1,0:T(8,128)S(1)}, f32[120,128]{1,0:T(8,128)S(1)}, u32[]{:S(2)}, u32[]{:S(2)}) collective-permute-start(f32[120,128]{1,0:T(8,128)S(1)} %get-tuple-element.38), channel_id=1, source_target_pairs={{0,19},{1,16},{2,17},{3,18},{16,35},{17,32},{18,33},{19,34},{32,51... | collective-permute-start | bytes 184328 | tf_op jit(solution)/shard_map/ppermute | solution.py:572
  28.8 10.0 %collective-permute-done.7.hl = f32[120,128]{1,0:T(8,128)S(1)} collective-permute-done((f32[120,128]{1,0:T(8,128)S(1)}, f32[120,128]{1,0:T(8,128)S(1)}, u32[]{:S(2)}, u32[]{:S(2)}) %collective-permute-start.7) | collective-permute-done | bytes 61472 | tf_op jit(solution)/shard_map/ppermute | solution.py:572
  38.9 0.0 collective-permute-start.8
  38.9 6.3 %collective-permute-done.8.lh = f32[120,128]{1,0:T(8,128)S(1)} collective-permute-done((f32[120,128]{1,0:T(8,128)S(1)}, f32[120,128]{1,0:T(8,128)S(1)}, u32[]{:S(2)}, u32[]{:S(2)}) %collective-permute-start.8) | collective-permute-done | bytes 61472 | tf_op jit(solution)/shard_map/ppermute | solution.py:572
  45.2 0.6 copy-done.12
  45.8 0.1 collective-permute-start.9
  45.9 8.4 %collective-permute-done.9.ll = f32[120,128]{1,0:T(8,128)S(1)} collective-permute-done((f32[120,128]{1,0:T(8,128)S(1)}, f32[120,128]{1,0:T(8,128)S(1)}, u32[]{:S(2)}, u32[]{:S(2)}) %collective-permute-start.9) | collective-permute-done | bytes 61472 | tf_op jit(solution)/shard_map/ppermute | solution.py:572
  54.3 0.6 copy-done.14
  54.9 0.0 collective-permute-start.6
  54.9 0.0 copy-start.10
  54.9 3.8 %shard_map.88 = (f32[2,16,16,128]{3,2,1,0:T(8,128)S(1)}, f32[4,128,128]{2,1,0:T(8,128)S(1)}, f32[2,16,16,128]{3,2,1,0:T(8,128)S(1)}, f32[14,32,128]{2,1,0:T(8,12...) custom-call(s32[16,16,128]{2,1,0:T(8,128)S(1)} %copy-done.1, ...), custom_call_target="tpu_custom_call" | custom-call | flops 1000000 | bytes 1000000 | tf_op jit(solution)/shard_map/pallas_call | solution.py:602
  58.7 0.7 copy-done.7
  59.4 0.9 collective-permute-done.6.hh
  60.3 0.0 collective-permute-done.2.z_from_high
  60.3 0.0 collective-permute-done.3.z_from_low
  60.3 0.0 collective-permute-done.4.x_from_high
  60.3 0.0 collective-permute-done.5.x_from_low
  60.4 0.0 copy-start.2
  60.4 0.9 copy-done.2
  61.3 0.8 copy-done.15
  62.1 21.0 %shard_map.89 = (f32[2,16,16,128]{3,2,1,0:T(8,128)}, f32[2,256,128]{2,1,0:T(8,128)S(1)}, f32[8,88,128]{2,1,0:T(8,128)}) custom-call(s32[6]{0:T(128)S(1)} %stack.15.place, f32[6,16,16,128]{3,2,1,0:T(8,128)S(1)} %get-tuple-element.29.units, f32[16,16,128]{2,1,0:T(8,128)S(1)} %copy-done.10, f32[44,16,128]{2,1,0:T(8,128)S(1)} %collective-permute-done.2.z_from_high, ...), custom_call_target="tpu_custom_call" | custom-call | flops 100000000 | bytes 1000000 | tf_op jit(solution)/shard_map/pallas_call | solution.py:611
  83.1 0.7 copy-done.5
  83.8 3.6 %all-to-all-start = ((f32[8,88,128]{2,1,0:T(8,128)}), f32[8,88,128]{2,1,0:T(8,128)S(1)}, u32[]{:S(2)}, u32[]{:S(2)}) async-start(f32[8,88,128]{2,1,0:T(8,128)} %get-tuple-element.45), calls=%async_computation | async-start | bytes 720896 | tf_op jit(solution)/shard_map/all_to_all | solution.py:619
  87.4 0.0 copy-start.6
  87.4 1.8 %collective-permute-start.15 = (f32[14,32,128]{2,1,0:T(8,128)S(1)}, f32[14,32,128]{2,1,0:T(8,128)S(1)}, u32[]{:S(2)}, u32[]{:S(2)}) collective-permute-start(f32[14,32,128]{2,1,0:T(8,128)S(1)} %copy-done.8), channel_id=1, source_target_pairs={{0,3},{1,0},{2,1},{3,2},{4,7},{5,4},{6,5},{7,6},{8,11},{9,8},{10,9... | collective-permute-start | bytes 688136 | tf_op jit(solution)/shard_map/ppermute | solution.py:564
  89.2 5.8 %all-to-all-done.gathered = f32[8,88,128]{2,1,0:T(8,128)S(1)} async-done(((f32[8,88,128]{2,1,0:T(8,128)}), f32[8,88,128]{2,1,0:T(8,128)S(1)}, u32[]{:S(2)}, u32[]{:S(2)}) %all-to-all-start) | async-done | bytes 360480 | tf_op jit(solution)/shard_map/all_to_all | solution.py:619
  95.0 0.7 shard_map.90
  95.8 3.4 %all-to-all-start.1 = ((f32[8,32,128]{2,1,0:T(8,128)}), f32[8,32,128]{2,1,0:T(8,128)S(1)}, u32[]{:S(2)}, u32[]{:S(2)}) async-start(f32[8,32,128]{2,1,0:T(8,128)} %shard_map.90), calls=%async_computation.1 | async-start | bytes 262144 | tf_op jit(solution)/shard_map/all_to_all | solution.py:621
  99.1 1.2 collective-permute-start.14
  100.4 1.4 %collective-permute-start.13 = (f32[14,32,128]{2,1,0:T(8,128)S(1)}, f32[14,32,128]{2,1,0:T(8,128)S(1)}, u32[]{:S(2)}, u32[]{:S(2)}) collective-permute-start(f32[14,32,128]{2,1,0:T(8,128)S(1)} %copy-done.8), channel_id=1, source_target_pairs={{0,1},{1,2},{2,3},{3,0},{4,5},{5,6},{6,7},{7,4},{8,9},{9,10},{10,1... | collective-permute-start | bytes 688136 | tf_op jit(solution)/shard_map/ppermute | solution.py:564
  101.8 3.9 %all-to-all-done.1.inflow = f32[8,32,128]{2,1,0:T(8,128)S(1)} async-done(((f32[8,32,128]{2,1,0:T(8,128)}), f32[8,32,128]{2,1,0:T(8,128)S(1)}, u32[]{:S(2)}, u32[]{:S(2)}) %all-to-all-start.1) | async-done | bytes 131104 | tf_op jit(solution)/shard_map/all_to_all | solution.py:621
  105.7 0.6 shard_map.91
  106.3 0.1 collective-permute-start.12
  106.4 3.3 %collective-permute-start.11 = (f32[88,128]{1,0:T(8,128)S(1)}, f32[88,128]{1,0:T(8,128)S(1)}, u32[]{:S(2)}, u32[]{:S(2)}) collective-permute-start(f32[88,128]{1,0:T(8,128)S(1)} %get-tuple-element.51.own), channel_id=1, source_target_pairs={{0,8},{4,12},{8,0},{12,4},{1,9},{5,13},{9,1},{13,5},{2,10},{6,14},... | collective-permute-start | bytes 135176 | tf_op jit(solution)/shard_map/ppermute | solution.py:564
  109.6 0.0 collective-permute-done.12.back_3
  109.6 2.1 %collective-permute-start.10 = (f32[88,128]{1,0:T(8,128)S(1)}, f32[88,128]{1,0:T(8,128)S(1)}, u32[]{:S(2)}, u32[]{:S(2)}) collective-permute-start(f32[88,128]{1,0:T(8,128)S(1)} %get-tuple-element.51.own), channel_id=1, source_target_pairs={{0,4},{4,8},{8,12},{12,0},{1,5},{5,9},{9,13},{13,1},{2,6},{6,10},{... | collective-permute-start | bytes 135176 | tf_op jit(solution)/shard_map/ppermute | solution.py:564
  111.8 0.7 collective-permute-done.11.back_2
  112.4 2.2 %collective-permute-done.10.back_1 = f32[88,128]{1,0:T(8,128)S(1)} collective-permute-done((f32[88,128]{1,0:T(8,128)S(1)}, f32[88,128]{1,0:T(8,128)S(1)}, u32[]{:S(2)}, u32[]{:S(2)}) %collective-permute-start.10) | collective-permute-done | bytes 45088 | tf_op jit(solution)/shard_map/ppermute | solution.py:564
  114.6 1.3 %shard_map.92 = (f32[2,16,16,128]{3,2,1,0:T(8,128)S(1)}, f32[8,32,128]{2,1,0:T(8,128)S(1)}) custom-call(s32[6]{0:T(128)S(1)} %stack.15.place, f32[4,128,128]{2,1,0:T(8,128)S(1)} %get-tuple-element.49.lines, f32[4,128,128]{2,1,0:T(8,128)S(1)} %get-tuple-element.46.wy, f32[14,32,128]{2,1,0:T(8,128)S(1)} %get-tuple-element.47.my, ...), custom_call_target="tpu_custom_call" | custom-call | flops 1000000 | bytes 1000000 | tf_op jit(solution)/shard_map/pallas_call | solution.py:629
  115.9 1.5 %collective-permute-start.18 = (f32[8,32,128]{2,1,0:T(8,128)S(1)}, f32[8,32,128]{2,1,0:T(8,128)S(1)}, u32[]{:S(2)}, u32[]{:S(2)}) collective-permute-start(f32[8,32,128]{2,1,0:T(8,128)S(1)} %get-tuple-element.55.ends_0), channel_id=1, source_target_pairs={{0,3},{1,0},{2,1},{3,2},{4,7},{5,4},{6,5},{7,6},{8,11},{9,8},{10,9... | collective-permute-start | bytes 393224 | tf_op jit(solution)/shard_map/ppermute | solution.py:564
  117.4 1.7 %collective-permute-start.17 = (f32[8,32,128]{2,1,0:T(8,128)S(1)}, f32[8,32,128]{2,1,0:T(8,128)S(1)}, u32[]{:S(2)}, u32[]{:S(2)}) collective-permute-start(f32[8,32,128]{2,1,0:T(8,128)S(1)} %get-tuple-element.55.ends_0), channel_id=1, source_target_pairs={{0,2},{1,3},{2,0},{3,1},{4,6},{5,7},{6,4},{7,5},{8,10},{9,11},{10,... | collective-permute-start | bytes 393224 | tf_op jit(solution)/shard_map/ppermute | solution.py:564
  119.0 0.0 collective-permute-done.13.maps_1
  119.0 2.1 %collective-permute-done.18.ends_3 = f32[8,32,128]{2,1,0:T(8,128)S(1)} collective-permute-done((f32[8,32,128]{2,1,0:T(8,128)S(1)}, f32[8,32,128]{2,1,0:T(8,128)S(1)}, u32[]{:S(2)}, u32[]{:S(2)}) %collective-permute-start.18) | collective-permute-done | bytes 131104 | tf_op jit(solution)/shard_map/ppermute | solution.py:564
  121.1 2.7 %collective-permute-done.17.ends_2 = f32[8,32,128]{2,1,0:T(8,128)S(1)} collective-permute-done((f32[8,32,128]{2,1,0:T(8,128)S(1)}, f32[8,32,128]{2,1,0:T(8,128)S(1)}, u32[]{:S(2)}, u32[]{:S(2)}) %collective-permute-start.17) | collective-permute-done | bytes 131104 | tf_op jit(solution)/shard_map/ppermute | solution.py:564
  123.8 1.4 %collective-permute-done.16.ends_1 = f32[8,32,128]{2,1,0:T(8,128)S(1)} collective-permute-done((f32[8,32,128]{2,1,0:T(8,128)S(1)}, f32[8,32,128]{2,1,0:T(8,128)S(1)}, u32[]{:S(2)}, u32[]{:S(2)}) %collective-permute-start.16) | collective-permute-done | bytes 131104 | tf_op jit(solution)/shard_map/ppermute | solution.py:564
  125.2 1.6 %shard_map.93 = f32[2,16,16,128]{3,2,1,0:T(8,128)} custom-call(s32[6]{0:T(128)S(1)} %stack.15.place, f32[2,16,16,128]{3,2,1,0:T(8,128)S(1)} %get-tuple-element.53.unsmoothed, f32[2,16,16,128]{3,2,1,0:T(8,128)S(1)} %get-tuple-element.52.wz, f32[14,32,128]{2,1,0:T(8,128)S(1)} %copy-done.8, f32[14,32,128]{2,1,0:T(8,128)S(1)} %collective-permute-done.13.maps_1, ...), custom_call_target="tpu_custom_call" | custom-call | flops 1000000 | bytes 1000000 | tf_op jit(solution)/shard_map/pallas_call | solution.py:636
  (25 shorter events, 0.1 us)
Async XLA Ops:
  0.6 0.9 copy-start
  1.5 0.9 copy-start.3
  2.5 0.9 copy-start.4
  3.4 0.9 copy-start.11
  4.3 0.7 copy-start.16
  8.3 5.0 %collective-permute-start = (f32[8,16,128]{2,1,0:T(8,128)S(1)}, f32[8,16,128]{2,1,0:T(8,128)S(1)}, u32[]{:S(2)}, u32[]{:S(2)}) collective-permute-start(f32[8,16,128]{2,1,0:T(8,128)S(1)} %get-tuple-element.30), channel_id=1, source_target_pairs={{0,12},{4,0},{8,4},{12,8},{1,13},{5,1},{9,5},{13,9},{2,14},{6,2},{... | collective-permute-start | bytes 196616 | tf_op jit(solution)/shard_map/ppermute | solution.py:564
  10.9 5.2 %collective-permute-start.1 = (f32[8,16,128]{2,1,0:T(8,128)S(1)}, f32[8,16,128]{2,1,0:T(8,128)S(1)}, u32[]{:S(2)}, u32[]{:S(2)}) collective-permute-start(f32[8,16,128]{2,1,0:T(8,128)S(1)} %get-tuple-element.31), channel_id=1, source_target_pairs={{0,4},{4,8},{8,12},{12,0},{1,5},{5,9},{9,13},{13,1},{2,6},{6,10},{... | collective-permute-start | bytes 196616 | tf_op jit(solution)/shard_map/ppermute | solution.py:564
  16.1 38.8 %copy-start.1 = (s32[16,16,128]{2,1,0:T(8,128)S(1)}, s32[16,16,128]{2,1,0:T(8,128)}, u32[]{:S(2)}) copy-start(s32[16,16,128]{2,1,0:T(8,128)} %classes.3) | copy-start | bytes 393220
  18.5 0.7 copy-start.9
  19.2 41.1 %collective-permute-start.2 = (f32[44,16,128]{2,1,0:T(8,128)}, f32[44,16,128]{2,1,0:T(8,128)S(1)}, u32[]{:S(2)}, u32[]{:S(2)}) collective-permute-start(f32[44,16,128]{2,1,0:T(8,128)} %get-tuple-element.33), channel_id=1, source_target_pairs={{0,3},{1,0},{2,1},{3,2},{4,7},{5,4},{6,5},{7,6},{8,11},{9,8},{10,9... | collective-permute-start | bytes 1081352 | tf_op jit(solution)/shard_map/ppermute | solution.py:564
  22.2 38.1 %collective-permute-start.3 = (f32[44,16,128]{2,1,0:T(8,128)}, f32[44,16,128]{2,1,0:T(8,128)S(1)}, u32[]{:S(2)}, u32[]{:S(2)}) collective-permute-start(f32[44,16,128]{2,1,0:T(8,128)} %get-tuple-element.34), channel_id=1, source_target_pairs={{0,1},{1,2},{2,3},{3,0},{4,5},{5,6},{6,7},{7,4},{8,9},{9,10},{10,1... | collective-permute-start | bytes 1081352 | tf_op jit(solution)/shard_map/ppermute | solution.py:564
  22.2 38.1 %collective-permute-start.4 = (f32[16,44,128]{2,1,0:T(8,128)}, f32[16,44,128]{2,1,0:T(8,128)S(1)}, u32[]{:S(2)}, u32[]{:S(2)}) collective-permute-start(f32[16,44,128]{2,1,0:T(8,128)} %get-tuple-element.35), channel_id=1, source_target_pairs={{0,112},{16,0},{32,16},{48,32},{64,48},{80,64},{96,80},{112,96},{1... | collective-permute-start | bytes 1081352 | tf_op jit(solution)/shard_map/ppermute | solution.py:564
  26.3 34.0 %collective-permute-start.5 = (f32[16,44,128]{2,1,0:T(8,128)}, f32[16,44,128]{2,1,0:T(8,128)S(1)}, u32[]{:S(2)}, u32[]{:S(2)}) collective-permute-start(f32[16,44,128]{2,1,0:T(8,128)} %get-tuple-element.36), channel_id=1, source_target_pairs={{0,16},{16,32},{32,48},{48,64},{64,80},{80,96},{96,112},{112,0},{1... | collective-permute-start | bytes 1081352 | tf_op jit(solution)/shard_map/ppermute | solution.py:564
  26.3 28.6 %copy-start.17 = (f32[3,2,12]{2,1,0:T(2,128)S(1)}, f32[3,2,12]{2,1,0:T(2,128)}, u32[]{:S(2)}) copy-start(f32[3,2,12]{2,1,0:T(2,128)} %param.13) | copy-start | bytes 868
  26.3 12.6 %collective-permute-start.7 = (f32[120,128]{1,0:T(8,128)S(1)}, f32[120,128]{1,0:T(8,128)S(1)}, u32[]{:S(2)}, u32[]{:S(2)}) collective-permute-start(f32[120,128]{1,0:T(8,128)S(1)} %get-tuple-element.38), channel_id=1, source_target_pairs={{0,19},{1,16},{2,17},{3,18},{16,35},{17,32},{18,33},{19,34},{32,51... | collective-permute-start | bytes 184328 | tf_op jit(solution)/shard_map/ppermute | solution.py:572
  38.9 6.3 %collective-permute-start.8 = (f32[120,128]{1,0:T(8,128)S(1)}, f32[120,128]{1,0:T(8,128)S(1)}, u32[]{:S(2)}, u32[]{:S(2)}) collective-permute-start(f32[120,128]{1,0:T(8,128)S(1)} %get-tuple-element.39), channel_id=1, source_target_pairs={{0,113},{1,114},{2,115},{3,112},{16,1},{17,2},{18,3},{19,0},{32,17... | collective-permute-start | bytes 184328 | tf_op jit(solution)/shard_map/ppermute | solution.py:572
  45.2 0.6 copy-start.12
  45.8 8.4 %collective-permute-start.9 = (f32[120,128]{1,0:T(8,128)S(1)}, f32[120,128]{1,0:T(8,128)S(1)}, u32[]{:S(2)}, u32[]{:S(2)}) collective-permute-start(f32[120,128]{1,0:T(8,128)S(1)} %get-tuple-element.40), channel_id=1, source_target_pairs={{0,17},{1,18},{2,19},{3,16},{16,33},{17,34},{18,35},{19,32},{32,49... | collective-permute-start | bytes 184328 | tf_op jit(solution)/shard_map/ppermute | solution.py:572
  54.3 0.6 copy-start.14
  54.9 5.4 %collective-permute-start.6 = (f32[120,128]{1,0:T(8,128)}, f32[120,128]{1,0:T(8,128)}, u32[]{:S(2)}, u32[]{:S(2)}) collective-permute-start(f32[120,128]{1,0:T(8,128)} %get-tuple-element.37._), channel_id=1, source_target_pairs={{0,115},{1,112},{2,113},{3,114},{16,3},{17,0},{18,1},{19,2},{32,19... | collective-permute-start | bytes 184328 | tf_op jit(solution)/shard_map/ppermute | solution.py:572
  54.9 5.4 %copy-start.10 = (f32[16,16,128]{2,1,0:T(8,128)S(1)}, f32[16,16,128]{2,1,0:T(8,128)}, u32[]{:S(2)}) copy-start(f32[16,16,128]{2,1,0:T(8,128)} %copy-done.9) | copy-start | bytes 393220
  54.9 5.4 %copy-start.13 = (f32[120,128]{1,0:T(8,128)S(1)}, f32[120,128]{1,0:T(8,128)}, u32[]{:S(2)}) copy-start(f32[120,128]{1,0:T(8,128)} %copy-done.12) | copy-start | bytes 184324
  58.7 0.7 copy-start.7
  60.4 1.0 copy-start.2
  61.3 0.8 copy-start.15
  83.1 0.7 copy-start.5
  83.8 3.6 %copy-start.8 = (f32[14,32,128]{2,1,0:T(8,128)S(1)}, f32[14,32,128]{2,1,0:T(8,128)}, u32[]{:S(2)}) copy-start(f32[14,32,128]{2,1,0:T(8,128)} %copy-done.7) | copy-start | bytes 688132
  83.8 11.2 %all-to-all-start = ((f32[8,88,128]{2,1,0:T(8,128)}), f32[8,88,128]{2,1,0:T(8,128)S(1)}, u32[]{:S(2)}, u32[]{:S(2)}) async-start(f32[8,88,128]{2,1,0:T(8,128)} %get-tuple-element.45), calls=%async_computation | async-start | bytes 720896 | tf_op jit(solution)/shard_map/all_to_all | solution.py:619
  87.4 18.3 %copy-start.6 = (f32[2,256,128]{2,1,0:T(8,128)S(1)}, f32[2,256,128]{2,1,0:T(8,128)}, u32[]{:S(2)}) copy-start(f32[2,256,128]{2,1,0:T(8,128)} %copy-done.5) | copy-start | bytes 786436
  87.4 31.6 %collective-permute-start.15 = (f32[14,32,128]{2,1,0:T(8,128)S(1)}, f32[14,32,128]{2,1,0:T(8,128)S(1)}, u32[]{:S(2)}, u32[]{:S(2)}) collective-permute-start(f32[14,32,128]{2,1,0:T(8,128)S(1)} %copy-done.8), channel_id=1, source_target_pairs={{0,3},{1,0},{2,1},{3,2},{4,7},{5,4},{6,5},{7,6},{8,11},{9,8},{10,9... | collective-permute-start | bytes 688136 | tf_op jit(solution)/shard_map/ppermute | solution.py:564
  95.8 9.9 %all-to-all-start.1 = ((f32[8,32,128]{2,1,0:T(8,128)}), f32[8,32,128]{2,1,0:T(8,128)S(1)}, u32[]{:S(2)}, u32[]{:S(2)}) async-start(f32[8,32,128]{2,1,0:T(8,128)} %shard_map.90), calls=%async_computation.1 | async-start | bytes 262144 | tf_op jit(solution)/shard_map/all_to_all | solution.py:621
  99.1 19.9 %collective-permute-start.14 = (f32[14,32,128]{2,1,0:T(8,128)S(1)}, f32[14,32,128]{2,1,0:T(8,128)S(1)}, u32[]{:S(2)}, u32[]{:S(2)}) collective-permute-start(f32[14,32,128]{2,1,0:T(8,128)S(1)} %copy-done.8), channel_id=1, source_target_pairs={{0,2},{1,3},{2,0},{3,1},{4,6},{5,7},{6,4},{7,5},{8,10},{9,11},{10,... | collective-permute-start | bytes 688136 | tf_op jit(solution)/shard_map/ppermute | solution.py:564
  100.4 18.6 %collective-permute-start.13 = (f32[14,32,128]{2,1,0:T(8,128)S(1)}, f32[14,32,128]{2,1,0:T(8,128)S(1)}, u32[]{:S(2)}, u32[]{:S(2)}) collective-permute-start(f32[14,32,128]{2,1,0:T(8,128)S(1)} %copy-done.8), channel_id=1, source_target_pairs={{0,1},{1,2},{2,3},{3,0},{4,5},{5,6},{6,7},{7,4},{8,9},{9,10},{10,1... | collective-permute-start | bytes 688136 | tf_op jit(solution)/shard_map/ppermute | solution.py:564
  106.3 3.3 %collective-permute-start.12 = (f32[88,128]{1,0:T(8,128)S(1)}, f32[88,128]{1,0:T(8,128)S(1)}, u32[]{:S(2)}, u32[]{:S(2)}) collective-permute-start(f32[88,128]{1,0:T(8,128)S(1)} %get-tuple-element.51.own), channel_id=1, source_target_pairs={{0,12},{4,0},{8,4},{12,8},{1,13},{5,1},{9,5},{13,9},{2,14},{6,2},{... | collective-permute-start | bytes 135176 | tf_op jit(solution)/shard_map/ppermute | solution.py:564
  106.4 6.1 %collective-permute-start.11 = (f32[88,128]{1,0:T(8,128)S(1)}, f32[88,128]{1,0:T(8,128)S(1)}, u32[]{:S(2)}, u32[]{:S(2)}) collective-permute-start(f32[88,128]{1,0:T(8,128)S(1)} %get-tuple-element.51.own), channel_id=1, source_target_pairs={{0,8},{4,12},{8,0},{12,4},{1,9},{5,13},{9,1},{13,5},{2,10},{6,14},... | collective-permute-start | bytes 135176 | tf_op jit(solution)/shard_map/ppermute | solution.py:564
  109.6 5.0 %collective-permute-start.10 = (f32[88,128]{1,0:T(8,128)S(1)}, f32[88,128]{1,0:T(8,128)S(1)}, u32[]{:S(2)}, u32[]{:S(2)}) collective-permute-start(f32[88,128]{1,0:T(8,128)S(1)} %get-tuple-element.51.own), channel_id=1, source_target_pairs={{0,4},{4,8},{8,12},{12,0},{1,5},{5,9},{9,13},{13,1},{2,6},{6,10},{... | collective-permute-start | bytes 135176 | tf_op jit(solution)/shard_map/ppermute | solution.py:564
  115.9 5.3 %collective-permute-start.18 = (f32[8,32,128]{2,1,0:T(8,128)S(1)}, f32[8,32,128]{2,1,0:T(8,128)S(1)}, u32[]{:S(2)}, u32[]{:S(2)}) collective-permute-start(f32[8,32,128]{2,1,0:T(8,128)S(1)} %get-tuple-element.55.ends_0), channel_id=1, source_target_pairs={{0,3},{1,0},{2,1},{3,2},{4,7},{5,4},{6,5},{7,6},{8,11},{9,8},{10,9... | collective-permute-start | bytes 393224 | tf_op jit(solution)/shard_map/ppermute | solution.py:564
  117.4 6.5 %collective-permute-start.17 = (f32[8,32,128]{2,1,0:T(8,128)S(1)}, f32[8,32,128]{2,1,0:T(8,128)S(1)}, u32[]{:S(2)}, u32[]{:S(2)}) collective-permute-start(f32[8,32,128]{2,1,0:T(8,128)S(1)} %get-tuple-element.55.ends_0), channel_id=1, source_target_pairs={{0,2},{1,3},{2,0},{3,1},{4,6},{5,7},{6,4},{7,5},{8,10},{9,11},{10,... | collective-permute-start | bytes 393224 | tf_op jit(solution)/shard_map/ppermute | solution.py:564
  119.0 6.2 %collective-permute-start.16 = (f32[8,32,128]{2,1,0:T(8,128)S(1)}, f32[8,32,128]{2,1,0:T(8,128)S(1)}, u32[]{:S(2)}, u32[]{:S(2)}) collective-permute-start(f32[8,32,128]{2,1,0:T(8,128)S(1)} %get-tuple-element.55.ends_0), channel_id=1, source_target_pairs={{0,1},{1,2},{2,3},{3,0},{4,5},{5,6},{6,7},{7,4},{8,9},{9,10},{10,1... | collective-permute-start | bytes 393224 | tf_op jit(solution)/shard_map/ppermute | solution.py:564

commit v2 on v1

--- a/solution.py
+++ b/solution.py
@@ -14,16 +14,20 @@
 F32 = jnp.float32
 VMEM = pl.BlockSpec(memory_space=pltpu.VMEM)
 SMEM = pl.BlockSpec(memory_space=pltpu.SMEM)
-
-
-def call(body, outs, specs, scratch=(), flops=1000000):
+HBM = pl.BlockSpec(memory_space=pltpu.HBM)
+
+
+def call(body, outs, specs, scratch=(), flops=1000000, limit=4, copies=0):
     return pl.pallas_call(
         body,
-        out_shape=[jax.ShapeDtypeStruct(shape, F32) for shape in outs],
+        out_shape=[shape if hasattr(shape, "dtype") else jax.ShapeDtypeStruct(shape, F32) for shape in outs],
         in_specs=specs,
         out_specs=[VMEM] * len(outs),
-        scratch_shapes=[pltpu.VMEM(shape, F32) for shape in scratch],
-        compiler_params=pltpu.CompilerParams(vmem_limit_bytes=40 * 1024 * 1024),
+        scratch_shapes=[
+            pltpu.VMEM(shape, F32) for shape in scratch
+        ]
+        + [pltpu.SemaphoreType.DMA((copies,))] * (copies > 0),
+        compiler_params=pltpu.CompilerParams(vmem_limit_bytes=limit * 1024 * 1024),
         cost_estimate=pl.CostEstimate(flops=flops, bytes_accessed=1000000, transcendentals=0),
     )
 
@@ -47,7 +51,34 @@
     return ((lane % 14 >= 7) & (lane < 70)) | (lane >= 121)
 
 
-def coefficients_kernel(source, capacity, transfer, classes, conductivity, units, to_low, to_high, edges):
+def by_pairs(place, axis, low, high):
+    is_even = place[axis] % 2 == 0
+    return jnp.where(is_even, high, low), jnp.where(is_even, low, high)
+
+
+def sides(place, axis, even, odd):
+    high, low = by_pairs(place, axis, odd, even)
+    return (
+        jnp.where(place[axis] > 0, low, 0.0),
+        jnp.where(place[axis] < place[axis + 3] - 1, high, 0.0),
+    )
+
+
+def brought(pairs, sems):
+    copies = [pltpu.make_async_copy(a, b, sems.at[i]) for i, (a, b) in enumerate(pairs)]
+    for copy in copies:
+        copy.start()
+    for copy in copies:
+        copy.wait()
+
+
+def coefficients_kernel(
+    place, source_in, capacity_in, transfer_in, classes_in, conductivity,
+    units, even, odd, classes,
+    edges, source, capacity, transfer, sems,
+):
+    brought(((source_in, source), (capacity_in, capacity), (transfer_in, transfer), (classes_in, classes)), sems)
+
     def layer(z, _):
         transfer_z = transfer[z]
         classes_z = classes[z]
@@ -67,16 +98,17 @@
         edges[z] = packed
         return 0
 
-    lax.fori_loop(0, STEPS, layer, 0)
+    lax.fori_loop(0, STEPS, layer, 0, unroll=4)
 
     def pair(z, _):
         upper, lower = (edges[z], edges[z + 8])
         lane = lanes(upper.shape)
-        to_low[z] = jnp.where(first_mask(lane), upper, pltpu.roll(lower, 121, 1))
-        to_high[z] = jnp.where(last_mask(lane), upper, pltpu.roll(lower, 7, 1))
-        return 0
-
-    lax.fori_loop(0, 8, pair, 0)
+        to_low = jnp.where(first_mask(lane), upper, pltpu.roll(lower, 121, 1))
+        to_high = jnp.where(last_mask(lane), upper, pltpu.roll(lower, 7, 1))
+        even[z], odd[z] = by_pairs(place, 1, to_low, to_high)
+        return 0
+
+    lax.fori_loop(0, 8, pair, 0, unroll=4)
 
 
 def face_rows():
@@ -99,43 +131,49 @@
     return rows, -(-offset // 8) * 8
 
 
-def halo_kernel(place, units, from_high, from_low, strips, z_low, z_high, x_low, x_high, ll, lh, hl, hh):
-    has_low = place[1] > 0
-    has_high = place[1] < place[4] - 1
-
+def halo_kernel(place, units, y_even, y_odd, strips, z_even, z_odd, x_even, x_odd):
     def pair(z, _):
-        high = jnp.where(has_high, from_high[z], 0.0)
-        low = jnp.where(has_low, from_low[z], 0.0)
+        low, high = sides(place, 1, y_even[z], y_odd[z])
         first = first_mask(lanes(high.shape))
         strips[z] = jnp.where(first, high, low)
         strips[z + 8] = jnp.where(first, pltpu.roll(high, 7, 1), pltpu.roll(low, 121, 1))
         return 0
 
-    lax.fori_loop(0, 8, pair, 0)
+    lax.fori_loop(0, 8, pair, 0, unroll=4)
 
     def read(unit, z, start, count):
         return strips[z, pl.ds(start, count)] if unit == 6 else units[unit, z, pl.ds(start, count)]
 
-    for out, side in ((z_low, 0), (z_high, 1)):
-        for d in range(DEEP):
-            z = STEPS - 1 - d if side else d
-            for unit in range(7):
-                if d < NEAR:
-                    out[unit * NEAR + d] = read(unit, z, 0, STEPS)
-                elif unit < 2:
-                    out[7 * NEAR + unit] = read(unit, z, 0, STEPS)
+    for d in range(DEEP):
+        for unit in range(7 if d < NEAR else 2):
+            at = unit * NEAR + d if d < NEAR else 7 * NEAR + unit
+            z_even[at], z_odd[at] = by_pairs(
+                place, 2, read(unit, d, 0, STEPS), read(unit, STEPS - 1 - d, 0, STEPS)
+            )
 
     def layer(z, _):
-        for out, side in ((x_low, 0), (x_high, 1)):
-            for unit, offset, count in face_rows()[0]:
-                out[z, pl.ds(offset, count)] = read(unit, z, STEPS - count if side else 0, count)
-        return 0
-
-    lax.fori_loop(0, STEPS, layer, 0)
-    for out, z_side, x_side in ((ll, 0, 0), (lh, 0, 1), (hl, 1, 0), (hh, 1, 1)):
-        for unit, d, offset, count in corner_rows()[0]:
-            z = STEPS - 1 - d if z_side else d
-            out[pl.ds(offset, count)] = read(unit, z, STEPS - count if x_side else 0, count)
+        for unit, offset, count in face_rows()[0]:
+            even, odd = by_pairs(place, 0, read(unit, z, 0, count), read(unit, z, STEPS - count, count))
+            x_even[z, pl.ds(offset, count)] = even
+            x_odd[z, pl.ds(offset, count)] = odd
+        return 0
+
+    lax.fori_loop(0, STEPS, layer, 0, unroll=2)
+
+
+def corner_kernel(place, x_even, x_odd, even, odd):
+    spans = {unit: (offset, count) for unit, offset, count in face_rows()[0]}
+    for unit, d, offset, count in corner_rows()[0]:
+        first, span = spans[unit]
+        ends = []
+        for z in (d, STEPS - 1 - d):
+            low = sides(place, 0, x_even[z, pl.ds(first + span - count, count)], x_odd[z, pl.ds(first + span - count, count)])[0]
+            high = sides(place, 0, x_even[z, pl.ds(first, count)], x_odd[z, pl.ds(first, count)])[1]
+            ends.append((low, high))
+        for x_side in range(2):
+            to_even, to_odd = by_pairs(place, 2, ends[0][x_side], ends[1][x_side])
+            even[x_side, pl.ds(offset, count)] = to_even
+            odd[x_side, pl.ds(offset, count)] = to_odd
 
 
 def forward(read_value, read_weight, state, write, count=4):
@@ -168,20 +206,24 @@
 PAIRS = [(a, b) for a in range(4) for b in range(a, 4)]
 
 
-def block_maps(read_weight, g):
-    def step(i, carry):
-        chain, sums = (list(carry[:4]), list(carry[4:]))
-        weight = read_weight(i, g)
-        keep = 1.0 - weight
-        for k in range(1, 4):
-            chain[k] = chain[k] + weight * chain[k - 1]
-        scaled = [weight * value for value in chain]
-        chain = [keep * value for value in chain]
-        sums = [total + scaled[a] * chain[b] for total, (a, b) in zip(sums, PAIRS)]
-        return tuple(chain + sums)
+def block_maps(read_weights):
+    def step(i, carries):
+        out = []
+        for read_weight, carry in zip(read_weights, carries):
+            chain, sums = (list(carry[:4]), list(carry[4:]))
+            weight = read_weight(i)
+            keep = 1.0 - weight
+            for k in range(1, 4):
+                chain[k] = chain[k] + weight * chain[k - 1]
+            scaled = [weight * value for value in chain]
+            chain = [keep * value for value in chain]
+            sums = [total + scaled[a] * chain[b] for total, (a, b) in zip(sums, PAIRS)]
+            out.append(tuple(chain + sums))
+        return tuple(out)
 
     zero = jnp.zeros((8, 128), F32)
-    return lax.fori_loop(0, STEPS, step, (zero + 1.0,) + (zero,) * 13, unroll=4)
+    start = (zero + 1.0,) + (zero,) * 13
+    return lax.fori_loop(0, STEPS, step, (start,) * len(read_weights), unroll=4)
 
 
 def pass_map(maps, state):
@@ -234,13 +276,13 @@
             wz[f, z] = picked(rates, 4 + f, here)
         return 0
 
-    lax.fori_loop(0, STEPS, by_layer, 0)
+    lax.fori_loop(0, STEPS, by_layer, 0, unroll=4)
 
     def by_row(z, _):
         by_x[pl.ds(z, STEPS, stride=STEPS), :] = classes[z].astype(F32)
         return 0
 
-    lax.fori_loop(0, STEPS, by_row, 0)
+    lax.fori_loop(0, STEPS, by_row, 0, unroll=4)
 
     def x_weights(i, _):
         here = by_x[pl.ds(pl.multiple_of(i * STEPS, 8), STEPS)]
@@ -248,7 +290,7 @@
             wx[f, i] = picked(rates, f, here)
         return 0
 
-    lax.fori_loop(0, STEPS, x_weights, 0)
+    lax.fori_loop(0, STEPS, x_weights, 0, unroll=4)
     for h in range(2):
         turned[h] = by_x[128 * h : 128 * h + 128].T
 
@@ -260,59 +302,53 @@
                 wy[2 * f + h, rows] = picked(rates, 2 + f, here)
         return 0
 
-    lax.fori_loop(0, STEPS, y_weights, 0)
+    lax.fori_loop(0, STEPS, y_weights, 0, unroll=4)
     for g in range(4):
         part = pl.ds(8 * (g % 2), 8)
-        for v, value in enumerate(block_maps(lambda i, g: wx[g // 2, i, part], g)):
-            mx[v, pl.ds(8 * g, 8)] = value
-        for v, value in enumerate(block_maps(lambda i, g: wz[g // 2, i, part], g)):
-            mz[v, pl.ds(8 * g, 8)] = value
-        for v, value in enumerate(block_maps(lambda i, g: wy[g, pl.ds(i, 8, stride=STEPS)], g)):
-            my[v, pl.ds(8 * g, 8)] = value
+        weights = (
+            lambda i, g=g: wx[g // 2, i, part],
+            lambda i, g=g: wz[g // 2, i, part],
+            lambda i, g=g: wy[g, pl.ds(i, 8, stride=STEPS)],
+        )
+        for out, maps in zip((mx, mz, my), block_maps(weights)):
+            for v in range(14):
+                out[v, pl.ds(8 * g, 8)] = maps[v]
     blocks = [[my[v, pl.ds(s, 4, stride=8)] for v in range(14)] for s in range(8)]
     for v, value in enumerate(merged_maps(blocks)):
         my_all[pl.ds(4 * v, 4)] = value
 
 
 def sweep_kernel(
-    place, units, strips, z_from_high, z_from_low, x_from_high, x_from_low, hh, hl, lh, ll, observed, wx, mx,
+    place, units, strips, z_even, z_odd, x_even, x_odd, corner_even, corner_odd, observed, wx, mx,
     predicted, increment, message,
     grid, side, even, odd, passed, ends,
 ):
     inside = slice(8, 8 + STEPS)
-    has = {
-        "x_low": place[0] > 0,
-        "x_high": place[0] < place[3] - 1,
-        "z_low": place[2] > 0,
-        "z_high": place[2] < place[5] - 1,
-    }
 
     def own(z, _):
         for unit in range(6):
             grid[unit, z + DEEP, inside] = units[unit, z]
         grid[6, z + DEEP, inside] = strips[z]
-        for ref, name in ((x_from_high, "x_high"), (x_from_low, "x_low")):
-            for unit, offset, count in face_rows()[0]:
-                start = 8 + STEPS if name == "x_high" else 8 - count
-                value = jnp.where(has[name], ref[z, pl.ds(offset, count)], 0.0)
-                grid[unit, z + DEEP, pl.ds(start, count)] = value
+        for unit, offset, count in face_rows()[0]:
+            rows = pl.ds(offset, count)
+            low, high = sides(place, 0, x_even[z, rows], x_odd[z, rows])
+            grid[unit, z + DEEP, pl.ds(8 - count, count)] = low
+            grid[unit, z + DEEP, pl.ds(8 + STEPS, count)] = high
         return 0
 
     lax.fori_loop(0, STEPS, own, 0)
-    for ref, name in ((z_from_high, "z_high"), (z_from_low, "z_low")):
-        for d in range(DEEP):
-            z = DEEP + STEPS + d if name == "z_high" else DEEP - 1 - d
-            for unit in range(7):
-                if d < NEAR:
-                    grid[unit, z, inside] = jnp.where(has[name], ref[unit * NEAR + d], 0.0)
-                elif unit < 2:
-                    grid[unit, z, inside] = jnp.where(has[name], ref[7 * NEAR + unit], 0.0)
-    for ref, z_name, x_name in ((hh, "z_high", "x_high"), (hl, "z_high", "x_low"), (lh, "z_low", "x_high"), (ll, "z_low", "x_low")):
-        valid = has[z_name] & has[x_name]
-        for unit, d, offset, count in corner_rows()[0]:
-            z = DEEP + STEPS + d if z_name == "z_high" else DEEP - 1 - d
-            start = 8 + STEPS if x_name == "x_high" else 8 - count
-            grid[unit, z, pl.ds(start, count)] = jnp.where(valid, ref[pl.ds(offset, count)], 0.0)
+    for d in range(DEEP):
+        for unit in range(7 if d < NEAR else 2):
+            at = unit * NEAR + d if d < NEAR else 7 * NEAR + unit
+            low, high = sides(place, 2, z_even[at], z_odd[at])
+            grid[unit, DEEP - 1 - d, inside] = low
+            grid[unit, DEEP + STEPS + d, inside] = high
+    for unit, d, offset, count in corner_rows()[0]:
+        rows = pl.ds(offset, count)
+        for x_side, start in enumerate((8 - count, 8 + STEPS)):
+            low, high = sides(place, 2, corner_even[x_side, rows], corner_odd[x_side, rows])
+            grid[unit, DEEP - 1 - d, pl.ds(start, count)] = low
+            grid[unit, DEEP + STEPS + d, pl.ds(start, count)] = high
 
     def unpack(z, _):
         packed = grid[6, z]
@@ -320,7 +356,7 @@
             side[unit, z] = pltpu.roll(packed, 128 - 14 * unit, 1) if unit else packed
         return 0
 
-    lax.fori_loop(0, PLANES, unpack, 0)
+    lax.fori_loop(0, PLANES, unpack, 0, unroll=5)
 
     def sweep(main_from, side_from, write):
         def layer(z, _):
@@ -370,7 +406,7 @@
                     change = observed[f, z - DEEP] - value
                     increment[f, pl.ds(z - DEEP, STEPS, stride=STEPS), :] = change
 
-        lax.fori_loop(DEEP - reach, DEEP + STEPS + reach, sweep(main_from, side_from, write), 0)
+        lax.fori_loop(DEEP - reach, DEEP + STEPS + reach, sweep(main_from, side_from, write), 0, unroll=8)
 
     def weight(i, g):
         return wx[g // 2, i, pl.ds(8 * (g % 2), 8)]
@@ -454,35 +490,47 @@
     message[pl.ds(32, 56)] = my_all[...]
 
 
-def own_inflow(position, count, maps, ends, zero):
-    def keep(valid, state):
-        return [jnp.where(valid, value, 0.0) for value in state]
-
-    low = zero
-    for s in range(count - 1, 0, -1):
-        low = keep(position >= s, plus(pass_map(maps(s), low), ends(s)[:4]))
-    right = [plus(pass_map(maps(0), low), ends(0)[:4])]
-    for d in range(1, count - 1):
-        right.append(plus(pass_map(maps(count - d), right[-1]), ends(count - d)[:4]))
-    high = zero
-    for d in range(count - 1, 0, -1):
-        s = count - d
-        state = plus(plus(pass_map(maps(s), high), couple(maps(s), right[d - 1])), ends(s)[4:])
-        high = keep(position + d < count, state)
-    return low, high
+def own_inflow(position, count, maps, ends, zero, write):
+    for p in range(count):
+
+        @pl.when(position == p)
+        def _(p=p):
+            low = zero
+            for j in range(p):
+                low = plus(pass_map(maps(j ^ p), low), ends(j ^ p)[:4])
+            inflow, lows = (low, [])
+            for j in range(p, count):
+                lows.append(inflow)
+                if j < count - 1:
+                    inflow = plus(pass_map(maps(j ^ p), inflow), ends(j ^ p)[:4])
+            high = zero
+            for j in range(count - 1, p, -1):
+                coupled = couple(maps(j ^ p), lows[j - p])
+                high = plus(plus(pass_map(maps(j ^ p), high), coupled), ends(j ^ p)[4:])
+            write(low, high)
 
 
 def y_finish_kernel(
-    place, lines, wy, my, block_ends, own, back_1, back_2, back_3, wz, unsmoothed, message, passed, start, done, by_row
+    place, lines, wy, my, block_ends, own, xor_1, xor_2, xor_3, wz, unsmoothed, message,
+    passed, start, done, by_row, inflow,
 ):
-    refs = (own, back_1, back_2, back_3)
-    low, high = own_inflow(
+    refs = (own, xor_1, xor_2, xor_3)
+
+    def write(low, high):
+        for k in range(4):
+            inflow[k, pl.ds(0, 4)] = low[k]
+            inflow[4 + k, pl.ds(0, 4)] = high[k]
+
+    own_inflow(
         place[1],
         4,
         lambda s: [refs[s][pl.ds(32 + 4 * v, 4)] for v in range(14)],
         lambda s: [refs[s][pl.ds(4 * v, 4)] for v in range(8)],
         [jnp.zeros((4, 128), F32)] * 4,
+        write,
     )
+    low = [inflow[k, pl.ds(0, 4)] for k in range(4)]
+    high = [inflow[4 + k, pl.ds(0, 4)] for k in range(4)]
     maps = [[my[v, pl.ds(s, 4, stride=8)] for v in range(14)] for s in range(8)]
     blocks = [[block_ends[v, pl.ds(s, 4, stride=8)] for v in range(8)] for s in range(8)]
     lows, highs = chained(maps, blocks, low, high)
@@ -526,22 +574,28 @@
 
 
 def z_finish_kernel(
-    place, unsmoothed, wz, maps_0, maps_1, maps_2, maps_3, ends_0, ends_1, ends_2, ends_3, smoothed, passed
+    place, unsmoothed, wz, maps_0, maps_1, maps_2, maps_3, ends_0, ends_1, ends_2, ends_3, smoothed, passed, inflow
 ):
     maps = (maps_0, maps_1, maps_2, maps_3)
     ends = (ends_0, ends_1, ends_2, ends_3)
-    lows, highs = ([], [])
     for g in range(4):
         rows = pl.ds(8 * g, 8)
-        low, high = own_inflow(
+
+        def write(low, high, rows=rows):
+            for k in range(4):
+                inflow[k, rows] = low[k]
+                inflow[4 + k, rows] = high[k]
+
+        own_inflow(
             place[2],
             4,
-            lambda s: [maps[s][v, rows] for v in range(14)],
-            lambda s: [ends[s][v, rows] for v in range(8)],
+            lambda s, rows=rows: [maps[s][v, rows] for v in range(14)],
+            lambda s, rows=rows: [ends[s][v, rows] for v in range(8)],
             [jnp.zeros((8, 128), F32)] * 4,
+            write,
         )
-        lows.append(low)
-        highs.append(high)
+    lows = [[inflow[k, pl.ds(8 * g, 8)] for k in range(4)] for g in range(4)]
+    highs = [[inflow[4 + k, pl.ds(8 * g, 8)] for k in range(4)] for g in range(4)]
 
     def value(i, g):
         return unsmoothed[g // 2, i, pl.ds(8 * (g % 2), 8)]
@@ -559,17 +613,26 @@
     backward(lambda i, g: passed[g // 2, i, pl.ds(8 * (g % 2), 8)], weight, highs, put_last)
 
 
-def turned_by(value, axis, step):
+def pair_swaps(axis, spare, value_even, value_odd):
+    axes = tuple(sorted((axis, spare)))
+    count, others = (lax.axis_size(axis), lax.axis_size(spare))
+
+    def flat(i, k):
+        return i * others + k if axis == axes[0] else k * count + i
+
+    odd = []
+    for i in range(count):
+        for k in range(others):
+            j = i + 1 if i % 2 else i - 1
+            odd.append((flat(i, k), flat(j, k) if 0 <= j < count else flat(i, k ^ 1)))
+    from_odd = lax.ppermute(value_odd, axes, odd)
+    from_even = lax.ppermute(value_even, axis, [(i, i ^ 1) for i in range(count)])
+    return from_even, from_odd
+
+
+def xor_gather(value, axis):
     count = lax.axis_size(axis)
-    return lax.ppermute(value, axis, [(i, (i + step) % count) for i in range(count)])
-
-
-def turned_both(value, x_step, z_step):
-    nx, nz = (lax.axis_size("gx"), lax.axis_size("gz"))
-    moves = [
-        (x * nz + z, (x + x_step) % nx * nz + (z + z_step) % nz) for x in range(nx) for z in range(nz)
-    ]
-    return lax.ppermute(value, ("gx", "gz"), moves)
+    return [value] + [lax.ppermute(value, axis, [(i, i ^ s) for i in range(count)]) for s in (3, 2, 1)][::-1]
 
 
 def local(source, capacity, transfer, observed, classes, conductivity, filter_rates):
@@ -577,26 +640,27 @@
     place = jnp.stack([lax.axis_index(a) for a in axes] + [jnp.int32(lax.axis_size(a)) for a in axes])
     rates = filter_rates.reshape(6, CLASSES)
     plane = (STEPS, STEPS, 128)
-    units, to_low, to_high, _ = call(
-        coefficients_kernel, [(6,) + plane, (8, STEPS, 128), (8, STEPS, 128), plane], [VMEM] * 4 + [SMEM]
-    )(source, capacity, transfer, classes, conductivity)
-    from_high = turned_by(to_low, "gy", -1)
-    from_low = turned_by(to_high, "gy", 1)
+    units, y_even, y_odd, classes = call(
+        coefficients_kernel,
+        [(6,) + plane, (8, STEPS, 128), (8, STEPS, 128), jax.ShapeDtypeStruct(plane, jnp.int32)],
+        [SMEM] + [HBM] * 4 + [SMEM],
+        [plane, (2,) + plane, (2,) + plane, plane],
+        limit=60,
+        copies=4,
+    )(place, source, capacity, transfer, classes, conductivity)
+    y_even, y_odd = pair_swaps("gy", "gz", y_even, y_odd)
 
     z_face = (7 * NEAR + 2, STEPS, 128)
     x_face = (STEPS, face_rows()[1], 128)
-    corner = (corner_rows()[1], 128)
-    strips, z_low, z_high, x_low, x_high, ll, lh, hl, hh = call(
-        halo_kernel, [plane, z_face, z_face, x_face, x_face] + [corner] * 4, [SMEM] + [VMEM] * 3
-    )(place, units, from_high, from_low)
-    z_from_high = turned_by(z_low, "gz", -1)
-    z_from_low = turned_by(z_high, "gz", 1)
-    x_from_high = turned_by(x_low, "gx", -1)
-    x_from_low = turned_by(x_high, "gx", 1)
-    from_hh = turned_both(ll, -1, -1)
-    from_hl = turned_both(lh, 1, -1)
-    from_lh = turned_both(hl, -1, 1)
-    from_ll = turned_both(hh, 1, 1)
+    corners = (2, corner_rows()[1], 128)
+    strips, z_even, z_odd, x_even, x_odd = call(
+        halo_kernel,
+        [plane, z_face, z_face, x_face, x_face],
+        [SMEM] + [VMEM] * 3,
+        limit=60,
+    )(place, units, y_even, y_odd)
+    x_even, x_odd = pair_swaps("gx", "gy", x_even, x_odd)
+    z_even, z_odd = pair_swaps("gz", "gy", z_even, z_odd)
 
     rows = (32, 128)
     wx, wy, wz, mx, my, my_all, mz, _, _ = call(
@@ -604,36 +668,42 @@
         [(2,) + plane, (4, 128, 128), (2,) + plane, (14,) + rows, (14,) + rows, (56, 128), (14,) + rows,
          (256, 128), (2, 128, 128)],
         [VMEM, SMEM, VMEM],
-    )(classes, rates, ll)
-    z_maps = [mz] + [turned_by(mz, "gz", s) for s in (1, 2, 3)]
+        limit=60,
+    )(classes, rates, strips)
+    x_even, wx = lax.optimization_barrier((x_even, wx))
+    corner_even, corner_odd = call(corner_kernel, [corners, corners], [SMEM] + [VMEM] * 2, limit=60)(place, x_even, x_odd)
+    corner_even, corner_odd = pair_swaps("gz", "gy", corner_even, corner_odd)
+    z_maps = xor_gather(mz, "gz")
 
     padded = (PLANES, 32, 128)
     predicted, increment, message = call(
         sweep_kernel,
         [(2,) + plane, (2, 256, 128), (8, 88, 128)],
-        [SMEM] + [VMEM] * 13,
+        [SMEM] + [VMEM] * 11,
         [(7,) + padded, (6,) + padded, (4,) + padded, (4,) + padded, (STEPS,) + rows, (8,) + rows],
         flops=100000000,
-    )(place, units, strips, z_from_high, z_from_low, x_from_high, x_from_low, from_hh, from_hl, from_lh, from_ll,
+        limit=60,
+    )(place, units, strips, z_even, z_odd, x_even, x_odd, corner_even, corner_odd,
       observed, wx, mx)
     gathered = lax.all_to_all(message, "gx", 0, 0, tiled=True)
     inflow, = call(solve_kernel, [(8, 32, 128)], [VMEM])(gathered)
     inflow = lax.all_to_all(inflow, "gx", 0, 0, tiled=True)
+    inflow, z_maps = lax.optimization_barrier((inflow, z_maps))
     lines, block_ends, y_ends = call(
         x_finish_kernel,
         [(4, 128, 128), (8,) + rows, (88, 128)],
         [VMEM] * 6,
         [(2, 256, 128), (8,) + rows],
     )(increment, wx, inflow, wy, my, my_all)
-    y_all = [y_ends] + [turned_by(y_ends, "gy", s) for s in (1, 2, 3)]
+    y_all = xor_gather(y_ends, "gy")
     unsmoothed, z_ends = call(
         y_finish_kernel,
         [(2,) + plane, (8,) + rows],
         [SMEM] + [VMEM] * 9,
-        [(2, 256, 128), (8,) + rows, (4, 128, 128), (2, 256, 128)],
+        [(2, 256, 128), (8,) + rows, (4, 128, 128), (2, 256, 128), (8, 8, 128)],
     )(place, lines, wy, my, block_ends, *y_all, wz)
-    z_all = [z_ends] + [turned_by(z_ends, "gz", s) for s in (1, 2, 3)]
-    smoothed, = call(z_finish_kernel, [(2,) + plane], [SMEM] + [VMEM] * 10, [(2,) + plane])(
+    z_all = xor_gather(z_ends, "gz")
+    smoothed, = call(z_finish_kernel, [(2,) + plane], [SMEM] + [VMEM] * 10, [(2,) + plane, (8,) + rows])(
         place, unsmoothed, wz, *z_maps, *z_all
     )
     return (predicted, smoothed)

time: 127 us -> 97.1 us (0.76)
  waiting for transfers between devices: 49.5 us -> 29.7 us
  Pallas kernels: 34.8 us -> 28.3 us
  local copies, waits for them, and re-layouts: 9.57 us -> 4.67 us
    ppermute x19 -> x17, waiting for transfers between devices: 39.8 us -> 22.5 us  [the longest x9 13.2 us: xor_gather(): lax.ppermute(value, axis, [(i, i ^ s) for i in range(count)])]
    pallas_call x1, Pallas kernels: 21 us -> 12 us  [local(): call(sweep_kernel, [(2,) + plane, (2, 256, 128), (8, 88, 128)], [SMEM] +...]
    unnamed x36 -> x34, local copies, waits for them, and re-layouts: 9.48 us -> 3.46 us
    all_to_all x1, starting transfers between devices: 3.61 us -> 7.19 us  [local(): gathered = lax.all_to_all(message, 'gx', 0, 0, tiled=True)]
    ppermute x19 -> x17, starting transfers between devices: 25.2 us -> 22 us  [the longest x9 13.4 us: xor_gather(): lax.ppermute(value, axis, [(i, i ^ s) for i in range(count)])]
    all_to_all x1, waiting for transfers between devices: 5.85 us -> 2.81 us  [local(): gathered = lax.all_to_all(message, 'gx', 0, 0, tiled=True)]
    pallas_call x2 -> x3, Pallas kernels: 4.11 us -> 6.38 us  [the longest x1 2.74 us: local(): call(halo_kernel, [plane, z_face, z_face, x_face, x_face], [SMEM] + [VMEM...]
  transfers between devices with their start and end apart: 21 -> 19, of which waited for: 13 -> 11; matrix products, arithmetic and copies ran while one was open for 0% -> 1% of each run, Pallas kernels for 5% -> 7%
where the time goes in v2:
time: 97.1 us; the launch traced here: 96.1 us
  starting transfers between devices  32.7 us (34%)
  waiting for transfers between devices  29.7 us (31%)
  Pallas kernels  28.3 us (29%)
  local copies, waits for them, and re-layouts  4.67 us (5%)
    ppermute x9, starting transfers between devices, xor_gather(): lax.ppermute(value, axis, [(i, i ^ s) for i in range(count)])  13.4 us
    ppermute x9, waiting for transfers between devices, xor_gather(): lax.ppermute(value, axis, [(i, i ^ s) for i in range(count)])  13.2 us
    pallas_call x1, Pallas kernels, local(): call(sweep_kernel, [(2,) + plane, (2, 256, 128), (8, 88, 128)], [SMEM] +...  12 us
    all_to_all x1, starting transfers between devices, local(): gathered = lax.all_to_all(message, 'gx', 0, 0, tiled=True)  7.19 us
    ppermute x4, waiting for transfers between devices, pair_swaps(): lax.ppermute(value_even, axis, [(i, i ^ 1) for i in range(count)])  6.51 us
    ppermute x4, starting transfers between devices, pair_swaps(): lax.ppermute(value_even, axis, [(i, i ^ 1) for i in range(count)])  5.41 us
    all_to_all x1, waiting for transfers between devices, local(): inflow = lax.all_to_all(inflow, 'gx', 0, 0, tiled=True)  4.32 us
    pallas_call x1, Pallas kernels, local(): call(maps_kernel, [(2,) + plane, (4, 128, 128), (2,) + plane, (14,) + row...  3.89 us
  transfers between devices with their start and end apart: 19, of which 11 were waited for; matrix products, arithmetic and copies ran while one was open for 1% of the time, Pallas kernels for 7%

profile of v2, /device:TPU:0, one launch (start us, length us, event | category | flops | bytes accessed | tf_op | source)
XLA Modules:
  0.0 96.1 jit_solution(14572657974050635373)
XLA Ops:
  0.6 0.6 stack.15.place
  1.2 3.5 %shard_map.86 = (f32[6,16,16,128]{3,2,1,0:T(8,128)}, f32[8,16,128]{2,1,0:T(8,128)}, f32[8,16,128]{2,1,0:T(8,128)}, s32[16,16,128]{2,1,0:T(8,128)}) custom-call(s32[6]{0:T(128)} %stack.15.place, f32[2,16,16,128]{3,2,1,0:T(8,128)} %source_in.1, f32[2,16,16,128]{3,2,1,0:T(8,128)} %capacity_in.1, f32[16,16,128]{2,1,0:T(8,128)} %transfer_in.1, ...), custom_call_target="tpu_custom_call" | custom-call | flops 1000000 | bytes 1000000 | tf_op jit(solution)/shard_map/pallas_call | solution.py:643
  4.7 0.1 collective-permute-start
  4.8 1.7 %collective-permute-start.1 = (f32[8,16,128]{2,1,0:T(8,128)}, f32[8,16,128]{2,1,0:T(8,128)S(1)}, u32[]{:S(2)}, u32[]{:S(2)}) collective-permute-start(f32[8,16,128]{2,1,0:T(8,128)} %get-tuple-element.37), channel_id=1, source_target_pairs={{0,1},{1,0},{2,3},{3,2},{4,8},{5,9},{6,10},{7,11},{8,4},{9,5},{10,... | collective-permute-start | bytes 196616 | tf_op jit(solution)/shard_map/ppermute | solution.py:628
  6.6 0.0 collective-permute-done.y_even
  6.6 2.8 %collective-permute-done.1.y_odd = f32[8,16,128]{2,1,0:T(8,128)S(1)} collective-permute-done((f32[8,16,128]{2,1,0:T(8,128)}, f32[8,16,128]{2,1,0:T(8,128)S(1)}, u32[]{:S(2)}, u32[]{:S(2)}) %collective-permute-start.1) | collective-permute-done | bytes 65568 | tf_op jit(solution)/shard_map/ppermute | solution.py:628
  9.4 0.0 copy-done.14
  9.4 0.6 copy-done.15
  10.0 2.7 %shard_map.87 = (f32[16,16,128]{2,1,0:T(8,128)}, f32[44,16,128]{2,1,0:T(8,128)}, f32[44,16,128]{2,1,0:T(8,128)}, f32[16,44,128]{2,1,0:T(8,128)}, f32[16,44,128]{2,1,0:T(8,128)}) custom-call(s32[6]{0:T(128)} %stack.15.place, f32[6,16,16,128]{3,2,1,0:T(8,128)} %get-tuple-element.35.units, f32[8,16,128]{2,1,0:T(8,128)} %copy-done.14, f32[8,16,128]{2,1,0:T(8,128)} %copy-done.15), custom_call_target="tpu_custom_call" | custom-call | flops 1000000 | bytes 1000000 | tf_op jit(solution)/shard_map/pallas_call | solution.py:656
  12.8 2.0 %collective-permute-start.4 = (f32[16,44,128]{2,1,0:T(8,128)}, f32[16,44,128]{2,1,0:T(8,128)S(1)}, u32[]{:S(2)}, u32[]{:S(2)}) collective-permute-start(f32[16,44,128]{2,1,0:T(8,128)} %get-tuple-element.41), channel_id=1, source_target_pairs={{0,16},{16,0},{32,48},{48,32},{64,80},{80,64},{96,112},{112,96},{1... | collective-permute-start | bytes 1081352 | tf_op jit(solution)/shard_map/ppermute | solution.py:629
  14.8 1.1 %collective-permute-start.5 = (f32[16,44,128]{2,1,0:T(8,128)}, f32[16,44,128]{2,1,0:T(8,128)S(1)}, u32[]{:S(2)}, u32[]{:S(2)}) collective-permute-start(f32[16,44,128]{2,1,0:T(8,128)} %get-tuple-element.45), channel_id=1, source_target_pairs={{0,4},{4,0},{8,12},{12,8},{16,32},{20,36},{24,40},{28,44},{32,16},... | collective-permute-start | bytes 1081352 | tf_op jit(solution)/shard_map/ppermute | solution.py:628
  15.8 1.6 %collective-permute-start.2 = (f32[44,16,128]{2,1,0:T(8,128)}, f32[44,16,128]{2,1,0:T(8,128)S(1)}, u32[]{:S(2)}, u32[]{:S(2)}) collective-permute-start(f32[44,16,128]{2,1,0:T(8,128)} %get-tuple-element.39), channel_id=1, source_target_pairs={{0,1},{1,0},{2,3},{3,2},{4,5},{5,4},{6,7},{7,6},{8,9},{9,8},{10,11... | collective-permute-start | bytes 1081352 | tf_op jit(solution)/shard_map/ppermute | solution.py:629
  17.4 0.0 collective-permute-start.3
  17.4 0.0 copy-done.16
  17.4 0.6 reshape.7.rates
  18.0 3.9 %shard_map.88 = (f32[2,16,16,128]{3,2,1,0:T(8,128)}, f32[4,128,128]{2,1,0:T(8,128)}, f32[2,16,16,128]{3,2,1,0:T(8,128)}, f32[14,32,128]{2,1,0:T(8,128)}, f32[14,...) custom-call(s32[16,16,128]{2,1,0:T(8,128)} %get-tuple-element.42.cla, ...), custom_call_target="tpu_custom_call" | custom-call | flops 1000000 | bytes 1000000 | tf_op jit(solution)/shard_map/pallas_call | solution.py:666
  21.9 2.5 %collective-permute-done.4.x_even = f32[16,44,128]{2,1,0:T(8,128)S(1)} collective-permute-done((f32[16,44,128]{2,1,0:T(8,128)}, f32[16,44,128]{2,1,0:T(8,128)S(1)}, u32[]{:S(2)}, u32[]{:S(2)}) %collective-permute-start.4) | collective-permute-done | bytes 360480 | tf_op jit(solution)/shard_map/ppermute | solution.py:629
  24.4 0.0 collective-permute-done.5.x_odd
  24.4 0.8 copy-done.8
  25.2 0.7 copy-done.9
  25.9 1.9 %shard_map.89 = (f32[2,120,128]{2,1,0:T(8,128)}, f32[2,120,128]{2,1,0:T(8,128)}) custom-call(s32[6]{0:T(128)} %stack.15.place, f32[16,44,128]{2,1,0:T(8,128)} %copy-done.8, f32[16,44,128]{2,1,0:T(8,128)} %copy-done.9), custom_call_target="tpu_custom_call" | custom-call | flops 1000000 | bytes 1000000 | tf_op jit(solution)/shard_map/pallas_call | solution.py:674
  27.8 1.8 %collective-permute-start.6 = (f32[2,120,128]{2,1,0:T(8,128)}, f32[2,120,128]{2,1,0:T(8,128)S(1)}, u32[]{:S(2)}, u32[]{:S(2)}) collective-permute-start(f32[2,120,128]{2,1,0:T(8,128)} %get-tuple-element.46), channel_id=1, source_target_pairs={{0,1},{1,0},{2,3},{3,2},{4,5},{5,4},{6,7},{7,6},{8,9},{9,8},{10,11... | collective-permute-start | bytes 368648 | tf_op jit(solution)/shard_map/ppermute | solution.py:629
  29.6 0.3 collective-permute-start.7
  29.9 0.0 collective-permute-done.2.z_even
  29.9 0.0 collective-permute-done.3.z_odd
  29.9 0.0 copy-start.11
  29.9 4.0 %collective-permute-done.6.corner_even = f32[2,120,128]{2,1,0:T(8,128)S(1)} collective-permute-done((f32[2,120,128]{2,1,0:T(8,128)}, f32[2,120,128]{2,1,0:T(8,128)S(1)}, u32[]{:S(2)}, u32[]{:S(2)}) %collective-permute-start.6) | collective-permute-done | bytes 122912 | tf_op jit(solution)/shard_map/ppermute | solution.py:629
  34.0 0.0 collective-permute-done.7.corner_odd
  34.0 0.0 copy-done.10
  34.0 0.6 copy-done.12
  34.6 0.1 copy-done.13
  34.7 12.0 %shard_map.90 = (f32[2,16,16,128]{3,2,1,0:T(8,128)}, f32[2,256,128]{2,1,0:T(8,128)}, f32[8,88,128]{2,1,0:T(8,128)}) custom-call(s32[6]{0:T(128)} %stack.15.place, f32[6,16,16,128]{3,2,1,0:T(8,128)} %get-tuple-element.35.units, f32[16,16,128]{2,1,0:T(8,128)} %get-tuple-element.38._.strips, f32[44,16,128]{2,1,0:T(8,128)} %copy-done.10, ...), custom_call_target="tpu_custom_call" | custom-call | flops 100000000 | bytes 1000000 | tf_op jit(solution)/shard_map/pallas_call | solution.py:679
  46.6 7.2 %all-to-all-start = ((f32[8,88,128]{2,1,0:T(8,128)}), f32[8,88,128]{2,1,0:T(8,128)S(1)}, u32[]{:S(2)}, u32[]{:S(2)}) async-start(f32[8,88,128]{2,1,0:T(8,128)} %get-tuple-element.52), calls=%async_computation | async-start | bytes 720896 | tf_op jit(solution)/shard_map/all_to_all | solution.py:688
  53.8 0.0 copy-done.5
  53.8 0.0 copy-start.2
  53.8 3.1 %collective-permute-start.10 = (f32[14,32,128]{2,1,0:T(8,128)S(1)}, f32[14,32,128]{2,1,0:T(8,128)S(1)}, u32[]{:S(2)}, u32[]{:S(2)}) collective-permute-start(f32[14,32,128]{2,1,0:T(8,128)S(1)} %copy-done.5), channel_id=1, source_target_pairs={{0,3},{1,2},{2,1},{3,0},{4,7},{5,6},{6,5},{7,4},{8,11},{9,10},{10,... | collective-permute-start | bytes 688136 | tf_op jit(solution)/shard_map/ppermute | solution.py:635
  56.9 1.1 %collective-permute-start.8 = (f32[14,32,128]{2,1,0:T(8,128)S(1)}, f32[14,32,128]{2,1,0:T(8,128)S(1)}, u32[]{:S(2)}, u32[]{:S(2)}) collective-permute-start(f32[14,32,128]{2,1,0:T(8,128)S(1)} %copy-done.5), channel_id=1, source_target_pairs={{0,1},{1,0},{2,3},{3,2},{4,5},{5,4},{6,7},{7,6},{8,9},{9,8},{10,11... | collective-permute-start | bytes 688136 | tf_op jit(solution)/shard_map/ppermute | solution.py:635
  58.0 0.6 collective-permute-start.9
  58.6 2.8 %all-to-all-done.gathered = f32[8,88,128]{2,1,0:T(8,128)S(1)} async-done(((f32[8,88,128]{2,1,0:T(8,128)}), f32[8,88,128]{2,1,0:T(8,128)S(1)}, u32[]{:S(2)}, u32[]{:S(2)}) %all-to-all-start) | async-done | bytes 360480 | tf_op jit(solution)/shard_map/all_to_all | solution.py:688
  61.4 0.8 shard_map.91
  62.2 3.5 %all-to-all-start.1 = ((f32[8,32,128]{2,1,0:T(8,128)}), f32[8,32,128]{2,1,0:T(8,128)S(1)}, u32[]{:S(2)}, u32[]{:S(2)}) async-start(f32[8,32,128]{2,1,0:T(8,128)} %shard_map.91), calls=%async_computation.1 | async-start | bytes 262144 | tf_op jit(solution)/shard_map/all_to_all | solution.py:690
  65.7 0.0 collective-permute-done.10.maps_3
  65.7 0.0 collective-permute-done.8.maps_1
  65.7 2.2 %collective-permute-done.9.maps_2 = f32[14,32,128]{2,1,0:T(8,128)S(1)} collective-permute-done((f32[14,32,128]{2,1,0:T(8,128)S(1)}, f32[14,32,128]{2,1,0:T(8,128)S(1)}, u32[]{:S(2)}, u32[]{:S(2)}) %collective-permute-start.9) | collective-permute-done | bytes 229408 | tf_op jit(solution)/shard_map/ppermute | solution.py:635
  67.9 4.3 %all-to-all-done.1.inflow = f32[8,32,128]{2,1,0:T(8,128)S(1)} async-done(((f32[8,32,128]{2,1,0:T(8,128)}), f32[8,32,128]{2,1,0:T(8,128)S(1)}, u32[]{:S(2)}, u32[]{:S(2)}) %all-to-all-start.1) | async-done | bytes 131104 | tf_op jit(solution)/shard_map/all_to_all | solution.py:690
  72.2 0.0 copy-done.2
  72.2 0.0 copy-done.3
  72.3 0.0 copy-start
  72.3 0.6 shard_map.92
  72.9 0.1 collective-permute-start.11
  73.0 0.8 collective-permute-start.12
  73.7 2.6 %collective-permute-start.13 = (f32[88,128]{1,0:T(8,128)S(1)}, f32[88,128]{1,0:T(8,128)S(1)}, u32[]{:S(2)}, u32[]{:S(2)}) collective-permute-start(f32[88,128]{1,0:T(8,128)S(1)} %get-tuple-element.60.own), channel_id=1, source_target_pairs={{0,12},{4,8},{8,4},{12,0},{1,13},{5,9},{9,5},{13,1},{2,14},{6,10},... | collective-permute-start | bytes 135176 | tf_op jit(solution)/shard_map/ppermute | solution.py:635
  76.3 0.0 collective-permute-done.11.xor_1
  76.3 2.6 %collective-permute-done.12.xor_2 = f32[88,128]{1,0:T(8,128)S(1)} collective-permute-done((f32[88,128]{1,0:T(8,128)S(1)}, f32[88,128]{1,0:T(8,128)S(1)}, u32[]{:S(2)}, u32[]{:S(2)}) %collective-permute-start.12) | collective-permute-done | bytes 45088 | tf_op jit(solution)/shard_map/ppermute | solution.py:635
  79.0 0.2 collective-permute-done.13.xor_3
  79.2 0.6 copy-done.7
  79.8 1.3 %shard_map.93 = (f32[2,16,16,128]{3,2,1,0:T(8,128)S(1)}, f32[8,32,128]{2,1,0:T(8,128)S(1)}) custom-call(s32[6]{0:T(128)S(1)} %copy-done.7, f32[4,128,128]{2,1,0:T(8,128)S(1)} %get-tuple-element.58.lines, f32[4,128,128]{2,1,0:T(8,128)S(1)} %copy-done.1, f32[14,32,128]{2,1,0:T(8,128)S(1)} %copy-done.3, f32[8,32,128]{2,1,0:T(8,128)S(1)} %get-tuple-element.59.block_ends, ...), custom_call_target="tpu_custom_call" | custom-call | flops 1000000 | bytes 1000000 | tf_op jit(solution)/shard_map/pallas_call | solution.py:699
  81.1 2.4 %collective-permute-start.14 = (f32[8,32,128]{2,1,0:T(8,128)S(1)}, f32[8,32,128]{2,1,0:T(8,128)S(1)}, u32[]{:S(2)}, u32[]{:S(2)}) collective-permute-start(f32[8,32,128]{2,1,0:T(8,128)S(1)} %get-tuple-element.67.ends_0), channel_id=1, source_target_pairs={{0,1},{1,0},{2,3},{3,2},{4,5},{5,4},{6,7},{7,6},{8,9},{9,8},{10,11... | collective-permute-start | bytes 393224 | tf_op jit(solution)/shard_map/ppermute | solution.py:635
  83.5 2.1 %collective-permute-start.15 = (f32[8,32,128]{2,1,0:T(8,128)S(1)}, f32[8,32,128]{2,1,0:T(8,128)S(1)}, u32[]{:S(2)}, u32[]{:S(2)}) collective-permute-start(f32[8,32,128]{2,1,0:T(8,128)S(1)} %get-tuple-element.67.ends_0), channel_id=1, source_target_pairs={{0,2},{1,3},{2,0},{3,1},{4,6},{5,7},{6,4},{7,5},{8,10},{9,11},{10,... | collective-permute-start | bytes 393224 | tf_op jit(solution)/shard_map/ppermute | solution.py:635
  85.6 0.6 collective-permute-start.16
  86.3 1.1 %collective-permute-done.14.ends_1 = f32[8,32,128]{2,1,0:T(8,128)S(1)} collective-permute-done((f32[8,32,128]{2,1,0:T(8,128)S(1)}, f32[8,32,128]{2,1,0:T(8,128)S(1)}, u32[]{:S(2)}, u32[]{:S(2)}) %collective-permute-start.14) | collective-permute-done | bytes 131104 | tf_op jit(solution)/shard_map/ppermute | solution.py:635
  87.4 4.7 %collective-permute-done.15.ends_2 = f32[8,32,128]{2,1,0:T(8,128)S(1)} collective-permute-done((f32[8,32,128]{2,1,0:T(8,128)S(1)}, f32[8,32,128]{2,1,0:T(8,128)S(1)}, u32[]{:S(2)}, u32[]{:S(2)}) %collective-permute-start.15) | collective-permute-done | bytes 131104 | tf_op jit(solution)/shard_map/ppermute | solution.py:635
  92.1 2.3 %collective-permute-done.16.ends_3 = f32[8,32,128]{2,1,0:T(8,128)S(1)} collective-permute-done((f32[8,32,128]{2,1,0:T(8,128)S(1)}, f32[8,32,128]{2,1,0:T(8,128)S(1)}, u32[]{:S(2)}, u32[]{:S(2)}) %collective-permute-start.16) | collective-permute-done | bytes 131104 | tf_op jit(solution)/shard_map/ppermute | solution.py:635
  94.4 1.7 %shard_map.94 = f32[2,16,16,128]{3,2,1,0:T(8,128)} custom-call(s32[6]{0:T(128)S(1)} %copy-done.7, f32[2,16,16,128]{3,2,1,0:T(8,128)S(1)} %get-tuple-element.62.unsmoothed, f32[2,16,16,128]{3,2,1,0:T(8,128)S(1)} %copy-done, f32[14,32,128]{2,1,0:T(8,128)S(1)} %copy-done.5, f32[14,32,128]{2,1,0:T(8,128)S(1)} %collective-permute-done.8.maps_1, ...), custom_call_target="tpu_custom_call" | custom-call | flops 1000000 | bytes 1000000 | tf_op jit(solution)/shard_map/pallas_call | solution.py:706
  (20 shorter events, 0.0 us)
Async XLA Ops:
  4.7 1.8 %collective-permute-start = (f32[8,16,128]{2,1,0:T(8,128)}, f32[8,16,128]{2,1,0:T(8,128)S(1)}, u32[]{:S(2)}, u32[]{:S(2)}) collective-permute-start(f32[8,16,128]{2,1,0:T(8,128)} %get-tuple-element.36), channel_id=1, source_target_pairs={{0,4},{4,0},{8,12},{12,8},{1,5},{5,1},{9,13},{13,9},{2,6},{6,2},{1... | collective-permute-start | bytes 196616 | tf_op jit(solution)/shard_map/ppermute | solution.py:629
  4.8 4.6 %collective-permute-start.1 = (f32[8,16,128]{2,1,0:T(8,128)}, f32[8,16,128]{2,1,0:T(8,128)S(1)}, u32[]{:S(2)}, u32[]{:S(2)}) collective-permute-start(f32[8,16,128]{2,1,0:T(8,128)} %get-tuple-element.37), channel_id=1, source_target_pairs={{0,1},{1,0},{2,3},{3,2},{4,8},{5,9},{6,10},{7,11},{8,4},{9,5},{10,... | collective-permute-start | bytes 196616 | tf_op jit(solution)/shard_map/ppermute | solution.py:628
  6.6 2.8 %copy-start.14 = (f32[8,16,128]{2,1,0:T(8,128)}, f32[8,16,128]{2,1,0:T(8,128)S(1)}, u32[]{:S(2)}) copy-start(f32[8,16,128]{2,1,0:T(8,128)S(1)} %collective-permute-done.y_even) | copy-start | bytes 196612
  9.4 0.6 copy-start.15
  12.8 4.7 %copy-start.16 = (f32[3,2,12]{2,1,0:T(2,128)S(1)}, f32[3,2,12]{2,1,0:T(2,128)}, u32[]{:S(2)}) copy-start(f32[3,2,12]{2,1,0:T(2,128)} %param.13) | copy-start | bytes 868
  12.8 11.6 %collective-permute-start.4 = (f32[16,44,128]{2,1,0:T(8,128)}, f32[16,44,128]{2,1,0:T(8,128)S(1)}, u32[]{:S(2)}, u32[]{:S(2)}) collective-permute-start(f32[16,44,128]{2,1,0:T(8,128)} %get-tuple-element.41), channel_id=1, source_target_pairs={{0,16},{16,0},{32,48},{48,32},{64,80},{80,64},{96,112},{112,96},{1... | collective-permute-start | bytes 1081352 | tf_op jit(solution)/shard_map/ppermute | solution.py:629
  14.8 9.6 %collective-permute-start.5 = (f32[16,44,128]{2,1,0:T(8,128)}, f32[16,44,128]{2,1,0:T(8,128)S(1)}, u32[]{:S(2)}, u32[]{:S(2)}) collective-permute-start(f32[16,44,128]{2,1,0:T(8,128)} %get-tuple-element.45), channel_id=1, source_target_pairs={{0,4},{4,0},{8,12},{12,8},{16,32},{20,36},{24,40},{28,44},{32,16},... | collective-permute-start | bytes 1081352 | tf_op jit(solution)/shard_map/ppermute | solution.py:628
  15.8 14.1 %collective-permute-start.2 = (f32[44,16,128]{2,1,0:T(8,128)}, f32[44,16,128]{2,1,0:T(8,128)S(1)}, u32[]{:S(2)}, u32[]{:S(2)}) collective-permute-start(f32[44,16,128]{2,1,0:T(8,128)} %get-tuple-element.39), channel_id=1, source_target_pairs={{0,1},{1,0},{2,3},{3,2},{4,5},{5,4},{6,7},{7,6},{8,9},{9,8},{10,11... | collective-permute-start | bytes 1081352 | tf_op jit(solution)/shard_map/ppermute | solution.py:629
  17.4 12.5 %collective-permute-start.3 = (f32[44,16,128]{2,1,0:T(8,128)}, f32[44,16,128]{2,1,0:T(8,128)S(1)}, u32[]{:S(2)}, u32[]{:S(2)}) collective-permute-start(f32[44,16,128]{2,1,0:T(8,128)} %get-tuple-element.40), channel_id=1, source_target_pairs={{0,4},{4,0},{8,12},{12,8},{1,2},{5,6},{9,10},{13,14},{2,1},{6,5},{... | collective-permute-start | bytes 1081352 | tf_op jit(solution)/shard_map/ppermute | solution.py:628
  24.4 0.8 copy-start.8
  25.2 0.7 copy-start.9
  27.8 6.1 %collective-permute-start.6 = (f32[2,120,128]{2,1,0:T(8,128)}, f32[2,120,128]{2,1,0:T(8,128)S(1)}, u32[]{:S(2)}, u32[]{:S(2)}) collective-permute-start(f32[2,120,128]{2,1,0:T(8,128)} %get-tuple-element.46), channel_id=1, source_target_pairs={{0,1},{1,0},{2,3},{3,2},{4,5},{5,4},{6,7},{7,6},{8,9},{9,8},{10,11... | collective-permute-start | bytes 368648 | tf_op jit(solution)/shard_map/ppermute | solution.py:629
  29.6 4.4 %collective-permute-start.7 = (f32[2,120,128]{2,1,0:T(8,128)}, f32[2,120,128]{2,1,0:T(8,128)S(1)}, u32[]{:S(2)}, u32[]{:S(2)}) collective-permute-start(f32[2,120,128]{2,1,0:T(8,128)} %get-tuple-element.47), channel_id=1, source_target_pairs={{0,4},{4,0},{8,12},{12,8},{1,2},{5,6},{9,10},{13,14},{2,1},{6,5},{... | collective-permute-start | bytes 368648 | tf_op jit(solution)/shard_map/ppermute | solution.py:628
  29.9 4.1 %copy-start.10 = (f32[44,16,128]{2,1,0:T(8,128)}, f32[44,16,128]{2,1,0:T(8,128)S(1)}, u32[]{:S(2)}) copy-start(f32[44,16,128]{2,1,0:T(8,128)S(1)} %collective-permute-done.2.z_even) | copy-start | bytes 1081348
  29.9 4.1 %copy-start.11 = (f32[44,16,128]{2,1,0:T(8,128)}, f32[44,16,128]{2,1,0:T(8,128)S(1)}, u32[]{:S(2)}) copy-start(f32[44,16,128]{2,1,0:T(8,128)S(1)} %collective-permute-done.3.z_odd) | copy-start | bytes 1081348
  34.0 0.6 copy-start.12
  34.0 0.7 copy-start.13
  46.6 7.2 %copy-start.5 = (f32[14,32,128]{2,1,0:T(8,128)S(1)}, f32[14,32,128]{2,1,0:T(8,128)}, u32[]{:S(2)}) copy-start(f32[14,32,128]{2,1,0:T(8,128)} %get-tuple-element.63.maps_0) | copy-start | bytes 688132
  46.6 25.6 %copy-start.4 = (f32[2,256,128]{2,1,0:T(8,128)S(1)}, f32[2,256,128]{2,1,0:T(8,128)}, u32[]{:S(2)}) copy-start(f32[2,256,128]{2,1,0:T(8,128)} %get-tuple-element.51.increment) | copy-start | bytes 786436
  46.6 25.6 %copy-start.6 = (f32[56,128]{1,0:T(8,128)S(1)}, f32[56,128]{1,0:T(8,128)}, u32[]{:S(2)}) copy-start(f32[56,128]{1,0:T(8,128)} %get-tuple-element.57.my_all) | copy-start | bytes 86020
  46.6 14.8 %all-to-all-start = ((f32[8,88,128]{2,1,0:T(8,128)}), f32[8,88,128]{2,1,0:T(8,128)S(1)}, u32[]{:S(2)}, u32[]{:S(2)}) async-start(f32[8,88,128]{2,1,0:T(8,128)} %get-tuple-element.52), calls=%async_computation | async-start | bytes 720896 | tf_op jit(solution)/shard_map/all_to_all | solution.py:688
  53.8 18.4 %copy-start.1 = (f32[4,128,128]{2,1,0:T(8,128)S(1)}, f32[4,128,128]{2,1,0:T(8,128)}, u32[]{:S(2)}) copy-start(f32[4,128,128]{2,1,0:T(8,128)} %get-tuple-element.55.wy) | copy-start | bytes 786436
  53.8 18.4 %copy-start.2 = (f32[2,16,16,128]{3,2,1,0:T(8,128)S(1)}, f32[2,16,16,128]{3,2,1,0:T(8,128)}, u32[]{:S(2)}) copy-start(f32[2,16,16,128]{3,2,1,0:T(8,128)} %get-tuple-element.48.wx) | copy-start | bytes 786436
  53.8 11.9 %collective-permute-start.10 = (f32[14,32,128]{2,1,0:T(8,128)S(1)}, f32[14,32,128]{2,1,0:T(8,128)S(1)}, u32[]{:S(2)}, u32[]{:S(2)}) collective-permute-start(f32[14,32,128]{2,1,0:T(8,128)S(1)} %copy-done.5), channel_id=1, source_target_pairs={{0,3},{1,2},{2,1},{3,0},{4,7},{5,6},{6,5},{7,4},{8,11},{9,10},{10,... | collective-permute-start | bytes 688136 | tf_op jit(solution)/shard_map/ppermute | solution.py:635
  56.9 8.8 %collective-permute-start.8 = (f32[14,32,128]{2,1,0:T(8,128)S(1)}, f32[14,32,128]{2,1,0:T(8,128)S(1)}, u32[]{:S(2)}, u32[]{:S(2)}) collective-permute-start(f32[14,32,128]{2,1,0:T(8,128)S(1)} %copy-done.5), channel_id=1, source_target_pairs={{0,1},{1,0},{2,3},{3,2},{4,5},{5,4},{6,7},{7,6},{8,9},{9,8},{10,11... | collective-permute-start | bytes 688136 | tf_op jit(solution)/shard_map/ppermute | solution.py:635
  58.0 9.9 %collective-permute-start.9 = (f32[14,32,128]{2,1,0:T(8,128)S(1)}, f32[14,32,128]{2,1,0:T(8,128)S(1)}, u32[]{:S(2)}, u32[]{:S(2)}) collective-permute-start(f32[14,32,128]{2,1,0:T(8,128)S(1)} %copy-done.5), channel_id=1, source_target_pairs={{0,2},{1,3},{2,0},{3,1},{4,6},{5,7},{6,4},{7,5},{8,10},{9,11},{10,... | collective-permute-start | bytes 688136 | tf_op jit(solution)/shard_map/ppermute | solution.py:635
  62.2 10.1 %copy-start.3 = (f32[14,32,128]{2,1,0:T(8,128)S(1)}, f32[14,32,128]{2,1,0:T(8,128)}, u32[]{:S(2)}) copy-start(f32[14,32,128]{2,1,0:T(8,128)} %get-tuple-element.56.my) | copy-start | bytes 688132
  62.2 10.0 %all-to-all-start.1 = ((f32[8,32,128]{2,1,0:T(8,128)}), f32[8,32,128]{2,1,0:T(8,128)S(1)}, u32[]{:S(2)}, u32[]{:S(2)}) async-start(f32[8,32,128]{2,1,0:T(8,128)} %shard_map.91), calls=%async_computation.1 | async-start | bytes 262144 | tf_op jit(solution)/shard_map/all_to_all | solution.py:690
  72.3 6.9 %copy-start = (f32[2,16,16,128]{3,2,1,0:T(8,128)S(1)}, f32[2,16,16,128]{3,2,1,0:T(8,128)}, u32[]{:S(2)}) copy-start(f32[2,16,16,128]{3,2,1,0:T(8,128)} %get-tuple-element.61.wz) | copy-start | bytes 786436
  72.9 3.5 %collective-permute-start.11 = (f32[88,128]{1,0:T(8,128)S(1)}, f32[88,128]{1,0:T(8,128)S(1)}, u32[]{:S(2)}, u32[]{:S(2)}) collective-permute-start(f32[88,128]{1,0:T(8,128)S(1)} %get-tuple-element.60.own), channel_id=1, source_target_pairs={{0,4},{4,0},{8,12},{12,8},{1,5},{5,1},{9,13},{13,9},{2,6},{6,2},{1... | collective-permute-start | bytes 135176 | tf_op jit(solution)/shard_map/ppermute | solution.py:635
  73.0 6.0 %collective-permute-start.12 = (f32[88,128]{1,0:T(8,128)S(1)}, f32[88,128]{1,0:T(8,128)S(1)}, u32[]{:S(2)}, u32[]{:S(2)}) collective-permute-start(f32[88,128]{1,0:T(8,128)S(1)} %get-tuple-element.60.own), channel_id=1, source_target_pairs={{0,8},{4,12},{8,0},{12,4},{1,9},{5,13},{9,1},{13,5},{2,10},{6,14},... | collective-permute-start | bytes 135176 | tf_op jit(solution)/shard_map/ppermute | solution.py:635
  73.7 5.5 %collective-permute-start.13 = (f32[88,128]{1,0:T(8,128)S(1)}, f32[88,128]{1,0:T(8,128)S(1)}, u32[]{:S(2)}, u32[]{:S(2)}) collective-permute-start(f32[88,128]{1,0:T(8,128)S(1)} %get-tuple-element.60.own), channel_id=1, source_target_pairs={{0,12},{4,8},{8,4},{12,0},{1,13},{5,9},{9,5},{13,1},{2,14},{6,10},... | collective-permute-start | bytes 135176 | tf_op jit(solution)/shard_map/ppermute | solution.py:635
  79.2 0.6 copy-start.7
  81.1 6.3 %collective-permute-start.14 = (f32[8,32,128]{2,1,0:T(8,128)S(1)}, f32[8,32,128]{2,1,0:T(8,128)S(1)}, u32[]{:S(2)}, u32[]{:S(2)}) collective-permute-start(f32[8,32,128]{2,1,0:T(8,128)S(1)} %get-tuple-element.67.ends_0), channel_id=1, source_target_pairs={{0,1},{1,0},{2,3},{3,2},{4,5},{5,4},{6,7},{7,6},{8,9},{9,8},{10,11... | collective-permute-start | bytes 393224 | tf_op jit(solution)/shard_map/ppermute | solution.py:635
  83.5 8.6 %collective-permute-start.15 = (f32[8,32,128]{2,1,0:T(8,128)S(1)}, f32[8,32,128]{2,1,0:T(8,128)S(1)}, u32[]{:S(2)}, u32[]{:S(2)}) collective-permute-start(f32[8,32,128]{2,1,0:T(8,128)S(1)} %get-tuple-element.67.ends_0), channel_id=1, source_target_pairs={{0,2},{1,3},{2,0},{3,1},{4,6},{5,7},{6,4},{7,5},{8,10},{9,11},{10,... | collective-permute-start | bytes 393224 | tf_op jit(solution)/shard_map/ppermute | solution.py:635
  85.6 8.8 %collective-permute-start.16 = (f32[8,32,128]{2,1,0:T(8,128)S(1)}, f32[8,32,128]{2,1,0:T(8,128)S(1)}, u32[]{:S(2)}, u32[]{:S(2)}) collective-permute-start(f32[8,32,128]{2,1,0:T(8,128)S(1)} %get-tuple-element.67.ends_0), channel_id=1, source_target_pairs={{0,3},{1,2},{2,1},{3,0},{4,7},{5,6},{6,5},{7,4},{8,11},{9,10},{10,... | collective-permute-start | bytes 393224 | tf_op jit(solution)/shard_map/ppermute | solution.py:635

commit v3 on v2

--- a/solution.py
+++ b/solution.py
@@ -73,10 +73,11 @@
 
 
 def coefficients_kernel(
-    place, source_in, capacity_in, transfer_in, classes_in, conductivity,
+    source_in, capacity_in, transfer_in, classes_in, conductivity,
     units, even, odd, classes,
     edges, source, capacity, transfer, sems,
 ):
+    place = {1: lax.axis_index("gy")}
     brought(((source_in, source), (capacity_in, capacity), (transfer_in, transfer), (classes_in, classes)), sems)
 
     def layer(z, _):
@@ -131,7 +132,26 @@
     return rows, -(-offset // 8) * 8
 
 
-def halo_kernel(place, units, y_even, y_odd, strips, z_even, z_odd, x_even, x_odd):
+def face_kernel(place, units, z_even, z_odd, x_even, x_odd):
+    for d in range(DEEP):
+        for unit in range(6 if d < NEAR else 2):
+            at = unit * NEAR + d if d < NEAR else 6 * NEAR + unit
+            z_even[at], z_odd[at] = by_pairs(place, 2, units[unit, d], units[unit, STEPS - 1 - d])
+
+    def layer(z, _):
+        for unit, offset, count in face_rows()[0][:6]:
+            low, high = (units[unit, z, pl.ds(0, count)], units[unit, z, pl.ds(STEPS - count, count)])
+            even, odd = by_pairs(place, 0, low, high)
+            x_even[z, pl.ds(offset, count)] = even
+            x_odd[z, pl.ds(offset, count)] = odd
+        return 0
+
+    lax.fori_loop(0, STEPS, layer, 0, unroll=2)
+
+
+def halo_kernel(
+    place, y_odd, y_even, z_even_in, z_odd_in, x_even_in, x_odd_in, strips, z_even, z_odd, x_even, x_odd
+):
     def pair(z, _):
         low, high = sides(place, 1, y_even[z], y_odd[z])
         first = first_mask(lanes(high.shape))
@@ -140,28 +160,27 @@
         return 0
 
     lax.fori_loop(0, 8, pair, 0, unroll=4)
-
-    def read(unit, z, start, count):
-        return strips[z, pl.ds(start, count)] if unit == 6 else units[unit, z, pl.ds(start, count)]
-
-    for d in range(DEEP):
-        for unit in range(7 if d < NEAR else 2):
-            at = unit * NEAR + d if d < NEAR else 7 * NEAR + unit
-            z_even[at], z_odd[at] = by_pairs(
-                place, 2, read(unit, d, 0, STEPS), read(unit, STEPS - 1 - d, 0, STEPS)
-            )
+    for out, value in ((z_even, z_even_in), (z_odd, z_odd_in)):
+        out[pl.ds(0, 6 * NEAR + 2)] = value[...]
+    for d in range(NEAR):
+        z_even[6 * NEAR + 2 + d], z_odd[6 * NEAR + 2 + d] = by_pairs(
+            place, 2, strips[d], strips[STEPS - 1 - d]
+        )
 
     def layer(z, _):
-        for unit, offset, count in face_rows()[0]:
-            even, odd = by_pairs(place, 0, read(unit, z, 0, count), read(unit, z, STEPS - count, count))
-            x_even[z, pl.ds(offset, count)] = even
-            x_odd[z, pl.ds(offset, count)] = odd
-        return 0
-
-    lax.fori_loop(0, STEPS, layer, 0, unroll=2)
-
-
-def corner_kernel(place, x_even, x_odd, even, odd):
+        _, offset, count = face_rows()[0][6]
+        x_even[z, pl.ds(0, offset)] = x_even_in[z, pl.ds(0, offset)]
+        x_odd[z, pl.ds(0, offset)] = x_odd_in[z, pl.ds(0, offset)]
+        low, high = (strips[z, pl.ds(0, count)], strips[z, pl.ds(STEPS - count, count)])
+        even, odd = by_pairs(place, 0, low, high)
+        x_even[z, pl.ds(offset, count)] = even
+        x_odd[z, pl.ds(offset, count)] = odd
+        return 0
+
+    lax.fori_loop(0, STEPS, layer, 0, unroll=4)
+
+
+def corner_kernel(place, x_odd, x_even, _, even, odd):
     spans = {unit: (offset, count) for unit, offset, count in face_rows()[0]}
     for unit, d, offset, count in corner_rows()[0]:
         first, span = spans[unit]
@@ -339,7 +358,8 @@
     lax.fori_loop(0, STEPS, own, 0)
     for d in range(DEEP):
         for unit in range(7 if d < NEAR else 2):
-            at = unit * NEAR + d if d < NEAR else 7 * NEAR + unit
+            at = unit * NEAR + d if d < NEAR else 6 * NEAR + unit
+            at = 6 * NEAR + 2 + d if unit == 6 else at
             low, high = sides(place, 2, z_even[at], z_odd[at])
             grid[unit, DEEP - 1 - d, inside] = low
             grid[unit, DEEP + STEPS + d, inside] = high
@@ -358,25 +378,33 @@
 
     lax.fori_loop(0, PLANES, unpack, 0, unroll=5)
 
-    def sweep(main_from, side_from, write):
+    everywhere = slice(0, 32)
+
+    def sweep(main_from, side_from, main_to, side_to, rows, side_rows):
+        def new_value(f, z, part, coefficients, source, here, other, below, above):
+            total = source(f, z - 1, part) + source(f, z + 1, part)
+            if part == everywhere:
+                total = total + (pltpu.roll(here, 1, 0) + pltpu.roll(here, 31, 0))
+            else:
+                low, high = (slice(part.start - 1, part.stop - 1), slice(part.start + 1, part.stop + 1))
+                total = total + (source(f, z, low) + source(f, z, high))
+            total = total + (below + above)
+            return coefficients[f, z, part] + coefficients[2 + f, z, part] * total + coefficients[4 + f, z, part] * other
+
         def layer(z, _):
-            main = [main_from(f, z) for f in range(2)]
-            edge = [side_from(f, z) for f in range(2)]
+            main = [main_from(f, z, rows) for f in range(2)]
+            edge = [side_from(f, z, rows) for f in range(2)]
             lane = lanes(main[0].shape)
-            new_main, new_edge = ([], [])
             for f in range(2):
                 below = (pltpu.roll(main[f], 1, 1), pltpu.roll(edge[f], 1, 1))
                 above = (pltpu.roll(main[f], 127, 1), pltpu.roll(edge[f], 127, 1))
-                for i, (here, source) in enumerate(((main[f], main_from), (edge[f], side_from))):
-                    total = source(f, z - 1) + source(f, z + 1)
-                    total = total + (pltpu.roll(here, 1, 0) + pltpu.roll(here, 31, 0))
-                    total = total + jnp.where(lane == 0, below[1 - i], below[i])
-                    total = total + jnp.where(lane == 127, above[1 - i], above[i])
-                    ref = side if i else grid
-                    other = edge[1 - f] if i else main[1 - f]
-                    new = ref[f, z] + ref[2 + f, z] * total + ref[4 + f, z] * other
-                    (new_edge if i else new_main).append(new)
-            write(z, new_main, new_edge)
+                beside = [
+                    (jnp.where(lane == 0, below[1 - i], below[i]), jnp.where(lane == 127, above[1 - i], above[i]))
+                    for i in range(2)
+                ]
+                main_to(f, z, rows, new_value(f, z, rows, grid, main_from, main[f], main[1 - f], *beside[0]))
+                if side_rows is not None:
+                    side_to(f, z, rows, new_value(f, z, rows, side, side_from, edge[f], edge[1 - f], *beside[1]))
             return 0
 
         return layer
@@ -385,28 +413,33 @@
     for s in range(2, SWEEPS + 1):
         reach = SWEEPS - s
         if s == 2:
-            main_from, side_from = (lambda f, z: grid[f, z], lambda f, z: side[f, z])
+            main_from, side_from = (lambda f, z, part: grid[f, z, part], lambda f, z, part: side[f, z, part])
         else:
             old = buffers[s % 2]
-            main_from = lambda f, z, old=old: old[f, z]
-            side_from = lambda f, z, old=old: old[2 + f, z]
-        if s < SWEEPS:
-            new = buffers[(s + 1) % 2]
-
-            def write(z, new_main, new_edge, new=new):
-                for f in range(2):
-                    new[f, z] = new_main[f]
-                    new[2 + f, z] = new_edge[f]
+            main_from = lambda f, z, part, old=old: old[f, z, part]
+            side_from = lambda f, z, part, old=old: old[2 + f, z, part]
+        new = buffers[(s + 1) % 2]
+
+        def main_to(f, z, part, value, new=new):
+            new[f, z, part] = value
+
+        def side_to(f, z, part, value, new=new):
+            new[2 + f, z, part] = value
+
+        def last_to(f, z, part, value):
+            predicted[f, z - DEEP] = value
+            increment[f, pl.ds(z - DEEP, STEPS, stride=STEPS), :] = observed[f, z - DEEP] - value
+
+        first, last = (DEEP - reach, DEEP + STEPS + reach - 1)
+        if reach == 0:
+            layer = sweep(main_from, side_from, last_to, None, inside, None)
+            lax.fori_loop(first, last + 1, layer, 0, unroll=8)
         else:
-
-            def write(z, new_main, new_edge):
-                for f in range(2):
-                    value = new_main[f][inside]
-                    predicted[f, z - DEEP] = value
-                    change = observed[f, z - DEEP] - value
-                    increment[f, pl.ds(z - DEEP, STEPS, stride=STEPS), :] = change
-
-        lax.fori_loop(DEEP - reach, DEEP + STEPS + reach, sweep(main_from, side_from, write), 0, unroll=8)
+            outermost = sweep(main_from, side_from, main_to, None, inside, None)
+            outermost(first, 0)
+            outermost(last, 0)
+            layer = sweep(main_from, side_from, main_to, side_to, everywhere, everywhere)
+            lax.fori_loop(first + 1, last, layer, 0, unroll=8)
 
     def weight(i, g):
         return wx[g // 2, i, pl.ds(8 * (g % 2), 8)]
@@ -429,7 +462,7 @@
             message[j, pl.ds(4 * v, 4)] = ends[v, rows] if v < 8 else mx[v - 8, rows]
 
 
-def solve_kernel(gathered, inflow):
+def solve_kernel(gathered, _, inflow):
     parts = [[gathered[s, pl.ds(4 * v, 4)] for v in range(22)] for s in range(8)]
     zero = [jnp.zeros((4, 128), F32)] * 4
     lows, highs = chained([p[8:] for p in parts], [p[:8] for p in parts], zero, zero)
@@ -511,7 +544,7 @@
 
 
 def y_finish_kernel(
-    place, lines, wy, my, block_ends, own, xor_1, xor_2, xor_3, wz, unsmoothed, message,
+    place, lines, wy, my, block_ends, own, xor_3, xor_2, xor_1, wz, unsmoothed, message,
     passed, start, done, by_row, inflow,
 ):
     refs = (own, xor_1, xor_2, xor_3)
@@ -574,7 +607,7 @@
 
 
 def z_finish_kernel(
-    place, unsmoothed, wz, maps_0, maps_1, maps_2, maps_3, ends_0, ends_1, ends_2, ends_3, smoothed, passed, inflow
+    place, unsmoothed, wz, maps_0, maps_1, maps_2, maps_3, ends_0, ends_3, ends_2, ends_1, smoothed, passed, inflow
 ):
     maps = (maps_0, maps_1, maps_2, maps_3)
     ends = (ends_0, ends_1, ends_2, ends_3)
@@ -625,14 +658,14 @@
         for k in range(others):
             j = i + 1 if i % 2 else i - 1
             odd.append((flat(i, k), flat(j, k) if 0 <= j < count else flat(i, k ^ 1)))
+    from_even = lax.ppermute(value_even, axis, [(i, i ^ 1) for i in range(count)])
     from_odd = lax.ppermute(value_odd, axes, odd)
-    from_even = lax.ppermute(value_even, axis, [(i, i ^ 1) for i in range(count)])
     return from_even, from_odd
 
 
 def xor_gather(value, axis):
     count = lax.axis_size(axis)
-    return [value] + [lax.ppermute(value, axis, [(i, i ^ s) for i in range(count)]) for s in (3, 2, 1)][::-1]
+    return [value] + [lax.ppermute(value, axis, [(i, i ^ s) for i in range(count)]) for s in (1, 2, 3)]
 
 
 def local(source, capacity, transfer, observed, classes, conductivity, filter_rates):
@@ -643,22 +676,22 @@
     units, y_even, y_odd, classes = call(
         coefficients_kernel,
         [(6,) + plane, (8, STEPS, 128), (8, STEPS, 128), jax.ShapeDtypeStruct(plane, jnp.int32)],
-        [SMEM] + [HBM] * 4 + [SMEM],
+        [HBM] * 4 + [SMEM],
         [plane, (2,) + plane, (2,) + plane, plane],
         limit=60,
         copies=4,
-    )(place, source, capacity, transfer, classes, conductivity)
+    )(source, capacity, transfer, classes, conductivity)
     y_even, y_odd = pair_swaps("gy", "gz", y_even, y_odd)
 
     z_face = (7 * NEAR + 2, STEPS, 128)
     x_face = (STEPS, face_rows()[1], 128)
     corners = (2, corner_rows()[1], 128)
+    z_own = (6 * NEAR + 2, STEPS, 128)
+    x_own = (STEPS, face_rows()[0][6][1], 128)
+    faces = call(face_kernel, [z_own, z_own, x_own, x_own], [SMEM, VMEM])(place, units)
     strips, z_even, z_odd, x_even, x_odd = call(
-        halo_kernel,
-        [plane, z_face, z_face, x_face, x_face],
-        [SMEM] + [VMEM] * 3,
-        limit=60,
-    )(place, units, y_even, y_odd)
+        halo_kernel, [plane, z_face, z_face, x_face, x_face], [SMEM] + [VMEM] * 6
+    )(place, y_odd, y_even, *faces)
     x_even, x_odd = pair_swaps("gx", "gy", x_even, x_odd)
     z_even, z_odd = pair_swaps("gz", "gy", z_even, z_odd)
 
@@ -668,10 +701,9 @@
         [(2,) + plane, (4, 128, 128), (2,) + plane, (14,) + rows, (14,) + rows, (56, 128), (14,) + rows,
          (256, 128), (2, 128, 128)],
         [VMEM, SMEM, VMEM],
-        limit=60,
     )(classes, rates, strips)
-    x_even, wx = lax.optimization_barrier((x_even, wx))
-    corner_even, corner_odd = call(corner_kernel, [corners, corners], [SMEM] + [VMEM] * 2, limit=60)(place, x_even, x_odd)
+    x_odd, wx = lax.optimization_barrier((x_odd, wx))
+    corner_even, corner_odd = call(corner_kernel, [corners, corners], [SMEM] + [VMEM] * 3)(place, x_odd, x_even, observed)
     corner_even, corner_odd = pair_swaps("gz", "gy", corner_even, corner_odd)
     z_maps = xor_gather(mz, "gz")
 
@@ -682,11 +714,11 @@
         [SMEM] + [VMEM] * 11,
         [(7,) + padded, (6,) + padded, (4,) + padded, (4,) + padded, (STEPS,) + rows, (8,) + rows],
         flops=100000000,
-        limit=60,
+        limit=16,
     )(place, units, strips, z_even, z_odd, x_even, x_odd, corner_even, corner_odd,
       observed, wx, mx)
     gathered = lax.all_to_all(message, "gx", 0, 0, tiled=True)
-    inflow, = call(solve_kernel, [(8, 32, 128)], [VMEM])(gathered)
+    inflow, = call(solve_kernel, [(8, 32, 128)], [VMEM] * 2)(gathered, increment)
     inflow = lax.all_to_all(inflow, "gx", 0, 0, tiled=True)
     inflow, z_maps = lax.optimization_barrier((inflow, z_maps))
     lines, block_ends, y_ends = call(
@@ -701,10 +733,10 @@
         [(2,) + plane, (8,) + rows],
         [SMEM] + [VMEM] * 9,
         [(2, 256, 128), (8,) + rows, (4, 128, 128), (2, 256, 128), (8, 8, 128)],
-    )(place, lines, wy, my, block_ends, *y_all, wz)
+    )(place, lines, wy, my, block_ends, y_all[0], *y_all[:0:-1], wz)
     z_all = xor_gather(z_ends, "gz")
     smoothed, = call(z_finish_kernel, [(2,) + plane], [SMEM] + [VMEM] * 10, [(2,) + plane, (8,) + rows])(
-        place, unsmoothed, wz, *z_maps, *z_all
+        place, unsmoothed, wz, *z_maps, z_all[0], *z_all[:0:-1]
     )
     return (predicted, smoothed)
 

time: 97.1 us -> 89 us (0.917)
  waiting for transfers between devices: 29.7 us -> 25.2 us
  Pallas kernels: 28.3 us -> 24.8 us
    ppermute x4, starting transfers between devices: 5.41 us -> 8.47 us  [pair_swaps(): lax.ppermute(value_even, axis, [(i, i ^ 1) for i in range(count)])]
    ppermute x4, waiting for transfers between devices: 2.82 us -> 0.01 us  [pair_swaps(): from_odd = lax.ppermute(value_odd, axes, odd)]
    ppermute x9, waiting for transfers between devices: 13.2 us -> 10.9 us  [xor_gather(): lax.ppermute(value, axis, [(i, i ^ s) for i in range(count)])]
    all_to_all x1, starting transfers between devices: 7.19 us -> 5.75 us  [local(): gathered = lax.all_to_all(message, 'gx', 0, 0, tiled=True)]
    pallas_call x1, Pallas kernels: 12 us -> 10.6 us  [local(): call(sweep_kernel, [(2,) + plane, (2, 256, 128), (8, 88, 128)], [SMEM] +...]
    ppermute x4, starting transfers between devices: 3.13 us -> 1.91 us  [pair_swaps(): from_odd = lax.ppermute(value_odd, axes, odd)]
    unnamed x34 -> x20, local copies, waits for them, and re-layouts: 3.46 us -> 4.31 us
    pallas_call x2 -> x3, Pallas kernels: 2.67 us -> 2.12 us  [the longest x1 0.74 us: local(): call(solve_kernel, [(8, 32, 128)], [VMEM] * 2)(gathered, increment)]
  transfers between devices with their start and end apart: 19 -> 19, of which waited for: 11 -> 10; matrix products, arithmetic and copies ran while one was open for 1% -> 0% of each run, Pallas kernels for 7% -> 6%
where the time goes in v3:
time: 89 us; the launch traced here: 87.5 us
  starting transfers between devices  32.4 us (36%)
  waiting for transfers between devices  25.2 us (28%)
  Pallas kernels  24.8 us (28%)
  local copies, waits for them, and re-layouts  4.4 us (5%)
    ppermute x9, starting transfers between devices, xor_gather(): lax.ppermute(value, axis, [(i, i ^ s) for i in range(count)])  12.9 us
    ppermute x9, waiting for transfers between devices, xor_gather(): lax.ppermute(value, axis, [(i, i ^ s) for i in range(count)])  10.9 us
    pallas_call x1, Pallas kernels, local(): call(sweep_kernel, [(2,) + plane, (2, 256, 128), (8, 88, 128)], [SMEM] +...  10.6 us
    ppermute x4, starting transfers between devices, pair_swaps(): lax.ppermute(value_even, axis, [(i, i ^ 1) for i in range(count)])  8.47 us
    ppermute x4, waiting for transfers between devices, pair_swaps(): lax.ppermute(value_even, axis, [(i, i ^ 1) for i in range(count)])  6.61 us
    all_to_all x1, starting transfers between devices, local(): gathered = lax.all_to_all(message, 'gx', 0, 0, tiled=True)  5.75 us
    all_to_all x1, waiting for transfers between devices, local(): inflow = lax.all_to_all(inflow, 'gx', 0, 0, tiled=True)  4.92 us
    unnamed x20, local copies, waits for them, and re-layouts  4.31 us
  transfers between devices with their start and end apart: 19, of which 10 were waited for; matrix products, arithmetic and copies ran while one was open for 0% of the time, Pallas kernels for 6%

profile of v3, /device:TPU:0, one launch (start us, length us, event | category | flops | bytes accessed | tf_op | source)
XLA Modules:
  0.0 87.5 jit_solution(2956468894278130041)
XLA Ops:
  0.6 3.5 %shard_map.86 = (f32[6,16,16,128]{3,2,1,0:T(8,128)}, f32[8,16,128]{2,1,0:T(8,128)}, f32[8,16,128]{2,1,0:T(8,128)}, s32[16,16,128]{2,1,0:T(8,128)}) custom-call(f32[2,16,16,128]{3,2,1,0:T(8,128)} %source_in.1, f32[2,16,16,128]{3,2,1,0:T(8,128)} %capacity_in.1, f32[16,16,128]{2,1,0:T(8,128)} %transfer_in.1, s32[16,16,128]{2,1,0:T(8,128)} %classes_in.1, ...), custom_call_target="tpu_custom_call" | custom-call | flops 1000000 | bytes 1000000 | tf_op jit(solution)/shard_map/pallas_call | solution.py:676
  4.1 1.7 %collective-permute-start = (f32[8,16,128]{2,1,0:T(8,128)}, f32[8,16,128]{2,1,0:T(8,128)S(1)}, u32[]{:S(2)}, u32[]{:S(2)}) collective-permute-start(f32[8,16,128]{2,1,0:T(8,128)} %get-tuple-element.40), channel_id=1, source_target_pairs={{0,1},{1,0},{2,3},{3,2},{4,8},{5,9},{6,10},{7,11},{8,4},{9,5},{10,... | collective-permute-start | bytes 196616 | tf_op jit(solution)/shard_map/ppermute | solution.py:662
  5.9 1.6 %collective-permute-start.1 = (f32[8,16,128]{2,1,0:T(8,128)}, f32[8,16,128]{2,1,0:T(8,128)S(1)}, u32[]{:S(2)}, u32[]{:S(2)}) collective-permute-start(f32[8,16,128]{2,1,0:T(8,128)} %get-tuple-element.41), channel_id=1, source_target_pairs={{0,4},{4,0},{8,12},{12,8},{1,5},{5,1},{9,13},{13,9},{2,6},{6,2},{1... | collective-permute-start | bytes 196616 | tf_op jit(solution)/shard_map/ppermute | solution.py:661
  7.4 0.1 stack.15.place
  7.5 0.0 copy-start
  7.5 1.1 %copy-done = f32[6,16,16,128]{3,2,1,0:T(8,128)S(1)} copy-done((f32[6,16,16,128]{3,2,1,0:T(8,128)S(1)}, f32[6,16,16,128]{3,2,1,0:T(8,128)}, u32[]{:S(2)}) %copy-start) | copy-done | bytes 786456
  8.7 0.7 shard_map.87
  9.4 0.0 collective-permute-done.y_odd
  9.4 0.0 collective-permute-done.1.y_even
  9.4 0.0 copy-start.9
  9.4 0.0 copy-start.8
  9.4 0.0 copy-start.2
  9.4 2.0 %shard_map.88 = (f32[16,16,128]{2,1,0:T(8,128)S(1)}, f32[44,16,128]{2,1,0:T(8,128)}, f32[44,16,128]{2,1,0:T(8,128)}, f32[16,44,128]{2,1,0:T(8,128)}, f32[16,44,128]{2,1,0:T(8,128)}) custom-call(s32[6]{0:T(128)S(1)} %stack.15.place, f32[8,16,128]{2,1,0:T(8,128)S(1)} %collective-permute-done.y_odd, f32[8,16,128]{2,1,0:T(8,128)S(1)} %collective-permute-done.1.y_even, ...), custom_call_target="tpu_custom_call" | custom-call | flops 1000000 | bytes 1000000 | tf_op jit(solution)/shard_map/pallas_call | solution.py:692
  11.4 0.0 copy-start.1
  11.4 0.2 collective-permute-start.5
  11.6 3.7 %collective-permute-start.4 = (f32[16,44,128]{2,1,0:T(8,128)}, f32[16,44,128]{2,1,0:T(8,128)S(1)}, u32[]{:S(2)}, u32[]{:S(2)}) collective-permute-start(f32[16,44,128]{2,1,0:T(8,128)} %get-tuple-element.49), channel_id=1, source_target_pairs={{0,16},{16,0},{32,48},{48,32},{64,80},{80,64},{96,112},{112,96},{1... | collective-permute-start | bytes 1081352 | tf_op jit(solution)/shard_map/ppermute | solution.py:661
  15.2 1.6 %collective-permute-start.2 = (f32[44,16,128]{2,1,0:T(8,128)}, f32[44,16,128]{2,1,0:T(8,128)S(1)}, u32[]{:S(2)}, u32[]{:S(2)}) collective-permute-start(f32[44,16,128]{2,1,0:T(8,128)} %get-tuple-element.47), channel_id=1, source_target_pairs={{0,1},{1,0},{2,3},{3,2},{4,5},{5,4},{6,7},{7,6},{8,9},{9,8},{10,11... | collective-permute-start | bytes 1081352 | tf_op jit(solution)/shard_map/ppermute | solution.py:661
  16.8 0.0 collective-permute-start.3
  16.8 0.0 copy-done.9
  16.8 0.0 copy-done.8
  16.8 3.0 %shard_map.89 = (f32[2,16,16,128]{3,2,1,0:T(8,128)S(1)}, f32[4,128,128]{2,1,0:T(8,128)S(1)}, f32[2,16,16,128]{3,2,1,0:T(8,128)S(1)}, f32[14,32,128]{2,1,0:T(8,12...) custom-call(s32[16,16,128]{2,1,0:T(8,128)S(1)} %copy-done.8, ...), custom_call_target="tpu_custom_call" | custom-call | flops 1000000 | bytes 1000000 | tf_op jit(solution)/shard_map/pallas_call | solution.py:699
  19.9 0.7 copy-done.6
  20.5 0.0 collective-permute-done.5.x_odd
  20.6 4.1 %collective-permute-done.4.x_even = f32[16,44,128]{2,1,0:T(8,128)S(1)} collective-permute-done((f32[16,44,128]{2,1,0:T(8,128)}, f32[16,44,128]{2,1,0:T(8,128)S(1)}, u32[]{:S(2)}, u32[]{:S(2)}) %collective-permute-start.4) | collective-permute-done | bytes 360480 | tf_op jit(solution)/shard_map/ppermute | solution.py:661
  24.6 0.0 copy-done.2
  24.6 0.7 shard_map.90
  25.3 1.7 %collective-permute-start.6 = (f32[2,120,128]{2,1,0:T(8,128)S(1)}, f32[2,120,128]{2,1,0:T(8,128)S(1)}, u32[]{:S(2)}, u32[]{:S(2)}) collective-permute-start(f32[2,120,128]{2,1,0:T(8,128)S(1)} %get-tuple-element.54), channel_id=1, source_target_pairs={{0,1},{1,0},{2,3},{3,2},{4,5},{5,4},{6,7},{7,6},{8,9},{9,8},{10,11... | collective-permute-start | bytes 368648 | tf_op jit(solution)/shard_map/ppermute | solution.py:661
  26.9 0.0 collective-permute-start.7
  26.9 0.0 collective-permute-done.2.z_even
  26.9 0.7 copy-done.4
  27.7 0.0 collective-permute-done.3.z_odd
  27.7 2.5 %collective-permute-done.6.corner_even = f32[2,120,128]{2,1,0:T(8,128)S(1)} collective-permute-done((f32[2,120,128]{2,1,0:T(8,128)S(1)}, f32[2,120,128]{2,1,0:T(8,128)S(1)}, u32[]{:S(2)}, u32[]{:S(2)}) %collective-permute-start.6) | collective-permute-done | bytes 122912 | tf_op jit(solution)/shard_map/ppermute | solution.py:661
  30.2 0.0 collective-permute-done.7.corner_odd
  30.2 0.0 copy-done.1
  30.2 1.0 %copy-done.5 = f32[44,16,128]{2,1,0:T(8,128)S(1)} copy-done((f32[44,16,128]{2,1,0:T(8,128)S(1)}, f32[44,16,128]{2,1,0:T(8,128)}, u32[]{:S(2)}) %copy-start.5) | copy-done | bytes 360472
  31.2 10.6 %shard_map.91 = (f32[2,16,16,128]{3,2,1,0:T(8,128)}, f32[2,256,128]{2,1,0:T(8,128)S(1)}, f32[8,88,128]{2,1,0:T(8,128)S(1)}) custom-call(s32[6]{0:T(128)S(1)} %stack.15.place, f32[6,16,16,128]{3,2,1,0:T(8,128)S(1)} %copy-done.1, f32[16,16,128]{2,1,0:T(8,128)S(1)} %get-tuple-element.46._.strips, f32[44,16,128]{2,1,0:T(8,128)S(1)} %copy-done.5, ...), custom_call_target="tpu_custom_call" | custom-call | flops 100000000 | bytes 1000000 | tf_op jit(solution)/shard_map/pallas_call | solution.py:711
  41.8 0.7 copy-done.3
  42.5 5.7 %all-to-all-start = ((f32[8,88,128]{2,1,0:T(8,128)}), f32[8,88,128]{2,1,0:T(8,128)S(1)}, u32[]{:S(2)}, u32[]{:S(2)}) async-start(f32[8,88,128]{2,1,0:T(8,128)} %copy-done.3), calls=%async_computation | async-start | bytes 720896 | tf_op jit(solution)/shard_map/all_to_all | solution.py:720
  48.3 0.0 copy-done.7
  48.3 3.1 %collective-permute-start.10 = (f32[14,32,128]{2,1,0:T(8,128)S(1)}, f32[14,32,128]{2,1,0:T(8,128)S(1)}, u32[]{:S(2)}, u32[]{:S(2)}) collective-permute-start(f32[14,32,128]{2,1,0:T(8,128)S(1)} %copy-done.7), channel_id=1, source_target_pairs={{0,3},{1,2},{2,1},{3,0},{4,7},{5,6},{6,5},{7,4},{8,11},{9,10},{10,... | collective-permute-start | bytes 688136 | tf_op jit(solution)/shard_map/ppermute | solution.py:668
  51.4 1.4 %collective-permute-start.8 = (f32[14,32,128]{2,1,0:T(8,128)S(1)}, f32[14,32,128]{2,1,0:T(8,128)S(1)}, u32[]{:S(2)}, u32[]{:S(2)}) collective-permute-start(f32[14,32,128]{2,1,0:T(8,128)S(1)} %copy-done.7), channel_id=1, source_target_pairs={{0,1},{1,0},{2,3},{3,2},{4,5},{5,4},{6,7},{7,6},{8,9},{9,8},{10,11... | collective-permute-start | bytes 688136 | tf_op jit(solution)/shard_map/ppermute | solution.py:668
  52.8 0.3 collective-permute-start.9
  53.1 2.8 %all-to-all-done.gathered = f32[8,88,128]{2,1,0:T(8,128)S(1)} async-done(((f32[8,88,128]{2,1,0:T(8,128)}), f32[8,88,128]{2,1,0:T(8,128)S(1)}, u32[]{:S(2)}, u32[]{:S(2)}) %all-to-all-start) | async-done | bytes 360480 | tf_op jit(solution)/shard_map/all_to_all | solution.py:720
  55.9 0.7 shard_map.92
  56.6 3.4 %all-to-all-start.1 = ((f32[8,32,128]{2,1,0:T(8,128)}), f32[8,32,128]{2,1,0:T(8,128)S(1)}, u32[]{:S(2)}, u32[]{:S(2)}) async-start(f32[8,32,128]{2,1,0:T(8,128)} %shard_map.92), calls=%async_computation.1 | async-start | bytes 262144 | tf_op jit(solution)/shard_map/all_to_all | solution.py:722
  60.0 0.0 collective-permute-done.10.maps_3
  60.0 0.0 collective-permute-done.8.maps_1
  60.0 1.6 %collective-permute-done.9.maps_2 = f32[14,32,128]{2,1,0:T(8,128)S(1)} collective-permute-done((f32[14,32,128]{2,1,0:T(8,128)S(1)}, f32[14,32,128]{2,1,0:T(8,128)S(1)}, u32[]{:S(2)}, u32[]{:S(2)}) %collective-permute-start.9) | collective-permute-done | bytes 229408 | tf_op jit(solution)/shard_map/ppermute | solution.py:668
  61.6 4.9 %all-to-all-done.1.inflow = f32[8,32,128]{2,1,0:T(8,128)S(1)} async-done(((f32[8,32,128]{2,1,0:T(8,128)}), f32[8,32,128]{2,1,0:T(8,128)S(1)}, u32[]{:S(2)}, u32[]{:S(2)}) %all-to-all-start.1) | async-done | bytes 131104 | tf_op jit(solution)/shard_map/all_to_all | solution.py:722
  66.5 0.6 shard_map.93
  67.1 0.1 collective-permute-start.11
  67.2 2.3 %collective-permute-start.12 = (f32[88,128]{1,0:T(8,128)S(1)}, f32[88,128]{1,0:T(8,128)S(1)}, u32[]{:S(2)}, u32[]{:S(2)}) collective-permute-start(f32[88,128]{1,0:T(8,128)S(1)} %get-tuple-element.68.own), channel_id=1, source_target_pairs={{0,8},{4,12},{8,0},{12,4},{1,9},{5,13},{9,1},{13,5},{2,10},{6,14},... | collective-permute-start | bytes 135176 | tf_op jit(solution)/shard_map/ppermute | solution.py:668
  69.5 1.0 %collective-permute-start.13 = (f32[88,128]{1,0:T(8,128)S(1)}, f32[88,128]{1,0:T(8,128)S(1)}, u32[]{:S(2)}, u32[]{:S(2)}) collective-permute-start(f32[88,128]{1,0:T(8,128)S(1)} %get-tuple-element.68.own), channel_id=1, source_target_pairs={{0,4},{4,0},{8,12},{12,8},{1,5},{5,1},{9,13},{13,9},{2,6},{6,2},{1... | collective-permute-start | bytes 135176 | tf_op jit(solution)/shard_map/ppermute | solution.py:668
  70.6 1.6 %collective-permute-done.11.xor_3 = f32[88,128]{1,0:T(8,128)S(1)} collective-permute-done((f32[88,128]{1,0:T(8,128)S(1)}, f32[88,128]{1,0:T(8,128)S(1)}, u32[]{:S(2)}, u32[]{:S(2)}) %collective-permute-start.11) | collective-permute-done | bytes 45088 | tf_op jit(solution)/shard_map/ppermute | solution.py:668
  72.2 0.7 collective-permute-done.12.xor_2
  72.9 0.0 collective-permute-done.13.xor_1
  72.9 1.3 %shard_map.94 = (f32[2,16,16,128]{3,2,1,0:T(8,128)S(1)}, f32[8,32,128]{2,1,0:T(8,128)S(1)}) custom-call(s32[6]{0:T(128)S(1)} %stack.15.place, f32[4,128,128]{2,1,0:T(8,128)S(1)} %get-tuple-element.66.lines, f32[4,128,128]{2,1,0:T(8,128)S(1)} %get-tuple-element.63.wy, f32[14,32,128]{2,1,0:T(8,128)S(1)} %get-tuple-element.64.my, ...), custom_call_target="tpu_custom_call" | custom-call | flops 1000000 | bytes 1000000 | tf_op jit(solution)/shard_map/pallas_call | solution.py:731
  74.1 3.1 %collective-permute-start.14 = (f32[8,32,128]{2,1,0:T(8,128)S(1)}, f32[8,32,128]{2,1,0:T(8,128)S(1)}, u32[]{:S(2)}, u32[]{:S(2)}) collective-permute-start(f32[8,32,128]{2,1,0:T(8,128)S(1)} %get-tuple-element.75.ends_0), channel_id=1, source_target_pairs={{0,3},{1,2},{2,1},{3,0},{4,7},{5,6},{6,5},{7,4},{8,11},{9,10},{10,... | collective-permute-start | bytes 393224 | tf_op jit(solution)/shard_map/ppermute | solution.py:668
  77.2 1.6 %collective-permute-start.15 = (f32[8,32,128]{2,1,0:T(8,128)S(1)}, f32[8,32,128]{2,1,0:T(8,128)S(1)}, u32[]{:S(2)}, u32[]{:S(2)}) collective-permute-start(f32[8,32,128]{2,1,0:T(8,128)S(1)} %get-tuple-element.75.ends_0), channel_id=1, source_target_pairs={{0,2},{1,3},{2,0},{3,1},{4,6},{5,7},{6,4},{7,5},{8,10},{9,11},{10,... | collective-permute-start | bytes 393224 | tf_op jit(solution)/shard_map/ppermute | solution.py:668
  78.8 0.0 collective-permute-start.16
  78.8 5.0 %collective-permute-done.14.ends_3 = f32[8,32,128]{2,1,0:T(8,128)S(1)} collective-permute-done((f32[8,32,128]{2,1,0:T(8,128)S(1)}, f32[8,32,128]{2,1,0:T(8,128)S(1)}, u32[]{:S(2)}, u32[]{:S(2)}) %collective-permute-start.14) | collective-permute-done | bytes 131104 | tf_op jit(solution)/shard_map/ppermute | solution.py:668
  83.8 1.3 %collective-permute-done.15.ends_2 = f32[8,32,128]{2,1,0:T(8,128)S(1)} collective-permute-done((f32[8,32,128]{2,1,0:T(8,128)S(1)}, f32[8,32,128]{2,1,0:T(8,128)S(1)}, u32[]{:S(2)}, u32[]{:S(2)}) %collective-permute-start.15) | collective-permute-done | bytes 131104 | tf_op jit(solution)/shard_map/ppermute | solution.py:668
  85.1 0.7 collective-permute-done.16.ends_1
  85.8 1.7 %shard_map.95 = f32[2,16,16,128]{3,2,1,0:T(8,128)} custom-call(s32[6]{0:T(128)S(1)} %stack.15.place, f32[2,16,16,128]{3,2,1,0:T(8,128)S(1)} %get-tuple-element.70.unsmoothed, f32[2,16,16,128]{3,2,1,0:T(8,128)S(1)} %get-tuple-element.69.wz, f32[14,32,128]{2,1,0:T(8,128)S(1)} %copy-done.7, f32[14,32,128]{2,1,0:T(8,128)S(1)} %collective-permute-done.8.maps_1, ...), custom_call_target="tpu_custom_call" | custom-call | flops 1000000 | bytes 1000000 | tf_op jit(solution)/shard_map/pallas_call | solution.py:738
  (7 shorter events, 0.0 us)
Async XLA Ops:
  4.1 5.3 %collective-permute-start = (f32[8,16,128]{2,1,0:T(8,128)}, f32[8,16,128]{2,1,0:T(8,128)S(1)}, u32[]{:S(2)}, u32[]{:S(2)}) collective-permute-start(f32[8,16,128]{2,1,0:T(8,128)} %get-tuple-element.40), channel_id=1, source_target_pairs={{0,1},{1,0},{2,3},{3,2},{4,8},{5,9},{6,10},{7,11},{8,4},{9,5},{10,... | collective-permute-start | bytes 196616 | tf_op jit(solution)/shard_map/ppermute | solution.py:662
  5.9 3.5 %collective-permute-start.1 = (f32[8,16,128]{2,1,0:T(8,128)}, f32[8,16,128]{2,1,0:T(8,128)S(1)}, u32[]{:S(2)}, u32[]{:S(2)}) collective-permute-start(f32[8,16,128]{2,1,0:T(8,128)} %get-tuple-element.41), channel_id=1, source_target_pairs={{0,4},{4,0},{8,12},{12,8},{1,5},{5,1},{9,13},{13,9},{2,6},{6,2},{1... | collective-permute-start | bytes 196616 | tf_op jit(solution)/shard_map/ppermute | solution.py:661
  7.5 1.1 %copy-start = (f32[6,16,16,128]{3,2,1,0:T(8,128)S(1)}, f32[6,16,16,128]{3,2,1,0:T(8,128)}, u32[]{:S(2)}) copy-start(f32[6,16,16,128]{3,2,1,0:T(8,128)} %get-tuple-element.39.units) | copy-start | bytes 2359300
  9.4 7.4 %copy-start.9 = (f32[3,2,12]{2,1,0:T(2,128)S(1)}, f32[3,2,12]{2,1,0:T(2,128)}, u32[]{:S(2)}) copy-start(f32[3,2,12]{2,1,0:T(2,128)} %param.13) | copy-start | bytes 868
  9.4 7.4 %copy-start.8 = (s32[16,16,128]{2,1,0:T(8,128)S(1)}, s32[16,16,128]{2,1,0:T(8,128)}, u32[]{:S(2)}) copy-start(s32[16,16,128]{2,1,0:T(8,128)} %get-tuple-element.51.classes) | copy-start | bytes 393220
  9.4 15.2 %copy-start.2 = (f32[2,16,16,128]{3,2,1,0:T(8,128)S(1)}, f32[2,16,16,128]{3,2,1,0:T(8,128)}, u32[]{:S(2)}) copy-start(f32[2,16,16,128]{3,2,1,0:T(8,128)} %observed.1) | copy-start | bytes 786436
  11.4 18.8 %copy-start.1 = (f32[6,16,16,128]{3,2,1,0:T(8,128)S(1)}, f32[6,16,16,128]{3,2,1,0:T(8,128)}, u32[]{:S(2)}) copy-start(f32[6,16,16,128]{3,2,1,0:T(8,128)} %get-tuple-element.39.units) | copy-start | bytes 2359300
  11.4 9.1 %collective-permute-start.5 = (f32[16,44,128]{2,1,0:T(8,128)}, f32[16,44,128]{2,1,0:T(8,128)S(1)}, u32[]{:S(2)}, u32[]{:S(2)}) collective-permute-start(f32[16,44,128]{2,1,0:T(8,128)} %get-tuple-element.50), channel_id=1, source_target_pairs={{0,4},{4,0},{8,12},{12,8},{16,32},{20,36},{24,40},{28,44},{32,16},... | collective-permute-start | bytes 1081352 | tf_op jit(solution)/shard_map/ppermute | solution.py:662
  11.6 13.0 %collective-permute-start.4 = (f32[16,44,128]{2,1,0:T(8,128)}, f32[16,44,128]{2,1,0:T(8,128)S(1)}, u32[]{:S(2)}, u32[]{:S(2)}) collective-permute-start(f32[16,44,128]{2,1,0:T(8,128)} %get-tuple-element.49), channel_id=1, source_target_pairs={{0,16},{16,0},{32,48},{48,32},{64,80},{80,64},{96,112},{112,96},{1... | collective-permute-start | bytes 1081352 | tf_op jit(solution)/shard_map/ppermute | solution.py:661
  15.2 11.7 %collective-permute-start.2 = (f32[44,16,128]{2,1,0:T(8,128)}, f32[44,16,128]{2,1,0:T(8,128)S(1)}, u32[]{:S(2)}, u32[]{:S(2)}) collective-permute-start(f32[44,16,128]{2,1,0:T(8,128)} %get-tuple-element.47), channel_id=1, source_target_pairs={{0,1},{1,0},{2,3},{3,2},{4,5},{5,4},{6,7},{7,6},{8,9},{9,8},{10,11... | collective-permute-start | bytes 1081352 | tf_op jit(solution)/shard_map/ppermute | solution.py:661
  16.8 10.9 %collective-permute-start.3 = (f32[44,16,128]{2,1,0:T(8,128)}, f32[44,16,128]{2,1,0:T(8,128)}, u32[]{:S(2)}, u32[]{:S(2)}) collective-permute-start(f32[44,16,128]{2,1,0:T(8,128)} %get-tuple-element.48), channel_id=1, source_target_pairs={{0,4},{4,0},{8,12},{12,8},{1,2},{5,6},{9,10},{13,14},{2,1},{6,5},{... | collective-permute-start | bytes 1081352 | tf_op jit(solution)/shard_map/ppermute | solution.py:662
  19.9 0.7 copy-start.6
  25.3 5.0 %collective-permute-start.6 = (f32[2,120,128]{2,1,0:T(8,128)S(1)}, f32[2,120,128]{2,1,0:T(8,128)S(1)}, u32[]{:S(2)}, u32[]{:S(2)}) collective-permute-start(f32[2,120,128]{2,1,0:T(8,128)S(1)} %get-tuple-element.54), channel_id=1, source_target_pairs={{0,1},{1,0},{2,3},{3,2},{4,5},{5,4},{6,7},{7,6},{8,9},{9,8},{10,11... | collective-permute-start | bytes 368648 | tf_op jit(solution)/shard_map/ppermute | solution.py:661
  26.9 3.3 %collective-permute-start.7 = (f32[2,120,128]{2,1,0:T(8,128)S(1)}, f32[2,120,128]{2,1,0:T(8,128)S(1)}, u32[]{:S(2)}, u32[]{:S(2)}) collective-permute-start(f32[2,120,128]{2,1,0:T(8,128)S(1)} %get-tuple-element.55), channel_id=1, source_target_pairs={{0,4},{4,0},{8,12},{12,8},{1,2},{5,6},{9,10},{13,14},{2,1},{6,5},{... | collective-permute-start | bytes 368648 | tf_op jit(solution)/shard_map/ppermute | solution.py:662
  26.9 0.7 copy-start.4
  30.2 1.0 %copy-start.5 = (f32[44,16,128]{2,1,0:T(8,128)S(1)}, f32[44,16,128]{2,1,0:T(8,128)}, u32[]{:S(2)}) copy-start(f32[44,16,128]{2,1,0:T(8,128)} %copy-done.4) | copy-start | bytes 1081348
  41.8 0.7 copy-start.3
  42.5 5.8 %copy-start.7 = (f32[14,32,128]{2,1,0:T(8,128)S(1)}, f32[14,32,128]{2,1,0:T(8,128)}, u32[]{:S(2)}) copy-start(f32[14,32,128]{2,1,0:T(8,128)} %copy-done.6) | copy-start | bytes 688132
  42.5 13.4 %all-to-all-start = ((f32[8,88,128]{2,1,0:T(8,128)}), f32[8,88,128]{2,1,0:T(8,128)S(1)}, u32[]{:S(2)}, u32[]{:S(2)}) async-start(f32[8,88,128]{2,1,0:T(8,128)} %copy-done.3), calls=%async_computation | async-start | bytes 720896 | tf_op jit(solution)/shard_map/all_to_all | solution.py:720
  48.3 11.7 %collective-permute-start.10 = (f32[14,32,128]{2,1,0:T(8,128)S(1)}, f32[14,32,128]{2,1,0:T(8,128)S(1)}, u32[]{:S(2)}, u32[]{:S(2)}) collective-permute-start(f32[14,32,128]{2,1,0:T(8,128)S(1)} %copy-done.7), channel_id=1, source_target_pairs={{0,3},{1,2},{2,1},{3,0},{4,7},{5,6},{6,5},{7,4},{8,11},{9,10},{10,... | collective-permute-start | bytes 688136 | tf_op jit(solution)/shard_map/ppermute | solution.py:668
  51.4 8.7 %collective-permute-start.8 = (f32[14,32,128]{2,1,0:T(8,128)S(1)}, f32[14,32,128]{2,1,0:T(8,128)S(1)}, u32[]{:S(2)}, u32[]{:S(2)}) collective-permute-start(f32[14,32,128]{2,1,0:T(8,128)S(1)} %copy-done.7), channel_id=1, source_target_pairs={{0,1},{1,0},{2,3},{3,2},{4,5},{5,4},{6,7},{7,6},{8,9},{9,8},{10,11... | collective-permute-start | bytes 688136 | tf_op jit(solution)/shard_map/ppermute | solution.py:668
  52.8 8.8 %collective-permute-start.9 = (f32[14,32,128]{2,1,0:T(8,128)S(1)}, f32[14,32,128]{2,1,0:T(8,128)S(1)}, u32[]{:S(2)}, u32[]{:S(2)}) collective-permute-start(f32[14,32,128]{2,1,0:T(8,128)S(1)} %copy-done.7), channel_id=1, source_target_pairs={{0,2},{1,3},{2,0},{3,1},{4,6},{5,7},{6,4},{7,5},{8,10},{9,11},{10,... | collective-permute-start | bytes 688136 | tf_op jit(solution)/shard_map/ppermute | solution.py:668
  56.6 9.9 %all-to-all-start.1 = ((f32[8,32,128]{2,1,0:T(8,128)}), f32[8,32,128]{2,1,0:T(8,128)S(1)}, u32[]{:S(2)}, u32[]{:S(2)}) async-start(f32[8,32,128]{2,1,0:T(8,128)} %shard_map.92), calls=%async_computation.1 | async-start | bytes 262144 | tf_op jit(solution)/shard_map/all_to_all | solution.py:722
  67.1 5.1 %collective-permute-start.11 = (f32[88,128]{1,0:T(8,128)S(1)}, f32[88,128]{1,0:T(8,128)S(1)}, u32[]{:S(2)}, u32[]{:S(2)}) collective-permute-start(f32[88,128]{1,0:T(8,128)S(1)} %get-tuple-element.68.own), channel_id=1, source_target_pairs={{0,12},{4,8},{8,4},{12,0},{1,13},{5,9},{9,5},{13,1},{2,14},{6,10},... | collective-permute-start | bytes 135176 | tf_op jit(solution)/shard_map/ppermute | solution.py:668
  67.2 5.6 %collective-permute-start.12 = (f32[88,128]{1,0:T(8,128)S(1)}, f32[88,128]{1,0:T(8,128)S(1)}, u32[]{:S(2)}, u32[]{:S(2)}) collective-permute-start(f32[88,128]{1,0:T(8,128)S(1)} %get-tuple-element.68.own), channel_id=1, source_target_pairs={{0,8},{4,12},{8,0},{12,4},{1,9},{5,13},{9,1},{13,5},{2,10},{6,14},... | collective-permute-start | bytes 135176 | tf_op jit(solution)/shard_map/ppermute | solution.py:668
  69.5 3.3 %collective-permute-start.13 = (f32[88,128]{1,0:T(8,128)S(1)}, f32[88,128]{1,0:T(8,128)S(1)}, u32[]{:S(2)}, u32[]{:S(2)}) collective-permute-start(f32[88,128]{1,0:T(8,128)S(1)} %get-tuple-element.68.own), channel_id=1, source_target_pairs={{0,4},{4,0},{8,12},{12,8},{1,5},{5,1},{9,13},{13,9},{2,6},{6,2},{1... | collective-permute-start | bytes 135176 | tf_op jit(solution)/shard_map/ppermute | solution.py:668
  74.1 9.7 %collective-permute-start.14 = (f32[8,32,128]{2,1,0:T(8,128)S(1)}, f32[8,32,128]{2,1,0:T(8,128)S(1)}, u32[]{:S(2)}, u32[]{:S(2)}) collective-permute-start(f32[8,32,128]{2,1,0:T(8,128)S(1)} %get-tuple-element.75.ends_0), channel_id=1, source_target_pairs={{0,3},{1,2},{2,1},{3,0},{4,7},{5,6},{6,5},{7,4},{8,11},{9,10},{10,... | collective-permute-start | bytes 393224 | tf_op jit(solution)/shard_map/ppermute | solution.py:668
  77.2 7.9 %collective-permute-start.15 = (f32[8,32,128]{2,1,0:T(8,128)S(1)}, f32[8,32,128]{2,1,0:T(8,128)S(1)}, u32[]{:S(2)}, u32[]{:S(2)}) collective-permute-start(f32[8,32,128]{2,1,0:T(8,128)S(1)} %get-tuple-element.75.ends_0), channel_id=1, source_target_pairs={{0,2},{1,3},{2,0},{3,1},{4,6},{5,7},{6,4},{7,5},{8,10},{9,11},{10,... | collective-permute-start | bytes 393224 | tf_op jit(solution)/shard_map/ppermute | solution.py:668
  78.8 7.0 %collective-permute-start.16 = (f32[8,32,128]{2,1,0:T(8,128)S(1)}, f32[8,32,128]{2,1,0:T(8,128)S(1)}, u32[]{:S(2)}, u32[]{:S(2)}) collective-permute-start(f32[8,32,128]{2,1,0:T(8,128)S(1)} %get-tuple-element.75.ends_0), channel_id=1, source_target_pairs={{0,1},{1,0},{2,3},{3,2},{4,5},{5,4},{6,7},{7,6},{8,9},{9,8},{10,11... | collective-permute-start | bytes 393224 | tf_op jit(solution)/shard_map/ppermute | solution.py:668

commit v4 on v3

--- a/solution.py
+++ b/solution.py
@@ -15,16 +15,19 @@
 VMEM = pl.BlockSpec(memory_space=pltpu.VMEM)
 SMEM = pl.BlockSpec(memory_space=pltpu.SMEM)
 HBM = pl.BlockSpec(memory_space=pltpu.HBM)
-
-
-def call(body, outs, specs, scratch=(), flops=1000000, limit=4, copies=0):
+ANY = pl.BlockSpec(memory_space=pl.ANY)
+
+
+def call(body, outs, specs, scratch=(), flops=1000000, limit=4, copies=0, out_specs=None, aliases=None):
     return pl.pallas_call(
         body,
         out_shape=[shape if hasattr(shape, "dtype") else jax.ShapeDtypeStruct(shape, F32) for shape in outs],
         in_specs=specs,
-        out_specs=[VMEM] * len(outs),
+        out_specs=out_specs or [VMEM] * len(outs),
+        input_output_aliases=aliases or {},
         scratch_shapes=[
-            pltpu.VMEM(shape, F32) for shape in scratch
+            pltpu.VMEM(*((shape.shape, shape.dtype) if hasattr(shape, "dtype") else (shape, F32)))
+            for shape in scratch
         ]
         + [pltpu.SemaphoreType.DMA((copies,))] * (copies > 0),
         compiler_params=pltpu.CompilerParams(vmem_limit_bytes=limit * 1024 * 1024),
@@ -74,8 +77,8 @@
 
 def coefficients_kernel(
     source_in, capacity_in, transfer_in, classes_in, conductivity,
-    units, even, odd, classes,
-    edges, source, capacity, transfer, sems,
+    units, even, odd,
+    edges, source, capacity, transfer, classes, sems,
 ):
     place = {1: lax.axis_index("gy")}
     brought(((source_in, source), (capacity_in, capacity), (transfer_in, transfer), (classes_in, classes)), sems)
@@ -99,7 +102,7 @@
         edges[z] = packed
         return 0
 
-    lax.fori_loop(0, STEPS, layer, 0, unroll=4)
+    lax.fori_loop(0, STEPS, layer, 0, unroll=8)
 
     def pair(z, _):
         upper, lower = (edges[z], edges[z + 8])
@@ -112,13 +115,18 @@
     lax.fori_loop(0, 8, pair, 0, unroll=4)
 
 
-def face_rows():
-    offset, rows = (0, [])
-    for unit in range(7):
-        count = DEEP if unit < 2 else NEAR
-        rows.append((unit, offset, count))
-        offset += count
-    return rows, offset
+def counts(unit):
+    return DEEP if unit < 2 else NEAR
+
+
+X_MAIN = sum(counts(unit) for unit in range(6))
+X_ROWS = STEPS * (X_MAIN + NEAR)
+
+
+def face_row(unit, z):
+    if unit == 6:
+        return STEPS * X_MAIN + z * NEAR
+    return z * X_MAIN + sum(counts(u) for u in range(unit))
 
 
 def corner_rows():
@@ -138,19 +146,18 @@
             at = unit * NEAR + d if d < NEAR else 6 * NEAR + unit
             z_even[at], z_odd[at] = by_pairs(place, 2, units[unit, d], units[unit, STEPS - 1 - d])
 
-    def layer(z, _):
-        for unit, offset, count in face_rows()[0][:6]:
+    for z in range(STEPS):
+        for unit in range(6):
+            count = counts(unit)
             low, high = (units[unit, z, pl.ds(0, count)], units[unit, z, pl.ds(STEPS - count, count)])
             even, odd = by_pairs(place, 0, low, high)
-            x_even[z, pl.ds(offset, count)] = even
-            x_odd[z, pl.ds(offset, count)] = odd
-        return 0
-
-    lax.fori_loop(0, STEPS, layer, 0, unroll=2)
+            x_even[pl.ds(face_row(unit, z), count)] = even
+            x_odd[pl.ds(face_row(unit, z), count)] = odd
 
 
 def halo_kernel(
-    place, y_odd, y_even, z_even_in, z_odd_in, x_even_in, x_odd_in, strips, z_even, z_odd, x_even, x_odd
+    place, y_odd, y_even, _z_even, _z_odd, _x_even, _x_odd, strips, z_even, z_odd, x_even, x_odd,
+    to_z_even, to_z_odd, to_x_even, to_x_odd, sems,
 ):
     def pair(z, _):
         low, high = sides(place, 1, y_even[z], y_odd[z])
@@ -160,34 +167,34 @@
         return 0
 
     lax.fori_loop(0, 8, pair, 0, unroll=4)
-    for out, value in ((z_even, z_even_in), (z_odd, z_odd_in)):
-        out[pl.ds(0, 6 * NEAR + 2)] = value[...]
     for d in range(NEAR):
-        z_even[6 * NEAR + 2 + d], z_odd[6 * NEAR + 2 + d] = by_pairs(
-            place, 2, strips[d], strips[STEPS - 1 - d]
-        )
-
-    def layer(z, _):
-        _, offset, count = face_rows()[0][6]
-        x_even[z, pl.ds(0, offset)] = x_even_in[z, pl.ds(0, offset)]
-        x_odd[z, pl.ds(0, offset)] = x_odd_in[z, pl.ds(0, offset)]
-        low, high = (strips[z, pl.ds(0, count)], strips[z, pl.ds(STEPS - count, count)])
+        to_z_even[d], to_z_odd[d] = by_pairs(place, 2, strips[d], strips[STEPS - 1 - d])
+    for z in range(STEPS):
+        low, high = (strips[z, pl.ds(0, NEAR)], strips[z, pl.ds(STEPS - NEAR, NEAR)])
         even, odd = by_pairs(place, 0, low, high)
-        x_even[z, pl.ds(offset, count)] = even
-        x_odd[z, pl.ds(offset, count)] = odd
-        return 0
-
-    lax.fori_loop(0, STEPS, layer, 0, unroll=4)
-
-
-def corner_kernel(place, x_odd, x_even, _, even, odd):
-    spans = {unit: (offset, count) for unit, offset, count in face_rows()[0]}
+        to_x_even[pl.ds(NEAR * z, NEAR)] = even
+        to_x_odd[pl.ds(NEAR * z, NEAR)] = odd
+    z_part = pl.ds(6 * NEAR + 2, NEAR)
+    x_part = pl.ds(STEPS * X_MAIN, STEPS * NEAR)
+    brought(
+        (
+            (to_z_even, z_even.at[z_part]),
+            (to_z_odd, z_odd.at[z_part]),
+            (to_x_even, x_even.at[x_part]),
+            (to_x_odd, x_odd.at[x_part]),
+        ),
+        sems,
+    )
+
+
+def corner_kernel(place, x_odd, x_even, _z_even, _observed, even, odd):
     for unit, d, offset, count in corner_rows()[0]:
-        first, span = spans[unit]
         ends = []
         for z in (d, STEPS - 1 - d):
-            low = sides(place, 0, x_even[z, pl.ds(first + span - count, count)], x_odd[z, pl.ds(first + span - count, count)])[0]
-            high = sides(place, 0, x_even[z, pl.ds(first, count)], x_odd[z, pl.ds(first, count)])[1]
+            first = face_row(unit, z)
+            last = first + counts(unit) - count
+            low = sides(place, 0, x_even[pl.ds(last, count)], x_odd[pl.ds(last, count)])[0]
+            high = sides(place, 0, x_even[pl.ds(first, count)], x_odd[pl.ds(first, count)])[1]
             ends.append((low, high))
         for x_side in range(2):
             to_even, to_odd = by_pairs(place, 2, ends[0][x_side], ends[1][x_side])
@@ -339,8 +346,8 @@
 
 def sweep_kernel(
     place, units, strips, z_even, z_odd, x_even, x_odd, corner_even, corner_odd, observed, wx, mx,
-    predicted, increment, message,
-    grid, side, even, odd, passed, ends,
+    predicted, increment, message_out,
+    grid, side, even, odd, passed, ends, message, sems,
 ):
     inside = slice(8, 8 + STEPS)
 
@@ -348,14 +355,16 @@
         for unit in range(6):
             grid[unit, z + DEEP, inside] = units[unit, z]
         grid[6, z + DEEP, inside] = strips[z]
-        for unit, offset, count in face_rows()[0]:
-            rows = pl.ds(offset, count)
-            low, high = sides(place, 0, x_even[z, rows], x_odd[z, rows])
+        return 0
+
+    lax.fori_loop(0, STEPS, own, 0, unroll=2)
+    for z in range(STEPS):
+        for unit in range(7):
+            count = counts(unit)
+            rows = pl.ds(face_row(unit, z), count)
+            low, high = sides(place, 0, x_even[rows], x_odd[rows])
             grid[unit, z + DEEP, pl.ds(8 - count, count)] = low
             grid[unit, z + DEEP, pl.ds(8 + STEPS, count)] = high
-        return 0
-
-    lax.fori_loop(0, STEPS, own, 0)
     for d in range(DEEP):
         for unit in range(7 if d < NEAR else 2):
             at = unit * NEAR + d if d < NEAR else 6 * NEAR + unit
@@ -460,6 +469,7 @@
         for v in range(22):
             rows = pl.ds(4 * j, 4)
             message[j, pl.ds(4 * v, 4)] = ends[v, rows] if v < 8 else mx[v - 8, rows]
+    brought(((message, message_out),), sems)
 
 
 def solve_kernel(gathered, _, inflow):
@@ -673,24 +683,28 @@
     place = jnp.stack([lax.axis_index(a) for a in axes] + [jnp.int32(lax.axis_size(a)) for a in axes])
     rates = filter_rates.reshape(6, CLASSES)
     plane = (STEPS, STEPS, 128)
-    units, y_even, y_odd, classes = call(
+    units, y_even, y_odd = call(
         coefficients_kernel,
-        [(6,) + plane, (8, STEPS, 128), (8, STEPS, 128), jax.ShapeDtypeStruct(plane, jnp.int32)],
+        [(6,) + plane, (8, STEPS, 128), (8, STEPS, 128)],
         [HBM] * 4 + [SMEM],
-        [plane, (2,) + plane, (2,) + plane, plane],
+        [plane, (2,) + plane, (2,) + plane, plane, jax.ShapeDtypeStruct(plane, jnp.int32)],
         limit=60,
         copies=4,
     )(source, capacity, transfer, classes, conductivity)
     y_even, y_odd = pair_swaps("gy", "gz", y_even, y_odd)
 
     z_face = (7 * NEAR + 2, STEPS, 128)
-    x_face = (STEPS, face_rows()[1], 128)
+    x_face = (X_ROWS, 128)
     corners = (2, corner_rows()[1], 128)
-    z_own = (6 * NEAR + 2, STEPS, 128)
-    x_own = (STEPS, face_rows()[0][6][1], 128)
-    faces = call(face_kernel, [z_own, z_own, x_own, x_own], [SMEM, VMEM])(place, units)
+    faces = call(face_kernel, [z_face, z_face, x_face, x_face], [SMEM, VMEM])(place, units)
     strips, z_even, z_odd, x_even, x_odd = call(
-        halo_kernel, [plane, z_face, z_face, x_face, x_face], [SMEM] + [VMEM] * 6
+        halo_kernel,
+        [plane, z_face, z_face, x_face, x_face],
+        [SMEM] + [VMEM] * 2 + [ANY] * 4,
+        [(NEAR,) + plane[1:]] * 2 + [(STEPS * NEAR, 128)] * 2,
+        out_specs=[VMEM] + [ANY] * 4,
+        aliases={3: 1, 4: 2, 5: 3, 6: 4},
+        copies=4,
     )(place, y_odd, y_even, *faces)
     x_even, x_odd = pair_swaps("gx", "gy", x_even, x_odd)
     z_even, z_odd = pair_swaps("gz", "gy", z_even, z_odd)
@@ -703,8 +717,11 @@
         [VMEM, SMEM, VMEM],
     )(classes, rates, strips)
     x_odd, wx = lax.optimization_barrier((x_odd, wx))
-    corner_even, corner_odd = call(corner_kernel, [corners, corners], [SMEM] + [VMEM] * 3)(place, x_odd, x_even, observed)
+    corner_even, corner_odd = call(corner_kernel, [corners, corners], [SMEM] + [VMEM] * 4)(
+        place, x_odd, x_even, z_even, observed
+    )
     corner_even, corner_odd = pair_swaps("gz", "gy", corner_even, corner_odd)
+
     z_maps = xor_gather(mz, "gz")
 
     padded = (PLANES, 32, 128)
@@ -712,7 +729,9 @@
         sweep_kernel,
         [(2,) + plane, (2, 256, 128), (8, 88, 128)],
         [SMEM] + [VMEM] * 11,
-        [(7,) + padded, (6,) + padded, (4,) + padded, (4,) + padded, (STEPS,) + rows, (8,) + rows],
+        [(7,) + padded, (6,) + padded, (4,) + padded, (4,) + padded, (STEPS,) + rows, (8,) + rows, (8, 88, 128)],
+        out_specs=[VMEM, VMEM, HBM],
+        copies=1,
         flops=100000000,
         limit=16,
     )(place, units, strips, z_even, z_odd, x_even, x_odd, corner_even, corner_odd,

time: 89 us -> 87.2 us (0.980)
  local copies, waits for them, and re-layouts: 4.4 us -> 1.95 us
  waiting for transfers between devices: 25.2 us -> 27.6 us
  starting transfers between devices: 32.4 us -> 30 us
    unnamed x20 -> x14, local copies, waits for them, and re-layouts: 4.31 us -> 1.85 us
    ppermute x4, waiting for transfers between devices: 6.61 us -> 8.92 us  [pair_swaps(): lax.ppermute(value_even, axis, [(i, i ^ 1) for i in range(count)])]
    ppermute x4, starting transfers between devices: 8.47 us -> 7.49 us  [pair_swaps(): lax.ppermute(value_even, axis, [(i, i ^ 1) for i in range(count)])]
    pallas_call x2, Pallas kernels: 1.38 us -> 2.32 us  [the longest x1 1.67 us: local(): call(face_kernel, [z_face, z_face, x_face, x_face], [SMEM, VMEM])]
    all_to_all x1, starting transfers between devices: 5.75 us -> 4.83 us  [local(): gathered = lax.all_to_all(message, 'gx', 0, 0, tiled=True)]
  transfers between devices with their start and end apart: 19 -> 19, of which waited for: 10 -> 11; matrix products, arithmetic and copies ran while one was open for 0% -> 0% of each run, Pallas kernels for 6% -> 7%
where the time goes in v4:
time: 87.2 us; the launch traced here: 85.8 us
  starting transfers between devices  30 us (34%)
  waiting for transfers between devices  27.6 us (32%)
  Pallas kernels  25.5 us (29%)
  local copies, waits for them, and re-layouts  1.95 us (2%)
    ppermute x9, starting transfers between devices, xor_gather(): lax.ppermute(value, axis, [(i, i ^ s) for i in range(count)])  12.5 us
    pallas_call x1, Pallas kernels, local(): call(sweep_kernel, [(2,) + plane, (2, 256, 128), (8, 88, 128)], [SMEM] +...  11 us
    ppermute x9, waiting for transfers between devices, xor_gather(): lax.ppermute(value, axis, [(i, i ^ s) for i in range(count)])  10.4 us
    ppermute x4, waiting for transfers between devices, pair_swaps(): lax.ppermute(value_even, axis, [(i, i ^ 1) for i in range(count)])  8.92 us
    ppermute x4, starting transfers between devices, pair_swaps(): lax.ppermute(value_even, axis, [(i, i ^ 1) for i in range(count)])  7.49 us
    all_to_all x1, waiting for transfers between devices, local(): inflow = lax.all_to_all(inflow, 'gx', 0, 0, tiled=True)  5.46 us
    all_to_all x1, starting transfers between devices, local(): gathered = lax.all_to_all(message, 'gx', 0, 0, tiled=True)  4.83 us
    all_to_all x1, starting transfers between devices, local(): inflow = lax.all_to_all(inflow, 'gx', 0, 0, tiled=True)  3.37 us
  transfers between devices with their start and end apart: 19, of which 11 were waited for; matrix products, arithmetic and copies ran while one was open for 0% of the time, Pallas kernels for 7%

profile of v4, /device:TPU:0, one launch (start us, length us, event | category | flops | bytes accessed | tf_op | source)
XLA Modules:
  0.0 85.8 jit_solution(5128905997083294247)
XLA Ops:
  0.6 3.3 %shard_map.86 = (f32[6,16,16,128]{3,2,1,0:T(8,128)}, f32[8,16,128]{2,1,0:T(8,128)}, f32[8,16,128]{2,1,0:T(8,128)}) custom-call(f32[2,16,16,128]{3,2,1,0:T(8,128)} %source_in.1, f32[2,16,16,128]{3,2,1,0:T(8,128)} %capacity_in.1, f32[16,16,128]{2,1,0:T(8,128)} %transfer_in.1, s32[16,16,128]{2,1,0:T(8,128)} %classes.1, f32[2,12]{1,0:T(2,128)} %conductivity.1), custom_call_target="tpu_custom_call" | custom-call | flops 1000000 | bytes 1000000 | tf_op jit(solution)/shard_map/pallas_call | solution.py:686
  3.9 1.7 %collective-permute-start = (f32[8,16,128]{2,1,0:T(8,128)}, f32[8,16,128]{2,1,0:T(8,128)S(1)}, u32[]{:S(2)}, u32[]{:S(2)}) collective-permute-start(f32[8,16,128]{2,1,0:T(8,128)} %get-tuple-element.39), channel_id=1, source_target_pairs={{0,1},{1,0},{2,3},{3,2},{4,8},{5,9},{6,10},{7,11},{8,4},{9,5},{10,... | collective-permute-start | bytes 196616 | tf_op jit(solution)/shard_map/ppermute | solution.py:672
  5.6 1.6 %collective-permute-start.1 = (f32[8,16,128]{2,1,0:T(8,128)}, f32[8,16,128]{2,1,0:T(8,128)S(1)}, u32[]{:S(2)}, u32[]{:S(2)}) collective-permute-start(f32[8,16,128]{2,1,0:T(8,128)} %get-tuple-element.40), channel_id=1, source_target_pairs={{0,4},{4,0},{8,12},{12,8},{1,5},{5,1},{9,13},{13,9},{2,6},{6,2},{1... | collective-permute-start | bytes 196616 | tf_op jit(solution)/shard_map/ppermute | solution.py:671
  7.2 0.1 stack.15.place
  7.3 0.0 copy-start
  7.3 1.1 %copy-done = f32[6,16,16,128]{3,2,1,0:T(8,128)S(1)} copy-done((f32[6,16,16,128]{3,2,1,0:T(8,128)S(1)}, f32[6,16,16,128]{3,2,1,0:T(8,128)}, u32[]{:S(2)}) %copy-start) | copy-done | bytes 786456
  8.4 1.7 %shard_map.87 = (f32[44,16,128]{2,1,0:T(8,128)S(1)}, f32[44,16,128]{2,1,0:T(8,128)}, f32[704,128]{1,0:T(8,128)}, f32[704,128]{1,0:T(8,128)}) custom-call(s32[6]{0:T(128)S(1)} %stack.15.place, f32[6,16,16,128]{3,2,1,0:T(8,128)S(1)} %copy-done), custom_call_target="tpu_custom_call" | custom-call | flops 1000000 | bytes 1000000 | tf_op jit(solution)/shard_map/pallas_call | solution.py:699
  10.1 0.0 collective-permute-done.y_odd
  10.1 0.0 collective-permute-done.1.y_even
  10.1 0.0 copy-start.6
  10.1 0.0 copy-start.3
  10.1 1.5 %shard_map.88 = (f32[16,16,128]{2,1,0:T(8,128)S(1)}, f32[44,16,128]{2,1,0:T(8,128)S(1)}, f32[44,16,128]{2,1,0:T(8,128)}, f32[704,128]{1,0:T(8,128)}, f32[704,128]{1,0:T(8,128)}) custom-call(s32[6]{0:T(128)S(1)} %stack.15.place, ...), custom_call_target="tpu_custom_call", output_to_operand_aliasing={{1}: (3, {}), {2}: (4, {}), {3}: (5, {}), {4}: (6, {})} | custom-call | flops 1000000 | bytes 1000000 | tf_op jit(solution)/shard_map/pallas_call | solution.py:700
  11.6 0.0 copy-start.2
  11.7 0.1 collective-permute-start.5
  11.7 1.7 %collective-permute-start.2 = (f32[44,16,128]{2,1,0:T(8,128)S(1)}, f32[44,16,128]{2,1,0:T(8,128)S(1)}, u32[]{:S(2)}, u32[]{:S(2)}) collective-permute-start(f32[44,16,128]{2,1,0:T(8,128)S(1)} %get-tuple-element.46), channel_id=1, source_target_pairs={{0,1},{1,0},{2,3},{3,2},{4,5},{5,4},{6,7},{7,6},{8,9},{9,8},{10,11... | collective-permute-start | bytes 1081352 | tf_op jit(solution)/shard_map/ppermute | solution.py:671
  13.4 3.7 %collective-permute-start.4 = (f32[704,128]{1,0:T(8,128)}, f32[704,128]{1,0:T(8,128)S(1)}, u32[]{:S(2)}, u32[]{:S(2)}) collective-permute-start(f32[704,128]{1,0:T(8,128)} %get-tuple-element.48), channel_id=1, source_target_pairs={{0,16},{16,0},{32,48},{48,32},{64,80},{80,64},{96,112},{112,96},{1... | collective-permute-start | bytes 1081352 | tf_op jit(solution)/shard_map/ppermute | solution.py:671
  17.1 0.0 collective-permute-start.3
  17.2 0.0 copy-done.6
  17.2 0.0 copy-done.3
  17.2 0.0 copy-start.1
  17.2 3.0 %shard_map.89 = (f32[2,16,16,128]{3,2,1,0:T(8,128)S(1)}, f32[4,128,128]{2,1,0:T(8,128)S(1)}, f32[2,16,16,128]{3,2,1,0:T(8,128)S(1)}, f32[14,32,128]{2,1,0:T(8,12...) custom-call(s32[16,16,128]{2,1,0:T(8,128)S(1)} %copy-done.3, ...), custom_call_target="tpu_custom_call" | custom-call | flops 1000000 | bytes 1000000 | tf_op jit(solution)/shard_map/pallas_call | solution.py:713
  20.2 0.0 copy-start.4
  20.2 0.7 copy-done.4
  20.9 0.0 collective-permute-done.5.x_odd
  20.9 1.7 %collective-permute-done.2._z_even.z_even = f32[44,16,128]{2,1,0:T(8,128)S(1)} collective-permute-done((f32[44,16,128]{2,1,0:T(8,128)S(1)}, f32[44,16,128]{2,1,0:T(8,128)S(1)}, u32[]{:S(2)}, u32[]{:S(2)}) %collective-permute-start.2) | collective-permute-done | bytes 360480 | tf_op jit(solution)/shard_map/ppermute | solution.py:671
  22.6 2.8 %collective-permute-done.4.x_even = f32[704,128]{1,0:T(8,128)S(1)} collective-permute-done((f32[704,128]{1,0:T(8,128)}, f32[704,128]{1,0:T(8,128)S(1)}, u32[]{:S(2)}, u32[]{:S(2)}) %collective-permute-start.4) | collective-permute-done | bytes 360480 | tf_op jit(solution)/shard_map/ppermute | solution.py:671
  25.4 0.0 copy-done.2
  25.4 0.7 shard_map.90
  26.0 0.5 collective-permute-start.6
  26.6 0.0 collective-permute-start.7
  26.6 0.0 collective-permute-done.3.z_odd
  26.6 4.4 %collective-permute-done.6.corner_even = f32[2,120,128]{2,1,0:T(8,128)S(1)} collective-permute-done((f32[2,120,128]{2,1,0:T(8,128)S(1)}, f32[2,120,128]{2,1,0:T(8,128)S(1)}, u32[]{:S(2)}, u32[]{:S(2)}) %collective-permute-start.6) | collective-permute-done | bytes 122912 | tf_op jit(solution)/shard_map/ppermute | solution.py:671
  31.0 0.0 collective-permute-done.7.corner_odd
  31.0 0.0 copy-done.1
  31.0 11.0 %shard_map.91 = (f32[2,16,16,128]{3,2,1,0:T(8,128)}, f32[2,256,128]{2,1,0:T(8,128)S(1)}, f32[8,88,128]{2,1,0:T(8,128)}) custom-call(s32[6]{0:T(128)S(1)} %stack.15.place, f32[6,16,16,128]{3,2,1,0:T(8,128)S(1)} %copy-done.1, f32[16,16,128]{2,1,0:T(8,128)S(1)} %get-tuple-element.45._.strips, f32[44,16,128]{2,1,0:T(8,128)S(1)} %collective-permute-done.2._z_even.z_even, ...), custom_call_target="tpu_custom_call" | custom-call | flops 100000000 | bytes 1000000 | tf_op jit(solution)/shard_map/pallas_call | solution.py:728
  42.1 0.0 copy-start.5
  42.1 4.8 %all-to-all-start = ((f32[8,88,128]{2,1,0:T(8,128)}), f32[8,88,128]{2,1,0:T(8,128)S(1)}, u32[]{:S(2)}, u32[]{:S(2)}) async-start(f32[8,88,128]{2,1,0:T(8,128)} %get-tuple-element.58), calls=%async_computation | async-start | bytes 720896 | tf_op jit(solution)/shard_map/all_to_all | solution.py:739
  46.9 0.0 copy-done.5
  46.9 2.7 %collective-permute-start.10 = (f32[14,32,128]{2,1,0:T(8,128)S(1)}, f32[14,32,128]{2,1,0:T(8,128)S(1)}, u32[]{:S(2)}, u32[]{:S(2)}) collective-permute-start(f32[14,32,128]{2,1,0:T(8,128)S(1)} %copy-done.5), channel_id=1, source_target_pairs={{0,3},{1,2},{2,1},{3,0},{4,7},{5,6},{6,5},{7,4},{8,11},{9,10},{10,... | collective-permute-start | bytes 688136 | tf_op jit(solution)/shard_map/ppermute | solution.py:678
  49.6 1.4 %collective-permute-start.8 = (f32[14,32,128]{2,1,0:T(8,128)S(1)}, f32[14,32,128]{2,1,0:T(8,128)S(1)}, u32[]{:S(2)}, u32[]{:S(2)}) collective-permute-start(f32[14,32,128]{2,1,0:T(8,128)S(1)} %copy-done.5), channel_id=1, source_target_pairs={{0,1},{1,0},{2,3},{3,2},{4,5},{5,4},{6,7},{7,6},{8,9},{9,8},{10,11... | collective-permute-start | bytes 688136 | tf_op jit(solution)/shard_map/ppermute | solution.py:678
  51.1 0.6 collective-permute-start.9
  51.7 2.8 %all-to-all-done.gathered = f32[8,88,128]{2,1,0:T(8,128)S(1)} async-done(((f32[8,88,128]{2,1,0:T(8,128)}), f32[8,88,128]{2,1,0:T(8,128)S(1)}, u32[]{:S(2)}, u32[]{:S(2)}) %all-to-all-start) | async-done | bytes 360480 | tf_op jit(solution)/shard_map/all_to_all | solution.py:739
  54.5 0.7 shard_map.92
  55.3 3.4 %all-to-all-start.1 = ((f32[8,32,128]{2,1,0:T(8,128)}), f32[8,32,128]{2,1,0:T(8,128)S(1)}, u32[]{:S(2)}, u32[]{:S(2)}) async-start(f32[8,32,128]{2,1,0:T(8,128)} %shard_map.92), calls=%async_computation.1 | async-start | bytes 262144 | tf_op jit(solution)/shard_map/all_to_all | solution.py:741
  58.6 0.0 collective-permute-done.10.maps_3
  58.7 0.0 collective-permute-done.8.maps_1
  58.7 1.0 %collective-permute-done.9.maps_2 = f32[14,32,128]{2,1,0:T(8,128)S(1)} collective-permute-done((f32[14,32,128]{2,1,0:T(8,128)S(1)}, f32[14,32,128]{2,1,0:T(8,128)S(1)}, u32[]{:S(2)}, u32[]{:S(2)}) %collective-permute-start.9) | collective-permute-done | bytes 229408 | tf_op jit(solution)/shard_map/ppermute | solution.py:678
  59.7 5.5 %all-to-all-done.1.inflow = f32[8,32,128]{2,1,0:T(8,128)S(1)} async-done(((f32[8,32,128]{2,1,0:T(8,128)}), f32[8,32,128]{2,1,0:T(8,128)S(1)}, u32[]{:S(2)}, u32[]{:S(2)}) %all-to-all-start.1) | async-done | bytes 131104 | tf_op jit(solution)/shard_map/all_to_all | solution.py:741
  65.2 0.6 shard_map.93
  65.8 0.1 collective-permute-start.11
  65.9 2.4 %collective-permute-start.12 = (f32[88,128]{1,0:T(8,128)S(1)}, f32[88,128]{1,0:T(8,128)S(1)}, u32[]{:S(2)}, u32[]{:S(2)}) collective-permute-start(f32[88,128]{1,0:T(8,128)S(1)} %get-tuple-element.66.own), channel_id=1, source_target_pairs={{0,8},{4,12},{8,0},{12,4},{1,9},{5,13},{9,1},{13,5},{2,10},{6,14},... | collective-permute-start | bytes 135176 | tf_op jit(solution)/shard_map/ppermute | solution.py:678
  68.3 0.9 %collective-permute-start.13 = (f32[88,128]{1,0:T(8,128)S(1)}, f32[88,128]{1,0:T(8,128)S(1)}, u32[]{:S(2)}, u32[]{:S(2)}) collective-permute-start(f32[88,128]{1,0:T(8,128)S(1)} %get-tuple-element.66.own), channel_id=1, source_target_pairs={{0,4},{4,0},{8,12},{12,8},{1,5},{5,1},{9,13},{13,9},{2,6},{6,2},{1... | collective-permute-start | bytes 135176 | tf_op jit(solution)/shard_map/ppermute | solution.py:678
  69.2 1.6 %collective-permute-done.11.xor_3 = f32[88,128]{1,0:T(8,128)S(1)} collective-permute-done((f32[88,128]{1,0:T(8,128)S(1)}, f32[88,128]{1,0:T(8,128)S(1)}, u32[]{:S(2)}, u32[]{:S(2)}) %collective-permute-start.11) | collective-permute-done | bytes 45088 | tf_op jit(solution)/shard_map/ppermute | solution.py:678
  70.8 0.7 collective-permute-done.12.xor_2
  71.5 0.0 collective-permute-done.13.xor_1
  71.5 1.3 %shard_map.94 = (f32[2,16,16,128]{3,2,1,0:T(8,128)S(1)}, f32[8,32,128]{2,1,0:T(8,128)S(1)}) custom-call(s32[6]{0:T(128)S(1)} %stack.15.place, f32[4,128,128]{2,1,0:T(8,128)S(1)} %get-tuple-element.64.lines, f32[4,128,128]{2,1,0:T(8,128)S(1)} %get-tuple-element.61.wy, f32[14,32,128]{2,1,0:T(8,128)S(1)} %get-tuple-element.62.my, ...), custom_call_target="tpu_custom_call" | custom-call | flops 1000000 | bytes 1000000 | tf_op jit(solution)/shard_map/pallas_call | solution.py:750
  72.8 2.7 %collective-permute-start.14 = (f32[8,32,128]{2,1,0:T(8,128)S(1)}, f32[8,32,128]{2,1,0:T(8,128)S(1)}, u32[]{:S(2)}, u32[]{:S(2)}) collective-permute-start(f32[8,32,128]{2,1,0:T(8,128)S(1)} %get-tuple-element.73.ends_0), channel_id=1, source_target_pairs={{0,3},{1,2},{2,1},{3,0},{4,7},{5,6},{6,5},{7,4},{8,11},{9,10},{10,... | collective-permute-start | bytes 393224 | tf_op jit(solution)/shard_map/ppermute | solution.py:678
  75.5 1.6 %collective-permute-start.15 = (f32[8,32,128]{2,1,0:T(8,128)S(1)}, f32[8,32,128]{2,1,0:T(8,128)S(1)}, u32[]{:S(2)}, u32[]{:S(2)}) collective-permute-start(f32[8,32,128]{2,1,0:T(8,128)S(1)} %get-tuple-element.73.ends_0), channel_id=1, source_target_pairs={{0,2},{1,3},{2,0},{3,1},{4,6},{5,7},{6,4},{7,5},{8,10},{9,11},{10,... | collective-permute-start | bytes 393224 | tf_op jit(solution)/shard_map/ppermute | solution.py:678
  77.1 0.0 collective-permute-start.16
  77.1 5.6 %collective-permute-done.14.ends_3 = f32[8,32,128]{2,1,0:T(8,128)S(1)} collective-permute-done((f32[8,32,128]{2,1,0:T(8,128)S(1)}, f32[8,32,128]{2,1,0:T(8,128)S(1)}, u32[]{:S(2)}, u32[]{:S(2)}) %collective-permute-start.14) | collective-permute-done | bytes 131104 | tf_op jit(solution)/shard_map/ppermute | solution.py:678
  82.7 0.7 collective-permute-done.15.ends_2
  83.4 0.7 collective-permute-done.16.ends_1
  84.1 1.7 %shard_map.95 = f32[2,16,16,128]{3,2,1,0:T(8,128)} custom-call(s32[6]{0:T(128)S(1)} %stack.15.place, f32[2,16,16,128]{3,2,1,0:T(8,128)S(1)} %get-tuple-element.68.unsmoothed, f32[2,16,16,128]{3,2,1,0:T(8,128)S(1)} %get-tuple-element.67.wz, f32[14,32,128]{2,1,0:T(8,128)S(1)} %copy-done.5, f32[14,32,128]{2,1,0:T(8,128)S(1)} %collective-permute-done.8.maps_1, ...), custom_call_target="tpu_custom_call" | custom-call | flops 1000000 | bytes 1000000 | tf_op jit(solution)/shard_map/pallas_call | solution.py:757
  (2 shorter events, 0.0 us)
Async XLA Ops:
  3.9 6.2 %collective-permute-start = (f32[8,16,128]{2,1,0:T(8,128)}, f32[8,16,128]{2,1,0:T(8,128)S(1)}, u32[]{:S(2)}, u32[]{:S(2)}) collective-permute-start(f32[8,16,128]{2,1,0:T(8,128)} %get-tuple-element.39), channel_id=1, source_target_pairs={{0,1},{1,0},{2,3},{3,2},{4,8},{5,9},{6,10},{7,11},{8,4},{9,5},{10,... | collective-permute-start | bytes 196616 | tf_op jit(solution)/shard_map/ppermute | solution.py:672
  5.6 4.5 %collective-permute-start.1 = (f32[8,16,128]{2,1,0:T(8,128)}, f32[8,16,128]{2,1,0:T(8,128)S(1)}, u32[]{:S(2)}, u32[]{:S(2)}) collective-permute-start(f32[8,16,128]{2,1,0:T(8,128)} %get-tuple-element.40), channel_id=1, source_target_pairs={{0,4},{4,0},{8,12},{12,8},{1,5},{5,1},{9,13},{13,9},{2,6},{6,2},{1... | collective-permute-start | bytes 196616 | tf_op jit(solution)/shard_map/ppermute | solution.py:671
  7.3 1.1 %copy-start = (f32[6,16,16,128]{3,2,1,0:T(8,128)S(1)}, f32[6,16,16,128]{3,2,1,0:T(8,128)}, u32[]{:S(2)}) copy-start(f32[6,16,16,128]{3,2,1,0:T(8,128)} %get-tuple-element.38.units) | copy-start | bytes 2359300
  10.1 7.1 %copy-start.6 = (f32[3,2,12]{2,1,0:T(2,128)S(1)}, f32[3,2,12]{2,1,0:T(2,128)}, u32[]{:S(2)}) copy-start(f32[3,2,12]{2,1,0:T(2,128)} %param.13) | copy-start | bytes 868
  10.1 7.1 %copy-start.3 = (s32[16,16,128]{2,1,0:T(8,128)S(1)}, s32[16,16,128]{2,1,0:T(8,128)}, u32[]{:S(2)}) copy-start(s32[16,16,128]{2,1,0:T(8,128)} %classes.1) | copy-start | bytes 393220
  11.6 13.7 %copy-start.2 = (f32[2,16,16,128]{3,2,1,0:T(8,128)S(1)}, f32[2,16,16,128]{3,2,1,0:T(8,128)}, u32[]{:S(2)}) copy-start(f32[2,16,16,128]{3,2,1,0:T(8,128)} %observed.1) | copy-start | bytes 786436
  11.7 9.2 %collective-permute-start.5 = (f32[704,128]{1,0:T(8,128)}, f32[704,128]{1,0:T(8,128)S(1)}, u32[]{:S(2)}, u32[]{:S(2)}) collective-permute-start(f32[704,128]{1,0:T(8,128)} %get-tuple-element.49), channel_id=1, source_target_pairs={{0,4},{4,0},{8,12},{12,8},{16,32},{20,36},{24,40},{28,44},{32,16},... | collective-permute-start | bytes 1081352 | tf_op jit(solution)/shard_map/ppermute | solution.py:672
  11.7 10.8 %collective-permute-start.2 = (f32[44,16,128]{2,1,0:T(8,128)S(1)}, f32[44,16,128]{2,1,0:T(8,128)S(1)}, u32[]{:S(2)}, u32[]{:S(2)}) collective-permute-start(f32[44,16,128]{2,1,0:T(8,128)S(1)} %get-tuple-element.46), channel_id=1, source_target_pairs={{0,1},{1,0},{2,3},{3,2},{4,5},{5,4},{6,7},{7,6},{8,9},{9,8},{10,11... | collective-permute-start | bytes 1081352 | tf_op jit(solution)/shard_map/ppermute | solution.py:671
  13.4 12.0 %collective-permute-start.4 = (f32[704,128]{1,0:T(8,128)}, f32[704,128]{1,0:T(8,128)S(1)}, u32[]{:S(2)}, u32[]{:S(2)}) collective-permute-start(f32[704,128]{1,0:T(8,128)} %get-tuple-element.48), channel_id=1, source_target_pairs={{0,16},{16,0},{32,48},{48,32},{64,80},{80,64},{96,112},{112,96},{1... | collective-permute-start | bytes 1081352 | tf_op jit(solution)/shard_map/ppermute | solution.py:671
  17.1 9.4 %collective-permute-start.3 = (f32[44,16,128]{2,1,0:T(8,128)}, f32[44,16,128]{2,1,0:T(8,128)S(1)}, u32[]{:S(2)}, u32[]{:S(2)}) collective-permute-start(f32[44,16,128]{2,1,0:T(8,128)} %get-tuple-element.47), channel_id=1, source_target_pairs={{0,4},{4,0},{8,12},{12,8},{1,2},{5,6},{9,10},{13,14},{2,1},{6,5},{... | collective-permute-start | bytes 1081352 | tf_op jit(solution)/shard_map/ppermute | solution.py:672
  17.2 13.8 %copy-start.1 = (f32[6,16,16,128]{3,2,1,0:T(8,128)S(1)}, f32[6,16,16,128]{3,2,1,0:T(8,128)}, u32[]{:S(2)}) copy-start(f32[6,16,16,128]{3,2,1,0:T(8,128)} %get-tuple-element.38.units) | copy-start | bytes 2359300
  20.2 0.7 copy-start.4
  26.0 5.0 %collective-permute-start.6 = (f32[2,120,128]{2,1,0:T(8,128)S(1)}, f32[2,120,128]{2,1,0:T(8,128)S(1)}, u32[]{:S(2)}, u32[]{:S(2)}) collective-permute-start(f32[2,120,128]{2,1,0:T(8,128)S(1)} %get-tuple-element.52), channel_id=1, source_target_pairs={{0,1},{1,0},{2,3},{3,2},{4,5},{5,4},{6,7},{7,6},{8,9},{9,8},{10,11... | collective-permute-start | bytes 368648 | tf_op jit(solution)/shard_map/ppermute | solution.py:671
  26.6 4.4 %collective-permute-start.7 = (f32[2,120,128]{2,1,0:T(8,128)S(1)}, f32[2,120,128]{2,1,0:T(8,128)S(1)}, u32[]{:S(2)}, u32[]{:S(2)}) collective-permute-start(f32[2,120,128]{2,1,0:T(8,128)S(1)} %get-tuple-element.53), channel_id=1, source_target_pairs={{0,4},{4,0},{8,12},{12,8},{1,2},{5,6},{9,10},{13,14},{2,1},{6,5},{... | collective-permute-start | bytes 368648 | tf_op jit(solution)/shard_map/ppermute | solution.py:672
  42.1 4.8 %copy-start.5 = (f32[14,32,128]{2,1,0:T(8,128)S(1)}, f32[14,32,128]{2,1,0:T(8,128)}, u32[]{:S(2)}) copy-start(f32[14,32,128]{2,1,0:T(8,128)} %copy-done.4) | copy-start | bytes 688132
  42.1 12.4 %all-to-all-start = ((f32[8,88,128]{2,1,0:T(8,128)}), f32[8,88,128]{2,1,0:T(8,128)S(1)}, u32[]{:S(2)}, u32[]{:S(2)}) async-start(f32[8,88,128]{2,1,0:T(8,128)} %get-tuple-element.58), calls=%async_computation | async-start | bytes 720896 | tf_op jit(solution)/shard_map/all_to_all | solution.py:739
  46.9 11.7 %collective-permute-start.10 = (f32[14,32,128]{2,1,0:T(8,128)S(1)}, f32[14,32,128]{2,1,0:T(8,128)S(1)}, u32[]{:S(2)}, u32[]{:S(2)}) collective-permute-start(f32[14,32,128]{2,1,0:T(8,128)S(1)} %copy-done.5), channel_id=1, source_target_pairs={{0,3},{1,2},{2,1},{3,0},{4,7},{5,6},{6,5},{7,4},{8,11},{9,10},{10,... | collective-permute-start | bytes 688136 | tf_op jit(solution)/shard_map/ppermute | solution.py:678
  49.6 9.0 %collective-permute-start.8 = (f32[14,32,128]{2,1,0:T(8,128)S(1)}, f32[14,32,128]{2,1,0:T(8,128)S(1)}, u32[]{:S(2)}, u32[]{:S(2)}) collective-permute-start(f32[14,32,128]{2,1,0:T(8,128)S(1)} %copy-done.5), channel_id=1, source_target_pairs={{0,1},{1,0},{2,3},{3,2},{4,5},{5,4},{6,7},{7,6},{8,9},{9,8},{10,11... | collective-permute-start | bytes 688136 | tf_op jit(solution)/shard_map/ppermute | solution.py:678
  51.1 8.6 %collective-permute-start.9 = (f32[14,32,128]{2,1,0:T(8,128)S(1)}, f32[14,32,128]{2,1,0:T(8,128)S(1)}, u32[]{:S(2)}, u32[]{:S(2)}) collective-permute-start(f32[14,32,128]{2,1,0:T(8,128)S(1)} %copy-done.5), channel_id=1, source_target_pairs={{0,2},{1,3},{2,0},{3,1},{4,6},{5,7},{6,4},{7,5},{8,10},{9,11},{10,... | collective-permute-start | bytes 688136 | tf_op jit(solution)/shard_map/ppermute | solution.py:678
  55.3 9.9 %all-to-all-start.1 = ((f32[8,32,128]{2,1,0:T(8,128)}), f32[8,32,128]{2,1,0:T(8,128)S(1)}, u32[]{:S(2)}, u32[]{:S(2)}) async-start(f32[8,32,128]{2,1,0:T(8,128)} %shard_map.92), calls=%async_computation.1 | async-start | bytes 262144 | tf_op jit(solution)/shard_map/all_to_all | solution.py:741
  65.8 5.1 %collective-permute-start.11 = (f32[88,128]{1,0:T(8,128)S(1)}, f32[88,128]{1,0:T(8,128)S(1)}, u32[]{:S(2)}, u32[]{:S(2)}) collective-permute-start(f32[88,128]{1,0:T(8,128)S(1)} %get-tuple-element.66.own), channel_id=1, source_target_pairs={{0,12},{4,8},{8,4},{12,0},{1,13},{5,9},{9,5},{13,1},{2,14},{6,10},... | collective-permute-start | bytes 135176 | tf_op jit(solution)/shard_map/ppermute | solution.py:678
  65.9 5.6 %collective-permute-start.12 = (f32[88,128]{1,0:T(8,128)S(1)}, f32[88,128]{1,0:T(8,128)S(1)}, u32[]{:S(2)}, u32[]{:S(2)}) collective-permute-start(f32[88,128]{1,0:T(8,128)S(1)} %get-tuple-element.66.own), channel_id=1, source_target_pairs={{0,8},{4,12},{8,0},{12,4},{1,9},{5,13},{9,1},{13,5},{2,10},{6,14},... | collective-permute-start | bytes 135176 | tf_op jit(solution)/shard_map/ppermute | solution.py:678
  68.3 3.2 %collective-permute-start.13 = (f32[88,128]{1,0:T(8,128)S(1)}, f32[88,128]{1,0:T(8,128)S(1)}, u32[]{:S(2)}, u32[]{:S(2)}) collective-permute-start(f32[88,128]{1,0:T(8,128)S(1)} %get-tuple-element.66.own), channel_id=1, source_target_pairs={{0,4},{4,0},{8,12},{12,8},{1,5},{5,1},{9,13},{13,9},{2,6},{6,2},{1... | collective-permute-start | bytes 135176 | tf_op jit(solution)/shard_map/ppermute | solution.py:678
  72.8 9.9 %collective-permute-start.14 = (f32[8,32,128]{2,1,0:T(8,128)S(1)}, f32[8,32,128]{2,1,0:T(8,128)S(1)}, u32[]{:S(2)}, u32[]{:S(2)}) collective-permute-start(f32[8,32,128]{2,1,0:T(8,128)S(1)} %get-tuple-element.73.ends_0), channel_id=1, source_target_pairs={{0,3},{1,2},{2,1},{3,0},{4,7},{5,6},{6,5},{7,4},{8,11},{9,10},{10,... | collective-permute-start | bytes 393224 | tf_op jit(solution)/shard_map/ppermute | solution.py:678
  75.5 7.8 %collective-permute-start.15 = (f32[8,32,128]{2,1,0:T(8,128)S(1)}, f32[8,32,128]{2,1,0:T(8,128)S(1)}, u32[]{:S(2)}, u32[]{:S(2)}) collective-permute-start(f32[8,32,128]{2,1,0:T(8,128)S(1)} %get-tuple-element.73.ends_0), channel_id=1, source_target_pairs={{0,2},{1,3},{2,0},{3,1},{4,6},{5,7},{6,4},{7,5},{8,10},{9,11},{10,... | collective-permute-start | bytes 393224 | tf_op jit(solution)/shard_map/ppermute | solution.py:678
  77.1 7.0 %collective-permute-start.16 = (f32[8,32,128]{2,1,0:T(8,128)S(1)}, f32[8,32,128]{2,1,0:T(8,128)S(1)}, u32[]{:S(2)}, u32[]{:S(2)}) collective-permute-start(f32[8,32,128]{2,1,0:T(8,128)S(1)} %get-tuple-element.73.ends_0), channel_id=1, source_target_pairs={{0,1},{1,0},{2,3},{3,2},{4,5},{5,4},{6,7},{7,6},{8,9},{9,8},{10,11... | collective-permute-start | bytes 393224 | tf_op jit(solution)/shard_map/ppermute | solution.py:678

commit v5 on v4

--- a/solution.py
+++ b/solution.py
@@ -345,9 +345,9 @@
 
 
 def sweep_kernel(
-    place, units, strips, z_even, z_odd, x_even, x_odd, corner_even, corner_odd, observed, wx, mx,
-    predicted, increment, message_out,
-    grid, side, even, odd, passed, ends, message, sems,
+    place, units, strips, z_even, z_odd, x_even, x_odd, corner_even, corner_odd, observed, wx,
+    predicted, increment, ends,
+    grid, side, even, odd, passed,
 ):
     inside = slice(8, 8 + STEPS)
 
@@ -465,31 +465,90 @@
         for k in range(4):
             ends[k, pl.ds(8 * g, 8)] = low[g][k]
             ends[4 + k, pl.ds(8 * g, 8)] = high[g][k]
-    for j in range(8):
-        for v in range(22):
-            rows = pl.ds(4 * j, 4)
-            message[j, pl.ds(4 * v, 4)] = ends[v, rows] if v < 8 else mx[v - 8, rows]
-    brought(((message, message_out),), sems)
-
-
-def solve_kernel(gathered, _, inflow):
-    parts = [[gathered[s, pl.ds(4 * v, 4)] for v in range(22)] for s in range(8)]
-    zero = [jnp.zeros((4, 128), F32)] * 4
-    lows, highs = chained([p[8:] for p in parts], [p[:8] for p in parts], zero, zero)
-    for s in range(8):
-        for k in range(4):
-            inflow[s, pl.ds(4 * k, 4)] = lows[s][k]
-            inflow[s, pl.ds(16 + 4 * k, 4)] = highs[s + 1][k]
+
+
+GROUPS = [pl.ds(8 * g, 8) for g in range(4)]
+
+
+def values_of(ref, rows, count):
+    return [ref[v, rows] for v in range(count)]
+
+
+def no_state(rows=8):
+    return [jnp.zeros((rows, 128), F32)] * 4
+
+
+def laid_end_to_end(first, second):
+    return [sum(first[k - m] * second[m] for m in range(k + 1)) for k in range(4)]
+
+
+def run_maps_kernel(place, maps_0, maps_1, maps_2, maps_3, joint, around):
+    maps = (maps_0, maps_1, maps_2, maps_3)
+    for p in range(4):
+
+        @pl.when(place[0] % 4 == p)
+        def _(p=p):
+            for rows in GROUPS:
+                run = [values_of(maps[j ^ p], rows, 14) for j in range(4)]
+                zero = jnp.zeros((8, 128), F32)
+                unit = [zero + 1.0] + [zero] * 3
+                before = unit
+                for j in range(p):
+                    before = laid_end_to_end(before, run[j][:4])
+                through = laid_end_to_end(before, run[p][:4])
+                after = merged_maps(run[p + 1 :]) if p < 3 else unit + [zero] * 10
+                for v, value in enumerate(merged_maps(run)[4:]):
+                    joint[v, rows] = value
+                for v, value in enumerate(before + through + after):
+                    around[v, rows] = value
+
+
+def run_ends_kernel(place, maps_0, maps_1, maps_2, maps_3, ends_0, ends_3, ends_2, ends_1, _, joint, inner):
+    maps, ends = ((maps_0, maps_1, maps_2, maps_3), (ends_0, ends_1, ends_2, ends_3))
+    for p in range(4):
+
+        @pl.when(place[0] % 4 == p)
+        def _(p=p):
+            for rows in GROUPS:
+                lows, highs = chained(
+                    [values_of(maps[j ^ p], rows, 14) for j in range(4)],
+                    [values_of(ends[j ^ p], rows, 8) for j in range(4)],
+                    no_state(),
+                    no_state(),
+                )
+                for k in range(4):
+                    joint[k, rows] = lows[4][k]
+                    joint[4 + k, rows] = highs[0][k]
+                    inner[k, rows] = lows[p][k]
+                    inner[4 + k, rows] = highs[p + 1][k]
+
+
+def outer_inflow(is_high, own_ends, other_ends, other_coupling):
+    low = [jnp.where(is_high, value, 0.0) for value in other_ends[:4]]
+    back = plus(couple([None] * 4 + other_coupling, own_ends[:4]), other_ends[4:])
+    return low, [jnp.where(is_high, 0.0, value) for value in back]
 
 
 def y_value(ref):
     return lambda i, g: ref[g, pl.ds(i, 8, stride=STEPS)]
 
 
-def x_finish_kernel(increment, wx, inflow, wy, my, my_all, lines, ends, message, passed, start):
-    for k in range(8):
-        for j in range(8):
-            start[k, pl.ds(4 * j, 4)] = inflow[j, pl.ds(4 * k, 4)]
+def x_finish_kernel(
+    place, increment, wx, around, inner, joint, other_joint, other_coupling, wy, my, my_all,
+    lines, ends, message, passed, start,
+):
+    for rows in GROUPS:
+        outer_low, outer_high = outer_inflow(
+            place[0] >= 4,
+            values_of(joint, rows, 8),
+            values_of(other_joint, rows, 8),
+            values_of(other_coupling, rows, 10),
+        )
+        maps, inside = (values_of(around, rows, 22), values_of(inner, rows, 8))
+        low = plus(inside[:4], pass_map(maps[:4], outer_low))
+        back = couple(maps[8:], pass_map(maps[4:8], outer_low))
+        high = plus(plus(inside[4:], pass_map(maps[8:], outer_high)), back)
+        inflow_writer(start, rows)(low, high)
 
     def weight(i, g):
         return wx[g // 2, i, pl.ds(8 * (g % 2), 8)]
@@ -533,47 +592,64 @@
     message[pl.ds(32, 56)] = my_all[...]
 
 
-def own_inflow(position, count, maps, ends, zero, write):
+def own_inflow(position, lines):
+    count = 4
     for p in range(count):
 
         @pl.when(position == p)
         def _(p=p):
-            low = zero
-            for j in range(p):
-                low = plus(pass_map(maps(j ^ p), low), ends(j ^ p)[:4])
-            inflow, lows = (low, [])
-            for j in range(p, count):
-                lows.append(inflow)
-                if j < count - 1:
-                    inflow = plus(pass_map(maps(j ^ p), inflow), ends(j ^ p)[:4])
-            high = zero
-            for j in range(count - 1, p, -1):
-                coupled = couple(maps(j ^ p), lows[j - p])
-                high = plus(plus(pass_map(maps(j ^ p), high), coupled), ends(j ^ p)[4:])
-            write(low, high)
-
-
-def y_finish_kernel(
-    place, lines, wy, my, block_ends, own, xor_3, xor_2, xor_1, wz, unsmoothed, message,
-    passed, start, done, by_row, inflow,
-):
-    refs = (own, xor_1, xor_2, xor_3)
-
+            for maps, ends, outer_low, outer_high, write in lines:
+                low = outer_low
+                for j in range(p):
+                    low = plus(pass_map(maps(j ^ p), low), ends(j ^ p)[:4])
+                inflow, lows = (low, [])
+                for j in range(p, count):
+                    lows.append(inflow)
+                    if j < count - 1:
+                        inflow = plus(pass_map(maps(j ^ p), inflow), ends(j ^ p)[:4])
+                high = outer_high
+                for j in range(count - 1, p, -1):
+                    coupled = couple(maps(j ^ p), lows[j - p])
+                    high = plus(plus(pass_map(maps(j ^ p), high), coupled), ends(j ^ p)[4:])
+                write(low, high)
+
+
+def inflow_writer(ref, rows):
     def write(low, high):
         for k in range(4):
-            inflow[k, pl.ds(0, 4)] = low[k]
-            inflow[4 + k, pl.ds(0, 4)] = high[k]
-
-    own_inflow(
-        place[1],
-        4,
-        lambda s: [refs[s][pl.ds(32 + 4 * v, 4)] for v in range(14)],
-        lambda s: [refs[s][pl.ds(4 * v, 4)] for v in range(8)],
-        [jnp.zeros((4, 128), F32)] * 4,
-        write,
+            ref[k, rows] = low[k]
+            ref[4 + k, rows] = high[k]
+
+    return write
+
+
+def pair_blocks(place, own, partner):
+    is_low = place[1] % 2 == 0
+    rows = [pl.ds(4 * v, 4) for v in range(22)]
+    blocks = (
+        [jnp.where(is_low, own[r], partner[r]) for r in rows],
+        [jnp.where(is_low, partner[r], own[r]) for r in rows],
     )
-    low = [inflow[k, pl.ds(0, 4)] for k in range(4)]
-    high = [inflow[4 + k, pl.ds(0, 4)] for k in range(4)]
+    return [b[8:] for b in blocks], [b[:8] for b in blocks]
+
+
+def y_pair_kernel(place, own, partner, joint):
+    maps, ends = pair_blocks(place, own, partner)
+    lows, highs = chained(maps, ends, no_state(4), no_state(4))
+    for v, value in enumerate(lows[2] + highs[0] + merged_maps(maps)):
+        joint[pl.ds(4 * v, 4)] = value
+
+
+def y_finish_kernel(
+    place, lines, wy, my, block_ends, own, partner, joint, other_joint, wz, unsmoothed, message,
+    passed, start, done, by_row,
+):
+    own_joint, other = ([ref[pl.ds(4 * v, 4)] for v in range(22)] for ref in (joint, other_joint))
+    outer = outer_inflow(place[1] >= 2, own_joint[:8], other[:8], other[12:])
+    pair_lows, pair_highs = chained(*pair_blocks(place, own, partner), *outer)
+    is_low = place[1] % 2 == 0
+    low = [jnp.where(is_low, a, b) for a, b in zip(pair_lows[0], pair_lows[1])]
+    high = [jnp.where(is_low, a, b) for a, b in zip(pair_highs[1], pair_highs[2])]
     maps = [[my[v, pl.ds(s, 4, stride=8)] for v in range(14)] for s in range(8)]
     blocks = [[block_ends[v, pl.ds(s, 4, stride=8)] for v in range(8)] for s in range(8)]
     lows, highs = chained(maps, blocks, low, high)
@@ -621,22 +697,19 @@
 ):
     maps = (maps_0, maps_1, maps_2, maps_3)
     ends = (ends_0, ends_1, ends_2, ends_3)
-    for g in range(4):
-        rows = pl.ds(8 * g, 8)
-
-        def write(low, high, rows=rows):
-            for k in range(4):
-                inflow[k, rows] = low[k]
-                inflow[4 + k, rows] = high[k]
-
-        own_inflow(
-            place[2],
-            4,
-            lambda s, rows=rows: [maps[s][v, rows] for v in range(14)],
-            lambda s, rows=rows: [ends[s][v, rows] for v in range(8)],
-            [jnp.zeros((8, 128), F32)] * 4,
-            write,
-        )
+    own_inflow(
+        place[2],
+        [
+            (
+                lambda s, rows=rows: values_of(maps[s], rows, 14),
+                lambda s, rows=rows: values_of(ends[s], rows, 8),
+                no_state(),
+                no_state(),
+                inflow_writer(inflow, rows),
+            )
+            for rows in GROUPS
+        ],
+    )
     lows = [[inflow[k, pl.ds(8 * g, 8)] for k in range(4)] for g in range(4)]
     highs = [[inflow[4 + k, pl.ds(8 * g, 8)] for k in range(4)] for g in range(4)]
 
@@ -673,9 +746,12 @@
     return from_even, from_odd
 
 
+def xor_swap(value, axis, s):
+    return lax.ppermute(value, axis, [(i, i ^ s) for i in range(lax.axis_size(axis))])
+
+
 def xor_gather(value, axis):
-    count = lax.axis_size(axis)
-    return [value] + [lax.ppermute(value, axis, [(i, i ^ s) for i in range(count)]) for s in (1, 2, 3)]
+    return [value] + [xor_swap(value, axis, s) for s in (1, 2, 3)]
 
 
 def local(source, capacity, transfer, observed, classes, conductivity, filter_rates):
@@ -716,43 +792,46 @@
          (256, 128), (2, 128, 128)],
         [VMEM, SMEM, VMEM],
     )(classes, rates, strips)
-    x_odd, wx = lax.optimization_barrier((x_odd, wx))
+    x_odd, wx, mx = lax.optimization_barrier((x_odd, wx, mx))
+    x_maps = [mx] + [xor_swap(mx, "gx", s) for s in (1, 2)]
     corner_even, corner_odd = call(corner_kernel, [corners, corners], [SMEM] + [VMEM] * 4)(
         place, x_odd, x_even, z_even, observed
     )
+    mx, corner_even, z_odd = lax.optimization_barrier((mx, corner_even, z_odd))
     corner_even, corner_odd = pair_swaps("gz", "gy", corner_even, corner_odd)
-
+    x_maps.append(xor_swap(mx, "gx", 3))
+
+    padded = (PLANES, 32, 128)
+    predicted, increment, x_ends = call(
+        sweep_kernel,
+        [(2,) + plane, (2, 256, 128), (8,) + rows],
+        [SMEM] + [VMEM] * 10,
+        [(7,) + padded, (6,) + padded, (4,) + padded, (4,) + padded, (STEPS,) + rows],
+        limit=16,
+    )(place, units, strips, z_even, z_odd, x_even, x_odd, corner_even, corner_odd, observed, wx)
+    x_all = xor_gather(x_ends, "gx")
+    coupling_x, around = call(run_maps_kernel, [(10,) + rows, (22,) + rows], [SMEM] + [VMEM] * 4)(place, *x_maps)
+    other_coupling = xor_swap(coupling_x, "gx", 4)
+    x_run = x_maps + [x_all[0]] + x_all[:0:-1]
+    joint, inner = call(run_ends_kernel, [(8,) + rows] * 2, [SMEM] + [VMEM] * 9)(place, *x_run, increment)
+    other_joint = xor_swap(joint, "gx", 4)
+    mz, joint = lax.optimization_barrier((mz, joint))
     z_maps = xor_gather(mz, "gz")
-
-    padded = (PLANES, 32, 128)
-    predicted, increment, message = call(
-        sweep_kernel,
-        [(2,) + plane, (2, 256, 128), (8, 88, 128)],
-        [SMEM] + [VMEM] * 11,
-        [(7,) + padded, (6,) + padded, (4,) + padded, (4,) + padded, (STEPS,) + rows, (8,) + rows, (8, 88, 128)],
-        out_specs=[VMEM, VMEM, HBM],
-        copies=1,
-        flops=100000000,
-        limit=16,
-    )(place, units, strips, z_even, z_odd, x_even, x_odd, corner_even, corner_odd,
-      observed, wx, mx)
-    gathered = lax.all_to_all(message, "gx", 0, 0, tiled=True)
-    inflow, = call(solve_kernel, [(8, 32, 128)], [VMEM] * 2)(gathered, increment)
-    inflow = lax.all_to_all(inflow, "gx", 0, 0, tiled=True)
-    inflow, z_maps = lax.optimization_barrier((inflow, z_maps))
     lines, block_ends, y_ends = call(
         x_finish_kernel,
         [(4, 128, 128), (8,) + rows, (88, 128)],
-        [VMEM] * 6,
+        [SMEM] + [VMEM] * 10,
         [(2, 256, 128), (8,) + rows],
-    )(increment, wx, inflow, wy, my, my_all)
-    y_all = xor_gather(y_ends, "gy")
+    )(place, increment, wx, around, inner, joint, other_joint, other_coupling, wy, my, my_all)
+    y_partner = xor_swap(y_ends, "gy", 1)
+    y_joint, = call(y_pair_kernel, [(88, 128)], [SMEM] + [VMEM] * 2)(place, y_ends, y_partner)
+    y_other = xor_swap(y_joint, "gy", 2)
     unsmoothed, z_ends = call(
         y_finish_kernel,
         [(2,) + plane, (8,) + rows],
         [SMEM] + [VMEM] * 9,
-        [(2, 256, 128), (8,) + rows, (4, 128, 128), (2, 256, 128), (8, 8, 128)],
-    )(place, lines, wy, my, block_ends, y_all[0], *y_all[:0:-1], wz)
+        [(2, 256, 128), (8,) + rows, (4, 128, 128), (2, 256, 128)],
+    )(place, lines, wy, my, block_ends, y_ends, y_partner, y_joint, y_other, wz)
     z_all = xor_gather(z_ends, "gz")
     smoothed, = call(z_finish_kernel, [(2,) + plane], [SMEM] + [VMEM] * 10, [(2,) + plane, (8,) + rows])(
         place, unsmoothed, wz, *z_maps, z_all[0], *z_all[:0:-1]

time: 87.2 us -> 83.8 us (0.961); the launches traced: 85.8 us -> 83.6 us
  waiting for transfers between devices: 27.6 us -> 20.3 us
  starting transfers between devices: 30 us -> 36.1 us
    ppermute x9 -> x16, starting transfers between devices: 12.5 us -> 25.5 us  [xor_swap(): lax.ppermute(value, axis, [(i, i ^ s) for i in range(lax.axis_size(axis))])]
    all_to_all x2 -> x0, waiting for transfers between devices: 8.29 us -> none  [the longest x1 5.46 us: local(): inflow = lax.all_to_all(inflow, 'gx', 0, 0, tiled=True)]
    all_to_all x2 -> x0, starting transfers between devices: 8.2 us -> none  [the longest x1 4.83 us: local(): gathered = lax.all_to_all(message, 'gx', 0, 0, tiled=True)]
    ppermute x9 -> x16, waiting for transfers between devices: 10.4 us -> 12 us  [xor_swap(): lax.ppermute(value, axis, [(i, i ^ s) for i in range(lax.axis_size(axis))])]
    pallas_call x3 -> x5, Pallas kernels: 12.4 us -> 13.6 us  [the longest x1 10.1 us: local(): call(sweep_kernel, [(2,) + plane, (2, 256, 128), (8,) + rows], [SMEM] + [...]
    ppermute x4, starting transfers between devices: 7.49 us -> 8.56 us  [pair_swaps(): lax.ppermute(value_even, axis, [(i, i ^ 1) for i in range(count)])]
    pallas_call x1, Pallas kernels: 1.67 us -> 0.65 us  [local(): call(face_kernel, [z_face, z_face, x_face, x_face], [SMEM, VMEM])]
    unnamed x14 -> x10, local copies, waits for them, and re-layouts: 1.85 us -> 1.16 us
  transfers between devices with their start and end apart: 19 -> 24, of which waited for: 11 -> 9; matrix products, arithmetic and copies ran while one was open for 0% -> 0% of each run, Pallas kernels for 7% -> 23%
where the time goes in v5:
time: 83.8 us; the launch traced here: 83.6 us
  starting transfers between devices  36.1 us (43%)
  Pallas kernels  25.1 us (30%)
  waiting for transfers between devices  20.3 us (24%)
  local copies, waits for them, and re-layouts  1.25 us (1%)
    ppermute x16, starting transfers between devices, xor_swap(): lax.ppermute(value, axis, [(i, i ^ s) for i in range(lax.axis_size(axis))])  25.5 us
    ppermute x16, waiting for transfers between devices, xor_swap(): lax.ppermute(value, axis, [(i, i ^ s) for i in range(lax.axis_size(axis))])  12 us
    pallas_call x1, Pallas kernels, local(): call(sweep_kernel, [(2,) + plane, (2, 256, 128), (8,) + rows], [SMEM] + [...  10.1 us
    ppermute x4, starting transfers between devices, pair_swaps(): lax.ppermute(value_even, axis, [(i, i ^ 1) for i in range(count)])  8.56 us
    ppermute x4, waiting for transfers between devices, pair_swaps(): lax.ppermute(value_even, axis, [(i, i ^ 1) for i in range(count)])  8.25 us
    pallas_call x1, Pallas kernels, local(): call(coefficients_kernel, [(6,) + plane, (8, STEPS, 128), (8, STEPS, 128)...  3.26 us
    pallas_call x1, Pallas kernels, local(): call(maps_kernel, [(2,) + plane, (4, 128, 128), (2,) + plane, (14,) + row...  3.02 us
    ppermute x4, starting transfers between devices, pair_swaps(): from_odd = lax.ppermute(value_odd, axes, odd)  2.06 us
  transfers between devices with their start and end apart: 24, of which 9 were waited for; matrix products, arithmetic and copies ran while one was open for 0% of the time, Pallas kernels for 23%

profile of v5, /device:TPU:0, one launch (start us, length us, event | category | flops | bytes accessed | tf_op | source)
XLA Modules:
  0.0 83.6 jit_solution(12714892805826669473)
XLA Ops:
  0.6 3.3 %shard_map.86 = (f32[6,16,16,128]{3,2,1,0:T(8,128)}, f32[8,16,128]{2,1,0:T(8,128)}, f32[8,16,128]{2,1,0:T(8,128)}) custom-call(f32[2,16,16,128]{3,2,1,0:T(8,128)} %source_in.1, f32[2,16,16,128]{3,2,1,0:T(8,128)} %capacity_in.1, f32[16,16,128]{2,1,0:T(8,128)} %transfer_in.1, s32[16,16,128]{2,1,0:T(8,128)} %classes.1, f32[2,12]{1,0:T(2,128)} %conductivity.1), custom_call_target="tpu_custom_call" | custom-call | flops 1000000 | bytes 1000000 | tf_op jit(solution)/shard_map/pallas_call | solution.py:762
  3.9 1.7 %collective-permute-start = (f32[8,16,128]{2,1,0:T(8,128)}, f32[8,16,128]{2,1,0:T(8,128)S(1)}, u32[]{:S(2)}, u32[]{:S(2)}) collective-permute-start(f32[8,16,128]{2,1,0:T(8,128)} %get-tuple-element.44), channel_id=1, source_target_pairs={{0,1},{1,0},{2,3},{3,2},{4,8},{5,9},{6,10},{7,11},{8,4},{9,5},{10,... | collective-permute-start | bytes 196616 | tf_op jit(solution)/shard_map/ppermute | solution.py:745
  5.6 1.6 %collective-permute-start.1 = (f32[8,16,128]{2,1,0:T(8,128)}, f32[8,16,128]{2,1,0:T(8,128)S(1)}, u32[]{:S(2)}, u32[]{:S(2)}) collective-permute-start(f32[8,16,128]{2,1,0:T(8,128)} %get-tuple-element.45), channel_id=1, source_target_pairs={{0,4},{4,0},{8,12},{12,8},{1,5},{5,1},{9,13},{13,9},{2,6},{6,2},{1... | collective-permute-start | bytes 196616 | tf_op jit(solution)/shard_map/ppermute | solution.py:744
  7.2 0.1 stack.15.place
  7.3 1.1 %copy-done = f32[6,16,16,128]{3,2,1,0:T(8,128)S(1)} copy-done((f32[6,16,16,128]{3,2,1,0:T(8,128)S(1)}, f32[6,16,16,128]{3,2,1,0:T(8,128)}, u32[]{:S(2)}) %copy-start) | copy-done | bytes 786456
  8.4 0.7 shard_map.87
  9.1 0.0 collective-permute-done.y_odd
  9.1 0.0 collective-permute-done.1.y_even
  9.1 0.0 copy-start.4
  9.1 0.0 copy-start.3
  9.1 1.1 %shard_map.88 = (f32[16,16,128]{2,1,0:T(8,128)S(1)}, f32[44,16,128]{2,1,0:T(8,128)S(1)}, f32[44,16,128]{2,1,0:T(8,128)S(1)}, f32[704,128]{1,0:T(8,128)S(1)}, f32[704,128]{1,0:T(8,128)S(1)}) custom-call(s32[6]{0:T(128)S(1)} %stack.15.place, ...), custom_call_target="tpu_custom_call", output_to_operand_aliasing={{1}: (3, {}), {2}: (4, {}), {3}: (5, {}), {4}: (6, {})} | custom-call | flops 1000000 | bytes 1000000 | tf_op jit(solution)/shard_map/pallas_call | solution.py:776
  10.2 0.0 copy-start.2
  10.2 0.3 collective-permute-start.3
  10.5 1.6 %collective-permute-start.2 = (f32[44,16,128]{2,1,0:T(8,128)S(1)}, f32[44,16,128]{2,1,0:T(8,128)S(1)}, u32[]{:S(2)}, u32[]{:S(2)}) collective-permute-start(f32[44,16,128]{2,1,0:T(8,128)S(1)} %get-tuple-element.51), channel_id=1, source_target_pairs={{0,1},{1,0},{2,3},{3,2},{4,5},{5,4},{6,7},{7,6},{8,9},{9,8},{10,11... | collective-permute-start | bytes 1081352 | tf_op jit(solution)/shard_map/ppermute | solution.py:744
  12.1 3.6 %collective-permute-start.4 = (f32[704,128]{1,0:T(8,128)S(1)}, f32[704,128]{1,0:T(8,128)S(1)}, u32[]{:S(2)}, u32[]{:S(2)}) collective-permute-start(f32[704,128]{1,0:T(8,128)S(1)} %get-tuple-element.57), channel_id=1, source_target_pairs={{0,16},{16,0},{32,48},{48,32},{64,80},{80,64},{96,112},{112,96},{1... | collective-permute-start | bytes 1081352 | tf_op jit(solution)/shard_map/ppermute | solution.py:744
  15.7 0.0 collective-permute-start.5
  15.7 3.0 %shard_map.89 = (f32[2,16,16,128]{3,2,1,0:T(8,128)S(1)}, f32[4,128,128]{2,1,0:T(8,128)S(1)}, f32[2,16,16,128]{3,2,1,0:T(8,128)S(1)}, f32[14,32,128]{2,1,0:T(8,12...) custom-call(s32[16,16,128]{2,1,0:T(8,128)S(1)} %copy-done.3, ...), custom_call_target="tpu_custom_call" | custom-call | flops 1000000 | bytes 1000000 | tf_op jit(solution)/shard_map/pallas_call | solution.py:789
  18.7 0.0 collective-permute-done.3.x_odd
  18.7 2.4 %collective-permute-done.2._z_even.z_even = f32[44,16,128]{2,1,0:T(8,128)S(1)} collective-permute-done((f32[44,16,128]{2,1,0:T(8,128)S(1)}, f32[44,16,128]{2,1,0:T(8,128)S(1)}, u32[]{:S(2)}, u32[]{:S(2)}) %collective-permute-start.2) | collective-permute-done | bytes 360480 | tf_op jit(solution)/shard_map/ppermute | solution.py:744
  21.1 2.8 %collective-permute-done.4.x_even = f32[704,128]{1,0:T(8,128)S(1)} collective-permute-done((f32[704,128]{1,0:T(8,128)S(1)}, f32[704,128]{1,0:T(8,128)S(1)}, u32[]{:S(2)}, u32[]{:S(2)}) %collective-permute-start.4) | collective-permute-done | bytes 360480 | tf_op jit(solution)/shard_map/ppermute | solution.py:744
  23.9 0.7 shard_map.90
  24.6 0.0 collective-permute-done.5.z_odd
  24.6 3.1 %collective-permute-start.10 = (f32[14,32,128]{2,1,0:T(8,128)S(1)}, f32[14,32,128]{2,1,0:T(8,128)S(1)}, u32[]{:S(2)}, u32[]{:S(2)}) collective-permute-start(f32[14,32,128]{2,1,0:T(8,128)S(1)} %get-tuple-element.66.maps_0), channel_id=1, source_target_pairs={{0,48},{16,32},{32,16},{48,0},{64,112},{80,96},{96,80},{112,64},{1... | collective-permute-start | bytes 688136 | tf_op jit(solution)/shard_map/ppermute | solution.py:750
  27.7 0.0 collective-permute-start.8
  27.7 1.6 %collective-permute-start.9 = (f32[14,32,128]{2,1,0:T(8,128)S(1)}, f32[14,32,128]{2,1,0:T(8,128)S(1)}, u32[]{:S(2)}, u32[]{:S(2)}) collective-permute-start(f32[14,32,128]{2,1,0:T(8,128)S(1)} %get-tuple-element.66.maps_0), channel_id=1, source_target_pairs={{0,32},{16,48},{32,0},{48,16},{64,96},{80,112},{96,64},{112,80},{1... | collective-permute-start | bytes 688136 | tf_op jit(solution)/shard_map/ppermute | solution.py:750
  29.4 1.8 %collective-permute-start.6 = (f32[2,120,128]{2,1,0:T(8,128)S(1)}, f32[2,120,128]{2,1,0:T(8,128)S(1)}, u32[]{:S(2)}, u32[]{:S(2)}) collective-permute-start(f32[2,120,128]{2,1,0:T(8,128)S(1)} %get-tuple-element.61), channel_id=1, source_target_pairs={{0,1},{1,0},{2,3},{3,2},{4,5},{5,4},{6,7},{7,6},{8,9},{9,8},{10,11... | collective-permute-start | bytes 368648 | tf_op jit(solution)/shard_map/ppermute | solution.py:744
  31.2 0.0 collective-permute-start.7
  31.2 3.1 %collective-permute-done.6.corner_even = f32[2,120,128]{2,1,0:T(8,128)S(1)} collective-permute-done((f32[2,120,128]{2,1,0:T(8,128)S(1)}, f32[2,120,128]{2,1,0:T(8,128)S(1)}, u32[]{:S(2)}, u32[]{:S(2)}) %collective-permute-start.6) | collective-permute-done | bytes 122912 | tf_op jit(solution)/shard_map/ppermute | solution.py:744
  34.3 0.0 collective-permute-done.7.corner_odd
  34.3 10.1 %shard_map.91 = (f32[2,16,16,128]{3,2,1,0:T(8,128)}, f32[2,256,128]{2,1,0:T(8,128)S(1)}, f32[8,32,128]{2,1,0:T(8,128)S(1)}) custom-call(s32[6]{0:T(128)S(1)} %stack.15.place, f32[6,16,16,128]{3,2,1,0:T(8,128)S(1)} %copy-done.1, f32[16,16,128]{2,1,0:T(8,128)S(1)} %get-tuple-element.50._.strips, f32[44,16,128]{2,1,0:T(8,128)S(1)} %collective-permute-done.2._z_even.z_even, ...), custom_call_target="tpu_custom_call" | custom-call | flops 1000000 | bytes 1000000 | tf_op jit(solution)/shard_map/pallas_call | solution.py:805
  44.3 3.0 %collective-permute-start.11 = (f32[8,32,128]{2,1,0:T(8,128)S(1)}, f32[8,32,128]{2,1,0:T(8,128)S(1)}, u32[]{:S(2)}, u32[]{:S(2)}) collective-permute-start(f32[8,32,128]{2,1,0:T(8,128)S(1)} %get-tuple-element.68.ends_0), channel_id=1, source_target_pairs={{0,48},{16,32},{32,16},{48,0},{64,112},{80,96},{96,80},{112,64},{1... | collective-permute-start | bytes 393224 | tf_op jit(solution)/shard_map/ppermute | solution.py:750
  47.4 0.0 collective-permute-start.12
  47.4 0.0 collective-permute-done.10.maps_3
  47.4 1.0 %collective-permute-start.13 = (f32[8,32,128]{2,1,0:T(8,128)S(1)}, f32[8,32,128]{2,1,0:T(8,128)S(1)}, u32[]{:S(2)}, u32[]{:S(2)}) collective-permute-start(f32[8,32,128]{2,1,0:T(8,128)S(1)} %get-tuple-element.68.ends_0), channel_id=1, source_target_pairs={{0,16},{16,0},{32,48},{48,32},{64,80},{80,64},{96,112},{112,96},{1... | collective-permute-start | bytes 393224 | tf_op jit(solution)/shard_map/ppermute | solution.py:750
  48.4 0.0 collective-permute-done.8.maps_1
  48.4 0.0 collective-permute-done.9.maps_2
  48.4 0.9 %shard_map.92 = (f32[10,32,128]{2,1,0:T(8,128)S(1)}, f32[22,32,128]{2,1,0:T(8,128)S(1)}) custom-call(s32[6]{0:T(128)S(1)} %stack.15.place, f32[14,32,128]{2,1,0:T(8,128)S(1)} %get-tuple-element.66.maps_0, f32[14,32,128]{2,1,0:T(8,128)S(1)} %collective-permute-done.8.maps_1, f32[14,32,128]{2,1,0:T(8,128)S(1)} %collective-permute-done.9.maps_2, ...), custom_call_target="tpu_custom_call" | custom-call | flops 1000000 | bytes 1000000 | tf_op jit(solution)/shard_map/pallas_call | solution.py:813
  49.4 3.5 %collective-permute-start.15 = (f32[10,32,128]{2,1,0:T(8,128)S(1)}, f32[10,32,128]{2,1,0:T(8,128)S(1)}, u32[]{:S(2)}, u32[]{:S(2)}) collective-permute-start(f32[10,32,128]{2,1,0:T(8,128)S(1)} %get-tuple-element.73), channel_id=1, source_target_pairs={{0,64},{16,80},{32,96},{48,112},{64,0},{80,16},{96,32},{112,48},{1... | collective-permute-start | bytes 491528 | tf_op jit(solution)/shard_map/ppermute | solution.py:750
  52.9 0.0 collective-permute-done.11.ends_3
  52.9 1.0 %collective-permute-done.12.ends_2 = f32[8,32,128]{2,1,0:T(8,128)S(1)} collective-permute-done((f32[8,32,128]{2,1,0:T(8,128)S(1)}, f32[8,32,128]{2,1,0:T(8,128)S(1)}, u32[]{:S(2)}, u32[]{:S(2)}) %collective-permute-start.12) | collective-permute-done | bytes 131104 | tf_op jit(solution)/shard_map/ppermute | solution.py:750
  53.9 0.0 collective-permute-done.13.ends_1
  53.9 0.8 shard_map.93
  54.6 2.5 %collective-permute-start.18 = (f32[14,32,128]{2,1,0:T(8,128)S(1)}, f32[14,32,128]{2,1,0:T(8,128)S(1)}, u32[]{:S(2)}, u32[]{:S(2)}) collective-permute-start(f32[14,32,128]{2,1,0:T(8,128)S(1)} %get-tuple-element.82.maps_0), channel_id=1, source_target_pairs={{0,1},{1,0},{2,3},{3,2},{4,5},{5,4},{6,7},{7,6},{8,9},{9,8},{10,11... | collective-permute-start | bytes 688136 | tf_op jit(solution)/shard_map/ppermute | solution.py:750
  57.1 1.9 %collective-permute-start.14 = (f32[8,32,128]{2,1,0:T(8,128)S(1)}, f32[8,32,128]{2,1,0:T(8,128)S(1)}, u32[]{:S(2)}, u32[]{:S(2)}) collective-permute-start(f32[8,32,128]{2,1,0:T(8,128)S(1)} %get-tuple-element.72.joint), channel_id=1, source_target_pairs={{0,64},{16,80},{32,96},{48,112},{64,0},{80,16},{96,32},{112,48},{1... | collective-permute-start | bytes 393224 | tf_op jit(solution)/shard_map/ppermute | solution.py:750
  59.1 1.7 %collective-permute-start.19 = (f32[14,32,128]{2,1,0:T(8,128)S(1)}, f32[14,32,128]{2,1,0:T(8,128)S(1)}, u32[]{:S(2)}, u32[]{:S(2)}) collective-permute-start(f32[14,32,128]{2,1,0:T(8,128)S(1)} %get-tuple-element.82.maps_0), channel_id=1, source_target_pairs={{0,2},{1,3},{2,0},{3,1},{4,6},{5,7},{6,4},{7,5},{8,10},{9,11},{10,... | collective-permute-start | bytes 688136 | tf_op jit(solution)/shard_map/ppermute | solution.py:750
  60.8 1.1 %collective-permute-start.20 = (f32[14,32,128]{2,1,0:T(8,128)S(1)}, f32[14,32,128]{2,1,0:T(8,128)S(1)}, u32[]{:S(2)}, u32[]{:S(2)}) collective-permute-start(f32[14,32,128]{2,1,0:T(8,128)S(1)} %get-tuple-element.82.maps_0), channel_id=1, source_target_pairs={{0,3},{1,2},{2,1},{3,0},{4,7},{5,6},{6,5},{7,4},{8,11},{9,10},{10,... | collective-permute-start | bytes 688136 | tf_op jit(solution)/shard_map/ppermute | solution.py:750
  61.8 0.3 collective-permute-done.14.other_joint
  62.1 0.0 collective-permute-done.15.other_coupling
  62.1 1.2 %shard_map.94 = (f32[4,128,128]{2,1,0:T(8,128)S(1)}, f32[8,32,128]{2,1,0:T(8,128)S(1)}, f32[88,128]{1,0:T(8,128)S(1)}) custom-call(s32[6]{0:T(128)S(1)} %stack.15.place, f32[2,256,128]{2,1,0:T(8,128)S(1)} %get-tuple-element.65._.increment, f32[2,16,16,128]{3,2,1,0:T(8,128)S(1)} %get-tuple-element.63.wx, f32[22,32,128]{2,1,0:T(8,128)S(1)} %get-tuple-element.67.around, ...), custom_call_target="tpu_custom_call" | custom-call | flops 1000000 | bytes 1000000 | tf_op jit(solution)/shard_map/pallas_call | solution.py:820
  63.3 0.1 collective-permute-start.16
  63.4 1.2 %collective-permute-done.16.partner = f32[88,128]{1,0:T(8,128)S(1)} collective-permute-done((f32[88,128]{1,0:T(8,128)S(1)}, f32[88,128]{1,0:T(8,128)S(1)}, u32[]{:S(2)}, u32[]{:S(2)}) %collective-permute-start.16) | collective-permute-done | bytes 45088 | tf_op jit(solution)/shard_map/ppermute | solution.py:750
  64.6 0.6 shard_map.95.joint
  65.2 1.7 %collective-permute-start.17 = (f32[88,128]{1,0:T(8,128)S(1)}, f32[88,128]{1,0:T(8,128)S(1)}, u32[]{:S(2)}, u32[]{:S(2)}) collective-permute-start(f32[88,128]{1,0:T(8,128)S(1)} %shard_map.95.joint), channel_id=1, source_target_pairs={{0,8},{4,12},{8,0},{12,4},{1,9},{5,13},{9,1},{13,5},{2,10},{6,14},... | collective-permute-start | bytes 135176 | tf_op jit(solution)/shard_map/ppermute | solution.py:750
  66.9 3.9 %collective-permute-done.17.other_joint = f32[88,128]{1,0:T(8,128)S(1)} collective-permute-done((f32[88,128]{1,0:T(8,128)S(1)}, f32[88,128]{1,0:T(8,128)S(1)}, u32[]{:S(2)}, u32[]{:S(2)}) %collective-permute-start.17) | collective-permute-done | bytes 45088 | tf_op jit(solution)/shard_map/ppermute | solution.py:750
  70.9 1.3 %shard_map.96 = (f32[2,16,16,128]{3,2,1,0:T(8,128)S(1)}, f32[8,32,128]{2,1,0:T(8,128)S(1)}) custom-call(s32[6]{0:T(128)S(1)} %stack.15.place, f32[4,128,128]{2,1,0:T(8,128)S(1)} %get-tuple-element.77.lines, f32[4,128,128]{2,1,0:T(8,128)S(1)} %get-tuple-element.74.wy, f32[14,32,128]{2,1,0:T(8,128)S(1)} %get-tuple-element.75.my, ...), custom_call_target="tpu_custom_call" | custom-call | flops 1000000 | bytes 1000000 | tf_op jit(solution)/shard_map/pallas_call | solution.py:829
  72.1 2.7 %collective-permute-start.21 = (f32[8,32,128]{2,1,0:T(8,128)S(1)}, f32[8,32,128]{2,1,0:T(8,128)S(1)}, u32[]{:S(2)}, u32[]{:S(2)}) collective-permute-start(f32[8,32,128]{2,1,0:T(8,128)S(1)} %get-tuple-element.83.ends_0), channel_id=1, source_target_pairs={{0,3},{1,2},{2,1},{3,0},{4,7},{5,6},{6,5},{7,4},{8,11},{9,10},{10,... | collective-permute-start | bytes 393224 | tf_op jit(solution)/shard_map/ppermute | solution.py:750
  74.8 0.0 collective-permute-start.22
  74.8 0.0 collective-permute-done.18.maps_1
  74.8 1.5 %collective-permute-start.23 = (f32[8,32,128]{2,1,0:T(8,128)S(1)}, f32[8,32,128]{2,1,0:T(8,128)S(1)}, u32[]{:S(2)}, u32[]{:S(2)}) collective-permute-start(f32[8,32,128]{2,1,0:T(8,128)S(1)} %get-tuple-element.83.ends_0), channel_id=1, source_target_pairs={{0,1},{1,0},{2,3},{3,2},{4,5},{5,4},{6,7},{7,6},{8,9},{9,8},{10,11... | collective-permute-start | bytes 393224 | tf_op jit(solution)/shard_map/ppermute | solution.py:750
  76.3 0.0 collective-permute-done.19.maps_2
  76.3 0.0 collective-permute-done.20.maps_3
  76.3 3.5 %collective-permute-done.21.ends_3 = f32[8,32,128]{2,1,0:T(8,128)S(1)} collective-permute-done((f32[8,32,128]{2,1,0:T(8,128)S(1)}, f32[8,32,128]{2,1,0:T(8,128)S(1)}, u32[]{:S(2)}, u32[]{:S(2)}) %collective-permute-start.21) | collective-permute-done | bytes 131104 | tf_op jit(solution)/shard_map/ppermute | solution.py:750
  79.8 2.1 %collective-permute-done.22.ends_2 = f32[8,32,128]{2,1,0:T(8,128)S(1)} collective-permute-done((f32[8,32,128]{2,1,0:T(8,128)S(1)}, f32[8,32,128]{2,1,0:T(8,128)S(1)}, u32[]{:S(2)}, u32[]{:S(2)}) %collective-permute-start.22) | collective-permute-done | bytes 131104 | tf_op jit(solution)/shard_map/ppermute | solution.py:750
  81.9 1.6 %shard_map.97 = f32[2,16,16,128]{3,2,1,0:T(8,128)} custom-call(s32[6]{0:T(128)S(1)} %stack.15.place, f32[2,16,16,128]{3,2,1,0:T(8,128)S(1)} %get-tuple-element.81.unsmoothed, f32[2,16,16,128]{3,2,1,0:T(8,128)S(1)} %get-tuple-element.80.wz, f32[14,32,128]{2,1,0:T(8,128)S(1)} %get-tuple-element.82.maps_0, f32[14,32,128]{2,1,0:T(8,128)S(1)} %collective-permute-done.18.maps_1, ...), custom_call_target="tpu_custom_call" | custom-call | flops 1000000 | bytes 1000000 | tf_op jit(solution)/shard_map/pallas_call | solution.py:836
  (9 shorter events, 0.0 us)
Async XLA Ops:
  3.9 5.2 %collective-permute-start = (f32[8,16,128]{2,1,0:T(8,128)}, f32[8,16,128]{2,1,0:T(8,128)S(1)}, u32[]{:S(2)}, u32[]{:S(2)}) collective-permute-start(f32[8,16,128]{2,1,0:T(8,128)} %get-tuple-element.44), channel_id=1, source_target_pairs={{0,1},{1,0},{2,3},{3,2},{4,8},{5,9},{6,10},{7,11},{8,4},{9,5},{10,... | collective-permute-start | bytes 196616 | tf_op jit(solution)/shard_map/ppermute | solution.py:745
  5.6 3.5 %collective-permute-start.1 = (f32[8,16,128]{2,1,0:T(8,128)}, f32[8,16,128]{2,1,0:T(8,128)S(1)}, u32[]{:S(2)}, u32[]{:S(2)}) collective-permute-start(f32[8,16,128]{2,1,0:T(8,128)} %get-tuple-element.45), channel_id=1, source_target_pairs={{0,4},{4,0},{8,12},{12,8},{1,5},{5,1},{9,13},{13,9},{2,6},{6,2},{1... | collective-permute-start | bytes 196616 | tf_op jit(solution)/shard_map/ppermute | solution.py:744
  7.3 1.1 %copy-start = (f32[6,16,16,128]{3,2,1,0:T(8,128)S(1)}, f32[6,16,16,128]{3,2,1,0:T(8,128)}, u32[]{:S(2)}) copy-start(f32[6,16,16,128]{3,2,1,0:T(8,128)} %get-tuple-element.43.units) | copy-start | bytes 2359300
  9.1 6.6 %copy-start.4 = (f32[3,2,12]{2,1,0:T(2,128)S(1)}, f32[3,2,12]{2,1,0:T(2,128)}, u32[]{:S(2)}) copy-start(f32[3,2,12]{2,1,0:T(2,128)} %param.13) | copy-start | bytes 868
  9.1 6.6 %copy-start.3 = (s32[16,16,128]{2,1,0:T(8,128)S(1)}, s32[16,16,128]{2,1,0:T(8,128)}, u32[]{:S(2)}) copy-start(s32[16,16,128]{2,1,0:T(8,128)} %classes.1) | copy-start | bytes 393220
  10.2 13.8 %copy-start.2 = (f32[2,16,16,128]{3,2,1,0:T(8,128)S(1)}, f32[2,16,16,128]{3,2,1,0:T(8,128)}, u32[]{:S(2)}) copy-start(f32[2,16,16,128]{3,2,1,0:T(8,128)} %observed.1) | copy-start | bytes 786436
  10.2 8.6 %collective-permute-start.3 = (f32[704,128]{1,0:T(8,128)S(1)}, f32[704,128]{1,0:T(8,128)S(1)}, u32[]{:S(2)}, u32[]{:S(2)}) collective-permute-start(f32[704,128]{1,0:T(8,128)S(1)} %get-tuple-element.52), channel_id=1, source_target_pairs={{0,4},{4,0},{8,12},{12,8},{16,32},{20,36},{24,40},{28,44},{32,16},... | collective-permute-start | bytes 1081352 | tf_op jit(solution)/shard_map/ppermute | solution.py:745
  10.5 10.6 %collective-permute-start.2 = (f32[44,16,128]{2,1,0:T(8,128)S(1)}, f32[44,16,128]{2,1,0:T(8,128)S(1)}, u32[]{:S(2)}, u32[]{:S(2)}) collective-permute-start(f32[44,16,128]{2,1,0:T(8,128)S(1)} %get-tuple-element.51), channel_id=1, source_target_pairs={{0,1},{1,0},{2,3},{3,2},{4,5},{5,4},{6,7},{7,6},{8,9},{9,8},{10,11... | collective-permute-start | bytes 1081352 | tf_op jit(solution)/shard_map/ppermute | solution.py:744
  12.1 11.8 %collective-permute-start.4 = (f32[704,128]{1,0:T(8,128)S(1)}, f32[704,128]{1,0:T(8,128)S(1)}, u32[]{:S(2)}, u32[]{:S(2)}) collective-permute-start(f32[704,128]{1,0:T(8,128)S(1)} %get-tuple-element.57), channel_id=1, source_target_pairs={{0,16},{16,0},{32,48},{48,32},{64,80},{80,64},{96,112},{112,96},{1... | collective-permute-start | bytes 1081352 | tf_op jit(solution)/shard_map/ppermute | solution.py:744
  15.7 8.9 %collective-permute-start.5 = (f32[44,16,128]{2,1,0:T(8,128)S(1)}, f32[44,16,128]{2,1,0:T(8,128)S(1)}, u32[]{:S(2)}, u32[]{:S(2)}) collective-permute-start(f32[44,16,128]{2,1,0:T(8,128)S(1)} %get-tuple-element.59), channel_id=1, source_target_pairs={{0,4},{4,0},{8,12},{12,8},{1,2},{5,6},{9,10},{13,14},{2,1},{6,5},{... | collective-permute-start | bytes 1081352 | tf_op jit(solution)/shard_map/ppermute | solution.py:745
  15.7 18.6 %copy-start.1 = (f32[6,16,16,128]{3,2,1,0:T(8,128)S(1)}, f32[6,16,16,128]{3,2,1,0:T(8,128)}, u32[]{:S(2)}) copy-start(f32[6,16,16,128]{3,2,1,0:T(8,128)} %get-tuple-element.43.units) | copy-start | bytes 2359300
  24.6 22.8 %collective-permute-start.10 = (f32[14,32,128]{2,1,0:T(8,128)S(1)}, f32[14,32,128]{2,1,0:T(8,128)S(1)}, u32[]{:S(2)}, u32[]{:S(2)}) collective-permute-start(f32[14,32,128]{2,1,0:T(8,128)S(1)} %get-tuple-element.66.maps_0), channel_id=1, source_target_pairs={{0,48},{16,32},{32,16},{48,0},{64,112},{80,96},{96,80},{112,64},{1... | collective-permute-start | bytes 688136 | tf_op jit(solution)/shard_map/ppermute | solution.py:750
  27.7 20.7 %collective-permute-start.8 = (f32[14,32,128]{2,1,0:T(8,128)S(1)}, f32[14,32,128]{2,1,0:T(8,128)S(1)}, u32[]{:S(2)}, u32[]{:S(2)}) collective-permute-start(f32[14,32,128]{2,1,0:T(8,128)S(1)} %get-tuple-element.66.maps_0), channel_id=1, source_target_pairs={{0,16},{16,0},{32,48},{48,32},{64,80},{80,64},{96,112},{112,96},{1... | collective-permute-start | bytes 688136 | tf_op jit(solution)/shard_map/ppermute | solution.py:750
  27.7 20.7 %collective-permute-start.9 = (f32[14,32,128]{2,1,0:T(8,128)S(1)}, f32[14,32,128]{2,1,0:T(8,128)S(1)}, u32[]{:S(2)}, u32[]{:S(2)}) collective-permute-start(f32[14,32,128]{2,1,0:T(8,128)S(1)} %get-tuple-element.66.maps_0), channel_id=1, source_target_pairs={{0,32},{16,48},{32,0},{48,16},{64,96},{80,112},{96,64},{112,80},{1... | collective-permute-start | bytes 688136 | tf_op jit(solution)/shard_map/ppermute | solution.py:750
  29.4 4.9 %collective-permute-start.6 = (f32[2,120,128]{2,1,0:T(8,128)S(1)}, f32[2,120,128]{2,1,0:T(8,128)S(1)}, u32[]{:S(2)}, u32[]{:S(2)}) collective-permute-start(f32[2,120,128]{2,1,0:T(8,128)S(1)} %get-tuple-element.61), channel_id=1, source_target_pairs={{0,1},{1,0},{2,3},{3,2},{4,5},{5,4},{6,7},{7,6},{8,9},{9,8},{10,11... | collective-permute-start | bytes 368648 | tf_op jit(solution)/shard_map/ppermute | solution.py:744
  31.2 3.1 %collective-permute-start.7 = (f32[2,120,128]{2,1,0:T(8,128)S(1)}, f32[2,120,128]{2,1,0:T(8,128)S(1)}, u32[]{:S(2)}, u32[]{:S(2)}) collective-permute-start(f32[2,120,128]{2,1,0:T(8,128)S(1)} %get-tuple-element.62), channel_id=1, source_target_pairs={{0,4},{4,0},{8,12},{12,8},{1,2},{5,6},{9,10},{13,14},{2,1},{6,5},{... | collective-permute-start | bytes 368648 | tf_op jit(solution)/shard_map/ppermute | solution.py:745
  44.3 8.5 %collective-permute-start.11 = (f32[8,32,128]{2,1,0:T(8,128)S(1)}, f32[8,32,128]{2,1,0:T(8,128)S(1)}, u32[]{:S(2)}, u32[]{:S(2)}) collective-permute-start(f32[8,32,128]{2,1,0:T(8,128)S(1)} %get-tuple-element.68.ends_0), channel_id=1, source_target_pairs={{0,48},{16,32},{32,16},{48,0},{64,112},{80,96},{96,80},{112,64},{1... | collective-permute-start | bytes 393224 | tf_op jit(solution)/shard_map/ppermute | solution.py:750
  47.4 6.5 %collective-permute-start.12 = (f32[8,32,128]{2,1,0:T(8,128)S(1)}, f32[8,32,128]{2,1,0:T(8,128)S(1)}, u32[]{:S(2)}, u32[]{:S(2)}) collective-permute-start(f32[8,32,128]{2,1,0:T(8,128)S(1)} %get-tuple-element.68.ends_0), channel_id=1, source_target_pairs={{0,32},{16,48},{32,0},{48,16},{64,96},{80,112},{96,64},{112,80},{1... | collective-permute-start | bytes 393224 | tf_op jit(solution)/shard_map/ppermute | solution.py:750
  47.4 6.5 %collective-permute-start.13 = (f32[8,32,128]{2,1,0:T(8,128)S(1)}, f32[8,32,128]{2,1,0:T(8,128)S(1)}, u32[]{:S(2)}, u32[]{:S(2)}) collective-permute-start(f32[8,32,128]{2,1,0:T(8,128)S(1)} %get-tuple-element.68.ends_0), channel_id=1, source_target_pairs={{0,16},{16,0},{32,48},{48,32},{64,80},{80,64},{96,112},{112,96},{1... | collective-permute-start | bytes 393224 | tf_op jit(solution)/shard_map/ppermute | solution.py:750
  49.4 12.7 %collective-permute-start.15 = (f32[10,32,128]{2,1,0:T(8,128)S(1)}, f32[10,32,128]{2,1,0:T(8,128)S(1)}, u32[]{:S(2)}, u32[]{:S(2)}) collective-permute-start(f32[10,32,128]{2,1,0:T(8,128)S(1)} %get-tuple-element.73), channel_id=1, source_target_pairs={{0,64},{16,80},{32,96},{48,112},{64,0},{80,16},{96,32},{112,48},{1... | collective-permute-start | bytes 491528 | tf_op jit(solution)/shard_map/ppermute | solution.py:750
  54.6 20.2 %collective-permute-start.18 = (f32[14,32,128]{2,1,0:T(8,128)S(1)}, f32[14,32,128]{2,1,0:T(8,128)S(1)}, u32[]{:S(2)}, u32[]{:S(2)}) collective-permute-start(f32[14,32,128]{2,1,0:T(8,128)S(1)} %get-tuple-element.82.maps_0), channel_id=1, source_target_pairs={{0,1},{1,0},{2,3},{3,2},{4,5},{5,4},{6,7},{7,6},{8,9},{9,8},{10,11... | collective-permute-start | bytes 688136 | tf_op jit(solution)/shard_map/ppermute | solution.py:750
  57.1 5.0 %collective-permute-start.14 = (f32[8,32,128]{2,1,0:T(8,128)S(1)}, f32[8,32,128]{2,1,0:T(8,128)S(1)}, u32[]{:S(2)}, u32[]{:S(2)}) collective-permute-start(f32[8,32,128]{2,1,0:T(8,128)S(1)} %get-tuple-element.72.joint), channel_id=1, source_target_pairs={{0,64},{16,80},{32,96},{48,112},{64,0},{80,16},{96,32},{112,48},{1... | collective-permute-start | bytes 393224 | tf_op jit(solution)/shard_map/ppermute | solution.py:750
  59.1 17.2 %collective-permute-start.19 = (f32[14,32,128]{2,1,0:T(8,128)S(1)}, f32[14,32,128]{2,1,0:T(8,128)S(1)}, u32[]{:S(2)}, u32[]{:S(2)}) collective-permute-start(f32[14,32,128]{2,1,0:T(8,128)S(1)} %get-tuple-element.82.maps_0), channel_id=1, source_target_pairs={{0,2},{1,3},{2,0},{3,1},{4,6},{5,7},{6,4},{7,5},{8,10},{9,11},{10,... | collective-permute-start | bytes 688136 | tf_op jit(solution)/shard_map/ppermute | solution.py:750
  60.8 15.5 %collective-permute-start.20 = (f32[14,32,128]{2,1,0:T(8,128)S(1)}, f32[14,32,128]{2,1,0:T(8,128)S(1)}, u32[]{:S(2)}, u32[]{:S(2)}) collective-permute-start(f32[14,32,128]{2,1,0:T(8,128)S(1)} %get-tuple-element.82.maps_0), channel_id=1, source_target_pairs={{0,3},{1,2},{2,1},{3,0},{4,7},{5,6},{6,5},{7,4},{8,11},{9,10},{10,... | collective-permute-start | bytes 688136 | tf_op jit(solution)/shard_map/ppermute | solution.py:750
  63.3 1.3 %collective-permute-start.16 = (f32[88,128]{1,0:T(8,128)S(1)}, f32[88,128]{1,0:T(8,128)S(1)}, u32[]{:S(2)}, u32[]{:S(2)}) collective-permute-start(f32[88,128]{1,0:T(8,128)S(1)} %get-tuple-element.79.own), channel_id=1, source_target_pairs={{0,4},{4,0},{8,12},{12,8},{1,5},{5,1},{9,13},{13,9},{2,6},{6,2},{1... | collective-permute-start | bytes 135176 | tf_op jit(solution)/shard_map/ppermute | solution.py:750
  65.2 5.6 %collective-permute-start.17 = (f32[88,128]{1,0:T(8,128)S(1)}, f32[88,128]{1,0:T(8,128)S(1)}, u32[]{:S(2)}, u32[]{:S(2)}) collective-permute-start(f32[88,128]{1,0:T(8,128)S(1)} %shard_map.95.joint), channel_id=1, source_target_pairs={{0,8},{4,12},{8,0},{12,4},{1,9},{5,13},{9,1},{13,5},{2,10},{6,14},... | collective-permute-start | bytes 135176 | tf_op jit(solution)/shard_map/ppermute | solution.py:750
  72.1 7.7 %collective-permute-start.21 = (f32[8,32,128]{2,1,0:T(8,128)S(1)}, f32[8,32,128]{2,1,0:T(8,128)S(1)}, u32[]{:S(2)}, u32[]{:S(2)}) collective-permute-start(f32[8,32,128]{2,1,0:T(8,128)S(1)} %get-tuple-element.83.ends_0), channel_id=1, source_target_pairs={{0,3},{1,2},{2,1},{3,0},{4,7},{5,6},{6,5},{7,4},{8,11},{9,10},{10,... | collective-permute-start | bytes 393224 | tf_op jit(solution)/shard_map/ppermute | solution.py:750
  74.8 7.1 %collective-permute-start.22 = (f32[8,32,128]{2,1,0:T(8,128)S(1)}, f32[8,32,128]{2,1,0:T(8,128)S(1)}, u32[]{:S(2)}, u32[]{:S(2)}) collective-permute-start(f32[8,32,128]{2,1,0:T(8,128)S(1)} %get-tuple-element.83.ends_0), channel_id=1, source_target_pairs={{0,2},{1,3},{2,0},{3,1},{4,6},{5,7},{6,4},{7,5},{8,10},{9,11},{10,... | collective-permute-start | bytes 393224 | tf_op jit(solution)/shard_map/ppermute | solution.py:750
  74.8 7.1 %collective-permute-start.23 = (f32[8,32,128]{2,1,0:T(8,128)S(1)}, f32[8,32,128]{2,1,0:T(8,128)S(1)}, u32[]{:S(2)}, u32[]{:S(2)}) collective-permute-start(f32[8,32,128]{2,1,0:T(8,128)S(1)} %get-tuple-element.83.ends_0), channel_id=1, source_target_pairs={{0,1},{1,0},{2,3},{3,2},{4,5},{5,4},{6,7},{7,6},{8,9},{9,8},{10,11... | collective-permute-start | bytes 393224 | tf_op jit(solution)/shard_map/ppermute | solution.py:750

commit v6 on v5

--- a/solution.py
+++ b/solution.py
@@ -793,13 +793,15 @@
         [VMEM, SMEM, VMEM],
     )(classes, rates, strips)
     x_odd, wx, mx = lax.optimization_barrier((x_odd, wx, mx))
-    x_maps = [mx] + [xor_swap(mx, "gx", s) for s in (1, 2)]
+    map_2 = xor_swap(mx, "gx", 2)
+    x_maps = [mx, xor_swap(mx, "gx", 1), map_2]
     corner_even, corner_odd = call(corner_kernel, [corners, corners], [SMEM] + [VMEM] * 4)(
-        place, x_odd, x_even, z_even, observed
+        place, x_odd, x_even, z_odd, observed
     )
     mx, corner_even, z_odd = lax.optimization_barrier((mx, corner_even, z_odd))
     corner_even, corner_odd = pair_swaps("gz", "gy", corner_even, corner_odd)
     x_maps.append(xor_swap(mx, "gx", 3))
+    x_maps[1], corner_odd = lax.optimization_barrier((x_maps[1], corner_odd))
 
     padded = (PLANES, 32, 128)
     predicted, increment, x_ends = call(

time: 83.8 us -> 83.2 us (level)
  waiting for transfers between devices: 20.3 us -> 19.1 us
    ppermute x4, waiting for transfers between devices: 8.25 us -> 5.18 us  [pair_swaps(): lax.ppermute(value_even, axis, [(i, i ^ 1) for i in range(count)])]
    ppermute x4, starting transfers between devices: 8.56 us -> 11.4 us  [pair_swaps(): lax.ppermute(value_even, axis, [(i, i ^ 1) for i in range(count)])]
    ppermute x16, starting transfers between devices: 25.5 us -> 23.2 us  [xor_swap(): lax.ppermute(value, axis, [(i, i ^ s) for i in range(lax.axis_size(axis))])]
    ppermute x16, waiting for transfers between devices: 12 us -> 13.9 us  [xor_swap(): lax.ppermute(value, axis, [(i, i ^ s) for i in range(lax.axis_size(axis))])]
  transfers between devices with their start and end apart: 24 -> 24, of which waited for: 9 -> 10; matrix products, arithmetic and copies ran while one was open for 0% -> 0% of each run, Pallas kernels for 23% -> 23%
where the time goes in v6:
time: 83.2 us; the launch traced here: 83 us
  starting transfers between devices  36.7 us (44%)
  Pallas kernels  25.1 us (30%)
  waiting for transfers between devices  19.1 us (23%)
  local copies, waits for them, and re-layouts  1.25 us (2%)
    ppermute x16, starting transfers between devices, xor_swap(): lax.ppermute(value, axis, [(i, i ^ s) for i in range(lax.axis_size(axis))])  23.2 us
    ppermute x16, waiting for transfers between devices, xor_swap(): lax.ppermute(value, axis, [(i, i ^ s) for i in range(lax.axis_size(axis))])  13.9 us
    ppermute x4, starting transfers between devices, pair_swaps(): lax.ppermute(value_even, axis, [(i, i ^ 1) for i in range(count)])  11.4 us
    pallas_call x1, Pallas kernels, local(): call(sweep_kernel, [(2,) + plane, (2, 256, 128), (8,) + rows], [SMEM] + [...  10 us
    ppermute x4, waiting for transfers between devices, pair_swaps(): lax.ppermute(value_even, axis, [(i, i ^ 1) for i in range(count)])  5.18 us
    pallas_call x1, Pallas kernels, local(): call(coefficients_kernel, [(6,) + plane, (8, STEPS, 128), (8, STEPS, 128)...  3.26 us
    pallas_call x1, Pallas kernels, local(): call(maps_kernel, [(2,) + plane, (4, 128, 128), (2,) + plane, (14,) + row...  3.02 us
    ppermute x4, starting transfers between devices, pair_swaps(): from_odd = lax.ppermute(value_odd, axes, odd)  2.14 us
  transfers between devices with their start and end apart: 24, of which 10 were waited for; matrix products, arithmetic and copies ran while one was open for 0% of the time, Pallas kernels for 23%

profile of v6, /device:TPU:0, one launch (start us, length us, event | category | flops | bytes accessed | tf_op | source)
XLA Modules:
  0.0 83.0 jit_solution(18125913947205223091)
XLA Ops:
  0.6 3.3 %shard_map.86 = (f32[6,16,16,128]{3,2,1,0:T(8,128)}, f32[8,16,128]{2,1,0:T(8,128)}, f32[8,16,128]{2,1,0:T(8,128)}) custom-call(f32[2,16,16,128]{3,2,1,0:T(8,128)} %source_in.1, f32[2,16,16,128]{3,2,1,0:T(8,128)} %capacity_in.1, f32[16,16,128]{2,1,0:T(8,128)} %transfer_in.1, s32[16,16,128]{2,1,0:T(8,128)} %classes.1, f32[2,12]{1,0:T(2,128)} %conductivity.1), custom_call_target="tpu_custom_call" | custom-call | flops 1000000 | bytes 1000000 | tf_op jit(solution)/shard_map/pallas_call | solution.py:762
  3.9 1.7 %collective-permute-start = (f32[8,16,128]{2,1,0:T(8,128)}, f32[8,16,128]{2,1,0:T(8,128)S(1)}, u32[]{:S(2)}, u32[]{:S(2)}) collective-permute-start(f32[8,16,128]{2,1,0:T(8,128)} %get-tuple-element.46), channel_id=1, source_target_pairs={{0,1},{1,0},{2,3},{3,2},{4,8},{5,9},{6,10},{7,11},{8,4},{9,5},{10,... | collective-permute-start | bytes 196616 | tf_op jit(solution)/shard_map/ppermute | solution.py:745
  5.6 1.6 %collective-permute-start.1 = (f32[8,16,128]{2,1,0:T(8,128)}, f32[8,16,128]{2,1,0:T(8,128)S(1)}, u32[]{:S(2)}, u32[]{:S(2)}) collective-permute-start(f32[8,16,128]{2,1,0:T(8,128)} %get-tuple-element.47), channel_id=1, source_target_pairs={{0,4},{4,0},{8,12},{12,8},{1,5},{5,1},{9,13},{13,9},{2,6},{6,2},{1... | collective-permute-start | bytes 196616 | tf_op jit(solution)/shard_map/ppermute | solution.py:744
  7.2 0.1 stack.15.place
  7.3 1.1 %copy-done = f32[6,16,16,128]{3,2,1,0:T(8,128)S(1)} copy-done((f32[6,16,16,128]{3,2,1,0:T(8,128)S(1)}, f32[6,16,16,128]{3,2,1,0:T(8,128)}, u32[]{:S(2)}) %copy-start) | copy-done | bytes 786456
  8.4 0.7 shard_map.87
  9.1 0.0 collective-permute-done.y_odd
  9.1 0.0 collective-permute-done.1.y_even
  9.1 0.0 copy-start.4
  9.1 0.0 copy-start.3
  9.1 1.1 %shard_map.88 = (f32[16,16,128]{2,1,0:T(8,128)S(1)}, f32[44,16,128]{2,1,0:T(8,128)S(1)}, f32[44,16,128]{2,1,0:T(8,128)S(1)}, f32[704,128]{1,0:T(8,128)S(1)}, f32[704,128]{1,0:T(8,128)S(1)}) custom-call(s32[6]{0:T(128)S(1)} %stack.15.place, ...), custom_call_target="tpu_custom_call", output_to_operand_aliasing={{1}: (3, {}), {2}: (4, {}), {3}: (5, {}), {4}: (6, {})} | custom-call | flops 1000000 | bytes 1000000 | tf_op jit(solution)/shard_map/pallas_call | solution.py:776
  10.2 0.0 copy-start.2
  10.2 0.3 collective-permute-start.3
  10.5 3.6 %collective-permute-start.4 = (f32[704,128]{1,0:T(8,128)S(1)}, f32[704,128]{1,0:T(8,128)S(1)}, u32[]{:S(2)}, u32[]{:S(2)}) collective-permute-start(f32[704,128]{1,0:T(8,128)S(1)} %get-tuple-element.59), channel_id=1, source_target_pairs={{0,16},{16,0},{32,48},{48,32},{64,80},{80,64},{96,112},{112,96},{1... | collective-permute-start | bytes 1081352 | tf_op jit(solution)/shard_map/ppermute | solution.py:744
  14.1 0.0 collective-permute-start.5
  14.1 3.1 %collective-permute-start.2 = (f32[44,16,128]{2,1,0:T(8,128)S(1)}, f32[44,16,128]{2,1,0:T(8,128)S(1)}, u32[]{:S(2)}, u32[]{:S(2)}) collective-permute-start(f32[44,16,128]{2,1,0:T(8,128)S(1)} %get-tuple-element.53), channel_id=1, source_target_pairs={{0,1},{1,0},{2,3},{3,2},{4,5},{5,4},{6,7},{7,6},{8,9},{9,8},{10,11... | collective-permute-start | bytes 1081352 | tf_op jit(solution)/shard_map/ppermute | solution.py:744
  17.3 3.0 %shard_map.89 = (f32[2,16,16,128]{3,2,1,0:T(8,128)S(1)}, f32[4,128,128]{2,1,0:T(8,128)S(1)}, f32[2,16,16,128]{3,2,1,0:T(8,128)S(1)}, f32[14,32,128]{2,1,0:T(8,12...) custom-call(s32[16,16,128]{2,1,0:T(8,128)S(1)} %copy-done.3, ...), custom_call_target="tpu_custom_call" | custom-call | flops 1000000 | bytes 1000000 | tf_op jit(solution)/shard_map/pallas_call | solution.py:789
  20.3 0.0 collective-permute-done.3.x_odd
  20.3 2.3 %collective-permute-done.4.x_even = f32[704,128]{1,0:T(8,128)S(1)} collective-permute-done((f32[704,128]{1,0:T(8,128)S(1)}, f32[704,128]{1,0:T(8,128)S(1)}, u32[]{:S(2)}, u32[]{:S(2)}) %collective-permute-start.4) | collective-permute-done | bytes 360480 | tf_op jit(solution)/shard_map/ppermute | solution.py:744
  22.6 0.0 collective-permute-done.5._z_even.z_odd
  22.6 0.7 shard_map.90
  23.3 0.1 collective-permute-start.8
  23.4 1.8 %collective-permute-start.7 = (f32[14,32,128]{2,1,0:T(8,128)S(1)}, f32[14,32,128]{2,1,0:T(8,128)S(1)}, u32[]{:S(2)}, u32[]{:S(2)}) collective-permute-start(f32[14,32,128]{2,1,0:T(8,128)S(1)} %get-tuple-element.70.maps_0), channel_id=1, source_target_pairs={{0,16},{16,0},{32,48},{48,32},{64,80},{80,64},{96,112},{112,96},{1... | collective-permute-start | bytes 688136 | tf_op jit(solution)/shard_map/ppermute | solution.py:750
  25.2 2.7 %collective-permute-start.10 = (f32[14,32,128]{2,1,0:T(8,128)S(1)}, f32[14,32,128]{2,1,0:T(8,128)S(1)}, u32[]{:S(2)}, u32[]{:S(2)}) collective-permute-start(f32[14,32,128]{2,1,0:T(8,128)S(1)} %get-tuple-element.70.maps_0), channel_id=1, source_target_pairs={{0,48},{16,32},{32,16},{48,0},{64,112},{80,96},{96,80},{112,64},{1... | collective-permute-start | bytes 688136 | tf_op jit(solution)/shard_map/ppermute | solution.py:750
  27.9 1.4 %collective-permute-start.9 = (f32[14,32,128]{2,1,0:T(8,128)S(1)}, f32[14,32,128]{2,1,0:T(8,128)S(1)}, u32[]{:S(2)}, u32[]{:S(2)}) collective-permute-start(f32[14,32,128]{2,1,0:T(8,128)S(1)} %get-tuple-element.70.maps_0), channel_id=1, source_target_pairs={{0,32},{16,48},{32,0},{48,16},{64,96},{80,112},{96,64},{112,80},{1... | collective-permute-start | bytes 688136 | tf_op jit(solution)/shard_map/ppermute | solution.py:750
  29.3 0.0 collective-permute-done.8.corner_odd
  29.3 3.1 %collective-permute-start.6 = (f32[2,120,128]{2,1,0:T(8,128)S(1)}, f32[2,120,128]{2,1,0:T(8,128)S(1)}, u32[]{:S(2)}, u32[]{:S(2)}) collective-permute-start(f32[2,120,128]{2,1,0:T(8,128)S(1)} %get-tuple-element.63), channel_id=1, source_target_pairs={{0,1},{1,0},{2,3},{3,2},{4,5},{5,4},{6,7},{7,6},{8,9},{9,8},{10,11... | collective-permute-start | bytes 368648 | tf_op jit(solution)/shard_map/ppermute | solution.py:744
  32.4 0.0 collective-permute-done.7.maps_1
  32.4 0.0 collective-permute-done.2.z_even
  32.4 2.9 %collective-permute-done.6.corner_even = f32[2,120,128]{2,1,0:T(8,128)S(1)} collective-permute-done((f32[2,120,128]{2,1,0:T(8,128)S(1)}, f32[2,120,128]{2,1,0:T(8,128)S(1)}, u32[]{:S(2)}, u32[]{:S(2)}) %collective-permute-start.6) | collective-permute-done | bytes 122912 | tf_op jit(solution)/shard_map/ppermute | solution.py:744
  35.2 10.0 %shard_map.91 = (f32[2,16,16,128]{3,2,1,0:T(8,128)}, f32[2,256,128]{2,1,0:T(8,128)S(1)}, f32[8,32,128]{2,1,0:T(8,128)S(1)}) custom-call(s32[6]{0:T(128)S(1)} %stack.15.place, f32[6,16,16,128]{3,2,1,0:T(8,128)S(1)} %copy-done.1, f32[16,16,128]{2,1,0:T(8,128)S(1)} %get-tuple-element.52._.strips, f32[44,16,128]{2,1,0:T(8,128)S(1)} %collective-permute-done.2.z_even, ...), custom_call_target="tpu_custom_call" | custom-call | flops 1000000 | bytes 1000000 | tf_op jit(solution)/shard_map/pallas_call | solution.py:807
  45.3 2.6 %collective-permute-start.11 = (f32[8,32,128]{2,1,0:T(8,128)S(1)}, f32[8,32,128]{2,1,0:T(8,128)S(1)}, u32[]{:S(2)}, u32[]{:S(2)}) collective-permute-start(f32[8,32,128]{2,1,0:T(8,128)S(1)} %get-tuple-element.72.ends_0), channel_id=1, source_target_pairs={{0,48},{16,32},{32,16},{48,0},{64,112},{80,96},{96,80},{112,64},{1... | collective-permute-start | bytes 393224 | tf_op jit(solution)/shard_map/ppermute | solution.py:750
  47.9 0.0 collective-permute-start.12
  47.9 1.5 %collective-permute-start.13 = (f32[8,32,128]{2,1,0:T(8,128)S(1)}, f32[8,32,128]{2,1,0:T(8,128)S(1)}, u32[]{:S(2)}, u32[]{:S(2)}) collective-permute-start(f32[8,32,128]{2,1,0:T(8,128)S(1)} %get-tuple-element.72.ends_0), channel_id=1, source_target_pairs={{0,16},{16,0},{32,48},{48,32},{64,80},{80,64},{96,112},{112,96},{1... | collective-permute-start | bytes 393224 | tf_op jit(solution)/shard_map/ppermute | solution.py:750
  49.4 0.0 collective-permute-done.10.maps_3
  49.4 0.0 collective-permute-done.9.maps_2
  49.4 0.9 %shard_map.92 = (f32[10,32,128]{2,1,0:T(8,128)S(1)}, f32[22,32,128]{2,1,0:T(8,128)S(1)}) custom-call(s32[6]{0:T(128)S(1)} %stack.15.place, f32[14,32,128]{2,1,0:T(8,128)S(1)} %get-tuple-element.70.maps_0, f32[14,32,128]{2,1,0:T(8,128)S(1)} %collective-permute-done.7.maps_1, f32[14,32,128]{2,1,0:T(8,128)S(1)} %collective-permute-done.9.maps_2, ...), custom_call_target="tpu_custom_call" | custom-call | flops 1000000 | bytes 1000000 | tf_op jit(solution)/shard_map/pallas_call | solution.py:815
  50.3 1.8 %collective-permute-start.15 = (f32[10,32,128]{2,1,0:T(8,128)S(1)}, f32[10,32,128]{2,1,0:T(8,128)S(1)}, u32[]{:S(2)}, u32[]{:S(2)}) collective-permute-start(f32[10,32,128]{2,1,0:T(8,128)S(1)} %get-tuple-element.77), channel_id=1, source_target_pairs={{0,64},{16,80},{32,96},{48,112},{64,0},{80,16},{96,32},{112,48},{1... | collective-permute-start | bytes 491528 | tf_op jit(solution)/shard_map/ppermute | solution.py:750
  52.1 0.2 collective-permute-done.11.ends_3
  52.2 2.1 %collective-permute-done.12.ends_2 = f32[8,32,128]{2,1,0:T(8,128)S(1)} collective-permute-done((f32[8,32,128]{2,1,0:T(8,128)S(1)}, f32[8,32,128]{2,1,0:T(8,128)S(1)}, u32[]{:S(2)}, u32[]{:S(2)}) %collective-permute-start.12) | collective-permute-done | bytes 131104 | tf_op jit(solution)/shard_map/ppermute | solution.py:750
  54.4 0.0 collective-permute-done.13.ends_1
  54.4 0.8 shard_map.93
  55.2 2.1 %collective-permute-start.18 = (f32[14,32,128]{2,1,0:T(8,128)S(1)}, f32[14,32,128]{2,1,0:T(8,128)S(1)}, u32[]{:S(2)}, u32[]{:S(2)}) collective-permute-start(f32[14,32,128]{2,1,0:T(8,128)S(1)} %get-tuple-element.86.maps_0), channel_id=1, source_target_pairs={{0,1},{1,0},{2,3},{3,2},{4,5},{5,4},{6,7},{7,6},{8,9},{9,8},{10,11... | collective-permute-start | bytes 688136 | tf_op jit(solution)/shard_map/ppermute | solution.py:750
  57.3 1.4 %collective-permute-start.14 = (f32[8,32,128]{2,1,0:T(8,128)S(1)}, f32[8,32,128]{2,1,0:T(8,128)S(1)}, u32[]{:S(2)}, u32[]{:S(2)}) collective-permute-start(f32[8,32,128]{2,1,0:T(8,128)S(1)} %get-tuple-element.76.joint), channel_id=1, source_target_pairs={{0,64},{16,80},{32,96},{48,112},{64,0},{80,16},{96,32},{112,48},{1... | collective-permute-start | bytes 393224 | tf_op jit(solution)/shard_map/ppermute | solution.py:750
  58.6 1.4 %collective-permute-start.19 = (f32[14,32,128]{2,1,0:T(8,128)S(1)}, f32[14,32,128]{2,1,0:T(8,128)S(1)}, u32[]{:S(2)}, u32[]{:S(2)}) collective-permute-start(f32[14,32,128]{2,1,0:T(8,128)S(1)} %get-tuple-element.86.maps_0), channel_id=1, source_target_pairs={{0,2},{1,3},{2,0},{3,1},{4,6},{5,7},{6,4},{7,5},{8,10},{9,11},{10,... | collective-permute-start | bytes 688136 | tf_op jit(solution)/shard_map/ppermute | solution.py:750
  60.0 1.3 %collective-permute-start.20 = (f32[14,32,128]{2,1,0:T(8,128)S(1)}, f32[14,32,128]{2,1,0:T(8,128)S(1)}, u32[]{:S(2)}, u32[]{:S(2)}) collective-permute-start(f32[14,32,128]{2,1,0:T(8,128)S(1)} %get-tuple-element.86.maps_0), channel_id=1, source_target_pairs={{0,3},{1,2},{2,1},{3,0},{4,7},{5,6},{6,5},{7,4},{8,11},{9,10},{10,... | collective-permute-start | bytes 688136 | tf_op jit(solution)/shard_map/ppermute | solution.py:750
  61.4 0.0 collective-permute-done.15.other_coupling
  61.4 0.8 collective-permute-done.14.other_joint
  62.2 1.2 %shard_map.94 = (f32[4,128,128]{2,1,0:T(8,128)S(1)}, f32[8,32,128]{2,1,0:T(8,128)S(1)}, f32[88,128]{1,0:T(8,128)S(1)}) custom-call(s32[6]{0:T(128)S(1)} %stack.15.place, f32[2,256,128]{2,1,0:T(8,128)S(1)} %get-tuple-element.68._.increment, f32[2,16,16,128]{3,2,1,0:T(8,128)S(1)} %get-tuple-element.66.wx, f32[22,32,128]{2,1,0:T(8,128)S(1)} %get-tuple-element.71.around, ...), custom_call_target="tpu_custom_call" | custom-call | flops 1000000 | bytes 1000000 | tf_op jit(solution)/shard_map/pallas_call | solution.py:822
  63.4 0.1 collective-permute-start.16
  63.5 1.2 %collective-permute-done.16.partner = f32[88,128]{1,0:T(8,128)S(1)} collective-permute-done((f32[88,128]{1,0:T(8,128)S(1)}, f32[88,128]{1,0:T(8,128)S(1)}, u32[]{:S(2)}, u32[]{:S(2)}) %collective-permute-start.16) | collective-permute-done | bytes 45088 | tf_op jit(solution)/shard_map/ppermute | solution.py:750
  64.8 0.6 shard_map.95.joint
  65.4 1.0 %collective-permute-start.17 = (f32[88,128]{1,0:T(8,128)S(1)}, f32[88,128]{1,0:T(8,128)S(1)}, u32[]{:S(2)}, u32[]{:S(2)}) collective-permute-start(f32[88,128]{1,0:T(8,128)S(1)} %shard_map.95.joint), channel_id=1, source_target_pairs={{0,8},{4,12},{8,0},{12,4},{1,9},{5,13},{9,1},{13,5},{2,10},{6,14},... | collective-permute-start | bytes 135176 | tf_op jit(solution)/shard_map/ppermute | solution.py:750
  66.3 4.7 %collective-permute-done.17.other_joint = f32[88,128]{1,0:T(8,128)S(1)} collective-permute-done((f32[88,128]{1,0:T(8,128)S(1)}, f32[88,128]{1,0:T(8,128)S(1)}, u32[]{:S(2)}, u32[]{:S(2)}) %collective-permute-start.17) | collective-permute-done | bytes 45088 | tf_op jit(solution)/shard_map/ppermute | solution.py:750
  71.0 1.3 %shard_map.96 = (f32[2,16,16,128]{3,2,1,0:T(8,128)S(1)}, f32[8,32,128]{2,1,0:T(8,128)S(1)}) custom-call(s32[6]{0:T(128)S(1)} %stack.15.place, f32[4,128,128]{2,1,0:T(8,128)S(1)} %get-tuple-element.81.lines, f32[4,128,128]{2,1,0:T(8,128)S(1)} %get-tuple-element.78.wy, f32[14,32,128]{2,1,0:T(8,128)S(1)} %get-tuple-element.79.my, ...), custom_call_target="tpu_custom_call" | custom-call | flops 1000000 | bytes 1000000 | tf_op jit(solution)/shard_map/pallas_call | solution.py:831
  72.3 1.5 %collective-permute-start.21 = (f32[8,32,128]{2,1,0:T(8,128)S(1)}, f32[8,32,128]{2,1,0:T(8,128)S(1)}, u32[]{:S(2)}, u32[]{:S(2)}) collective-permute-start(f32[8,32,128]{2,1,0:T(8,128)S(1)} %get-tuple-element.87.ends_0), channel_id=1, source_target_pairs={{0,3},{1,2},{2,1},{3,0},{4,7},{5,6},{6,5},{7,4},{8,11},{9,10},{10,... | collective-permute-start | bytes 393224 | tf_op jit(solution)/shard_map/ppermute | solution.py:750
  73.7 0.8 collective-permute-start.22
  74.5 0.0 collective-permute-done.18.maps_1
  74.5 1.9 %collective-permute-start.23 = (f32[8,32,128]{2,1,0:T(8,128)S(1)}, f32[8,32,128]{2,1,0:T(8,128)S(1)}, u32[]{:S(2)}, u32[]{:S(2)}) collective-permute-start(f32[8,32,128]{2,1,0:T(8,128)S(1)} %get-tuple-element.87.ends_0), channel_id=1, source_target_pairs={{0,1},{1,0},{2,3},{3,2},{4,5},{5,4},{6,7},{7,6},{8,9},{9,8},{10,11... | collective-permute-start | bytes 393224 | tf_op jit(solution)/shard_map/ppermute | solution.py:750
  76.4 0.0 collective-permute-done.20.maps_3
  76.4 3.4 %collective-permute-done.21.ends_3 = f32[8,32,128]{2,1,0:T(8,128)S(1)} collective-permute-done((f32[8,32,128]{2,1,0:T(8,128)S(1)}, f32[8,32,128]{2,1,0:T(8,128)S(1)}, u32[]{:S(2)}, u32[]{:S(2)}) %collective-permute-start.21) | collective-permute-done | bytes 131104 | tf_op jit(solution)/shard_map/ppermute | solution.py:750
  79.9 0.9 %collective-permute-done.22.ends_2 = f32[8,32,128]{2,1,0:T(8,128)S(1)} collective-permute-done((f32[8,32,128]{2,1,0:T(8,128)S(1)}, f32[8,32,128]{2,1,0:T(8,128)S(1)}, u32[]{:S(2)}, u32[]{:S(2)}) %collective-permute-start.22) | collective-permute-done | bytes 131104 | tf_op jit(solution)/shard_map/ppermute | solution.py:750
  80.8 0.6 collective-permute-done.23.ends_1
  81.3 1.6 %shard_map.97 = f32[2,16,16,128]{3,2,1,0:T(8,128)} custom-call(s32[6]{0:T(128)S(1)} %stack.15.place, f32[2,16,16,128]{3,2,1,0:T(8,128)S(1)} %get-tuple-element.85.unsmoothed, f32[2,16,16,128]{3,2,1,0:T(8,128)S(1)} %get-tuple-element.84.wz, f32[14,32,128]{2,1,0:T(8,128)S(1)} %get-tuple-element.86.maps_0, f32[14,32,128]{2,1,0:T(8,128)S(1)} %collective-permute-done.18.maps_1, ...), custom_call_target="tpu_custom_call" | custom-call | flops 1000000 | bytes 1000000 | tf_op jit(solution)/shard_map/pallas_call | solution.py:838
  (9 shorter events, 0.0 us)
Async XLA Ops:
  3.9 5.2 %collective-permute-start = (f32[8,16,128]{2,1,0:T(8,128)}, f32[8,16,128]{2,1,0:T(8,128)S(1)}, u32[]{:S(2)}, u32[]{:S(2)}) collective-permute-start(f32[8,16,128]{2,1,0:T(8,128)} %get-tuple-element.46), channel_id=1, source_target_pairs={{0,1},{1,0},{2,3},{3,2},{4,8},{5,9},{6,10},{7,11},{8,4},{9,5},{10,... | collective-permute-start | bytes 196616 | tf_op jit(solution)/shard_map/ppermute | solution.py:745
  5.6 3.5 %collective-permute-start.1 = (f32[8,16,128]{2,1,0:T(8,128)}, f32[8,16,128]{2,1,0:T(8,128)S(1)}, u32[]{:S(2)}, u32[]{:S(2)}) collective-permute-start(f32[8,16,128]{2,1,0:T(8,128)} %get-tuple-element.47), channel_id=1, source_target_pairs={{0,4},{4,0},{8,12},{12,8},{1,5},{5,1},{9,13},{13,9},{2,6},{6,2},{1... | collective-permute-start | bytes 196616 | tf_op jit(solution)/shard_map/ppermute | solution.py:744
  7.3 1.1 %copy-start = (f32[6,16,16,128]{3,2,1,0:T(8,128)S(1)}, f32[6,16,16,128]{3,2,1,0:T(8,128)}, u32[]{:S(2)}) copy-start(f32[6,16,16,128]{3,2,1,0:T(8,128)} %get-tuple-element.45.units) | copy-start | bytes 2359300
  9.1 8.2 %copy-start.4 = (f32[3,2,12]{2,1,0:T(2,128)S(1)}, f32[3,2,12]{2,1,0:T(2,128)}, u32[]{:S(2)}) copy-start(f32[3,2,12]{2,1,0:T(2,128)} %param.13) | copy-start | bytes 868
  9.1 8.2 %copy-start.3 = (s32[16,16,128]{2,1,0:T(8,128)S(1)}, s32[16,16,128]{2,1,0:T(8,128)}, u32[]{:S(2)}) copy-start(s32[16,16,128]{2,1,0:T(8,128)} %classes.1) | copy-start | bytes 393220
  10.2 12.5 %copy-start.2 = (f32[2,16,16,128]{3,2,1,0:T(8,128)S(1)}, f32[2,16,16,128]{3,2,1,0:T(8,128)}, u32[]{:S(2)}) copy-start(f32[2,16,16,128]{3,2,1,0:T(8,128)} %observed.1) | copy-start | bytes 786436
  10.2 10.1 %collective-permute-start.3 = (f32[704,128]{1,0:T(8,128)S(1)}, f32[704,128]{1,0:T(8,128)S(1)}, u32[]{:S(2)}, u32[]{:S(2)}) collective-permute-start(f32[704,128]{1,0:T(8,128)S(1)} %get-tuple-element.54), channel_id=1, source_target_pairs={{0,4},{4,0},{8,12},{12,8},{16,32},{20,36},{24,40},{28,44},{32,16},... | collective-permute-start | bytes 1081352 | tf_op jit(solution)/shard_map/ppermute | solution.py:745
  10.5 12.1 %collective-permute-start.4 = (f32[704,128]{1,0:T(8,128)S(1)}, f32[704,128]{1,0:T(8,128)S(1)}, u32[]{:S(2)}, u32[]{:S(2)}) collective-permute-start(f32[704,128]{1,0:T(8,128)S(1)} %get-tuple-element.59), channel_id=1, source_target_pairs={{0,16},{16,0},{32,48},{48,32},{64,80},{80,64},{96,112},{112,96},{1... | collective-permute-start | bytes 1081352 | tf_op jit(solution)/shard_map/ppermute | solution.py:744
  14.1 8.5 %collective-permute-start.5 = (f32[44,16,128]{2,1,0:T(8,128)S(1)}, f32[44,16,128]{2,1,0:T(8,128)S(1)}, u32[]{:S(2)}, u32[]{:S(2)}) collective-permute-start(f32[44,16,128]{2,1,0:T(8,128)S(1)} %get-tuple-element.60), channel_id=1, source_target_pairs={{0,4},{4,0},{8,12},{12,8},{1,2},{5,6},{9,10},{13,14},{2,1},{6,5},{... | collective-permute-start | bytes 1081352 | tf_op jit(solution)/shard_map/ppermute | solution.py:745
  14.1 18.2 %collective-permute-start.2 = (f32[44,16,128]{2,1,0:T(8,128)S(1)}, f32[44,16,128]{2,1,0:T(8,128)S(1)}, u32[]{:S(2)}, u32[]{:S(2)}) collective-permute-start(f32[44,16,128]{2,1,0:T(8,128)S(1)} %get-tuple-element.53), channel_id=1, source_target_pairs={{0,1},{1,0},{2,3},{3,2},{4,5},{5,4},{6,7},{7,6},{8,9},{9,8},{10,11... | collective-permute-start | bytes 1081352 | tf_op jit(solution)/shard_map/ppermute | solution.py:744
  17.3 17.9 %copy-start.1 = (f32[6,16,16,128]{3,2,1,0:T(8,128)S(1)}, f32[6,16,16,128]{3,2,1,0:T(8,128)}, u32[]{:S(2)}) copy-start(f32[6,16,16,128]{3,2,1,0:T(8,128)} %get-tuple-element.45.units) | copy-start | bytes 2359300
  23.3 6.0 %collective-permute-start.8 = (f32[2,120,128]{2,1,0:T(8,128)S(1)}, f32[2,120,128]{2,1,0:T(8,128)S(1)}, u32[]{:S(2)}, u32[]{:S(2)}) collective-permute-start(f32[2,120,128]{2,1,0:T(8,128)S(1)} %get-tuple-element.64), channel_id=1, source_target_pairs={{0,4},{4,0},{8,12},{12,8},{1,2},{5,6},{9,10},{13,14},{2,1},{6,5},{... | collective-permute-start | bytes 368648 | tf_op jit(solution)/shard_map/ppermute | solution.py:745
  23.4 9.0 %collective-permute-start.7 = (f32[14,32,128]{2,1,0:T(8,128)S(1)}, f32[14,32,128]{2,1,0:T(8,128)S(1)}, u32[]{:S(2)}, u32[]{:S(2)}) collective-permute-start(f32[14,32,128]{2,1,0:T(8,128)S(1)} %get-tuple-element.70.maps_0), channel_id=1, source_target_pairs={{0,16},{16,0},{32,48},{48,32},{64,80},{80,64},{96,112},{112,96},{1... | collective-permute-start | bytes 688136 | tf_op jit(solution)/shard_map/ppermute | solution.py:750
  25.2 24.1 %collective-permute-start.10 = (f32[14,32,128]{2,1,0:T(8,128)S(1)}, f32[14,32,128]{2,1,0:T(8,128)S(1)}, u32[]{:S(2)}, u32[]{:S(2)}) collective-permute-start(f32[14,32,128]{2,1,0:T(8,128)S(1)} %get-tuple-element.70.maps_0), channel_id=1, source_target_pairs={{0,48},{16,32},{32,16},{48,0},{64,112},{80,96},{96,80},{112,64},{1... | collective-permute-start | bytes 688136 | tf_op jit(solution)/shard_map/ppermute | solution.py:750
  27.9 21.4 %collective-permute-start.9 = (f32[14,32,128]{2,1,0:T(8,128)S(1)}, f32[14,32,128]{2,1,0:T(8,128)S(1)}, u32[]{:S(2)}, u32[]{:S(2)}) collective-permute-start(f32[14,32,128]{2,1,0:T(8,128)S(1)} %get-tuple-element.70.maps_0), channel_id=1, source_target_pairs={{0,32},{16,48},{32,0},{48,16},{64,96},{80,112},{96,64},{112,80},{1... | collective-permute-start | bytes 688136 | tf_op jit(solution)/shard_map/ppermute | solution.py:750
  29.3 5.9 %collective-permute-start.6 = (f32[2,120,128]{2,1,0:T(8,128)S(1)}, f32[2,120,128]{2,1,0:T(8,128)S(1)}, u32[]{:S(2)}, u32[]{:S(2)}) collective-permute-start(f32[2,120,128]{2,1,0:T(8,128)S(1)} %get-tuple-element.63), channel_id=1, source_target_pairs={{0,1},{1,0},{2,3},{3,2},{4,5},{5,4},{6,7},{7,6},{8,9},{9,8},{10,11... | collective-permute-start | bytes 368648 | tf_op jit(solution)/shard_map/ppermute | solution.py:744
  45.3 7.0 %collective-permute-start.11 = (f32[8,32,128]{2,1,0:T(8,128)S(1)}, f32[8,32,128]{2,1,0:T(8,128)S(1)}, u32[]{:S(2)}, u32[]{:S(2)}) collective-permute-start(f32[8,32,128]{2,1,0:T(8,128)S(1)} %get-tuple-element.72.ends_0), channel_id=1, source_target_pairs={{0,48},{16,32},{32,16},{48,0},{64,112},{80,96},{96,80},{112,64},{1... | collective-permute-start | bytes 393224 | tf_op jit(solution)/shard_map/ppermute | solution.py:750
  47.9 6.5 %collective-permute-start.12 = (f32[8,32,128]{2,1,0:T(8,128)S(1)}, f32[8,32,128]{2,1,0:T(8,128)S(1)}, u32[]{:S(2)}, u32[]{:S(2)}) collective-permute-start(f32[8,32,128]{2,1,0:T(8,128)S(1)} %get-tuple-element.72.ends_0), channel_id=1, source_target_pairs={{0,32},{16,48},{32,0},{48,16},{64,96},{80,112},{96,64},{112,80},{1... | collective-permute-start | bytes 393224 | tf_op jit(solution)/shard_map/ppermute | solution.py:750
  47.9 6.5 %collective-permute-start.13 = (f32[8,32,128]{2,1,0:T(8,128)S(1)}, f32[8,32,128]{2,1,0:T(8,128)S(1)}, u32[]{:S(2)}, u32[]{:S(2)}) collective-permute-start(f32[8,32,128]{2,1,0:T(8,128)S(1)} %get-tuple-element.72.ends_0), channel_id=1, source_target_pairs={{0,16},{16,0},{32,48},{48,32},{64,80},{80,64},{96,112},{112,96},{1... | collective-permute-start | bytes 393224 | tf_op jit(solution)/shard_map/ppermute | solution.py:750
  50.3 11.1 %collective-permute-start.15 = (f32[10,32,128]{2,1,0:T(8,128)S(1)}, f32[10,32,128]{2,1,0:T(8,128)S(1)}, u32[]{:S(2)}, u32[]{:S(2)}) collective-permute-start(f32[10,32,128]{2,1,0:T(8,128)S(1)} %get-tuple-element.77), channel_id=1, source_target_pairs={{0,64},{16,80},{32,96},{48,112},{64,0},{80,16},{96,32},{112,48},{1... | collective-permute-start | bytes 491528 | tf_op jit(solution)/shard_map/ppermute | solution.py:750
  55.2 19.3 %collective-permute-start.18 = (f32[14,32,128]{2,1,0:T(8,128)S(1)}, f32[14,32,128]{2,1,0:T(8,128)S(1)}, u32[]{:S(2)}, u32[]{:S(2)}) collective-permute-start(f32[14,32,128]{2,1,0:T(8,128)S(1)} %get-tuple-element.86.maps_0), channel_id=1, source_target_pairs={{0,1},{1,0},{2,3},{3,2},{4,5},{5,4},{6,7},{7,6},{8,9},{9,8},{10,11... | collective-permute-start | bytes 688136 | tf_op jit(solution)/shard_map/ppermute | solution.py:750
  57.3 5.0 %collective-permute-start.14 = (f32[8,32,128]{2,1,0:T(8,128)S(1)}, f32[8,32,128]{2,1,0:T(8,128)S(1)}, u32[]{:S(2)}, u32[]{:S(2)}) collective-permute-start(f32[8,32,128]{2,1,0:T(8,128)S(1)} %get-tuple-element.76.joint), channel_id=1, source_target_pairs={{0,64},{16,80},{32,96},{48,112},{64,0},{80,16},{96,32},{112,48},{1... | collective-permute-start | bytes 393224 | tf_op jit(solution)/shard_map/ppermute | solution.py:750
  58.6 17.8 %collective-permute-start.19 = (f32[14,32,128]{2,1,0:T(8,128)S(1)}, f32[14,32,128]{2,1,0:T(8,128)S(1)}, u32[]{:S(2)}, u32[]{:S(2)}) collective-permute-start(f32[14,32,128]{2,1,0:T(8,128)S(1)} %get-tuple-element.86.maps_0), channel_id=1, source_target_pairs={{0,2},{1,3},{2,0},{3,1},{4,6},{5,7},{6,4},{7,5},{8,10},{9,11},{10,... | collective-permute-start | bytes 688136 | tf_op jit(solution)/shard_map/ppermute | solution.py:750
  60.0 16.4 %collective-permute-start.20 = (f32[14,32,128]{2,1,0:T(8,128)S(1)}, f32[14,32,128]{2,1,0:T(8,128)S(1)}, u32[]{:S(2)}, u32[]{:S(2)}) collective-permute-start(f32[14,32,128]{2,1,0:T(8,128)S(1)} %get-tuple-element.86.maps_0), channel_id=1, source_target_pairs={{0,3},{1,2},{2,1},{3,0},{4,7},{5,6},{6,5},{7,4},{8,11},{9,10},{10,... | collective-permute-start | bytes 688136 | tf_op jit(solution)/shard_map/ppermute | solution.py:750
  63.4 1.3 %collective-permute-start.16 = (f32[88,128]{1,0:T(8,128)S(1)}, f32[88,128]{1,0:T(8,128)S(1)}, u32[]{:S(2)}, u32[]{:S(2)}) collective-permute-start(f32[88,128]{1,0:T(8,128)S(1)} %get-tuple-element.83.own), channel_id=1, source_target_pairs={{0,4},{4,0},{8,12},{12,8},{1,5},{5,1},{9,13},{13,9},{2,6},{6,2},{1... | collective-permute-start | bytes 135176 | tf_op jit(solution)/shard_map/ppermute | solution.py:750
  65.4 5.6 %collective-permute-start.17 = (f32[88,128]{1,0:T(8,128)S(1)}, f32[88,128]{1,0:T(8,128)S(1)}, u32[]{:S(2)}, u32[]{:S(2)}) collective-permute-start(f32[88,128]{1,0:T(8,128)S(1)} %shard_map.95.joint), channel_id=1, source_target_pairs={{0,8},{4,12},{8,0},{12,4},{1,9},{5,13},{9,1},{13,5},{2,10},{6,14},... | collective-permute-start | bytes 135176 | tf_op jit(solution)/shard_map/ppermute | solution.py:750
  72.3 7.6 %collective-permute-start.21 = (f32[8,32,128]{2,1,0:T(8,128)S(1)}, f32[8,32,128]{2,1,0:T(8,128)S(1)}, u32[]{:S(2)}, u32[]{:S(2)}) collective-permute-start(f32[8,32,128]{2,1,0:T(8,128)S(1)} %get-tuple-element.87.ends_0), channel_id=1, source_target_pairs={{0,3},{1,2},{2,1},{3,0},{4,7},{5,6},{6,5},{7,4},{8,11},{9,10},{10,... | collective-permute-start | bytes 393224 | tf_op jit(solution)/shard_map/ppermute | solution.py:750
  73.7 7.0 %collective-permute-start.22 = (f32[8,32,128]{2,1,0:T(8,128)S(1)}, f32[8,32,128]{2,1,0:T(8,128)S(1)}, u32[]{:S(2)}, u32[]{:S(2)}) collective-permute-start(f32[8,32,128]{2,1,0:T(8,128)S(1)} %get-tuple-element.87.ends_0), channel_id=1, source_target_pairs={{0,2},{1,3},{2,0},{3,1},{4,6},{5,7},{6,4},{7,5},{8,10},{9,11},{10,... | collective-permute-start | bytes 393224 | tf_op jit(solution)/shard_map/ppermute | solution.py:750
  74.5 6.8 %collective-permute-start.23 = (f32[8,32,128]{2,1,0:T(8,128)S(1)}, f32[8,32,128]{2,1,0:T(8,128)S(1)}, u32[]{:S(2)}, u32[]{:S(2)}) collective-permute-start(f32[8,32,128]{2,1,0:T(8,128)S(1)} %get-tuple-element.87.ends_0), channel_id=1, source_target_pairs={{0,1},{1,0},{2,3},{3,2},{4,5},{5,4},{6,7},{7,6},{8,9},{9,8},{10,11... | collective-permute-start | bytes 393224 | tf_op jit(solution)/shard_map/ppermute | solution.py:750

commit v7 on v6

--- a/solution.py
+++ b/solution.py
@@ -385,7 +385,7 @@
             side[unit, z] = pltpu.roll(packed, 128 - 14 * unit, 1) if unit else packed
         return 0
 
-    lax.fori_loop(0, PLANES, unpack, 0, unroll=5)
+    lax.fori_loop(0, PLANES, unpack, 0, unroll=10)
 
     everywhere = slice(0, 32)
 
@@ -448,7 +448,9 @@
             outermost(first, 0)
             outermost(last, 0)
             layer = sweep(main_from, side_from, main_to, side_to, everywhere, everywhere)
-            lax.fori_loop(first + 1, last, layer, 0, unroll=8)
+            count = last - first - 1
+            even_unroll = min(u for u in range(8, count + 1) if count % u == 0)
+            lax.fori_loop(first + 1, last, layer, 0, unroll=even_unroll)
 
     def weight(i, g):
         return wx[g // 2, i, pl.ds(8 * (g % 2), 8)]

time: 83.2 us -> 81.9 us (0.984)
  Pallas kernels: 25.1 us -> 23.8 us
    pallas_call x1, Pallas kernels: 10 us -> 8.74 us  [local(): call(sweep_kernel, [(2,) + plane, (2, 256, 128), (8,) + rows], [SMEM] + [...]
  transfers between devices with their start and end apart: 24 -> 24, of which waited for: 10 -> 10; matrix products, arithmetic and copies ran while one was open for 0% -> 0% of each run, Pallas kernels for 23% -> 22%
where the time goes in v7:
time: 81.9 us; the launch traced here: 81.7 us
  starting transfers between devices  36.7 us (45%)
  Pallas kernels  23.8 us (29%)
  waiting for transfers between devices  19.1 us (23%)
  local copies, waits for them, and re-layouts  1.25 us (2%)
    ppermute x16, starting transfers between devices, xor_swap(): lax.ppermute(value, axis, [(i, i ^ s) for i in range(lax.axis_size(axis))])  23.2 us
    ppermute x16, waiting for transfers between devices, xor_swap(): lax.ppermute(value, axis, [(i, i ^ s) for i in range(lax.axis_size(axis))])  13.9 us
    ppermute x4, starting transfers between devices, pair_swaps(): lax.ppermute(value_even, axis, [(i, i ^ 1) for i in range(count)])  11.4 us
    pallas_call x1, Pallas kernels, local(): call(sweep_kernel, [(2,) + plane, (2, 256, 128), (8,) + rows], [SMEM] + [...  8.74 us
    ppermute x4, waiting for transfers between devices, pair_swaps(): lax.ppermute(value_even, axis, [(i, i ^ 1) for i in range(count)])  5.18 us
    pallas_call x1, Pallas kernels, local(): call(coefficients_kernel, [(6,) + plane, (8, STEPS, 128), (8, STEPS, 128)...  3.26 us
    pallas_call x1, Pallas kernels, local(): call(maps_kernel, [(2,) + plane, (4, 128, 128), (2,) + plane, (14,) + row...  3.02 us
    ppermute x4, starting transfers between devices, pair_swaps(): from_odd = lax.ppermute(value_odd, axes, odd)  2.14 us
  transfers between devices with their start and end apart: 24, of which 10 were waited for; matrix products, arithmetic and copies ran while one was open for 0% of the time, Pallas kernels for 22%

profile of v7, /device:TPU:0, one launch (start us, length us, event | category | flops | bytes accessed | tf_op | source)
XLA Modules:
  0.0 81.7 jit_solution(950374042306812719)
XLA Ops:
  0.6 3.3 %shard_map.86 = (f32[6,16,16,128]{3,2,1,0:T(8,128)}, f32[8,16,128]{2,1,0:T(8,128)}, f32[8,16,128]{2,1,0:T(8,128)}) custom-call(f32[2,16,16,128]{3,2,1,0:T(8,128)} %source_in.1, f32[2,16,16,128]{3,2,1,0:T(8,128)} %capacity_in.1, f32[16,16,128]{2,1,0:T(8,128)} %transfer_in.1, s32[16,16,128]{2,1,0:T(8,128)} %classes.1, f32[2,12]{1,0:T(2,128)} %conductivity.1), custom_call_target="tpu_custom_call" | custom-call | flops 1000000 | bytes 1000000 | tf_op jit(solution)/shard_map/pallas_call | solution.py:764
  3.9 1.7 %collective-permute-start = (f32[8,16,128]{2,1,0:T(8,128)}, f32[8,16,128]{2,1,0:T(8,128)S(1)}, u32[]{:S(2)}, u32[]{:S(2)}) collective-permute-start(f32[8,16,128]{2,1,0:T(8,128)} %get-tuple-element.46), channel_id=1, source_target_pairs={{0,1},{1,0},{2,3},{3,2},{4,8},{5,9},{6,10},{7,11},{8,4},{9,5},{10,... | collective-permute-start | bytes 196616 | tf_op jit(solution)/shard_map/ppermute | solution.py:747
  5.6 1.6 %collective-permute-start.1 = (f32[8,16,128]{2,1,0:T(8,128)}, f32[8,16,128]{2,1,0:T(8,128)S(1)}, u32[]{:S(2)}, u32[]{:S(2)}) collective-permute-start(f32[8,16,128]{2,1,0:T(8,128)} %get-tuple-element.47), channel_id=1, source_target_pairs={{0,4},{4,0},{8,12},{12,8},{1,5},{5,1},{9,13},{13,9},{2,6},{6,2},{1... | collective-permute-start | bytes 196616 | tf_op jit(solution)/shard_map/ppermute | solution.py:746
  7.2 0.1 stack.15.place
  7.3 1.1 %copy-done = f32[6,16,16,128]{3,2,1,0:T(8,128)S(1)} copy-done((f32[6,16,16,128]{3,2,1,0:T(8,128)S(1)}, f32[6,16,16,128]{3,2,1,0:T(8,128)}, u32[]{:S(2)}) %copy-start) | copy-done | bytes 786456
  8.4 0.7 shard_map.87
  9.1 0.0 collective-permute-done.y_odd
  9.1 0.0 collective-permute-done.1.y_even
  9.1 0.0 copy-start.4
  9.1 0.0 copy-start.3
  9.1 1.1 %shard_map.88 = (f32[16,16,128]{2,1,0:T(8,128)S(1)}, f32[44,16,128]{2,1,0:T(8,128)S(1)}, f32[44,16,128]{2,1,0:T(8,128)S(1)}, f32[704,128]{1,0:T(8,128)S(1)}, f32[704,128]{1,0:T(8,128)S(1)}) custom-call(s32[6]{0:T(128)S(1)} %stack.15.place, ...), custom_call_target="tpu_custom_call", output_to_operand_aliasing={{1}: (3, {}), {2}: (4, {}), {3}: (5, {}), {4}: (6, {})} | custom-call | flops 1000000 | bytes 1000000 | tf_op jit(solution)/shard_map/pallas_call | solution.py:778
  10.2 0.0 copy-start.2
  10.2 0.3 collective-permute-start.3
  10.5 3.6 %collective-permute-start.4 = (f32[704,128]{1,0:T(8,128)S(1)}, f32[704,128]{1,0:T(8,128)S(1)}, u32[]{:S(2)}, u32[]{:S(2)}) collective-permute-start(f32[704,128]{1,0:T(8,128)S(1)} %get-tuple-element.59), channel_id=1, source_target_pairs={{0,16},{16,0},{32,48},{48,32},{64,80},{80,64},{96,112},{112,96},{1... | collective-permute-start | bytes 1081352 | tf_op jit(solution)/shard_map/ppermute | solution.py:746
  14.1 0.0 collective-permute-start.5
  14.1 3.1 %collective-permute-start.2 = (f32[44,16,128]{2,1,0:T(8,128)S(1)}, f32[44,16,128]{2,1,0:T(8,128)S(1)}, u32[]{:S(2)}, u32[]{:S(2)}) collective-permute-start(f32[44,16,128]{2,1,0:T(8,128)S(1)} %get-tuple-element.53), channel_id=1, source_target_pairs={{0,1},{1,0},{2,3},{3,2},{4,5},{5,4},{6,7},{7,6},{8,9},{9,8},{10,11... | collective-permute-start | bytes 1081352 | tf_op jit(solution)/shard_map/ppermute | solution.py:746
  17.3 3.0 %shard_map.89 = (f32[2,16,16,128]{3,2,1,0:T(8,128)S(1)}, f32[4,128,128]{2,1,0:T(8,128)S(1)}, f32[2,16,16,128]{3,2,1,0:T(8,128)S(1)}, f32[14,32,128]{2,1,0:T(8,12...) custom-call(s32[16,16,128]{2,1,0:T(8,128)S(1)} %copy-done.3, ...), custom_call_target="tpu_custom_call" | custom-call | flops 1000000 | bytes 1000000 | tf_op jit(solution)/shard_map/pallas_call | solution.py:791
  20.3 0.0 collective-permute-done.3.x_odd
  20.3 2.3 %collective-permute-done.4.x_even = f32[704,128]{1,0:T(8,128)S(1)} collective-permute-done((f32[704,128]{1,0:T(8,128)S(1)}, f32[704,128]{1,0:T(8,128)S(1)}, u32[]{:S(2)}, u32[]{:S(2)}) %collective-permute-start.4) | collective-permute-done | bytes 360480 | tf_op jit(solution)/shard_map/ppermute | solution.py:746
  22.6 0.0 collective-permute-done.5._z_even.z_odd
  22.6 0.7 shard_map.90
  23.3 0.1 collective-permute-start.8
  23.4 1.8 %collective-permute-start.7 = (f32[14,32,128]{2,1,0:T(8,128)S(1)}, f32[14,32,128]{2,1,0:T(8,128)S(1)}, u32[]{:S(2)}, u32[]{:S(2)}) collective-permute-start(f32[14,32,128]{2,1,0:T(8,128)S(1)} %get-tuple-element.70.maps_0), channel_id=1, source_target_pairs={{0,16},{16,0},{32,48},{48,32},{64,80},{80,64},{96,112},{112,96},{1... | collective-permute-start | bytes 688136 | tf_op jit(solution)/shard_map/ppermute | solution.py:752
  25.2 2.7 %collective-permute-start.10 = (f32[14,32,128]{2,1,0:T(8,128)S(1)}, f32[14,32,128]{2,1,0:T(8,128)S(1)}, u32[]{:S(2)}, u32[]{:S(2)}) collective-permute-start(f32[14,32,128]{2,1,0:T(8,128)S(1)} %get-tuple-element.70.maps_0), channel_id=1, source_target_pairs={{0,48},{16,32},{32,16},{48,0},{64,112},{80,96},{96,80},{112,64},{1... | collective-permute-start | bytes 688136 | tf_op jit(solution)/shard_map/ppermute | solution.py:752
  27.9 1.4 %collective-permute-start.9 = (f32[14,32,128]{2,1,0:T(8,128)S(1)}, f32[14,32,128]{2,1,0:T(8,128)S(1)}, u32[]{:S(2)}, u32[]{:S(2)}) collective-permute-start(f32[14,32,128]{2,1,0:T(8,128)S(1)} %get-tuple-element.70.maps_0), channel_id=1, source_target_pairs={{0,32},{16,48},{32,0},{48,16},{64,96},{80,112},{96,64},{112,80},{1... | collective-permute-start | bytes 688136 | tf_op jit(solution)/shard_map/ppermute | solution.py:752
  29.3 0.0 collective-permute-done.8.corner_odd
  29.3 3.1 %collective-permute-start.6 = (f32[2,120,128]{2,1,0:T(8,128)S(1)}, f32[2,120,128]{2,1,0:T(8,128)S(1)}, u32[]{:S(2)}, u32[]{:S(2)}) collective-permute-start(f32[2,120,128]{2,1,0:T(8,128)S(1)} %get-tuple-element.63), channel_id=1, source_target_pairs={{0,1},{1,0},{2,3},{3,2},{4,5},{5,4},{6,7},{7,6},{8,9},{9,8},{10,11... | collective-permute-start | bytes 368648 | tf_op jit(solution)/shard_map/ppermute | solution.py:746
  32.4 0.0 collective-permute-done.7.maps_1
  32.4 0.0 collective-permute-done.2.z_even
  32.4 2.9 %collective-permute-done.6.corner_even = f32[2,120,128]{2,1,0:T(8,128)S(1)} collective-permute-done((f32[2,120,128]{2,1,0:T(8,128)S(1)}, f32[2,120,128]{2,1,0:T(8,128)S(1)}, u32[]{:S(2)}, u32[]{:S(2)}) %collective-permute-start.6) | collective-permute-done | bytes 122912 | tf_op jit(solution)/shard_map/ppermute | solution.py:746
  35.2 8.7 %shard_map.91 = (f32[2,16,16,128]{3,2,1,0:T(8,128)}, f32[2,256,128]{2,1,0:T(8,128)S(1)}, f32[8,32,128]{2,1,0:T(8,128)S(1)}) custom-call(s32[6]{0:T(128)S(1)} %stack.15.place, f32[6,16,16,128]{3,2,1,0:T(8,128)S(1)} %copy-done.1, f32[16,16,128]{2,1,0:T(8,128)S(1)} %get-tuple-element.52._.strips, f32[44,16,128]{2,1,0:T(8,128)S(1)} %collective-permute-done.2.z_even, ...), custom_call_target="tpu_custom_call" | custom-call | flops 1000000 | bytes 1000000 | tf_op jit(solution)/shard_map/pallas_call | solution.py:809
  44.0 2.6 %collective-permute-start.11 = (f32[8,32,128]{2,1,0:T(8,128)S(1)}, f32[8,32,128]{2,1,0:T(8,128)S(1)}, u32[]{:S(2)}, u32[]{:S(2)}) collective-permute-start(f32[8,32,128]{2,1,0:T(8,128)S(1)} %get-tuple-element.72.ends_0), channel_id=1, source_target_pairs={{0,48},{16,32},{32,16},{48,0},{64,112},{80,96},{96,80},{112,64},{1... | collective-permute-start | bytes 393224 | tf_op jit(solution)/shard_map/ppermute | solution.py:752
  46.6 0.0 collective-permute-start.12
  46.6 1.5 %collective-permute-start.13 = (f32[8,32,128]{2,1,0:T(8,128)S(1)}, f32[8,32,128]{2,1,0:T(8,128)S(1)}, u32[]{:S(2)}, u32[]{:S(2)}) collective-permute-start(f32[8,32,128]{2,1,0:T(8,128)S(1)} %get-tuple-element.72.ends_0), channel_id=1, source_target_pairs={{0,16},{16,0},{32,48},{48,32},{64,80},{80,64},{96,112},{112,96},{1... | collective-permute-start | bytes 393224 | tf_op jit(solution)/shard_map/ppermute | solution.py:752
  48.1 0.0 collective-permute-done.10.maps_3
  48.1 0.0 collective-permute-done.9.maps_2
  48.1 0.9 %shard_map.92 = (f32[10,32,128]{2,1,0:T(8,128)S(1)}, f32[22,32,128]{2,1,0:T(8,128)S(1)}) custom-call(s32[6]{0:T(128)S(1)} %stack.15.place, f32[14,32,128]{2,1,0:T(8,128)S(1)} %get-tuple-element.70.maps_0, f32[14,32,128]{2,1,0:T(8,128)S(1)} %collective-permute-done.7.maps_1, f32[14,32,128]{2,1,0:T(8,128)S(1)} %collective-permute-done.9.maps_2, ...), custom_call_target="tpu_custom_call" | custom-call | flops 1000000 | bytes 1000000 | tf_op jit(solution)/shard_map/pallas_call | solution.py:817
  49.0 1.8 %collective-permute-start.15 = (f32[10,32,128]{2,1,0:T(8,128)S(1)}, f32[10,32,128]{2,1,0:T(8,128)S(1)}, u32[]{:S(2)}, u32[]{:S(2)}) collective-permute-start(f32[10,32,128]{2,1,0:T(8,128)S(1)} %get-tuple-element.77), channel_id=1, source_target_pairs={{0,64},{16,80},{32,96},{48,112},{64,0},{80,16},{96,32},{112,48},{1... | collective-permute-start | bytes 491528 | tf_op jit(solution)/shard_map/ppermute | solution.py:752
  50.8 0.2 collective-permute-done.11.ends_3
  50.9 2.1 %collective-permute-done.12.ends_2 = f32[8,32,128]{2,1,0:T(8,128)S(1)} collective-permute-done((f32[8,32,128]{2,1,0:T(8,128)S(1)}, f32[8,32,128]{2,1,0:T(8,128)S(1)}, u32[]{:S(2)}, u32[]{:S(2)}) %collective-permute-start.12) | collective-permute-done | bytes 131104 | tf_op jit(solution)/shard_map/ppermute | solution.py:752
  53.1 0.0 collective-permute-done.13.ends_1
  53.1 0.8 shard_map.93
  53.8 2.1 %collective-permute-start.18 = (f32[14,32,128]{2,1,0:T(8,128)S(1)}, f32[14,32,128]{2,1,0:T(8,128)S(1)}, u32[]{:S(2)}, u32[]{:S(2)}) collective-permute-start(f32[14,32,128]{2,1,0:T(8,128)S(1)} %get-tuple-element.86.maps_0), channel_id=1, source_target_pairs={{0,1},{1,0},{2,3},{3,2},{4,5},{5,4},{6,7},{7,6},{8,9},{9,8},{10,11... | collective-permute-start | bytes 688136 | tf_op jit(solution)/shard_map/ppermute | solution.py:752
  56.0 1.4 %collective-permute-start.14 = (f32[8,32,128]{2,1,0:T(8,128)S(1)}, f32[8,32,128]{2,1,0:T(8,128)S(1)}, u32[]{:S(2)}, u32[]{:S(2)}) collective-permute-start(f32[8,32,128]{2,1,0:T(8,128)S(1)} %get-tuple-element.76.joint), channel_id=1, source_target_pairs={{0,64},{16,80},{32,96},{48,112},{64,0},{80,16},{96,32},{112,48},{1... | collective-permute-start | bytes 393224 | tf_op jit(solution)/shard_map/ppermute | solution.py:752
  57.3 1.4 %collective-permute-start.19 = (f32[14,32,128]{2,1,0:T(8,128)S(1)}, f32[14,32,128]{2,1,0:T(8,128)S(1)}, u32[]{:S(2)}, u32[]{:S(2)}) collective-permute-start(f32[14,32,128]{2,1,0:T(8,128)S(1)} %get-tuple-element.86.maps_0), channel_id=1, source_target_pairs={{0,2},{1,3},{2,0},{3,1},{4,6},{5,7},{6,4},{7,5},{8,10},{9,11},{10,... | collective-permute-start | bytes 688136 | tf_op jit(solution)/shard_map/ppermute | solution.py:752
  58.7 1.3 %collective-permute-start.20 = (f32[14,32,128]{2,1,0:T(8,128)S(1)}, f32[14,32,128]{2,1,0:T(8,128)S(1)}, u32[]{:S(2)}, u32[]{:S(2)}) collective-permute-start(f32[14,32,128]{2,1,0:T(8,128)S(1)} %get-tuple-element.86.maps_0), channel_id=1, source_target_pairs={{0,3},{1,2},{2,1},{3,0},{4,7},{5,6},{6,5},{7,4},{8,11},{9,10},{10,... | collective-permute-start | bytes 688136 | tf_op jit(solution)/shard_map/ppermute | solution.py:752
  60.1 0.8 %collective-permute-done.14.other_joint = f32[8,32,128]{2,1,0:T(8,128)S(1)} collective-permute-done((f32[8,32,128]{2,1,0:T(8,128)S(1)}, f32[8,32,128]{2,1,0:T(8,128)S(1)}, u32[]{:S(2)}, u32[]{:S(2)}) %collective-permute-start.14) | collective-permute-done | bytes 131104 | tf_op jit(solution)/shard_map/ppermute | solution.py:752
  60.9 1.2 %shard_map.94 = (f32[4,128,128]{2,1,0:T(8,128)S(1)}, f32[8,32,128]{2,1,0:T(8,128)S(1)}, f32[88,128]{1,0:T(8,128)S(1)}) custom-call(s32[6]{0:T(128)S(1)} %stack.15.place, f32[2,256,128]{2,1,0:T(8,128)S(1)} %get-tuple-element.68._.increment, f32[2,16,16,128]{3,2,1,0:T(8,128)S(1)} %get-tuple-element.66.wx, f32[22,32,128]{2,1,0:T(8,128)S(1)} %get-tuple-element.71.around, ...), custom_call_target="tpu_custom_call" | custom-call | flops 1000000 | bytes 1000000 | tf_op jit(solution)/shard_map/pallas_call | solution.py:824
  62.1 0.1 collective-permute-start.16
  62.2 1.2 %collective-permute-done.16.partner = f32[88,128]{1,0:T(8,128)S(1)} collective-permute-done((f32[88,128]{1,0:T(8,128)S(1)}, f32[88,128]{1,0:T(8,128)S(1)}, u32[]{:S(2)}, u32[]{:S(2)}) %collective-permute-start.16) | collective-permute-done | bytes 45088 | tf_op jit(solution)/shard_map/ppermute | solution.py:752
  63.4 0.6 shard_map.95.joint
  64.0 1.0 %collective-permute-start.17 = (f32[88,128]{1,0:T(8,128)S(1)}, f32[88,128]{1,0:T(8,128)S(1)}, u32[]{:S(2)}, u32[]{:S(2)}) collective-permute-start(f32[88,128]{1,0:T(8,128)S(1)} %shard_map.95.joint), channel_id=1, source_target_pairs={{0,8},{4,12},{8,0},{12,4},{1,9},{5,13},{9,1},{13,5},{2,10},{6,14},... | collective-permute-start | bytes 135176 | tf_op jit(solution)/shard_map/ppermute | solution.py:752
  65.0 4.7 %collective-permute-done.17.other_joint = f32[88,128]{1,0:T(8,128)S(1)} collective-permute-done((f32[88,128]{1,0:T(8,128)S(1)}, f32[88,128]{1,0:T(8,128)S(1)}, u32[]{:S(2)}, u32[]{:S(2)}) %collective-permute-start.17) | collective-permute-done | bytes 45088 | tf_op jit(solution)/shard_map/ppermute | solution.py:752
  69.7 1.3 %shard_map.96 = (f32[2,16,16,128]{3,2,1,0:T(8,128)S(1)}, f32[8,32,128]{2,1,0:T(8,128)S(1)}) custom-call(s32[6]{0:T(128)S(1)} %stack.15.place, f32[4,128,128]{2,1,0:T(8,128)S(1)} %get-tuple-element.81.lines, f32[4,128,128]{2,1,0:T(8,128)S(1)} %get-tuple-element.78.wy, f32[14,32,128]{2,1,0:T(8,128)S(1)} %get-tuple-element.79.my, ...), custom_call_target="tpu_custom_call" | custom-call | flops 1000000 | bytes 1000000 | tf_op jit(solution)/shard_map/pallas_call | solution.py:833
  70.9 1.5 %collective-permute-start.21 = (f32[8,32,128]{2,1,0:T(8,128)S(1)}, f32[8,32,128]{2,1,0:T(8,128)S(1)}, u32[]{:S(2)}, u32[]{:S(2)}) collective-permute-start(f32[8,32,128]{2,1,0:T(8,128)S(1)} %get-tuple-element.87.ends_0), channel_id=1, source_target_pairs={{0,3},{1,2},{2,1},{3,0},{4,7},{5,6},{6,5},{7,4},{8,11},{9,10},{10,... | collective-permute-start | bytes 393224 | tf_op jit(solution)/shard_map/ppermute | solution.py:752
  72.4 0.8 collective-permute-start.22
  73.2 0.0 collective-permute-done.18.maps_1
  73.2 1.9 %collective-permute-start.23 = (f32[8,32,128]{2,1,0:T(8,128)S(1)}, f32[8,32,128]{2,1,0:T(8,128)S(1)}, u32[]{:S(2)}, u32[]{:S(2)}) collective-permute-start(f32[8,32,128]{2,1,0:T(8,128)S(1)} %get-tuple-element.87.ends_0), channel_id=1, source_target_pairs={{0,1},{1,0},{2,3},{3,2},{4,5},{5,4},{6,7},{7,6},{8,9},{9,8},{10,11... | collective-permute-start | bytes 393224 | tf_op jit(solution)/shard_map/ppermute | solution.py:752
  75.1 0.0 collective-permute-done.19.maps_2
  75.1 0.0 collective-permute-done.20.maps_3
  75.1 3.4 %collective-permute-done.21.ends_3 = f32[8,32,128]{2,1,0:T(8,128)S(1)} collective-permute-done((f32[8,32,128]{2,1,0:T(8,128)S(1)}, f32[8,32,128]{2,1,0:T(8,128)S(1)}, u32[]{:S(2)}, u32[]{:S(2)}) %collective-permute-start.21) | collective-permute-done | bytes 131104 | tf_op jit(solution)/shard_map/ppermute | solution.py:752
  78.6 0.9 %collective-permute-done.22.ends_2 = f32[8,32,128]{2,1,0:T(8,128)S(1)} collective-permute-done((f32[8,32,128]{2,1,0:T(8,128)S(1)}, f32[8,32,128]{2,1,0:T(8,128)S(1)}, u32[]{:S(2)}, u32[]{:S(2)}) %collective-permute-start.22) | collective-permute-done | bytes 131104 | tf_op jit(solution)/shard_map/ppermute | solution.py:752
  79.5 0.6 collective-permute-done.23.ends_1
  80.0 1.6 %shard_map.97 = f32[2,16,16,128]{3,2,1,0:T(8,128)} custom-call(s32[6]{0:T(128)S(1)} %stack.15.place, f32[2,16,16,128]{3,2,1,0:T(8,128)S(1)} %get-tuple-element.85.unsmoothed, f32[2,16,16,128]{3,2,1,0:T(8,128)S(1)} %get-tuple-element.84.wz, f32[14,32,128]{2,1,0:T(8,128)S(1)} %get-tuple-element.86.maps_0, f32[14,32,128]{2,1,0:T(8,128)S(1)} %collective-permute-done.18.maps_1, ...), custom_call_target="tpu_custom_call" | custom-call | flops 1000000 | bytes 1000000 | tf_op jit(solution)/shard_map/pallas_call | solution.py:840
  (9 shorter events, 0.0 us)
Async XLA Ops:
  3.9 5.2 %collective-permute-start = (f32[8,16,128]{2,1,0:T(8,128)}, f32[8,16,128]{2,1,0:T(8,128)S(1)}, u32[]{:S(2)}, u32[]{:S(2)}) collective-permute-start(f32[8,16,128]{2,1,0:T(8,128)} %get-tuple-element.46), channel_id=1, source_target_pairs={{0,1},{1,0},{2,3},{3,2},{4,8},{5,9},{6,10},{7,11},{8,4},{9,5},{10,... | collective-permute-start | bytes 196616 | tf_op jit(solution)/shard_map/ppermute | solution.py:747
  5.6 3.5 %collective-permute-start.1 = (f32[8,16,128]{2,1,0:T(8,128)}, f32[8,16,128]{2,1,0:T(8,128)S(1)}, u32[]{:S(2)}, u32[]{:S(2)}) collective-permute-start(f32[8,16,128]{2,1,0:T(8,128)} %get-tuple-element.47), channel_id=1, source_target_pairs={{0,4},{4,0},{8,12},{12,8},{1,5},{5,1},{9,13},{13,9},{2,6},{6,2},{1... | collective-permute-start | bytes 196616 | tf_op jit(solution)/shard_map/ppermute | solution.py:746
  7.3 1.1 %copy-start = (f32[6,16,16,128]{3,2,1,0:T(8,128)S(1)}, f32[6,16,16,128]{3,2,1,0:T(8,128)}, u32[]{:S(2)}) copy-start(f32[6,16,16,128]{3,2,1,0:T(8,128)} %get-tuple-element.45.units) | copy-start | bytes 2359300
  9.1 8.2 %copy-start.4 = (f32[3,2,12]{2,1,0:T(2,128)S(1)}, f32[3,2,12]{2,1,0:T(2,128)}, u32[]{:S(2)}) copy-start(f32[3,2,12]{2,1,0:T(2,128)} %param.13) | copy-start | bytes 868
  9.1 8.2 %copy-start.3 = (s32[16,16,128]{2,1,0:T(8,128)S(1)}, s32[16,16,128]{2,1,0:T(8,128)}, u32[]{:S(2)}) copy-start(s32[16,16,128]{2,1,0:T(8,128)} %classes.1) | copy-start | bytes 393220
  10.2 12.5 %copy-start.2 = (f32[2,16,16,128]{3,2,1,0:T(8,128)S(1)}, f32[2,16,16,128]{3,2,1,0:T(8,128)}, u32[]{:S(2)}) copy-start(f32[2,16,16,128]{3,2,1,0:T(8,128)} %observed.1) | copy-start | bytes 786436
  10.2 10.1 %collective-permute-start.3 = (f32[704,128]{1,0:T(8,128)S(1)}, f32[704,128]{1,0:T(8,128)S(1)}, u32[]{:S(2)}, u32[]{:S(2)}) collective-permute-start(f32[704,128]{1,0:T(8,128)S(1)} %get-tuple-element.54), channel_id=1, source_target_pairs={{0,4},{4,0},{8,12},{12,8},{16,32},{20,36},{24,40},{28,44},{32,16},... | collective-permute-start | bytes 1081352 | tf_op jit(solution)/shard_map/ppermute | solution.py:747
  10.5 12.1 %collective-permute-start.4 = (f32[704,128]{1,0:T(8,128)S(1)}, f32[704,128]{1,0:T(8,128)S(1)}, u32[]{:S(2)}, u32[]{:S(2)}) collective-permute-start(f32[704,128]{1,0:T(8,128)S(1)} %get-tuple-element.59), channel_id=1, source_target_pairs={{0,16},{16,0},{32,48},{48,32},{64,80},{80,64},{96,112},{112,96},{1... | collective-permute-start | bytes 1081352 | tf_op jit(solution)/shard_map/ppermute | solution.py:746
  14.1 8.5 %collective-permute-start.5 = (f32[44,16,128]{2,1,0:T(8,128)S(1)}, f32[44,16,128]{2,1,0:T(8,128)S(1)}, u32[]{:S(2)}, u32[]{:S(2)}) collective-permute-start(f32[44,16,128]{2,1,0:T(8,128)S(1)} %get-tuple-element.60), channel_id=1, source_target_pairs={{0,4},{4,0},{8,12},{12,8},{1,2},{5,6},{9,10},{13,14},{2,1},{6,5},{... | collective-permute-start | bytes 1081352 | tf_op jit(solution)/shard_map/ppermute | solution.py:747
  14.1 18.2 %collective-permute-start.2 = (f32[44,16,128]{2,1,0:T(8,128)S(1)}, f32[44,16,128]{2,1,0:T(8,128)S(1)}, u32[]{:S(2)}, u32[]{:S(2)}) collective-permute-start(f32[44,16,128]{2,1,0:T(8,128)S(1)} %get-tuple-element.53), channel_id=1, source_target_pairs={{0,1},{1,0},{2,3},{3,2},{4,5},{5,4},{6,7},{7,6},{8,9},{9,8},{10,11... | collective-permute-start | bytes 1081352 | tf_op jit(solution)/shard_map/ppermute | solution.py:746
  17.3 17.9 %copy-start.1 = (f32[6,16,16,128]{3,2,1,0:T(8,128)S(1)}, f32[6,16,16,128]{3,2,1,0:T(8,128)}, u32[]{:S(2)}) copy-start(f32[6,16,16,128]{3,2,1,0:T(8,128)} %get-tuple-element.45.units) | copy-start | bytes 2359300
  23.3 6.0 %collective-permute-start.8 = (f32[2,120,128]{2,1,0:T(8,128)S(1)}, f32[2,120,128]{2,1,0:T(8,128)S(1)}, u32[]{:S(2)}, u32[]{:S(2)}) collective-permute-start(f32[2,120,128]{2,1,0:T(8,128)S(1)} %get-tuple-element.64), channel_id=1, source_target_pairs={{0,4},{4,0},{8,12},{12,8},{1,2},{5,6},{9,10},{13,14},{2,1},{6,5},{... | collective-permute-start | bytes 368648 | tf_op jit(solution)/shard_map/ppermute | solution.py:747
  23.4 9.0 %collective-permute-start.7 = (f32[14,32,128]{2,1,0:T(8,128)S(1)}, f32[14,32,128]{2,1,0:T(8,128)S(1)}, u32[]{:S(2)}, u32[]{:S(2)}) collective-permute-start(f32[14,32,128]{2,1,0:T(8,128)S(1)} %get-tuple-element.70.maps_0), channel_id=1, source_target_pairs={{0,16},{16,0},{32,48},{48,32},{64,80},{80,64},{96,112},{112,96},{1... | collective-permute-start | bytes 688136 | tf_op jit(solution)/shard_map/ppermute | solution.py:752
  25.2 22.8 %collective-permute-start.10 = (f32[14,32,128]{2,1,0:T(8,128)S(1)}, f32[14,32,128]{2,1,0:T(8,128)S(1)}, u32[]{:S(2)}, u32[]{:S(2)}) collective-permute-start(f32[14,32,128]{2,1,0:T(8,128)S(1)} %get-tuple-element.70.maps_0), channel_id=1, source_target_pairs={{0,48},{16,32},{32,16},{48,0},{64,112},{80,96},{96,80},{112,64},{1... | collective-permute-start | bytes 688136 | tf_op jit(solution)/shard_map/ppermute | solution.py:752
  27.9 20.1 %collective-permute-start.9 = (f32[14,32,128]{2,1,0:T(8,128)S(1)}, f32[14,32,128]{2,1,0:T(8,128)S(1)}, u32[]{:S(2)}, u32[]{:S(2)}) collective-permute-start(f32[14,32,128]{2,1,0:T(8,128)S(1)} %get-tuple-element.70.maps_0), channel_id=1, source_target_pairs={{0,32},{16,48},{32,0},{48,16},{64,96},{80,112},{96,64},{112,80},{1... | collective-permute-start | bytes 688136 | tf_op jit(solution)/shard_map/ppermute | solution.py:752
  29.3 5.9 %collective-permute-start.6 = (f32[2,120,128]{2,1,0:T(8,128)S(1)}, f32[2,120,128]{2,1,0:T(8,128)S(1)}, u32[]{:S(2)}, u32[]{:S(2)}) collective-permute-start(f32[2,120,128]{2,1,0:T(8,128)S(1)} %get-tuple-element.63), channel_id=1, source_target_pairs={{0,1},{1,0},{2,3},{3,2},{4,5},{5,4},{6,7},{7,6},{8,9},{9,8},{10,11... | collective-permute-start | bytes 368648 | tf_op jit(solution)/shard_map/ppermute | solution.py:746
  44.0 7.0 %collective-permute-start.11 = (f32[8,32,128]{2,1,0:T(8,128)S(1)}, f32[8,32,128]{2,1,0:T(8,128)S(1)}, u32[]{:S(2)}, u32[]{:S(2)}) collective-permute-start(f32[8,32,128]{2,1,0:T(8,128)S(1)} %get-tuple-element.72.ends_0), channel_id=1, source_target_pairs={{0,48},{16,32},{32,16},{48,0},{64,112},{80,96},{96,80},{112,64},{1... | collective-permute-start | bytes 393224 | tf_op jit(solution)/shard_map/ppermute | solution.py:752
  46.6 6.5 %collective-permute-start.12 = (f32[8,32,128]{2,1,0:T(8,128)S(1)}, f32[8,32,128]{2,1,0:T(8,128)S(1)}, u32[]{:S(2)}, u32[]{:S(2)}) collective-permute-start(f32[8,32,128]{2,1,0:T(8,128)S(1)} %get-tuple-element.72.ends_0), channel_id=1, source_target_pairs={{0,32},{16,48},{32,0},{48,16},{64,96},{80,112},{96,64},{112,80},{1... | collective-permute-start | bytes 393224 | tf_op jit(solution)/shard_map/ppermute | solution.py:752
  46.6 6.5 %collective-permute-start.13 = (f32[8,32,128]{2,1,0:T(8,128)S(1)}, f32[8,32,128]{2,1,0:T(8,128)S(1)}, u32[]{:S(2)}, u32[]{:S(2)}) collective-permute-start(f32[8,32,128]{2,1,0:T(8,128)S(1)} %get-tuple-element.72.ends_0), channel_id=1, source_target_pairs={{0,16},{16,0},{32,48},{48,32},{64,80},{80,64},{96,112},{112,96},{1... | collective-permute-start | bytes 393224 | tf_op jit(solution)/shard_map/ppermute | solution.py:752
  49.0 11.1 %collective-permute-start.15 = (f32[10,32,128]{2,1,0:T(8,128)S(1)}, f32[10,32,128]{2,1,0:T(8,128)S(1)}, u32[]{:S(2)}, u32[]{:S(2)}) collective-permute-start(f32[10,32,128]{2,1,0:T(8,128)S(1)} %get-tuple-element.77), channel_id=1, source_target_pairs={{0,64},{16,80},{32,96},{48,112},{64,0},{80,16},{96,32},{112,48},{1... | collective-permute-start | bytes 491528 | tf_op jit(solution)/shard_map/ppermute | solution.py:752
  53.8 19.3 %collective-permute-start.18 = (f32[14,32,128]{2,1,0:T(8,128)S(1)}, f32[14,32,128]{2,1,0:T(8,128)S(1)}, u32[]{:S(2)}, u32[]{:S(2)}) collective-permute-start(f32[14,32,128]{2,1,0:T(8,128)S(1)} %get-tuple-element.86.maps_0), channel_id=1, source_target_pairs={{0,1},{1,0},{2,3},{3,2},{4,5},{5,4},{6,7},{7,6},{8,9},{9,8},{10,11... | collective-permute-start | bytes 688136 | tf_op jit(solution)/shard_map/ppermute | solution.py:752
  56.0 5.0 %collective-permute-start.14 = (f32[8,32,128]{2,1,0:T(8,128)S(1)}, f32[8,32,128]{2,1,0:T(8,128)S(1)}, u32[]{:S(2)}, u32[]{:S(2)}) collective-permute-start(f32[8,32,128]{2,1,0:T(8,128)S(1)} %get-tuple-element.76.joint), channel_id=1, source_target_pairs={{0,64},{16,80},{32,96},{48,112},{64,0},{80,16},{96,32},{112,48},{1... | collective-permute-start | bytes 393224 | tf_op jit(solution)/shard_map/ppermute | solution.py:752
  57.3 17.8 %collective-permute-start.19 = (f32[14,32,128]{2,1,0:T(8,128)S(1)}, f32[14,32,128]{2,1,0:T(8,128)S(1)}, u32[]{:S(2)}, u32[]{:S(2)}) collective-permute-start(f32[14,32,128]{2,1,0:T(8,128)S(1)} %get-tuple-element.86.maps_0), channel_id=1, source_target_pairs={{0,2},{1,3},{2,0},{3,1},{4,6},{5,7},{6,4},{7,5},{8,10},{9,11},{10,... | collective-permute-start | bytes 688136 | tf_op jit(solution)/shard_map/ppermute | solution.py:752
  58.7 16.4 %collective-permute-start.20 = (f32[14,32,128]{2,1,0:T(8,128)S(1)}, f32[14,32,128]{2,1,0:T(8,128)S(1)}, u32[]{:S(2)}, u32[]{:S(2)}) collective-permute-start(f32[14,32,128]{2,1,0:T(8,128)S(1)} %get-tuple-element.86.maps_0), channel_id=1, source_target_pairs={{0,3},{1,2},{2,1},{3,0},{4,7},{5,6},{6,5},{7,4},{8,11},{9,10},{10,... | collective-permute-start | bytes 688136 | tf_op jit(solution)/shard_map/ppermute | solution.py:752
  62.1 1.3 %collective-permute-start.16 = (f32[88,128]{1,0:T(8,128)S(1)}, f32[88,128]{1,0:T(8,128)S(1)}, u32[]{:S(2)}, u32[]{:S(2)}) collective-permute-start(f32[88,128]{1,0:T(8,128)S(1)} %get-tuple-element.83.own), channel_id=1, source_target_pairs={{0,4},{4,0},{8,12},{12,8},{1,5},{5,1},{9,13},{13,9},{2,6},{6,2},{1... | collective-permute-start | bytes 135176 | tf_op jit(solution)/shard_map/ppermute | solution.py:752
  64.0 5.6 %collective-permute-start.17 = (f32[88,128]{1,0:T(8,128)S(1)}, f32[88,128]{1,0:T(8,128)S(1)}, u32[]{:S(2)}, u32[]{:S(2)}) collective-permute-start(f32[88,128]{1,0:T(8,128)S(1)} %shard_map.95.joint), channel_id=1, source_target_pairs={{0,8},{4,12},{8,0},{12,4},{1,9},{5,13},{9,1},{13,5},{2,10},{6,14},... | collective-permute-start | bytes 135176 | tf_op jit(solution)/shard_map/ppermute | solution.py:752
  70.9 7.6 %collective-permute-start.21 = (f32[8,32,128]{2,1,0:T(8,128)S(1)}, f32[8,32,128]{2,1,0:T(8,128)S(1)}, u32[]{:S(2)}, u32[]{:S(2)}) collective-permute-start(f32[8,32,128]{2,1,0:T(8,128)S(1)} %get-tuple-element.87.ends_0), channel_id=1, source_target_pairs={{0,3},{1,2},{2,1},{3,0},{4,7},{5,6},{6,5},{7,4},{8,11},{9,10},{10,... | collective-permute-start | bytes 393224 | tf_op jit(solution)/shard_map/ppermute | solution.py:752
  72.4 7.0 %collective-permute-start.22 = (f32[8,32,128]{2,1,0:T(8,128)S(1)}, f32[8,32,128]{2,1,0:T(8,128)S(1)}, u32[]{:S(2)}, u32[]{:S(2)}) collective-permute-start(f32[8,32,128]{2,1,0:T(8,128)S(1)} %get-tuple-element.87.ends_0), channel_id=1, source_target_pairs={{0,2},{1,3},{2,0},{3,1},{4,6},{5,7},{6,4},{7,5},{8,10},{9,11},{10,... | collective-permute-start | bytes 393224 | tf_op jit(solution)/shard_map/ppermute | solution.py:752
  73.2 6.8 %collective-permute-start.23 = (f32[8,32,128]{2,1,0:T(8,128)S(1)}, f32[8,32,128]{2,1,0:T(8,128)S(1)}, u32[]{:S(2)}, u32[]{:S(2)}) collective-permute-start(f32[8,32,128]{2,1,0:T(8,128)S(1)} %get-tuple-element.87.ends_0), channel_id=1, source_target_pairs={{0,1},{1,0},{2,3},{3,2},{4,5},{5,4},{6,7},{7,6},{8,9},{9,8},{10,11... | collective-permute-start | bytes 393224 | tf_op jit(solution)/shard_map/ppermute | solution.py:752
